TPU v7x, 32 devices: a whole 2x2x4 slice. The times are simulated.
32 devices in a mesh: lon: 2 (over x), lat: 4 (over z), grp: 4 (over y, core).
Axes of the slice: x: 2, y: 2, z: 4, core: 2. Of those that a mesh axis runs over, the one named last changes fastest.
Arguments:
- sea_surface: float32 [16, 256, 1024], P('grp', 'lat', 'lon'), may hold values from -6 to 6
- velocity: float32 [2, 16, 256, 1024], P(None, 'grp', 'lat', 'lon'), may hold values from -2 to 2
- levels: int32 [256, 1024], P('lat', 'lon'), may hold values from 1 to 50
- wind_basis: bfloat16 [16, 256, 1024], P(None, 'lat', 'lon'), may hold values from -1.5 to 1.5
- proposals: float32 [16, 16], replicated, may hold values from -4 to 4
- member_ids: int32 [16], replicated, may hold values from 0 to 15, each once
- conv_weight: bfloat16 [128, 256], replicated, may hold values from -0.5 to 0.5
- couple_in: float32 [264, 512], replicated, may hold values from -0.375 to 0.375
- couple_in_bias: float32 [512], replicated, may hold values from -3 to 3
- couple_out: float32 [512, 16], replicated, may hold values from -0.25 to 0.25
- couple_out_bias: float32 [16], replicated, may hold values from -3 to 3
Outputs:
- surface_out: float32 [16, 256, 1024], P('grp', 'lat', 'lon')
- velocity_out: float32 [2, 16, 256, 1024], P(None, 'grp', 'lat', 'lon')
- summary: float32 [2, 4, 4, 16, 256], P('lon', 'lat', 'grp')
- weight_step: float32 [176656], replicated
Inputs may be any that keep to these rules, and one draw needn't show every extreme that they name: member_ids is a permutation of 0 to 15.
All inputs are finite; a program needn't handle non-finite values.
Results may differ from a plain program's by a relative error of at most 0.0031.
Values may be sent and summed in bfloat16 or wider, within the bound.
No kernel may reach another device: no remote copies, remote signals or barrier semaphores. Data moves between devices by JAX's collectives and lax.ppermute only.
A program may use at most 128 MiB of HBM per device.

v0:
```python
from functools import partial
import math

import jax
import jax.numpy as jnp
from jax import lax
from jax.sharding import PartitionSpec as P

STEPS = 8
NLEV = 50
PH = 8
PW = 16


GRAVITY = 0.45
DRAG_RATE = 0.02
CORI_BASE = 0.05
CORI_SLOPE = 0.1
WIND_SCALE = 0.05
EPSILON = 1e-06
PRECISE = lax.Precision.HIGHEST


def extended(value, sides, width, wrap):
    for axis, dim in sides:
        count, length = (lax.axis_size(axis), value.shape[dim])
        up = [(i, (i + 1) % count) for i in range(count if wrap else count - 1)]
        down = [(j, i) for i, j in up]
        last = lax.slice_in_dim(value, length - width, length, axis=dim)
        initial = lax.slice_in_dim(value, 0, width, axis=dim)
        before = lax.ppermute(last, axis, up)
        after = lax.ppermute(initial, axis, down)
        value = jnp.concatenate([before, value, after], axis=dim)
    return value


def passed_along(value, axis, steps):
    count = lax.axis_size(axis)
    pairs = [(source, (source + steps) % count) for source in range(count)]
    return lax.ppermute(value, axis, pairs)


def from_behind(block, axis, distance):
    devices = range(lax.axis_size(axis))
    route = [(i - distance, i) for i in devices if i - distance in devices]
    return lax.ppermute(block, axis, route)


def to_patches(band_rows, kernel_rows, kernel_cols):
    count, height, breadth = band_rows.shape
    blocks = band_rows.reshape(
        count, height // kernel_rows, kernel_rows, breadth // kernel_cols, kernel_cols
    )
    return blocks.transpose(0, 1, 3, 2, 4).reshape(-1, kernel_rows * kernel_cols)


def flow_loss(params, w_in, b_in, w_out, b_out, summary):
    half_count = params.shape[1] // 2
    lower = params[:, :half_count]
    upper = params[:, half_count:]
    context = jnp.concatenate([lower, summary], axis=1)
    hidden = jnp.tanh(jnp.dot(context, w_in, precision=PRECISE) + b_in)
    out_raw = jnp.dot(hidden, w_out, precision=PRECISE) + b_out
    log_scale = jnp.tanh(out_raw[:, :half_count])
    latent = upper * jnp.exp(log_scale) + out_raw[:, half_count:]
    return jnp.sum(0.5 * latent * latent - log_scale)


def pick_rows(proposals, member_ids, members):
    slot_ids = jnp.arange(member_ids.shape[0], dtype=jnp.int32)
    chosen = jnp.sum(
        jnp.where(members[:, None] == slot_ids[None, :], member_ids[None, :], 0), axis=1
    )
    onehot = (chosen[:, None] == slot_ids[None, :]).astype(jnp.float32)
    return jnp.dot(onehot, proposals, precision=PRECISE)


def depth_rim(sea_depth, rim_width):
    widened = extended(sea_depth, (("lon", 1),), rim_width, True)
    return extended(widened, (("lat", 0),), rim_width, False)


def flow_rim(velocities):
    widened = extended(velocities, (("lon", 3),), 1, True)
    return extended(widened, (("lat", 2),), 1, False)


def level_lower(new_level):
    west_edge = passed_along(new_level[:, :, -1:], "lon", 1)
    south_edge = from_behind(new_level[:, -1:, :], "lat", 1)
    west_level = jnp.concatenate([west_edge, new_level[:, :, :-1]], axis=2)
    south_level = jnp.concatenate([south_edge, new_level[:, :-1, :]], axis=1)
    return (west_level, south_level)


def velocity_update(
    east_flow,
    north_flow,
    east_wide,
    north_wide,
    new_level,
    west_level,
    south_level,
    cori_u,
    cori_v,
    forcing,
):
    v_mean = 0.25 * (
        north_wide[:, 1:-1, 1:-1]
        + north_wide[:, 2:, 1:-1]
        + north_wide[:, 1:-1, :-2]
        + north_wide[:, 2:, :-2]
    )
    u_mean = 0.25 * (
        east_wide[:, 1:-1, 1:-1]
        + east_wide[:, 1:-1, 2:]
        + east_wide[:, :-2, 1:-1]
        + east_wide[:, :-2, 2:]
    )
    new_east = (
        east_flow
        + cori_u * v_mean
        - GRAVITY * (new_level - west_level)
        - DRAG_RATE * east_flow
        + forcing
    )
    new_north = (
        north_flow - cori_v * u_mean - GRAVITY * (new_level - south_level) - DRAG_RATE * north_flow
    )
    return (new_east, new_north)


def shards(
    sea_surface,
    velocity,
    levels,
    wind_basis,
    proposals,
    member_ids,
    conv_weight,
    couple_in,
    couple_in_bias,
    couple_out,
    couple_out_bias,
):
    members_here, tile_rows, tile_cols = sea_surface.shape
    lat_count = lax.axis_size("lat")
    lon_count = lax.axis_size("lon")
    lat_index = lax.axis_index("lat")
    lon_index = lax.axis_index("lon")
    grp_index = lax.axis_index("grp")
    total_rows = tile_rows * lat_count
    total_cols = tile_cols * lon_count
    sea_depth = levels.astype(jnp.float32) / NLEV
    rim_width = 1
    depth_wide = depth_rim(sea_depth, rim_width)
    row_index = (lat_index * tile_rows + jnp.arange(tile_rows, dtype=jnp.int32)).astype(
        jnp.float32
    )[:, None]
    cori_u = CORI_BASE + CORI_SLOPE * (row_index + 0.5) / total_rows
    cori_v = CORI_BASE + CORI_SLOPE * row_index / total_rows
    local_members = grp_index * members_here + jnp.arange(members_here, dtype=jnp.int32)
    coeff_rows = pick_rows(proposals, member_ids, local_members).astype(jnp.bfloat16)
    forcing = WIND_SCALE * jnp.dot(
        coeff_rows, wind_basis.reshape(wind_basis.shape[0], -1), preferred_element_type=jnp.float32
    ).reshape(members_here, tile_rows, tile_cols)
    sea_level, east_flow, north_flow = (sea_surface, velocity[0], velocity[1])
    frames = []
    hu_face = 0.5 * (depth_wide[1:-1, 1:] + depth_wide[1:-1, :-1])
    hv_face = 0.5 * (depth_wide[1:, 1:-1] + depth_wide[:-1, 1:-1])
    for step_index in range(STEPS):
        velocities = flow_rim(jnp.stack([east_flow, north_flow]))
        east_wide, north_wide = (velocities[0], velocities[1])
        flux_x = hu_face * east_wide[:, 1:-1, 1:]
        flux_y = hv_face * north_wide[:, 1:, 1:-1]
        new_level = sea_level - (
            flux_x[:, :, 1:] - flux_x[:, :, :-1] + flux_y[:, 1:, :] - flux_y[:, :-1, :]
        )
        west_level, south_level = level_lower(new_level)
        east_flow, north_flow = velocity_update(
            east_flow,
            north_flow,
            east_wide,
            north_wide,
            new_level,
            west_level,
            south_level,
            cori_u,
            cori_v,
            forcing,
        )
        sea_level = new_level
        frames.append(sea_level.astype(jnp.bfloat16))
    frames = jnp.stack(frames)
    all_items = frames.shape[0] * members_here
    item_count = all_items // lon_count
    feat_count = conv_weight.shape[1]
    inv_root = 1.0 / math.sqrt(tile_rows // PH * (total_cols // PW))
    item_ids = lon_index * item_count + jnp.arange(item_count, dtype=jnp.int32)
    sample_members = grp_index * members_here + item_ids % members_here
    params = pick_rows(proposals, member_ids, sample_members)
    loss_fn = partial(flow_loss, params)
    blocks = frames.reshape(lon_count, item_count, tile_rows, tile_cols)
    band_rows = lax.all_to_all(blocks, "lon", split_axis=0, concat_axis=3, tiled=True)[0]
    patch_rows = to_patches(band_rows, PH, PW)
    activation = jnp.tanh(
        jnp.dot(patch_rows, conv_weight, preferred_element_type=jnp.float32)
    ).reshape(item_count, -1, feat_count)
    summary = jnp.sum(activation, axis=1) * inv_root
    loss_value, pullback = jax.vjp(
        loss_fn, couple_in, couple_in_bias, couple_out, couple_out_bias, summary
    )
    g_in, g_in_b, g_out, g_out_b, d_summary = pullback(jnp.ones_like(loss_value))
    d_pre = (
        ((d_summary * inv_root)[:, None, :] * (1.0 - activation * activation))
        .astype(jnp.bfloat16)
        .reshape(-1, feat_count)
    )
    g_conv = lax.dot_general(
        patch_rows, d_pre, (((0,), (0,)), ((), ())), preferred_element_type=jnp.float32
    )
    grad_local = jnp.concatenate(
        [g_conv.reshape(-1), g_in.reshape(-1), g_in_b, g_out.reshape(-1), g_out_b]
    )
    grad_total = lax.psum(grad_local, ("lon", "lat", "grp"))
    weight_step = -grad_total / jnp.sqrt(jnp.mean(grad_total * grad_total) + EPSILON)
    return (
        sea_level,
        jnp.stack([east_flow, north_flow]),
        summary.reshape(1, 1, 1, item_count, feat_count),
        weight_step,
    )


def solution(mesh):
    in_specs = (
        P("grp", "lat", "lon"),
        P(None, "grp", "lat", "lon"),
        P("lat", "lon"),
        P(None, "lat", "lon"),
        P(),
        P(),
        P(),
        P(),
        P(),
        P(),
        P(),
    )
    out_specs = (
        P("grp", "lat", "lon"),
        P(None, "grp", "lat", "lon"),
        P("lon", "lat", "grp", None, None),
        P(),
    )
    return jax.shard_map(shards, mesh=mesh, in_specs=in_specs, out_specs=out_specs, check_vma=False)
```

profile of v0, /device:TPU:0, one launch (start us, length us, event | category | flops | bytes accessed | tf_op | source)
XLA Modules:
  0.0 491.8 jit_solution(12430370337397486672)
XLA Ops:
  9.4 3.0 collective-permute-start.3
  15.0 10.4 %collective-permute-done = f32[64,1]{1,0:T(8,128)S(1)} collective-permute-done((f32[64,1]{1,0:T(8,128)S(1)}, f32[64,1]{1,0:T(8,128)S(1)}, u32[]{:S(2)}, u32[]{:S(2)}) %collective-permute-start) | collective-permute-done | bytes 288 | tf_op jit(solution)/shard_map/ppermute | solution.py:32
  25.8 3.7 collective-permute-start.7
  32.4 5.2 %collective-permute-start.4 = (f32[2,4,1,514]{3,1,2,0:T(4,128)S(1)}, f32[2,4,1,514]{3,1,2,0:T(4,128)S(1)}, u32[]{:S(2)}, u32[]{:S(2)}) collective-permute-start(f32[2,4,1,514]{3,1,2,0:T(4,128)S(1)} %get-tuple-element.50), channel_id=1, source_target_pairs={{0,4},{4,8},{8,12},{1,5},{5,9},{9,13},{2,6},{6,10},{10,14},{3,7},{... | collective-permute-start | bytes 49352 | tf_op jit(solution)/shard_map/ppermute | solution.py:31
  43.6 4.2 collective-permute-start.9
  49.1 2.5 fusion.85
  53.9 5.1 %collective-permute-done.11 = f32[2,4,64,1]{3,1,2,0:T(4,128)S(1)} collective-permute-done((f32[2,4,64,1]{3,1,2,0:T(4,128)S(1)}, f32[2,4,64,1]{3,1,2,0:T(4,128)S(1)}, u32[]{:S(2)}, u32[]{:S(2)}) %collective-permute-start.11) | collective-permute-done | bytes 2080 | tf_op jit(solution)/shard_map/ppermute | solution.py:32
  59.0 2.8 collective-permute-done.10
  63.2 4.5 collective-permute-start.12
  71.6 4.2 collective-permute-start.15
  76.5 5.8 %collective-permute-done.14 = f32[4,64,1]{2,0,1:T(4,128)S(1)} collective-permute-done((f32[4,64,1]{2,0,1:T(4,128)S(1)}, f32[4,64,1]{2,0,1:T(4,128)S(1)}, u32[]{:S(2)}, u32[]{:S(2)}) %collective-permute-start.14) | collective-permute-done | bytes 1056 | tf_op jit(solution)/shard_map/ppermute | solution.py:40
  87.0 4.3 collective-permute-done.17
  91.3 2.8 collective-permute-done.16
  95.5 4.7 collective-permute-start.18
  103.9 4.2 collective-permute-start.21
  108.8 5.2 %collective-permute-done.20 = f32[4,64,1]{2,0,1:T(4,128)S(1)} collective-permute-done((f32[4,64,1]{2,0,1:T(4,128)S(1)}, f32[4,64,1]{2,0,1:T(4,128)S(1)}, u32[]{:S(2)}, u32[]{:S(2)}) %collective-permute-start.20) | collective-permute-done | bytes 1056 | tf_op jit(solution)/shard_map/ppermute | solution.py:40
  118.7 4.3 collective-permute-done.23
  123.0 2.8 collective-permute-done.22
  127.2 4.5 collective-permute-start.24
  135.5 4.2 collective-permute-start.27
  140.5 4.4 collective-permute-done.26
  149.6 4.3 collective-permute-done.29
  153.9 3.3 collective-permute-done.28
  158.6 4.8 collective-permute-start.30
  167.2 4.4 collective-permute-start.33
  172.4 4.4 collective-permute-done.32
  181.4 5.8 %collective-permute-done.35 = f32[2,4,64,1]{3,1,2,0:T(4,128)S(1)} collective-permute-done((f32[2,4,64,1]{3,1,2,0:T(4,128)S(1)}, f32[2,4,64,1]{3,1,2,0:T(4,128)S(1)}, u32[]{:S(2)}, u32[]{:S(2)}) %collective-permute-start.35) | collective-permute-done | bytes 2080 | tf_op jit(solution)/shard_map/ppermute | solution.py:32
  187.2 2.8 collective-permute-done.34
  191.4 4.6 collective-permute-start.36
  199.7 4.2 collective-permute-start.39
  204.7 4.4 collective-permute-done.38
  213.7 4.3 collective-permute-done.41
  218.0 4.7 collective-permute-done.40
  224.2 4.9 collective-permute-start.42
  232.8 4.2 collective-permute-start.45
  237.8 4.4 collective-permute-done.44
  246.8 7.2 %collective-permute-done.47 = f32[2,4,64,1]{3,1,2,0:T(4,128)S(1)} collective-permute-done((f32[2,4,64,1]{3,1,2,0:T(4,128)S(1)}, f32[2,4,64,1]{3,1,2,0:T(4,128)S(1)}, u32[]{:S(2)}, u32[]{:S(2)}) %collective-permute-start.47) | collective-permute-done | bytes 2080 | tf_op jit(solution)/shard_map/ppermute | solution.py:32
  254.1 5.6 %collective-permute-done.46 = f32[2,4,64,1]{3,1,2,0:T(4,128)S(1)} collective-permute-done((f32[2,4,64,1]{3,1,2,0:T(4,128)S(1)}, f32[2,4,64,1]{3,1,2,0:T(4,128)S(1)}, u32[]{:S(2)}, u32[]{:S(2)}) %collective-permute-start.46) | collective-permute-done | bytes 2080 | tf_op jit(solution)/shard_map/ppermute | solution.py:31
  261.1 4.6 collective-permute-start.48
  272.2 4.8 all-to-all-start
  282.6 5.0 %collective-permute-start.51 = (f32[4,1,512]{2,0,1:T(4,128)}, f32[4,1,512]{2,0,1:T(4,128)}, u32[]{:S(2)}, u32[]{:S(2)}) collective-permute-start(f32[4,1,512]{2,0,1:T(4,128)} %slice.989), channel_id=1, source_target_pairs={{0,4},{4,8},{8,12},{1,5},{5,9},{9,13},{2,6},{6,10},{10,14},{3,7},{... | collective-permute-start | bytes 24584 | tf_op jit(solution)/shard_map/ppermute | solution.py:46
  287.6 4.4 all-to-all-done
  292.1 3.8 copy.46
  295.8 14.4 %reshape_squeeze.3 = bf16[16,8,8,64,16]{4,3,2,1,0:T(8,128)(2,1)} reshape(bf16[1,16,64,2,512]{4,3,2,1,0:T(2,128)(2,1)S(1)} %copy.46) | data formatting | bytes 4194304 | tf_op jit(solution)/shard_map/reshape;squeeze | solution.py:51
  310.2 16.6 %copy.47 = bf16[16,8,64,8,16]{2,1,0,4,3:T(8,128)(2,1)} copy(bf16[16,8,64,8,16]{4,2,3,1,0:T(8,128)(2,1)} %bitcast.134) | data formatting | bytes 4194304 | tf_op jit(solution)/shard_map/transpose | solution.py:54
  326.8 5.7 %reshape.101 = bf16[8192,128]{0,1:T(8,128)(2,1)S(1)} reshape(bf16[16,8,64,8,16]{2,1,0,4,3:T(8,128)(2,1)} %copy.47) | data formatting | bytes 4194304 | tf_op jit(solution)/shard_map/reshape | solution.py:54
  350.0 3.3 fusion.15
  354.8 125.1 %all-reduce.4.cloned.1.call-done = f32[176656]{0:T(1024)} async-done(((f32[176656]{0:T(1024)}), f32[176656]{0:T(1024)}) %all-reduce.4.cloned.1.call-update) | async-done | bytes 706640 | tf_op jit(solution)/shard_map/psum | solution.py:225
  (230 shorter events, 116.5 us)
Async XLA Ops:
  9.4 21.6 %collective-permute-start.3 = (f32[2,4,64,1]{3,1,2,0:T(4,128)S(1)}, f32[2,4,64,1]{3,1,2,0:T(4,128)S(1)}, u32[]{:S(2)}, u32[]{:S(2)}) collective-permute-start(f32[2,4,64,1]{3,1,2,0:T(4,128)S(1)} %get-tuple-element.83), channel_id=1, source_target_pairs={{16,0},{0,16},{17,1},{1,17},{18,2},{2,18},{19,3},{3,19},{20,4},{4,... | collective-permute-start | bytes 6152 | tf_op jit(solution)/shard_map/ppermute | solution.py:32
  12.4 18.6 %collective-permute-start.2 = (f32[2,4,64,1]{3,1,2,0:T(4,128)S(1)}, f32[2,4,64,1]{3,1,2,0:T(4,128)S(1)}, u32[]{:S(2)}, u32[]{:S(2)}) collective-permute-start(f32[2,4,64,1]{3,1,2,0:T(4,128)S(1)} %get-tuple-element.82), channel_id=1, source_target_pairs={{0,16},{16,0},{1,17},{17,1},{2,18},{18,2},{3,19},{19,3},{4,20},{20... | collective-permute-start | bytes 6152 | tf_op jit(solution)/shard_map/ppermute | solution.py:31
  12.6 12.8 %collective-permute-start = (f32[64,1]{1,0:T(8,128)S(1)}, f32[64,1]{1,0:T(8,128)S(1)}, u32[]{:S(2)}, u32[]{:S(2)}) collective-permute-start(f32[64,1]{1,0:T(8,128)S(1)} %get-tuple-element.101), channel_id=1, source_target_pairs={{16,0},{0,16},{17,1},{1,17},{18,2},{2,18},{19,3},{3,19},{20,4},{4,... | collective-permute-start | bytes 776 | tf_op jit(solution)/shard_map/ppermute | solution.py:32
  14.5 11.2 %collective-permute-start.1 = (f32[64,1]{1,0:T(8,128)S(1)}, f32[64,1]{1,0:T(8,128)S(1)}, u32[]{:S(2)}, u32[]{:S(2)}) collective-permute-start(f32[64,1]{1,0:T(8,128)S(1)} %get-tuple-element.100), channel_id=1, source_target_pairs={{0,16},{16,0},{1,17},{17,1},{2,18},{18,2},{3,19},{19,3},{4,20},{20... | collective-permute-start | bytes 776 | tf_op jit(solution)/shard_map/ppermute | solution.py:31
  25.8 11.7 %collective-permute-start.7 = (f32[1,514]{1,0:T(1,128)S(1)}, f32[1,514]{1,0:T(1,128)S(1)}, u32[]{:S(2)}, u32[]{:S(2)}) collective-permute-start(f32[1,514]{1,0:T(1,128)S(1)} %get-tuple-element.99), channel_id=1, source_target_pairs={{0,4},{4,8},{8,12},{1,5},{5,9},{9,13},{2,6},{6,10},{10,14},{3,7},{... | collective-permute-start | bytes 6176 | tf_op jit(solution)/shard_map/ppermute | solution.py:31
  29.5 8.0 %collective-permute-start.6 = (f32[1,514]{1,0:T(1,128)S(1)}, f32[1,514]{1,0:T(1,128)S(1)}, u32[]{:S(2)}, u32[]{:S(2)}) collective-permute-start(f32[1,514]{1,0:T(1,128)S(1)} %get-tuple-element.98), channel_id=1, source_target_pairs={{4,0},{8,4},{12,8},{5,1},{9,5},{13,9},{6,2},{10,6},{14,10},{7,3},{... | collective-permute-start | bytes 6176 | tf_op jit(solution)/shard_map/ppermute | solution.py:32
  31.1 6.6 %collective-permute-start.5 = (f32[2,4,1,514]{3,1,2,0:T(4,128)S(1)}, f32[2,4,1,514]{3,1,2,0:T(4,128)S(1)}, u32[]{:S(2)}, u32[]{:S(2)}) collective-permute-start(f32[2,4,1,514]{3,1,2,0:T(4,128)S(1)} %get-tuple-element.51), channel_id=1, source_target_pairs={{4,0},{8,4},{12,8},{5,1},{9,5},{13,9},{6,2},{10,6},{14,10},{7,3},{... | collective-permute-start | bytes 49352 | tf_op jit(solution)/shard_map/ppermute | solution.py:32
  32.4 6.6 %collective-permute-start.4 = (f32[2,4,1,514]{3,1,2,0:T(4,128)S(1)}, f32[2,4,1,514]{3,1,2,0:T(4,128)S(1)}, u32[]{:S(2)}, u32[]{:S(2)}) collective-permute-start(f32[2,4,1,514]{3,1,2,0:T(4,128)S(1)} %get-tuple-element.50), channel_id=1, source_target_pairs={{0,4},{4,8},{8,12},{1,5},{5,9},{9,13},{2,6},{6,10},{10,14},{3,7},{... | collective-permute-start | bytes 49352 | tf_op jit(solution)/shard_map/ppermute | solution.py:31
  51.8 7.2 %collective-permute-start.11 = (f32[2,4,64,1]{3,1,2,0:T(4,128)S(1)}, f32[2,4,64,1]{3,1,2,0:T(4,128)S(1)}, u32[]{:S(2)}, u32[]{:S(2)}) collective-permute-start(f32[2,4,64,1]{3,1,2,0:T(4,128)S(1)} %get-tuple-element.81), channel_id=1, source_target_pairs={{16,0},{0,16},{17,1},{1,17},{18,2},{2,18},{19,3},{3,19},{20,4},{4,... | collective-permute-start | bytes 6152 | tf_op jit(solution)/shard_map/ppermute | solution.py:32
  52.4 9.4 %collective-permute-start.10 = (f32[2,4,64,1]{3,1,2,0:T(4,128)S(1)}, f32[2,4,64,1]{3,1,2,0:T(4,128)S(1)}, u32[]{:S(2)}, u32[]{:S(2)}) collective-permute-start(f32[2,4,64,1]{3,1,2,0:T(4,128)S(1)} %get-tuple-element.80), channel_id=1, source_target_pairs={{0,16},{16,0},{1,17},{17,1},{2,18},{18,2},{3,19},{19,3},{4,20},{20... | collective-permute-start | bytes 6152 | tf_op jit(solution)/shard_map/ppermute | solution.py:31
  61.9 5.9 %collective-permute-start.13 = (f32[2,4,1,514]{3,1,2,0:T(4,128)S(1)}, f32[2,4,1,514]{3,1,2,0:T(4,128)S(1)}, u32[]{:S(2)}, u32[]{:S(2)}) collective-permute-start(f32[2,4,1,514]{3,1,2,0:T(4,128)S(1)} %get-tuple-element.47), channel_id=1, source_target_pairs={{4,0},{8,4},{12,8},{5,1},{9,5},{13,9},{6,2},{10,6},{14,10},{7,3},{... | collective-permute-start | bytes 49352 | tf_op jit(solution)/shard_map/ppermute | solution.py:32
  63.2 6.0 %collective-permute-start.12 = (f32[2,4,1,514]{3,1,2,0:T(4,128)S(1)}, f32[2,4,1,514]{3,1,2,0:T(4,128)S(1)}, u32[]{:S(2)}, u32[]{:S(2)}) collective-permute-start(f32[2,4,1,514]{3,1,2,0:T(4,128)S(1)} %get-tuple-element.46), channel_id=1, source_target_pairs={{0,4},{4,8},{8,12},{1,5},{5,9},{9,13},{2,6},{6,10},{10,14},{3,7},{... | collective-permute-start | bytes 49352 | tf_op jit(solution)/shard_map/ppermute | solution.py:31
  71.6 10.8 %collective-permute-start.15 = (f32[4,1,512]{2,0,1:T(4,128)S(1)}, f32[4,1,512]{2,0,1:T(4,128)S(1)}, u32[]{:S(2)}, u32[]{:S(2)}) collective-permute-start(f32[4,1,512]{2,0,1:T(4,128)S(1)} %slice.869), channel_id=1, source_target_pairs={{0,4},{4,8},{8,12},{1,5},{5,9},{9,13},{2,6},{6,10},{10,14},{3,7},{... | collective-permute-start | bytes 24584 | tf_op jit(solution)/shard_map/ppermute | solution.py:46
  75.9 6.4 %collective-permute-start.14 = (f32[4,64,1]{2,0,1:T(4,128)S(1)}, f32[4,64,1]{2,0,1:T(4,128)S(1)}, u32[]{:S(2)}, u32[]{:S(2)}) collective-permute-start(f32[4,64,1]{2,0,1:T(4,128)S(1)} %slice.863), channel_id=1, source_target_pairs={{0,16},{16,0},{1,17},{17,1},{2,18},{18,2},{3,19},{19,3},{4,20},{20... | collective-permute-start | bytes 3080 | tf_op jit(solution)/shard_map/ppermute | solution.py:40
  84.9 6.4 %collective-permute-start.17 = (f32[2,4,64,1]{3,1,2,0:T(4,128)S(1)}, f32[2,4,64,1]{3,1,2,0:T(4,128)S(1)}, u32[]{:S(2)}, u32[]{:S(2)}) collective-permute-start(f32[2,4,64,1]{3,1,2,0:T(4,128)S(1)} %get-tuple-element.79), channel_id=1, source_target_pairs={{16,0},{0,16},{17,1},{1,17},{18,2},{2,18},{19,3},{3,19},{20,4},{4,... | collective-permute-start | bytes 6152 | tf_op jit(solution)/shard_map/ppermute | solution.py:32
  85.5 8.6 %collective-permute-start.16 = (f32[2,4,64,1]{3,1,2,0:T(4,128)S(1)}, f32[2,4,64,1]{3,1,2,0:T(4,128)S(1)}, u32[]{:S(2)}, u32[]{:S(2)}) collective-permute-start(f32[2,4,64,1]{3,1,2,0:T(4,128)S(1)} %get-tuple-element.78), channel_id=1, source_target_pairs={{0,16},{16,0},{1,17},{17,1},{2,18},{18,2},{3,19},{19,3},{4,20},{20... | collective-permute-start | bytes 6152 | tf_op jit(solution)/shard_map/ppermute | solution.py:31
  94.2 6.0 %collective-permute-start.19 = (f32[2,4,1,514]{3,1,2,0:T(4,128)S(1)}, f32[2,4,1,514]{3,1,2,0:T(4,128)S(1)}, u32[]{:S(2)}, u32[]{:S(2)}) collective-permute-start(f32[2,4,1,514]{3,1,2,0:T(4,128)S(1)} %get-tuple-element.45), channel_id=1, source_target_pairs={{4,0},{8,4},{12,8},{5,1},{9,5},{13,9},{6,2},{10,6},{14,10},{7,3},{... | collective-permute-start | bytes 49352 | tf_op jit(solution)/shard_map/ppermute | solution.py:32
  95.5 6.0 %collective-permute-start.18 = (f32[2,4,1,514]{3,1,2,0:T(4,128)S(1)}, f32[2,4,1,514]{3,1,2,0:T(4,128)S(1)}, u32[]{:S(2)}, u32[]{:S(2)}) collective-permute-start(f32[2,4,1,514]{3,1,2,0:T(4,128)S(1)} %get-tuple-element.44), channel_id=1, source_target_pairs={{0,4},{4,8},{8,12},{1,5},{5,9},{9,13},{2,6},{6,10},{10,14},{3,7},{... | collective-permute-start | bytes 49352 | tf_op jit(solution)/shard_map/ppermute | solution.py:31
  103.9 10.2 %collective-permute-start.21 = (f32[4,1,512]{2,0,1:T(4,128)S(1)}, f32[4,1,512]{2,0,1:T(4,128)S(1)}, u32[]{:S(2)}, u32[]{:S(2)}) collective-permute-start(f32[4,1,512]{2,0,1:T(4,128)S(1)} %slice.889), channel_id=1, source_target_pairs={{0,4},{4,8},{8,12},{1,5},{5,9},{9,13},{2,6},{6,10},{10,14},{3,7},{... | collective-permute-start | bytes 24584 | tf_op jit(solution)/shard_map/ppermute | solution.py:46
  108.2 5.8 %collective-permute-start.20 = (f32[4,64,1]{2,0,1:T(4,128)S(1)}, f32[4,64,1]{2,0,1:T(4,128)S(1)}, u32[]{:S(2)}, u32[]{:S(2)}) collective-permute-start(f32[4,64,1]{2,0,1:T(4,128)S(1)} %slice.883), channel_id=1, source_target_pairs={{0,16},{16,0},{1,17},{17,1},{2,18},{18,2},{3,19},{19,3},{4,20},{20... | collective-permute-start | bytes 3080 | tf_op jit(solution)/shard_map/ppermute | solution.py:40
  116.6 6.4 %collective-permute-start.23 = (f32[2,4,64,1]{3,1,2,0:T(4,128)S(1)}, f32[2,4,64,1]{3,1,2,0:T(4,128)S(1)}, u32[]{:S(2)}, u32[]{:S(2)}) collective-permute-start(f32[2,4,64,1]{3,1,2,0:T(4,128)S(1)} %get-tuple-element.77), channel_id=1, source_target_pairs={{16,0},{0,16},{17,1},{1,17},{18,2},{2,18},{19,3},{3,19},{20,4},{4,... | collective-permute-start | bytes 6152 | tf_op jit(solution)/shard_map/ppermute | solution.py:32
  117.2 8.6 %collective-permute-start.22 = (f32[2,4,64,1]{3,1,2,0:T(4,128)S(1)}, f32[2,4,64,1]{3,1,2,0:T(4,128)S(1)}, u32[]{:S(2)}, u32[]{:S(2)}) collective-permute-start(f32[2,4,64,1]{3,1,2,0:T(4,128)S(1)} %get-tuple-element.76), channel_id=1, source_target_pairs={{0,16},{16,0},{1,17},{17,1},{2,18},{18,2},{3,19},{19,3},{4,20},{20... | collective-permute-start | bytes 6152 | tf_op jit(solution)/shard_map/ppermute | solution.py:31
  125.9 5.9 %collective-permute-start.25 = (f32[2,4,1,514]{3,1,2,0:T(4,128)S(1)}, f32[2,4,1,514]{3,1,2,0:T(4,128)S(1)}, u32[]{:S(2)}, u32[]{:S(2)}) collective-permute-start(f32[2,4,1,514]{3,1,2,0:T(4,128)S(1)} %get-tuple-element.43), channel_id=1, source_target_pairs={{4,0},{8,4},{12,8},{5,1},{9,5},{13,9},{6,2},{10,6},{14,10},{7,3},{... | collective-permute-start | bytes 49352 | tf_op jit(solution)/shard_map/ppermute | solution.py:32
  127.2 6.0 %collective-permute-start.24 = (f32[2,4,1,514]{3,1,2,0:T(4,128)S(1)}, f32[2,4,1,514]{3,1,2,0:T(4,128)S(1)}, u32[]{:S(2)}, u32[]{:S(2)}) collective-permute-start(f32[2,4,1,514]{3,1,2,0:T(4,128)S(1)} %get-tuple-element.42), channel_id=1, source_target_pairs={{0,4},{4,8},{8,12},{1,5},{5,9},{9,13},{2,6},{6,10},{10,14},{3,7},{... | collective-permute-start | bytes 49352 | tf_op jit(solution)/shard_map/ppermute | solution.py:31
  135.5 9.4 %collective-permute-start.27 = (f32[4,1,512]{2,0,1:T(4,128)S(1)}, f32[4,1,512]{2,0,1:T(4,128)S(1)}, u32[]{:S(2)}, u32[]{:S(2)}) collective-permute-start(f32[4,1,512]{2,0,1:T(4,128)S(1)} %slice.909), channel_id=1, source_target_pairs={{0,4},{4,8},{8,12},{1,5},{5,9},{9,13},{2,6},{6,10},{10,14},{3,7},{... | collective-permute-start | bytes 24584 | tf_op jit(solution)/shard_map/ppermute | solution.py:46
  147.5 6.4 %collective-permute-start.29 = (f32[2,4,64,1]{3,1,2,0:T(4,128)S(1)}, f32[2,4,64,1]{3,1,2,0:T(4,128)S(1)}, u32[]{:S(2)}, u32[]{:S(2)}) collective-permute-start(f32[2,4,64,1]{3,1,2,0:T(4,128)S(1)} %get-tuple-element.75), channel_id=1, source_target_pairs={{16,0},{0,16},{17,1},{1,17},{18,2},{2,18},{19,3},{3,19},{20,4},{4,... | collective-permute-start | bytes 6152 | tf_op jit(solution)/shard_map/ppermute | solution.py:32
  148.1 9.1 %collective-permute-start.28 = (f32[2,4,64,1]{3,1,2,0:T(4,128)S(1)}, f32[2,4,64,1]{3,1,2,0:T(4,128)S(1)}, u32[]{:S(2)}, u32[]{:S(2)}) collective-permute-start(f32[2,4,64,1]{3,1,2,0:T(4,128)S(1)} %get-tuple-element.74), channel_id=1, source_target_pairs={{0,16},{16,0},{1,17},{17,1},{2,18},{18,2},{3,19},{19,3},{4,20},{20... | collective-permute-start | bytes 6152 | tf_op jit(solution)/shard_map/ppermute | solution.py:31
  157.3 6.1 %collective-permute-start.31 = (f32[2,4,1,514]{3,1,2,0:T(4,128)S(1)}, f32[2,4,1,514]{3,1,2,0:T(4,128)S(1)}, u32[]{:S(2)}, u32[]{:S(2)}) collective-permute-start(f32[2,4,1,514]{3,1,2,0:T(4,128)S(1)} %get-tuple-element.41), channel_id=1, source_target_pairs={{4,0},{8,4},{12,8},{5,1},{9,5},{13,9},{6,2},{10,6},{14,10},{7,3},{... | collective-permute-start | bytes 49352 | tf_op jit(solution)/shard_map/ppermute | solution.py:32
  158.6 6.3 %collective-permute-start.30 = (f32[2,4,1,514]{3,1,2,0:T(4,128)S(1)}, f32[2,4,1,514]{3,1,2,0:T(4,128)S(1)}, u32[]{:S(2)}, u32[]{:S(2)}) collective-permute-start(f32[2,4,1,514]{3,1,2,0:T(4,128)S(1)} %get-tuple-element.40), channel_id=1, source_target_pairs={{0,4},{4,8},{8,12},{1,5},{5,9},{9,13},{2,6},{6,10},{10,14},{3,7},{... | collective-permute-start | bytes 49352 | tf_op jit(solution)/shard_map/ppermute | solution.py:31
  167.2 9.6 %collective-permute-start.33 = (f32[4,1,512]{2,0,1:T(4,128)S(1)}, f32[4,1,512]{2,0,1:T(4,128)S(1)}, u32[]{:S(2)}, u32[]{:S(2)}) collective-permute-start(f32[4,1,512]{2,0,1:T(4,128)S(1)} %slice.929), channel_id=1, source_target_pairs={{0,4},{4,8},{8,12},{1,5},{5,9},{9,13},{2,6},{6,10},{10,14},{3,7},{... | collective-permute-start | bytes 24584 | tf_op jit(solution)/shard_map/ppermute | solution.py:46
  179.3 7.8 %collective-permute-start.35 = (f32[2,4,64,1]{3,1,2,0:T(4,128)S(1)}, f32[2,4,64,1]{3,1,2,0:T(4,128)S(1)}, u32[]{:S(2)}, u32[]{:S(2)}) collective-permute-start(f32[2,4,64,1]{3,1,2,0:T(4,128)S(1)} %get-tuple-element.73), channel_id=1, source_target_pairs={{16,0},{0,16},{17,1},{1,17},{18,2},{2,18},{19,3},{3,19},{20,4},{4,... | collective-permute-start | bytes 6152 | tf_op jit(solution)/shard_map/ppermute | solution.py:32
  179.9 10.1 %collective-permute-start.34 = (f32[2,4,64,1]{3,1,2,0:T(4,128)S(1)}, f32[2,4,64,1]{3,1,2,0:T(4,128)S(1)}, u32[]{:S(2)}, u32[]{:S(2)}) collective-permute-start(f32[2,4,64,1]{3,1,2,0:T(4,128)S(1)} %get-tuple-element.72), channel_id=1, source_target_pairs={{0,16},{16,0},{1,17},{17,1},{2,18},{18,2},{3,19},{19,3},{4,20},{20... | collective-permute-start | bytes 6152 | tf_op jit(solution)/shard_map/ppermute | solution.py:31
  190.1 5.9 %collective-permute-start.37 = (f32[2,4,1,514]{3,1,2,0:T(4,128)S(1)}, f32[2,4,1,514]{3,1,2,0:T(4,128)S(1)}, u32[]{:S(2)}, u32[]{:S(2)}) collective-permute-start(f32[2,4,1,514]{3,1,2,0:T(4,128)S(1)} %get-tuple-element.39), channel_id=1, source_target_pairs={{4,0},{8,4},{12,8},{5,1},{9,5},{13,9},{6,2},{10,6},{14,10},{7,3},{... | collective-permute-start | bytes 49352 | tf_op jit(solution)/shard_map/ppermute | solution.py:32
  191.4 6.0 %collective-permute-start.36 = (f32[2,4,1,514]{3,1,2,0:T(4,128)S(1)}, f32[2,4,1,514]{3,1,2,0:T(4,128)S(1)}, u32[]{:S(2)}, u32[]{:S(2)}) collective-permute-start(f32[2,4,1,514]{3,1,2,0:T(4,128)S(1)} %get-tuple-element.38), channel_id=1, source_target_pairs={{0,4},{4,8},{8,12},{1,5},{5,9},{9,13},{2,6},{6,10},{10,14},{3,7},{... | collective-permute-start | bytes 49352 | tf_op jit(solution)/shard_map/ppermute | solution.py:31
  199.7 9.4 %collective-permute-start.39 = (f32[4,1,512]{2,0,1:T(4,128)S(1)}, f32[4,1,512]{2,0,1:T(4,128)S(1)}, u32[]{:S(2)}, u32[]{:S(2)}) collective-permute-start(f32[4,1,512]{2,0,1:T(4,128)S(1)} %slice.949), channel_id=1, source_target_pairs={{0,4},{4,8},{8,12},{1,5},{5,9},{9,13},{2,6},{6,10},{10,14},{3,7},{... | collective-permute-start | bytes 24584 | tf_op jit(solution)/shard_map/ppermute | solution.py:46
  211.6 6.4 %collective-permute-start.41 = (f32[2,4,64,1]{3,1,2,0:T(4,128)S(1)}, f32[2,4,64,1]{3,1,2,0:T(4,128)S(1)}, u32[]{:S(2)}, u32[]{:S(2)}) collective-permute-start(f32[2,4,64,1]{3,1,2,0:T(4,128)S(1)} %get-tuple-element.71), channel_id=1, source_target_pairs={{16,0},{0,16},{17,1},{1,17},{18,2},{2,18},{19,3},{3,19},{20,4},{4,... | collective-permute-start | bytes 6152 | tf_op jit(solution)/shard_map/ppermute | solution.py:32
  212.2 10.6 %collective-permute-start.40 = (f32[2,4,64,1]{3,1,2,0:T(4,128)S(1)}, f32[2,4,64,1]{3,1,2,0:T(4,128)S(1)}, u32[]{:S(2)}, u32[]{:S(2)}) collective-permute-start(f32[2,4,64,1]{3,1,2,0:T(4,128)S(1)} %get-tuple-element.70), channel_id=1, source_target_pairs={{0,16},{16,0},{1,17},{17,1},{2,18},{18,2},{3,19},{19,3},{4,20},{20... | collective-permute-start | bytes 6152 | tf_op jit(solution)/shard_map/ppermute | solution.py:31
  222.9 6.2 %collective-permute-start.43 = (f32[2,4,1,514]{3,1,2,0:T(4,128)S(1)}, f32[2,4,1,514]{3,1,2,0:T(4,128)S(1)}, u32[]{:S(2)}, u32[]{:S(2)}) collective-permute-start(f32[2,4,1,514]{3,1,2,0:T(4,128)S(1)} %get-tuple-element.37), channel_id=1, source_target_pairs={{4,0},{8,4},{12,8},{5,1},{9,5},{13,9},{6,2},{10,6},{14,10},{7,3},{... | collective-permute-start | bytes 49352 | tf_op jit(solution)/shard_map/ppermute | solution.py:32
  224.2 6.3 %collective-permute-start.42 = (f32[2,4,1,514]{3,1,2,0:T(4,128)S(1)}, f32[2,4,1,514]{3,1,2,0:T(4,128)S(1)}, u32[]{:S(2)}, u32[]{:S(2)}) collective-permute-start(f32[2,4,1,514]{3,1,2,0:T(4,128)S(1)} %get-tuple-element.36), channel_id=1, source_target_pairs={{0,4},{4,8},{8,12},{1,5},{5,9},{9,13},{2,6},{6,10},{10,14},{3,7},{... | collective-permute-start | bytes 49352 | tf_op jit(solution)/shard_map/ppermute | solution.py:31
  232.8 9.4 %collective-permute-start.45 = (f32[4,1,512]{2,0,1:T(4,128)S(1)}, f32[4,1,512]{2,0,1:T(4,128)S(1)}, u32[]{:S(2)}, u32[]{:S(2)}) collective-permute-start(f32[4,1,512]{2,0,1:T(4,128)S(1)} %slice.969), channel_id=1, source_target_pairs={{0,4},{4,8},{8,12},{1,5},{5,9},{9,13},{2,6},{6,10},{10,14},{3,7},{... | collective-permute-start | bytes 24584 | tf_op jit(solution)/shard_map/ppermute | solution.py:46
  244.7 9.3 %collective-permute-start.47 = (f32[2,4,64,1]{3,1,2,0:T(4,128)S(1)}, f32[2,4,64,1]{3,1,2,0:T(4,128)S(1)}, u32[]{:S(2)}, u32[]{:S(2)}) collective-permute-start(f32[2,4,64,1]{3,1,2,0:T(4,128)S(1)} %get-tuple-element.69), channel_id=1, source_target_pairs={{16,0},{0,16},{17,1},{1,17},{18,2},{2,18},{19,3},{3,19},{20,4},{4,... | collective-permute-start | bytes 6152 | tf_op jit(solution)/shard_map/ppermute | solution.py:32
  245.3 14.3 %collective-permute-start.46 = (f32[2,4,64,1]{3,1,2,0:T(4,128)S(1)}, f32[2,4,64,1]{3,1,2,0:T(4,128)S(1)}, u32[]{:S(2)}, u32[]{:S(2)}) collective-permute-start(f32[2,4,64,1]{3,1,2,0:T(4,128)S(1)} %get-tuple-element.68), channel_id=1, source_target_pairs={{0,16},{16,0},{1,17},{17,1},{2,18},{18,2},{3,19},{19,3},{4,20},{20... | collective-permute-start | bytes 6152 | tf_op jit(solution)/shard_map/ppermute | solution.py:31
  259.8 5.9 %collective-permute-start.49 = (f32[2,4,1,514]{3,1,2,0:T(4,128)S(1)}, f32[2,4,1,514]{3,1,2,0:T(4,128)S(1)}, u32[]{:S(2)}, u32[]{:S(2)}) collective-permute-start(f32[2,4,1,514]{3,1,2,0:T(4,128)S(1)} %get-tuple-element.35), channel_id=1, source_target_pairs={{4,0},{8,4},{12,8},{5,1},{9,5},{13,9},{6,2},{10,6},{14,10},{7,3},{... | collective-permute-start | bytes 49352 | tf_op jit(solution)/shard_map/ppermute | solution.py:32
  261.1 6.1 %collective-permute-start.48 = (f32[2,4,1,514]{3,1,2,0:T(4,128)S(1)}, f32[2,4,1,514]{3,1,2,0:T(4,128)S(1)}, u32[]{:S(2)}, u32[]{:S(2)}) collective-permute-start(f32[2,4,1,514]{3,1,2,0:T(4,128)S(1)} %get-tuple-element.34), channel_id=1, source_target_pairs={{0,4},{4,8},{8,12},{1,5},{5,9},{9,13},{2,6},{6,10},{10,14},{3,7},{... | collective-permute-start | bytes 49352 | tf_op jit(solution)/shard_map/ppermute | solution.py:31
  272.2 19.9 %all-to-all-start = ((bf16[2,16,64,512]{3,2,1,0:T(8,128)(2,1)}), bf16[2,16,64,512]{3,2,1,0:T(8,128)(2,1)}, u32[]{:S(2)}, u32[]{:S(2)}) async-start(bf16[2,16,64,512]{3,2,1,0:T(8,128)(2,1)} %bitcast.184), calls=%async_computation | async-start | bytes 4194304 | tf_op jit(solution)/shard_map/all_to_all | solution.py:204
  277.0 202.9 %all-reduce.4.cloned.1.call-start = ((), (), s32[]{:S(2)}) async-start(), calls=%async_computation.1 | async-start | bytes 1417216 | tf_op jit(solution)/shard_map/psum | solution.py:225
  280.7 69.3 %collective-permute-start.50 = (f32[4,64,1]{2,0,1:T(4,128)}, f32[4,64,1]{2,0,1:T(4,128)}, u32[]{:S(2)}, u32[]{:S(2)}) collective-permute-start(f32[4,64,1]{2,0,1:T(4,128)} %slice.983), channel_id=1, source_target_pairs={{0,16},{16,0},{1,17},{17,1},{2,18},{18,2},{3,19},{19,3},{4,20},{20... | collective-permute-start | bytes 3080 | tf_op jit(solution)/shard_map/ppermute | solution.py:40
  282.6 67.3 %collective-permute-start.51 = (f32[4,1,512]{2,0,1:T(4,128)}, f32[4,1,512]{2,0,1:T(4,128)}, u32[]{:S(2)}, u32[]{:S(2)}) collective-permute-start(f32[4,1,512]{2,0,1:T(4,128)} %slice.989), channel_id=1, source_target_pairs={{0,4},{4,8},{8,12},{1,5},{5,9},{9,13},{2,6},{6,10},{10,14},{3,7},{... | collective-permute-start | bytes 24584 | tf_op jit(solution)/shard_map/ppermute | solution.py:46
  (24 other events, 480.6 us)
Sparse Core Ops, SparseCore 0:
  350.0 129.7 all-reduce.3
where the time goes:
time: 501 us; the launch traced here: 492 us
  waiting for transfers between devices  242 us (48%)
  starting transfers between devices  120 us (24%)
  local copies, waits for them, and re-layouts  62 us (12%)
  other arithmetic  43.2 us (9%)
  between operations  16.3 us (3%)
  matrix products  9.02 us (2%)
    psum x1, waiting for transfers between devices, shards(): grad_total = lax.psum(grad_local, ('lon', 'lat', 'grp'))  125 us
    ppermute x18, starting transfers between devices, extended(): before = lax.ppermute(last, axis, up)  52.1 us
    ppermute x18, waiting for transfers between devices, extended(): after = lax.ppermute(initial, axis, down)  45.9 us
    ppermute x18, waiting for transfers between devices, extended(): before = lax.ppermute(last, axis, up)  36.6 us
    ppermute x8, starting transfers between devices, from_behind(): return lax.ppermute(block, axis, route)  34.6 us
    ppermute x8, waiting for transfers between devices, passed_along(): return lax.ppermute(value, axis, pairs)  28.6 us
    ppermute x18, starting transfers between devices, extended(): after = lax.ppermute(initial, axis, down)  20.8 us
    transpose x1, local copies, waits for them, and re-layouts, to_patches(): blocks.transpose(0, 1, 3, 2, 4).reshape(-1, kernel_rows * kernel_cols)  16.6 us
  transfers between devices with their start and end apart: 54, of which 33 were waited for; matrix products, arithmetic and copies ran while one was open for 14% of the time, Pallas kernels for 0%

commit v1 on v0

v1 whole, which is shorter than its diff:
```python
import math

import jax
import jax.numpy as jnp
from jax import lax
from jax.experimental import pallas as pl
from jax.experimental.pallas import tpu as pltpu
from jax.sharding import PartitionSpec as P

STEPS = 8
NLEV = 50
PH = 8
PW = 16
HALO = 8
PAD = 16

GRAVITY = 0.45
DRAG_RATE = 0.02
CORI_BASE = 0.05
CORI_SLOPE = 0.1
WIND_SCALE = 0.05
EPSILON = 1e-06
PRECISE = lax.Precision.HIGHEST
F32 = jnp.float32
BF16 = jnp.bfloat16
LANES = 128
MEBI = 2**20


def vmem():
    return pl.BlockSpec(memory_space=pltpu.VMEM)


def smem():
    return pl.BlockSpec(memory_space=pltpu.SMEM)


def params_of(mebi, **rest):
    return pltpu.CompilerParams(vmem_limit_bytes=mebi * MEBI, **rest)


def lane_ids(rows):
    return lax.broadcasted_iota(jnp.int32, (rows, LANES), 1)


def plane_matrix(cols, inverse=False):
    patches = cols // PW
    src = lax.broadcasted_iota(jnp.int32, (cols, cols), 1 if inverse else 0)
    dst = lax.broadcasted_iota(jnp.int32, (cols, cols), 0 if inverse else 1)
    return jnp.where(src == (dst % patches) * PW + dst // patches, 1.0, 0.0).astype(BF16)


def moved(value, matrix):
    high = value.astype(BF16)
    rest = (value - high.astype(F32)).astype(BF16)
    return jnp.dot(high, matrix, preferred_element_type=F32) + jnp.dot(
        rest, matrix, preferred_element_type=F32
    )


def by_segment(pieces, segment):
    out = pieces[-1]
    for index in range(len(pieces) - 2, -1, -1):
        out = jnp.where(segment == index, pieces[index], out)
    return out


def turned(value, shift):
    shift = shift % LANES
    return value if shift == 0 else pltpu.roll(value, shift, 1)


def planes_from(parts, patches):
    rows = parts[0].shape[0]
    per = LANES // patches
    segment = lane_ids(rows) // patches
    planes = []
    for k in range(PW):
        group, place = divmod(k, per)
        block = slice(group * LANES, (group + 1) * LANES)
        planes.append(
            by_segment(
                [turned(part[:, block], (m - place) * patches) for m, part in enumerate(parts)],
                segment,
            )
        )
    return planes


def edges_of(firsts, lasts, patches):
    rows = firsts[0].shape[0]
    lane = lane_ids(rows)
    out = jnp.zeros((rows, LANES), F32)
    for m, (first, last) in enumerate(zip(firsts, lasts)):
        both = jnp.where(lane < HALO, first, turned(last, 2 * HALO))
        here = (lane >= m * patches) & (lane < m * patches + 2 * HALO)
        out = jnp.where(here, turned(both, m * patches), out)
    return out


def pack_kernel(members, ids, sea, vel, levels, wind, props, force, low, high, side, low_c, high_c):
    rows, cols = levels.shape
    patches = cols // PW
    base = lax.axis_index("grp") * members
    kinds = wind.shape[0]
    coeff = [
        props[pl.ds(ids[base + m], 1), :].astype(BF16).astype(F32) * WIND_SCALE
        for m in range(members)
    ]
    for r0 in range(0, rows, 16):
        acc = [jnp.zeros((16, cols), F32) for _ in range(members)]
        for k in range(kinds):
            basis = wind[k, r0 : r0 + 16, :].astype(F32)
            for m in range(members):
                acc[m] = acc[m] + coeff[m][:, k : k + 1] * basis
        for m in range(members):
            force[m, r0 : r0 + 16, :] = acc[m]
    depth = levels[...].astype(F32)
    groups = [lambda rs, m=m: sea[m, rs, :] for m in range(members)]
    groups += [lambda rs, m=m, d=d: vel[d, m, rs, :] for d in range(2) for m in range(members)]
    groups += [lambda rs, m=m: force[m, rs, :] for m in range(members)]
    groups += [lambda rs: depth[rs, :], lambda rs: jnp.zeros((HALO, cols), F32)]
    for out, rs in ((low, slice(0, HALO)), (high, slice(rows - HALO, rows))):
        for g in range(0, len(groups), 2):
            pair = jnp.concatenate([groups[g](rs), groups[g + 1](rs)], axis=0)
            out[g * HALO : (g + 2) * HALO, :] = pair.astype(BF16)
    firsts, lasts = slice(0, LANES), slice(cols - LANES, cols)
    fields = [
        [lambda cs, m=m: sea[m, :, cs] for m in range(members)],
        [lambda cs, m=m: vel[0, m, :, cs] for m in range(members)],
        [lambda cs, m=m: vel[1, m, :, cs] for m in range(members)],
        [lambda cs, m=m: force[m, :, cs] for m in range(members)],
        [lambda cs: depth[:, cs]] * members,
    ]
    lows, highs = [], []
    for i, field in enumerate(fields):
        edge = edges_of([f(firsts) for f in field], [f(lasts) for f in field], patches)
        side[i * rows : (i + 1) * rows, :] = edge.astype(BF16)
        lows.append(edge[:HALO])
        highs.append(edge[rows - HALO :])
    blank = jnp.zeros((HALO, LANES), F32)
    low_c[...] = jnp.concatenate(lows + [blank], axis=0).astype(BF16)
    high_c[...] = jnp.concatenate(highs + [blank], axis=0).astype(BF16)


def planar_kernel(members, sea, vel, force, levels, out):
    rows, cols = levels.shape
    patches = cols // PW
    matrix = plane_matrix(cols)
    scale = 1.0 / GRAVITY
    for i, field in enumerate((sea, vel.at[0], vel.at[1], force)):
        value = field[...].reshape(members * rows, cols)
        spread = moved(value if i == 0 else value * scale, matrix)
        parts = [spread[m * rows : (m + 1) * rows] for m in range(members)]
        for k, plane in enumerate(planes_from(parts, patches)):
            out[i, k] = plane
    spread = jnp.dot(levels[...].astype(F32).astype(BF16), matrix, preferred_element_type=F32)
    for k, plane in enumerate(planes_from([spread] * members, patches)):
        out[4, k] = plane


def back_kernel(members, state, sea, vel):
    rows, cols = sea.shape[1:]
    patches = cols // PW
    per = LANES // patches
    matrix = plane_matrix(cols, inverse=True)
    segment = lane_ids(rows) // patches
    for i in range(3):
        parts = []
        for m in range(members):
            groups = []
            for g in range(PW // per):
                pieces = [turned(state[i, g * per + j], (j - m) * patches) for j in range(per)]
                groups.append(by_segment(pieces, segment))
            parts.append(jnp.concatenate(groups, axis=1))
        value = moved(jnp.concatenate(parts, axis=0), matrix)
        for m in range(members):
            part = value[m * rows : (m + 1) * rows]
            if i == 0:
                sea[m] = part
            else:
                vel[i - 1, m] = part * GRAVITY


def flow_step(src, dst, hu, hv, hvu, cu, cv, force, last_mask, rows, patches):
    strip = PW
    end = PAD + rows + HALO
    half = (rows + 2 * HALO) // 2
    keep = 1.0 - DRAG_RATE
    for r0 in range(PAD - HALO, end, half):
        here, up, down = pl.ds(r0, half), pl.ds(r0 + 1, half), pl.ds(r0 - 1, half)
        last = lane_ids(half) % patches == patches - 1

        def wrap_left(plane, rim):
            return pltpu.roll(jnp.where(last, rim, plane), 1, 1)

        def wrap_right(plane, rim):
            return jnp.where(last, pltpu.roll(rim, PW - 1, 1), pltpu.roll(plane, LANES - 1, 1))

        def new_level(p, fx, fx_right):
            n_up = src[2, p, up, :]
            n = src[2, p, here, :]
            fy = hvu[p, here, :] * n_up - hv[p, here, :] * n
            level = src[0, p, here, :] - ((fx_right - fx) + fy)
            dst[0, p, here, :] = level
            return level, n, n + n_up

        def new_flow(p, e, e_right, em, em_right, n, v, level, level_left):
            u = (e + e_right) + (em + em_right)
            dst[1, p, here, :] = (
                keep * e + cu[here, :] * v - (level - level_left) + force[p, here, :]
            )
            level_down = dst[0, p, down, :]
            north = keep * n - cv[here, :] * u - (level - level_down)
            if r0 + half == end:
                dst[2, p, pl.ds(r0, half - HALO), :] = north[: half - HALO]
                dst[2, p, pl.ds(end - HALO, HALO), :] = north[half - HALO :] * last_mask
            else:
                dst[2, p, here, :] = north

        e_rim = src[1, strip, here, :]
        em_rim = src[1, strip, down, :]
        fx_rim = hu[strip, here, :] * e_rim
        level_rim, n_rim, vs_rim = new_level(strip, fx_rim, pltpu.roll(fx_rim, LANES - 1, 1))
        new_flow(
            strip,
            e_rim,
            pltpu.roll(e_rim, LANES - 1, 1),
            em_rim,
            pltpu.roll(em_rim, LANES - 1, 1),
            n_rim,
            vs_rim + pltpu.roll(vs_rim, 1, 1),
            level_rim,
            pltpu.roll(level_rim, 1, 1),
        )
        e_end = wrap_right(src[1, 0, here, :], e_rim)
        em_end = wrap_right(src[1, 0, down, :], em_rim)
        e_last = src[1, PW - 1, here, :]
        level_last, n_last, vs_last = new_level(
            PW - 1, hu[PW - 1, here, :] * e_last, hu[PW + 1, here, :] * e_end
        )
        level_left = wrap_left(level_last, level_rim)
        vs_left = wrap_left(vs_last, vs_rim)
        e = src[1, 0, here, :]
        em = src[1, 0, down, :]
        fx = hu[0, here, :] * e
        for p in range(PW):
            if p < PW - 1:
                e_right = src[1, p + 1, here, :]
                em_right = src[1, p + 1, down, :]
                fx_right = hu[p + 1, here, :] * e_right
                level, n, vs = new_level(p, fx, fx_right)
            else:
                e_right, em_right, fx_right = e_end, em_end, None
                level, n, vs = level_last, n_last, vs_last
            new_flow(p, e, e_right, em, em_right, n, vs + vs_left, level, level_left)
            level_left, vs_left, e, em, fx = level, vs, e_right, em_right, fx_right


def flow_kernel(
    members,
    rows,
    cols,
    lat_count,
    planes,
    south,
    north,
    side,
    east,
    west,
    south_east,
    south_west,
    north_east,
    north_west,
    weight,
    partial,
    gram,
    final,
    state_a,
    state_b,
    force,
    depth,
    hu,
    hv,
    hvu,
    cu,
    cv,
    w_rows,
    w_planes,
    patch_t,
    slope,
):
    patches = cols // PW
    turn = pl.program_id(0)
    lat = lax.axis_index("lat")
    strip = PW
    height = rows + 2 * PAD
    wide = rows + 2 * HALO
    inner = slice(PAD, PAD + rows)
    scale = 1.0 / GRAVITY

    @pl.when(turn == 0)
    def _():
        for state in (state_a, state_b):
            for i in range(3):
                for p in range(PW + 1):
                    state[i, p, 0:HALO, :] = jnp.zeros((HALO, LANES), F32)
                    state[i, p, height - HALO : height, :] = jnp.zeros((HALO, LANES), F32)
        homes = (state_a.at[0], state_a.at[1], state_a.at[2], force, depth)
        for i, home in enumerate(homes):
            for k in range(PW):
                home[k, inner, :] = planes[i, k]
        for p in range(PW + 1):
            depth[p, 0:HALO, :] = jnp.zeros((HALO, LANES), F32)
            depth[p, height - HALO : height, :] = jnp.zeros((HALO, LANES), F32)
        matrix = plane_matrix(cols)

        def strip_of(own, from_east, from_west):
            place = lane_ids(own.shape[0]) % patches
            return jnp.where(
                place < 2 * HALO,
                own,
                jnp.where(
                    place < 3 * HALO,
                    pltpu.roll(from_east, 2 * HALO, 1),
                    pltpu.roll(from_west, LANES - 2 * HALO, 1),
                ),
            )

        for i, home in enumerate(homes):
            factor = 1.0 if i in (0, 4) else scale
            rs = slice(i * rows, (i + 1) * rows)
            rim = strip_of(side[rs, :].astype(F32), east[rs, :].astype(F32), west[rs, :].astype(F32))
            home[strip, inner, :] = rim * factor
        for got, got_east, got_west, r0 in (
            (south, south_east, south_west, PAD - HALO),
            (north, north_east, north_west, PAD + rows),
        ):
            place = slice(r0, r0 + HALO)
            spread = jnp.dot(got[...], matrix, preferred_element_type=F32)
            plain = got[...].astype(F32)
            east_c = got_east[...].astype(F32)
            west_c = got_west[...].astype(F32)
            for i, home in enumerate(homes):
                factor = 1.0 if i in (0, 4) else scale
                if i < 4:
                    starts = [(i * members + m) * HALO for m in range(members)]
                else:
                    starts = [4 * members * HALO] * members
                parts = [spread[s : s + HALO] for s in starts]
                for k, plane in enumerate(planes_from(parts, patches)):
                    home[k, place, :] = plane * factor
                own = edges_of(
                    [plain[s : s + HALO, :LANES] for s in starts],
                    [plain[s : s + HALO, cols - LANES :] for s in starts],
                    patches,
                )
                rs = slice(i * HALO, (i + 1) * HALO)
                home[strip, place, :] = strip_of(own, east_c[rs], west_c[rs]) * factor
        span = slice(PAD - HALO, PAD + rows + HALO)
        row = lax.broadcasted_iota(jnp.int32, (wide, LANES), 0) + (lat * rows - HALO)
        inside = (row >= 0) & (row < lat_count * rows)
        place = row.astype(F32)
        total = lat_count * rows
        cu[span, :] = jnp.where(
            inside, 0.25 * (CORI_BASE + CORI_SLOPE * (place + 0.5) / total), 0.0
        )
        cv[span, :] = jnp.where(inside, 0.25 * (CORI_BASE + CORI_SLOPE * place / total), 0.0)
        half_depth = 0.5 * GRAVITY / NLEV
        last = lane_ids(wide) % patches == patches - 1
        for p in range(PW + 1):
            here = depth[p, span, :]
            if p == 0:
                left = pltpu.roll(
                    jnp.where(last, depth[strip, span, :], depth[PW - 1, span, :]), 1, 1
                )
            elif p == strip:
                left = pltpu.roll(here, 1, 1)
            else:
                left = depth[p - 1, span, :]
            below = depth[p, PAD - HALO - 1 : PAD + rows + HALO - 1, :]
            above = depth[p, PAD - HALO + 1 : PAD + rows + HALO + 1, :]
            hu[p, span, :] = half_depth * (here + left)
            hv[p, span, :] = half_depth * (here + below)
            hvu[p, span, :] = jnp.where(inside, half_depth * (here + above), 0.0)
        hu[PW + 1, span, :] = jnp.where(
            last,
            pltpu.roll(hu[strip, span, :], PW - 1, 1),
            pltpu.roll(hu[0, span, :], LANES - 1, 1),
        )
        for h in range(w_rows.shape[0]):
            cs = slice(h * LANES, (h + 1) * LANES)
            w_rows[h] = weight[:, cs].astype(F32)
            w_planes[:, cs] = jnp.concatenate(
                [w_rows[h, pl.ds(k, PH, stride=PW), :] for k in range(PW)], axis=0
            ).astype(BF16)

    last_mask = jnp.where(lat < lat_count - 1, 1.0, 0.0)
    count = rows // PH
    for sub, (src, dst) in enumerate(((state_a, state_b), (state_b, state_a))):
        flow_step(src, dst, hu, hv, hvu, cu, cv, force, last_mask, rows, patches)
        total = None
        for b in range(count):
            cells = dst[0, 0:PW, PAD + b * PH : PAD + (b + 1) * PH, :].reshape(PW * PH, LANES)
            cells_t = cells.T.astype(BF16)
            act = jnp.tanh(jnp.dot(cells_t, w_planes[...], preferred_element_type=F32))
            total = act if total is None else total + act
            fall = (1.0 - act * act).astype(BF16)
            for m in range(members):
                rs = slice(m * patches, (m + 1) * patches)
                to = slice(b * patches, (b + 1) * patches)
                patch_t[m, to, :] = cells_t[rs]
                slope[m, to, :] = fall[rs]
        sums = jnp.sum(total.reshape(members, patches, total.shape[1]), axis=1)
        partial[sub * members : (sub + 1) * members, :] = sums
        for m in range(members):
            gram[sub * members + m] = lax.dot_general(
                patch_t[m], slope[m], (((0,), (0,)), ((), ())), preferred_element_type=F32
            )

    @pl.when(turn == pl.num_programs(0) - 1)
    def _():
        for i in range(3):
            for k in range(PW):
                final[i, k] = state_a[i, k, inner, :]


def picked(ids_col, props, members_col):
    count = props.shape[0]
    slots = members_col.shape[0]
    slot = lax.broadcasted_iota(jnp.int32, (slots, count), 1)
    first = jnp.where(members_col == slot, 1.0, 0.0).astype(F32)
    second = jnp.where(
        ids_col[...] == lax.broadcasted_iota(jnp.int32, (count, count), 1), 1.0, 0.0
    ).astype(F32)
    rows = jnp.dot(second, props[...], precision=PRECISE, preferred_element_type=F32)
    return jnp.dot(first, rows, precision=PRECISE, preferred_element_type=F32)


def mm(a, b, ca=1, cb=0):
    return lax.dot_general(
        a, b, (((ca,), (cb,)), ((), ())), precision=PRECISE, preferred_element_type=F32
    )


def flow_grads(params, summary, w_in, b_in, w_out, b_out):
    half = params.shape[1] // 2
    lower, upper = params[:, :half], params[:, half:]
    w_low, w_sum = w_in[0:half, :], w_in[half:, :]
    hidden = jnp.tanh(mm(summary, w_sum) + mm(lower, w_low) + b_in[...])
    raw = mm(hidden, w_out[...]) + b_out[...]
    log_scale = jnp.tanh(raw[:, :half])
    grown = upper * jnp.exp(log_scale)
    latent = grown + raw[:, half:]
    d_scale = (latent * grown - 1.0) * (1.0 - log_scale * log_scale)
    d_raw = jnp.concatenate([d_scale, latent], axis=1)
    d_hidden = mm(d_raw, w_out[...], 1, 1) * (1.0 - hidden * hidden)
    return lower, hidden, d_raw, d_hidden


def member_column(count, members, groups):
    row = lax.broadcasted_iota(jnp.int32, (count, 1), 0)
    base = lax.axis_index("grp") * members
    if groups is None:
        return base + row % members
    per, order = groups
    out = jnp.zeros((count, 1), jnp.int32)
    for index, flip in enumerate(order):
        grp = lax.axis_index("grp") ^ flip
        out = jnp.where(row // per == index, grp * members + row % members, out)
    return out


def local_kernel(
    members, inv_root, mine, theirs, ids, props, w_in, b_in, w_out, b_out, gram, summary, kept, sent, held, total, sem
):
    copy = pltpu.make_async_copy(gram, held, sem)
    copy.start()
    sums = (mine[...] + theirs[...]) * inv_root
    summary[...] = sums
    count = sums.shape[0]
    params = picked(ids, props, member_column(count, members, None))
    half = params.shape[1] // 2
    _, _, _, d_hidden = flow_grads(params, sums, w_in, b_in, w_out, b_out)
    d_summary = mm(d_hidden, w_in[half:, :], 1, 1) * inv_root
    copy.wait()
    acc = jnp.zeros(held.shape[1:], F32)
    for i in range(count):
        acc = acc + held[i] * d_summary[i : i + 1, :]
    total[...] = acc
    cells = acc.shape[0] // 2
    core = lax.axis_index("grp") % 2
    kept[...] = total[pl.ds(pl.multiple_of(core * cells, 8), cells), :]
    sent[...] = total[pl.ds(pl.multiple_of((1 - core) * cells, 8), cells), :]


def couple_kernel(members, per, order, summary, ids, props, w_in, b_in, w_out, b_out, rows, square, staged):
    sums = summary[...]
    params = picked(ids, props, member_column(sums.shape[0], members, (per, order)))
    lower, hidden, d_raw, d_hidden = flow_grads(params, sums, w_in, b_in, w_out, b_out)
    g_low = mm(lower, d_hidden, 0, 0)
    g_sum = mm(sums, d_hidden, 0, 0)
    g_out = mm(hidden, d_raw, 0, 0)
    g_in_b = jnp.sum(d_hidden, axis=0, keepdims=True)
    g_out_b = jnp.sum(d_raw, axis=0, keepdims=True)
    hid = d_hidden.shape[1]
    per_row = hid // LANES
    half = lower.shape[1]
    feats = sums.shape[1]
    width = d_raw.shape[1]
    fold = LANES // width
    base = (half + feats) * per_row
    after = base + per_row
    tail = after + hid // fold
    rows[base:, :] = jnp.zeros((rows.shape[0] - base, LANES), F32)
    for q in range(per_row):
        cs = slice(q * LANES, (q + 1) * LANES)
        rows[pl.ds(q, half, stride=per_row), :] = g_low[:, cs]
        rows[pl.ds(half * per_row + q, feats, stride=per_row), :] = g_sum[:, cs]
        rows[base + q : base + q + 1, :] = g_in_b[:, cs]
    staged[...] = jnp.concatenate([g_out, jnp.zeros((hid, LANES - width), F32)], axis=1)
    packed = jnp.zeros((hid // fold, LANES), F32)
    for j in range(fold):
        packed = packed + turned(staged[pl.ds(j, hid // fold, stride=fold), :], j * width)
    rows[after:tail, :] = packed
    rows[tail : tail + 1, :] = jnp.concatenate(
        [g_out_b, jnp.zeros((1, LANES - width), F32)], axis=1
    )
    whole = rows[...]
    square[...] = jnp.sum(whole * whole, axis=0, keepdims=True)


def finish_kernel(count, mine, theirs, couple, square, out, whole):
    core = lax.axis_index("grp") % 2
    cells = mine.shape[0]
    per_row = mine.shape[1] // LANES
    for h in range(per_row):
        cs = slice(h * LANES, (h + 1) * LANES)
        whole[h, pl.ds(pl.multiple_of(core * cells, 8), cells), :] = mine[:, cs]
        whole[h, pl.ds(pl.multiple_of((1 - core) * cells, 8), cells), :] = theirs[:, cs]
    conv = whole[...]
    squares = jnp.sum(conv * conv) + jnp.sum(square[...])
    scale = -lax.rsqrt(jnp.full((1, 1), squares, F32) / count + EPSILON)
    for r in range(PH):
        for h in range(per_row):
            part = whole[h, pl.ds(r, PW, stride=PH), :]
            out[pl.ds(r * PW * per_row + h, PW, stride=per_row), :] = part * scale
    used = 2 * cells * per_row
    out[used : used + couple.shape[0], :] = couple[...] * scale


def neighbour(value, axis, step):
    count = lax.axis_size(axis)
    pairs = [(i, (i + step) % count) for i in range(count)]
    return lax.ppermute(value, axis, pairs)


def from_lat(value, step):
    count = lax.axis_size("lat")
    return lax.ppermute(value, "lat", [(i, i + step) for i in range(count) if 0 <= i + step < count])


def from_corner(value, lon_step, lat_step):
    lon, lat = lax.axis_size("lon"), lax.axis_size("lat")
    pairs = [
        (i * lat + j, (i + lon_step) % lon * lat + j + lat_step)
        for i in range(lon)
        for j in range(lat)
        if 0 <= j + lat_step < lat
    ]
    return lax.ppermute(value, ("lon", "lat"), pairs)


def swapped(value, axis, flip):
    count = lax.axis_size(axis)
    return lax.ppermute(value, axis, [(i, i ^ flip) for i in range(count)])


def flips(axis):
    count = lax.axis_size(axis)
    return [1 << i for i in range(count.bit_length() - 1)]


def shape(*dims, dtype=F32):
    return jax.ShapeDtypeStruct(dims, dtype)


def shards(
    sea_surface,
    velocity,
    levels,
    wind_basis,
    proposals,
    member_ids,
    conv_weight,
    couple_in,
    couple_in_bias,
    couple_out,
    couple_out_bias,
):
    members, rows, cols = sea_surface.shape
    lat_count, lon_count = lax.axis_size("lat"), lax.axis_size("lon")
    cells, feats = conv_weight.shape
    hid, width = couple_out.shape
    patches = cols // PW
    samples = STEPS * members
    groups = (4 * members + 2) * HALO
    height = rows + 2 * PAD
    inv_root = 1.0 / math.sqrt(rows // PH * (cols * lon_count // PW))

    force, low, high, side, low_c, high_c = pl.pallas_call(
        lambda *refs: pack_kernel(members, *refs),
        out_shape=(
            shape(members, rows, cols),
            shape(groups, cols, dtype=BF16),
            shape(groups, cols, dtype=BF16),
            shape(5 * rows, LANES, dtype=BF16),
            shape(6 * HALO, LANES, dtype=BF16),
            shape(6 * HALO, LANES, dtype=BF16),
        ),
        in_specs=[smem()] + [vmem()] * 5,
        out_specs=(vmem(),) * 6,
        compiler_params=params_of(16),
        name="pack_edges",
    )(member_ids, sea_surface, velocity, levels, wind_basis, proposals)

    south = from_lat(high, 1)
    north = from_lat(low, -1)
    west = neighbour(side, "lon", 1)
    south_west = from_corner(high_c, 1, 1)
    north_west = from_corner(low_c, 1, -1)
    if lon_count == 2:
        east, south_east, north_east = west, south_west, north_west
    else:
        east = neighbour(side, "lon", -1)
        south_east = from_corner(high_c, -1, 1)
        north_east = from_corner(low_c, -1, -1)

    planes = pl.pallas_call(
        lambda *refs: planar_kernel(members, *refs),
        out_shape=shape(5, PW, rows, LANES),
        in_specs=[vmem()] * 4,
        out_specs=vmem(),
        compiler_params=params_of(24),
        cost_estimate=pl.CostEstimate(flops=2 * 10**9, bytes_accessed=6 * MEBI, transcendentals=0),
        name="to_planes",
    )(sea_surface, velocity, force, levels)

    whole = lambda *dims: pl.BlockSpec(dims, lambda i: (0,) * len(dims))
    partial, gram, final = pl.pallas_call(
        lambda *refs: flow_kernel(members, rows, cols, lat_count, *refs),
        grid=(STEPS // 2,),
        out_shape=(
            shape(samples, feats),
            shape(samples, cells, feats),
            shape(3, PW, rows, LANES),
        ),
        in_specs=[
            whole(5, PW, rows, LANES),
            whole(groups, cols),
            whole(groups, cols),
            whole(5 * rows, LANES),
            whole(5 * rows, LANES),
            whole(5 * rows, LANES),
            whole(6 * HALO, LANES),
            whole(6 * HALO, LANES),
            whole(6 * HALO, LANES),
            whole(6 * HALO, LANES),
            whole(cells, feats),
        ],
        out_specs=(
            pl.BlockSpec((2 * members, feats), lambda i: (i, 0)),
            pl.BlockSpec((2 * members, cells, feats), lambda i: (i, 0, 0)),
            whole(3, PW, rows, LANES),
        ),
        scratch_shapes=[
            pltpu.VMEM((3, PW + 1, height, LANES), F32),
            pltpu.VMEM((3, PW + 1, height, LANES), F32),
            pltpu.VMEM((PW + 1, height, LANES), F32),
            pltpu.VMEM((PW + 1, height, LANES), F32),
            pltpu.VMEM((PW + 2, height, LANES), F32),
            pltpu.VMEM((PW + 1, height, LANES), F32),
            pltpu.VMEM((PW + 1, height, LANES), F32),
            pltpu.VMEM((height, LANES), F32),
            pltpu.VMEM((height, LANES), F32),
            pltpu.VMEM((feats // LANES, cells, LANES), F32),
            pltpu.VMEM((cells, feats), BF16),
            pltpu.VMEM((members, rows // PH * patches, cells), BF16),
            pltpu.VMEM((members, rows // PH * patches, feats), BF16),
        ],
        compiler_params=params_of(48),
        name="flow_embed",
    )(
        planes,
        south,
        north,
        side,
        east,
        west,
        south_east,
        south_west,
        north_east,
        north_west,
        conv_weight,
    )

    if lon_count == 2:
        others = swapped(partial, "lon", 1)
    else:
        others = lax.psum(partial, "lon") - partial

    surface_out, velocity_out = pl.pallas_call(
        lambda *refs: back_kernel(members, *refs),
        out_shape=(shape(members, rows, cols), shape(2, members, rows, cols)),
        in_specs=[vmem()],
        out_specs=(vmem(), vmem()),
        compiler_params=params_of(24),
        cost_estimate=pl.CostEstimate(flops=2 * 10**9, bytes_accessed=6 * MEBI, transcendentals=0),
        name="from_planes",
    )(final)

    ids_col = member_ids.reshape(-1, 1)
    b_in = couple_in_bias.reshape(1, -1)
    b_out = couple_out_bias.reshape(1, -1)
    summaries, kept, sent = pl.pallas_call(
        lambda *refs: local_kernel(members, inv_root, *refs),
        out_shape=(
            shape(samples, feats),
            shape(cells // 2, feats),
            shape(cells // 2, feats),
        ),
        in_specs=[vmem()] * 8 + [pl.BlockSpec(memory_space=pl.ANY)],
        out_specs=(vmem(),) * 3,
        scratch_shapes=[
            pltpu.VMEM((samples, cells, feats), F32),
            pltpu.VMEM((cells, feats), F32),
            pltpu.SemaphoreType.DMA,
        ],
        compiler_params=params_of(24),
        name="local_loss",
    )(partial, others, ids_col, proposals, couple_in, b_in, couple_out, b_out, gram)

    conv = kept + swapped(sent, "grp", 1)
    for axis in ("grp", "lon", "lat"):
        for flip in flips(axis):
            if axis != "grp" or flip > 1:
                conv = conv + swapped(conv, axis, flip)
    conv_other = swapped(conv, "grp", 1)

    gathered = summaries
    order = [0]
    for axis in ("grp", "lat"):
        for flip in flips(axis):
            if axis != "grp" or flip > 1:
                gathered = jnp.concatenate([gathered, swapped(gathered, axis, flip)], axis=0)
                order = order + [(o ^ flip if axis == "grp" else o) for o in order]
    gathered = jnp.concatenate([gathered, swapped(gathered, "grp", 1)], axis=0)
    order = order + [o ^ 1 for o in order]

    low_rows = (couple_in.size + hid + couple_out.size) // LANES + 1
    low_rows = -(-low_rows // 8) * 8
    count = cells * feats + couple_in.size + hid + couple_out.size + width
    couple, square = pl.pallas_call(
        lambda *refs: couple_kernel(members, samples, order, *refs),
        out_shape=(shape(low_rows, LANES), shape(1, LANES)),
        in_specs=[vmem()] * 7,
        out_specs=(vmem(), vmem()),
        scratch_shapes=[pltpu.VMEM((hid, LANES), F32)],
        compiler_params=params_of(32),
        cost_estimate=pl.CostEstimate(flops=3 * 10**9, bytes_accessed=3 * MEBI, transcendentals=0),
        name="couple_grads",
    )(gathered, ids_col, proposals, couple_in, b_in, couple_out, b_out)

    stepped = pl.pallas_call(
        lambda *refs: finish_kernel(count, *refs),
        out_shape=shape(cells * feats // LANES + low_rows, LANES),
        in_specs=[vmem()] * 4,
        out_specs=vmem(),
        scratch_shapes=[pltpu.VMEM((feats // LANES, cells, LANES), F32)],
        compiler_params=params_of(16),
        name="finish",
    )(conv, conv_other, couple, square)
    weight_step = stepped.reshape(-1)[:count]

    items = samples // lon_count
    own = lax.dynamic_slice_in_dim(summaries, lax.axis_index("lon") * items, items, axis=0)
    return (surface_out, velocity_out, own.reshape(1, 1, 1, items, feats), weight_step)


def solution(mesh):
    in_specs = (
        P("grp", "lat", "lon"),
        P(None, "grp", "lat", "lon"),
        P("lat", "lon"),
        P(None, "lat", "lon"),
        P(),
        P(),
        P(),
        P(),
        P(),
        P(),
        P(),
    )
    out_specs = (
        P("grp", "lat", "lon"),
        P(None, "grp", "lat", "lon"),
        P("lon", "lat", "grp", None, None),
        P(),
    )
    return jax.shard_map(shards, mesh=mesh, in_specs=in_specs, out_specs=out_specs, check_vma=False)
```

time: 501 us -> 88.2 us (0.18); the launches traced: 492 us -> 87.7 us
  waiting for transfers between devices: 242 us -> 20.6 us
  starting transfers between devices: 120 us -> 25.8 us
  local copies, waits for them, and re-layouts: 62 us -> 8.83 us
  other arithmetic: 43.2 us -> 0.08 us
  Pallas kernels: 0 us -> 31.4 us
  between operations: 16.3 us -> 0.91 us
  matrix products: 9.02 us -> 0 us
    psum x1 -> x0, waiting for transfers between devices: 125 us -> none  [shards(): grad_total = lax.psum(grad_local, ('lon', 'lat', 'grp'))]
    ppermute x52 -> x16, waiting for transfers between devices: 112 us -> 20.6 us  [the longest x11 18 us: swapped(): return lax.ppermute(value, axis, [(i, i ^ flip) for i in range(count)])]
    ppermute x52 -> x16, starting transfers between devices: 115 us -> 25.8 us  [the longest x11 12.2 us: swapped(): return lax.ppermute(value, axis, [(i, i ^ flip) for i in range(count)])]
    pallas_call x0 -> x7, Pallas kernels: none -> 31.4 us  [the longest x1 12.9 us: shards(): pl.pallas_call(lambda *refs: flow_kernel(members, rows, cols, lat_count,...]
    transpose x1 -> x0, local copies, waits for them, and re-layouts: 16.6 us -> none  [to_patches(): blocks.transpose(0, 1, 3, 2, 4).reshape(-1, kernel_rows * kernel_cols)]
    another operation x2 -> x0, local copies, waits for them, and re-layouts: 16.2 us -> none  [the longest x1 14.4 us: to_patches(): band_rows.reshape(count, height // kernel_rows, kernel_rows, breadth // k...]
    add x8 -> x5, other arithmetic: 13.9 us -> 0.05 us  [the longest x4 0.04 us: shards(): conv = conv + swapped(conv, axis, flip)]
    dot_general x11 -> x0, matrix products: 9.02 us -> none  [the longest x1 2.49 us: shards(): jnp.dot(coeff_rows, wind_basis.reshape(wind_basis.shape[0], -1), preferre...]
  transfers between devices with their start and end apart: 54 -> 16, of which waited for: 33 -> 8; matrix products, arithmetic and copies ran while one was open for 14% -> 1% of each run, Pallas kernels for 0% -> 15%
where the time goes in v1:
time: 88.2 us; the launch traced here: 87.7 us
  Pallas kernels  31.4 us (36%)
  starting transfers between devices  25.8 us (29%)
  waiting for transfers between devices  20.6 us (23%)
  local copies, waits for them, and re-layouts  8.83 us (10%)
  between operations  0.91 us (1%)
    ppermute x11, waiting for transfers between devices, swapped(): return lax.ppermute(value, axis, [(i, i ^ flip) for i in range(count)])  18 us
    pallas_call x1, Pallas kernels, shards(): pl.pallas_call(lambda *refs: flow_kernel(members, rows, cols, lat_count,...  12.9 us
    ppermute x11, starting transfers between devices, swapped(): return lax.ppermute(value, axis, [(i, i ^ flip) for i in range(count)])  12.2 us
    unnamed x39, local copies, waits for them, and re-layouts  8.12 us
    pallas_call x1, Pallas kernels, shards(): pl.pallas_call(lambda *refs: couple_kernel(members, samples, order, *refs...  7.97 us
    ppermute x2, starting transfers between devices, from_corner(): return lax.ppermute(value, ('lon', 'lat'), pairs)  5.81 us
    ppermute x2, starting transfers between devices, from_lat(): lax.ppermute(value, 'lat', [(i, i + step) for i in range(count) if 0 <= i...  4.77 us
    ppermute x1, starting transfers between devices, neighbour(): return lax.ppermute(value, axis, pairs)  3 us
  transfers between devices with their start and end apart: 16, of which 8 were waited for; matrix products, arithmetic and copies ran while one was open for 1% of the time, Pallas kernels for 15%

profile of v1, /device:TPU:0, one launch (start us, length us, event | category | flops | bytes accessed | tf_op | source)
XLA Modules:
  0.0 87.7 jit_solution(4861918818424006008)
XLA Ops:
  0.6 1.2 %copy-done.1 = bf16[16,64,512]{2,1,0:T(8,128)(2,1)S(1)} copy-done((bf16[16,64,512]{2,1,0:T(8,128)(2,1)S(1)}, bf16[16,64,512]{2,1,0:T(8,128)(2,1)}, u32[]{:S(2)}) %copy-start.1) | copy-done | bytes 1048600
  1.9 1.2 %copy-done.2 = f32[2,4,64,512]{3,2,1,0:T(8,128)S(1)} copy-done((f32[2,4,64,512]{3,2,1,0:T(8,128)S(1)}, f32[2,4,64,512]{3,2,1,0:T(8,128)}, u32[]{:S(2)}) %copy-start.2) | copy-done | bytes 1048600
  3.1 1.0 %copy-done.5 = f32[4,64,512]{2,1,0:T(8,128)S(1)} copy-done((f32[4,64,512]{2,1,0:T(8,128)S(1)}, f32[4,64,512]{2,1,0:T(8,128)}, u32[]{:S(2)}) %copy-start.5) | copy-done | bytes 524312
  4.1 0.9 %copy-done.7 = s32[64,512]{1,0:T(8,128)S(1)} copy-done((s32[64,512]{1,0:T(8,128)S(1)}, s32[64,512]{1,0:T(8,128)}, u32[]{:S(2)}) %copy-start.7) | copy-done | bytes 131096
  5.0 0.7 copy-done.10
  5.7 0.7 copy-done.13
  6.4 1.5 %pack_edges.1 = (f32[4,64,512]{2,1,0:T(8,128)S(1)}, bf16[144,512]{1,0:T(8,128)(2,1)S(1)}, bf16[144,512]{1,0:T(8,128)(2,1)S(1)}, bf16[320,128]{1,0:T(8,128)(2,1)S...) custom-call(s32[16]{0:T(128)S(1)} %copy-done.13, f32[4,64,512]{2,1,0:T(8,128)S(1)} %copy-done.5, ...), custom_call_target="tpu_custom_call" | custom-call | tf_op jit(solution)/shard_map/pack_edges/pallas_call | solution.py:611
  7.9 3.0 %collective-permute-start.2 = (bf16[320,128]{1,0:T(8,128)(2,1)S(1)}, bf16[320,128]{1,0:T(8,128)(2,1)S(1)}, u32[]{:S(2)}, u32[]{:S(2)}) collective-permute-start(bf16[320,128]{1,0:T(8,128)(2,1)S(1)} %get-tuple-element.23.refs_3_), channel_id=1, source_target_pairs={{0,16},{16,0},{1,17},{17,1},{2,18},{18,2},{3,19},{19,3},{4,20},{20... | collective-permute-start | bytes 245768 | tf_op jit(solution)/shard_map/ppermute | solution.py:555
  10.9 3.5 %collective-permute-start = (bf16[144,512]{1,0:T(8,128)(2,1)S(1)}, bf16[144,512]{1,0:T(8,128)(2,1)S(1)}, u32[]{:S(2)}, u32[]{:S(2)}) collective-permute-start(bf16[144,512]{1,0:T(8,128)(2,1)S(1)} %get-tuple-element.21), channel_id=1, source_target_pairs={{0,4},{4,8},{8,12},{1,5},{5,9},{9,13},{2,6},{6,10},{10,14},{3,7},{... | collective-permute-start | bytes 442376 | tf_op jit(solution)/shard_map/ppermute | solution.py:560
  14.4 1.3 %collective-permute-start.1 = (bf16[144,512]{1,0:T(8,128)(2,1)S(1)}, bf16[144,512]{1,0:T(8,128)(2,1)S(1)}, u32[]{:S(2)}, u32[]{:S(2)}) collective-permute-start(bf16[144,512]{1,0:T(8,128)(2,1)S(1)} %get-tuple-element.22), channel_id=1, source_target_pairs={{4,0},{8,4},{12,8},{5,1},{9,5},{13,9},{6,2},{10,6},{14,10},{7,3},{... | collective-permute-start | bytes 442376 | tf_op jit(solution)/shard_map/ppermute | solution.py:560
  15.7 4.5 %collective-permute-start.3 = (bf16[48,128]{1,0:T(8,128)(2,1)S(1)}, bf16[48,128]{1,0:T(8,128)(2,1)S(1)}, u32[]{:S(2)}, u32[]{:S(2)}) collective-permute-start(bf16[48,128]{1,0:T(8,128)(2,1)S(1)} %get-tuple-element.24), channel_id=1, source_target_pairs={{0,20},{4,24},{8,28},{16,4},{20,8},{24,12},{1,21},{5,25},{9,29},{1... | collective-permute-start | bytes 36872 | tf_op jit(solution)/shard_map/ppermute | solution.py:571
  20.3 1.3 %collective-permute-start.4 = (bf16[48,128]{1,0:T(8,128)(2,1)S(1)}, bf16[48,128]{1,0:T(8,128)(2,1)S(1)}, u32[]{:S(2)}, u32[]{:S(2)}) collective-permute-start(bf16[48,128]{1,0:T(8,128)(2,1)S(1)} %get-tuple-element.25), channel_id=1, source_target_pairs={{4,16},{8,20},{12,24},{20,0},{24,4},{28,8},{5,17},{9,21},{13,25},{... | collective-permute-start | bytes 36872 | tf_op jit(solution)/shard_map/ppermute | solution.py:571
  21.6 0.0 copy-start.9
  21.6 2.4 %to_planes.1.refs_0_ = f32[5,16,64,128]{3,2,1,0:T(8,128)S(1)} custom-call(f32[4,64,512]{2,1,0:T(8,128)S(1)} %copy-done.6, f32[2,4,64,512]{3,2,1,0:T(8,128)S(1)} %copy-done.3, f32[4,64,512]{2,1,0:T(8,128)S(1)} %get-tuple-element.20.refs_2_, s32[64,512]{1,0:T(8,128)S(1)} %copy-done.8), custom_call_target="tpu_custom_call" | custom-call | flops 2000000000 | bytes 6291456 | tf_op jit(solution)/shard_map/to_planes/pallas_call | solution.py:639
  24.0 0.0 copy-start.16
  24.0 0.0 copy-start.14
  24.0 0.0 copy-start.4
  24.0 0.0 copy-start.11
  24.0 0.0 copy-start.12
  24.1 0.0 copy-start.15
  24.1 2.7 %collective-permute-done.4.refs_8_.refs_9_ = bf16[48,128]{1,0:T(8,128)(2,1)S(1)} collective-permute-done((bf16[48,128]{1,0:T(8,128)(2,1)S(1)}, bf16[48,128]{1,0:T(8,128)(2,1)S(1)}, u32[]{:S(2)}, u32[]{:S(2)}) %collective-permute-start.4) | collective-permute-done | bytes 12320 | tf_op jit(solution)/shard_map/ppermute | solution.py:571
  26.7 0.0 collective-permute-done.2.refs_4_.refs_5_
  26.8 12.9 %flow_embed.1 = (f32[32,256]{1,0:T(8,128)S(1)}, f32[32,128,256]{2,1,0:T(8,128)}, f32[3,16,64,128]{3,2,1,0:T(8,128)S(1)}) custom-call(f32[5,16,64,128]{3,2,1,0:T(8,128)S(1)} %to_planes.1.refs_0_, bf16[144,512]{1,0:T(8,128)(2,1)S(1)} %collective-permute-done.refs_1_, bf16[144,512]{1,0:T(8,128)(2,1)S(1)} %collective-permute-done.1.refs_2_, ...), custom_call_target="tpu_custom_call" | custom-call | tf_op jit(solution)/shard_map/flow_embed/pallas_call | solution.py:650
  39.6 1.5 %collective-permute-start.5 = (f32[32,256]{1,0:T(8,128)S(1)}, f32[32,256]{1,0:T(8,128)S(1)}, u32[]{:S(2)}, u32[]{:S(2)}) collective-permute-start(f32[32,256]{1,0:T(8,128)S(1)} %get-tuple-element.29.refs_0_), channel_id=1, source_target_pairs={{0,16},{16,0},{1,17},{17,1},{2,18},{18,2},{3,19},{19,3},{4,20},{20... | collective-permute-start | bytes 98312 | tf_op jit(solution)/shard_map/ppermute | solution.py:576
  41.1 0.1 copy.16.refs_6_.refs_5_
  41.3 0.1 copy.15.refs_2_.refs_1_
  41.4 2.2 %collective-permute-done.5.refs_1_ = f32[32,256]{1,0:T(8,128)S(1)} collective-permute-done((f32[32,256]{1,0:T(8,128)S(1)}, f32[32,256]{1,0:T(8,128)S(1)}, u32[]{:S(2)}, u32[]{:S(2)}) %collective-permute-start.5) | collective-permute-done | bytes 32800 | tf_op jit(solution)/shard_map/ppermute | solution.py:576
  43.6 2.2 %copy-done = f32[32,128,256]{2,1,0:T(8,128)S(1)} copy-done((f32[32,128,256]{2,1,0:T(8,128)S(1)}, f32[32,128,256]{2,1,0:T(8,128)}, u32[]{:S(2)}) %copy-start) | copy-done | bytes 4194328
  45.8 2.9 %local_loss.1 = (f32[32,256]{1,0:T(8,128)S(1)}, f32[64,256]{1,0:T(8,128)S(1)}, f32[64,256]{1,0:T(8,128)S(1)}) custom-call(f32[32,256]{1,0:T(8,128)S(1)} %get-tuple-element.29.refs_0_, f32[32,256]{1,0:T(8,128)S(1)} %collective-permute-done.5.refs_1_, s32[16,1]{1,0:T(8,128)S(1)} %copy.15.refs_2_.refs_1_, f32[16,16]{1,0:T(8,128)S(1)} %copy-done.11, ...), custom_call_target="tpu_custom_call" | custom-call | tf_op jit(solution)/shard_map/local_loss/pallas_call | solution.py:725
  48.6 1.6 %collective-permute-start.12 = (f32[32,256]{1,0:T(8,128)S(1)}, f32[32,256]{1,0:T(8,128)S(1)}, u32[]{:S(2)}, u32[]{:S(2)}) collective-permute-start(f32[32,256]{1,0:T(8,128)S(1)} %get-tuple-element.31), channel_id=1, source_target_pairs={{0,2},{1,3},{2,0},{3,1},{4,6},{5,7},{6,4},{7,5},{8,10},{9,11},{10,... | collective-permute-start | bytes 98312 | tf_op jit(solution)/shard_map/ppermute | solution.py:576
  50.2 2.4 %collective-permute-done.12 = f32[32,256]{1,0:T(8,128)S(1)} collective-permute-done((f32[32,256]{1,0:T(8,128)S(1)}, f32[32,256]{1,0:T(8,128)S(1)}, u32[]{:S(2)}, u32[]{:S(2)}) %collective-permute-start.12) | collective-permute-done | bytes 32800 | tf_op jit(solution)/shard_map/ppermute | solution.py:576
  52.6 1.6 %collective-permute-start.13 = (f32[64,256]{1,0:T(8,128)S(1)}, f32[64,256]{1,0:T(8,128)S(1)}, u32[]{:S(2)}, u32[]{:S(2)}) collective-permute-start(f32[64,256]{1,0:T(8,128)S(1)} %pad_maximum_fusion.2), channel_id=1, source_target_pairs={{0,4},{4,0},{8,12},{12,8},{1,5},{5,1},{9,13},{13,9},{2,6},{6,2},{1... | collective-permute-start | bytes 196616 | tf_op jit(solution)/shard_map/ppermute | solution.py:576
  54.2 2.7 %from_planes.1 = (f32[4,64,512]{2,1,0:T(8,128)}, f32[2,4,64,512]{3,2,1,0:T(8,128)}) custom-call(f32[3,16,64,128]{3,2,1,0:T(8,128)S(1)} %get-tuple-element.26.refs_0_), custom_call_target="tpu_custom_call" | custom-call | flops 2000000000 | bytes 6291456 | tf_op jit(solution)/shard_map/from_planes/pallas_call | solution.py:712
  56.9 2.6 %collective-permute-start.14 = (f32[128,256]{1,0:T(8,128)S(1)}, f32[128,256]{1,0:T(8,128)S(1)}, u32[]{:S(2)}, u32[]{:S(2)}) collective-permute-start(f32[128,256]{1,0:T(8,128)S(1)} %pad_maximum_fusion.1), channel_id=1, source_target_pairs={{0,8},{4,12},{8,0},{12,4},{1,9},{5,13},{9,1},{13,5},{2,10},{6,14},... | collective-permute-start | bytes 393224 | tf_op jit(solution)/shard_map/ppermute | solution.py:576
  59.6 1.6 %collective-permute-start.7 = (f32[64,256]{1,0:T(8,128)S(1)}, f32[64,256]{1,0:T(8,128)S(1)}, u32[]{:S(2)}, u32[]{:S(2)}) collective-permute-start(f32[64,256]{1,0:T(8,128)S(1)} %add.19), channel_id=1, source_target_pairs={{0,2},{1,3},{2,0},{3,1},{4,6},{5,7},{6,4},{7,5},{8,10},{9,11},{10,... | collective-permute-start | bytes 196616 | tf_op jit(solution)/shard_map/ppermute | solution.py:576
  61.2 0.6 dynamic-slice_bitcast_fusion
  61.8 2.1 %collective-permute-done.7 = f32[64,256]{1,0:T(8,128)S(1)} collective-permute-done((f32[64,256]{1,0:T(8,128)S(1)}, f32[64,256]{1,0:T(8,128)S(1)}, u32[]{:S(2)}, u32[]{:S(2)}) %collective-permute-start.7) | collective-permute-done | bytes 65568 | tf_op jit(solution)/shard_map/ppermute | solution.py:576
  63.9 1.6 %collective-permute-start.8 = (f32[64,256]{1,0:T(8,128)S(1)}, f32[64,256]{1,0:T(8,128)S(1)}, u32[]{:S(2)}, u32[]{:S(2)}) collective-permute-start(f32[64,256]{1,0:T(8,128)S(1)} %add.20), channel_id=1, source_target_pairs={{0,16},{16,0},{1,17},{17,1},{2,18},{18,2},{3,19},{19,3},{4,20},{20... | collective-permute-start | bytes 196616 | tf_op jit(solution)/shard_map/ppermute | solution.py:576
  65.5 1.0 %collective-permute-done.14 = f32[128,256]{1,0:T(8,128)S(1)} collective-permute-done((f32[128,256]{1,0:T(8,128)S(1)}, f32[128,256]{1,0:T(8,128)S(1)}, u32[]{:S(2)}, u32[]{:S(2)}) %collective-permute-start.14) | collective-permute-done | bytes 131104 | tf_op jit(solution)/shard_map/ppermute | solution.py:576
  66.5 0.1 collective-permute-start.15
  66.7 1.6 %collective-permute-done.8 = f32[64,256]{1,0:T(8,128)S(1)} collective-permute-done((f32[64,256]{1,0:T(8,128)S(1)}, f32[64,256]{1,0:T(8,128)S(1)}, u32[]{:S(2)}, u32[]{:S(2)}) %collective-permute-start.8) | collective-permute-done | bytes 65568 | tf_op jit(solution)/shard_map/ppermute | solution.py:576
  68.3 1.0 %collective-permute-start.9 = (f32[64,256]{1,0:T(8,128)S(1)}, f32[64,256]{1,0:T(8,128)S(1)}, u32[]{:S(2)}, u32[]{:S(2)}) collective-permute-start(f32[64,256]{1,0:T(8,128)S(1)} %add.21), channel_id=1, source_target_pairs={{0,4},{4,0},{8,12},{12,8},{1,5},{5,1},{9,13},{13,9},{2,6},{6,2},{1... | collective-permute-start | bytes 196616 | tf_op jit(solution)/shard_map/ppermute | solution.py:576
  69.3 3.3 %collective-permute-done.9 = f32[64,256]{1,0:T(8,128)S(1)} collective-permute-done((f32[64,256]{1,0:T(8,128)S(1)}, f32[64,256]{1,0:T(8,128)S(1)}, u32[]{:S(2)}, u32[]{:S(2)}) %collective-permute-start.9) | collective-permute-done | bytes 65568 | tf_op jit(solution)/shard_map/ppermute | solution.py:576
  72.6 0.6 collective-permute-start.10
  73.3 5.3 %collective-permute-done.10 = f32[64,256]{1,0:T(8,128)S(1)} collective-permute-done((f32[64,256]{1,0:T(8,128)S(1)}, f32[64,256]{1,0:T(8,128)S(1)}, u32[]{:S(2)}, u32[]{:S(2)}) %collective-permute-start.10) | collective-permute-done | bytes 65568 | tf_op jit(solution)/shard_map/ppermute | solution.py:576
  78.6 0.1 collective-permute-start.11
  78.7 8.0 %couple_grads.1 = (f32[1128,128]{1,0:T(8,128)S(1)}, f32[1,128]{1,0:T(1,128)S(1)}) custom-call(f32[512,256]{1,0:T(8,128)S(1)} %constant_dynamic-update-slice_fusion.refs_0_, s32[16,1]{1,0:T(8,128)S(1)} %copy.15.refs_2_.refs_1_, f32[16,16]{1,0:T(8,128)S(1)} %copy-done.11, f32[264,512]{1,0:T(8,128)S(1)} %copy-done.4, f32[1,512]{1,0:T(1,128)S(1)} %bitcast.8, ...), custom_call_target="tpu_custom_call" | custom-call | flops 3000000000 | bytes 3145728 | tf_op jit(solution)/shard_map/couple_grads/pallas_call | solution.py:763
  86.6 1.1 %finish.1 = f32[1384,128]{1,0:T(8,128)} custom-call(f32[64,256]{1,0:T(8,128)S(1)} %add.23.refs_0_, f32[64,256]{1,0:T(8,128)S(1)} %collective-permute-done.11.refs_1_, f32[1128,128]{1,0:T(8,128)S(1)} %get-tuple-element.34.refs_2_, f32[1,128]{1,0:T(1,128)S(1)} %get-tuple-element.35.refs_3_), custom_call_target="tpu_custom_call" | custom-call | tf_op jit(solution)/shard_map/finish/pallas_call | solution.py:774
  (41 shorter events, 0.2 us)
Async XLA Ops:
  0.6 1.2 %copy-start.1 = (bf16[16,64,512]{2,1,0:T(8,128)(2,1)S(1)}, bf16[16,64,512]{2,1,0:T(8,128)(2,1)}, u32[]{:S(2)}) copy-start(bf16[16,64,512]{2,1,0:T(8,128)(2,1)} %refs_4_.2) | copy-start | bytes 3145732
  1.9 1.2 %copy-start.2 = (f32[2,4,64,512]{3,2,1,0:T(8,128)S(1)}, f32[2,4,64,512]{3,2,1,0:T(8,128)}, u32[]{:S(2)}) copy-start(f32[2,4,64,512]{3,2,1,0:T(8,128)} %refs_1_.3) | copy-start | bytes 3145732
  3.1 1.0 %copy-start.5 = (f32[4,64,512]{2,1,0:T(8,128)S(1)}, f32[4,64,512]{2,1,0:T(8,128)}, u32[]{:S(2)}) copy-start(f32[4,64,512]{2,1,0:T(8,128)} %refs_0_.3) | copy-start | bytes 1572868
  4.1 0.9 %copy-start.7 = (s32[64,512]{1,0:T(8,128)S(1)}, s32[64,512]{1,0:T(8,128)}, u32[]{:S(2)}) copy-start(s32[64,512]{1,0:T(8,128)} %refs_3_.5) | copy-start | bytes 393220
  5.0 0.7 copy-start.10
  5.7 0.7 copy-start.13
  6.4 15.2 %copy-start.3 = (f32[2,4,64,512]{3,2,1,0:T(8,128)S(1)}, f32[2,4,64,512]{3,2,1,0:T(8,128)}, u32[]{:S(2)}) copy-start(f32[2,4,64,512]{3,2,1,0:T(8,128)} %refs_1_.3) | copy-start | bytes 3145732
  6.4 15.2 %copy-start.6 = (f32[4,64,512]{2,1,0:T(8,128)S(1)}, f32[4,64,512]{2,1,0:T(8,128)}, u32[]{:S(2)}) copy-start(f32[4,64,512]{2,1,0:T(8,128)} %refs_0_.3) | copy-start | bytes 1572868
  6.4 15.2 %copy-start.8 = (s32[64,512]{1,0:T(8,128)S(1)}, s32[64,512]{1,0:T(8,128)}, u32[]{:S(2)}) copy-start(s32[64,512]{1,0:T(8,128)} %refs_3_.5) | copy-start | bytes 393220
  7.9 18.8 %collective-permute-start.2 = (bf16[320,128]{1,0:T(8,128)(2,1)S(1)}, bf16[320,128]{1,0:T(8,128)(2,1)S(1)}, u32[]{:S(2)}, u32[]{:S(2)}) collective-permute-start(bf16[320,128]{1,0:T(8,128)(2,1)S(1)} %get-tuple-element.23.refs_3_), channel_id=1, source_target_pairs={{0,16},{16,0},{1,17},{17,1},{2,18},{18,2},{3,19},{19,3},{4,20},{20... | collective-permute-start | bytes 245768 | tf_op jit(solution)/shard_map/ppermute | solution.py:555
  10.9 15.8 %collective-permute-start = (bf16[144,512]{1,0:T(8,128)(2,1)S(1)}, bf16[144,512]{1,0:T(8,128)(2,1)S(1)}, u32[]{:S(2)}, u32[]{:S(2)}) collective-permute-start(bf16[144,512]{1,0:T(8,128)(2,1)S(1)} %get-tuple-element.21), channel_id=1, source_target_pairs={{0,4},{4,8},{8,12},{1,5},{5,9},{9,13},{2,6},{6,10},{10,14},{3,7},{... | collective-permute-start | bytes 442376 | tf_op jit(solution)/shard_map/ppermute | solution.py:560
  14.4 12.3 %collective-permute-start.1 = (bf16[144,512]{1,0:T(8,128)(2,1)S(1)}, bf16[144,512]{1,0:T(8,128)(2,1)S(1)}, u32[]{:S(2)}, u32[]{:S(2)}) collective-permute-start(bf16[144,512]{1,0:T(8,128)(2,1)S(1)} %get-tuple-element.22), channel_id=1, source_target_pairs={{4,0},{8,4},{12,8},{5,1},{9,5},{13,9},{6,2},{10,6},{14,10},{7,3},{... | collective-permute-start | bytes 442376 | tf_op jit(solution)/shard_map/ppermute | solution.py:560
  15.7 8.3 %collective-permute-start.3 = (bf16[48,128]{1,0:T(8,128)(2,1)S(1)}, bf16[48,128]{1,0:T(8,128)(2,1)S(1)}, u32[]{:S(2)}, u32[]{:S(2)}) collective-permute-start(bf16[48,128]{1,0:T(8,128)(2,1)S(1)} %get-tuple-element.24), channel_id=1, source_target_pairs={{0,20},{4,24},{8,28},{16,4},{20,8},{24,12},{1,21},{5,25},{9,29},{1... | collective-permute-start | bytes 36872 | tf_op jit(solution)/shard_map/ppermute | solution.py:571
  20.3 6.5 %collective-permute-start.4 = (bf16[48,128]{1,0:T(8,128)(2,1)S(1)}, bf16[48,128]{1,0:T(8,128)(2,1)S(1)}, u32[]{:S(2)}, u32[]{:S(2)}) collective-permute-start(bf16[48,128]{1,0:T(8,128)(2,1)S(1)} %get-tuple-element.25), channel_id=1, source_target_pairs={{4,16},{8,20},{12,24},{20,0},{24,4},{28,8},{5,17},{9,21},{13,25},{... | collective-permute-start | bytes 36872 | tf_op jit(solution)/shard_map/ppermute | solution.py:571
  21.6 5.2 %copy-start.9 = (bf16[128,256]{1,0:T(8,128)(2,1)S(1)}, bf16[128,256]{1,0:T(8,128)(2,1)}, u32[]{:S(2)}) copy-start(bf16[128,256]{1,0:T(8,128)(2,1)} %refs_10_.1) | copy-start | bytes 196612
  24.0 17.1 %copy-start.16 = (f32[512,16]{0,1:T(8,128)S(1)}, f32[512,16]{0,1:T(8,128)}, u32[]{:S(2)}) copy-start(f32[512,16]{0,1:T(8,128)} %param.20) | copy-start | bytes 98308
  24.0 17.3 %copy-start.14 = (s32[16]{0:T(128)S(1)}, s32[16]{0:T(128)}, u32[]{:S(2)}) copy-start(s32[16]{0:T(128)} %refs_0_.2) | copy-start | bytes 196
  24.0 19.5 %copy-start.4 = (f32[264,512]{1,0:T(8,128)S(1)}, f32[264,512]{1,0:T(8,128)}, u32[]{:S(2)}) copy-start(f32[264,512]{1,0:T(8,128)} %refs_3_.7) | copy-start | bytes 1622020
  24.0 19.5 %copy-start.11 = (f32[16,16]{1,0:T(8,128)S(1)}, f32[16,16]{1,0:T(8,128)}, u32[]{:S(2)}) copy-start(f32[16,16]{1,0:T(8,128)} %refs_2_.3) | copy-start | bytes 3076
  24.0 19.5 %copy-start.12 = (f32[512]{0:T(512)S(1)}, f32[512]{0:T(512)}, u32[]{:S(2)}) copy-start(f32[512]{0:T(512)} %param.19) | copy-start | bytes 6148
  24.1 19.5 %copy-start.15 = (f32[16]{0:T(128)S(1)}, f32[16]{0:T(128)}, u32[]{:S(2)}) copy-start(f32[16]{0:T(128)} %param.21) | copy-start | bytes 196
  39.6 3.9 %collective-permute-start.5 = (f32[32,256]{1,0:T(8,128)S(1)}, f32[32,256]{1,0:T(8,128)S(1)}, u32[]{:S(2)}, u32[]{:S(2)}) collective-permute-start(f32[32,256]{1,0:T(8,128)S(1)} %get-tuple-element.29.refs_0_), channel_id=1, source_target_pairs={{0,16},{16,0},{1,17},{17,1},{2,18},{18,2},{3,19},{19,3},{4,20},{20... | collective-permute-start | bytes 98312 | tf_op jit(solution)/shard_map/ppermute | solution.py:576
  43.6 2.2 %copy-start = (f32[32,128,256]{2,1,0:T(8,128)S(1)}, f32[32,128,256]{2,1,0:T(8,128)}, u32[]{:S(2)}) copy-start(f32[32,128,256]{2,1,0:T(8,128)} %get-tuple-element.30.refs_8_) | copy-start | bytes 12582916
  48.6 4.0 %collective-permute-start.12 = (f32[32,256]{1,0:T(8,128)S(1)}, f32[32,256]{1,0:T(8,128)S(1)}, u32[]{:S(2)}, u32[]{:S(2)}) collective-permute-start(f32[32,256]{1,0:T(8,128)S(1)} %get-tuple-element.31), channel_id=1, source_target_pairs={{0,2},{1,3},{2,0},{3,1},{4,6},{5,7},{6,4},{7,5},{8,10},{9,11},{10,... | collective-permute-start | bytes 98312 | tf_op jit(solution)/shard_map/ppermute | solution.py:576
  52.6 4.3 %collective-permute-start.13 = (f32[64,256]{1,0:T(8,128)S(1)}, f32[64,256]{1,0:T(8,128)S(1)}, u32[]{:S(2)}, u32[]{:S(2)}) collective-permute-start(f32[64,256]{1,0:T(8,128)S(1)} %pad_maximum_fusion.2), channel_id=1, source_target_pairs={{0,4},{4,0},{8,12},{12,8},{1,5},{5,1},{9,13},{13,9},{2,6},{6,2},{1... | collective-permute-start | bytes 196616 | tf_op jit(solution)/shard_map/ppermute | solution.py:576
  56.9 2.6 %collective-permute-start.6 = (f32[64,256]{1,0:T(8,128)S(1)}, f32[64,256]{1,0:T(8,128)S(1)}, u32[]{:S(2)}, u32[]{:S(2)}) collective-permute-start(f32[64,256]{1,0:T(8,128)S(1)} %get-tuple-element.33), channel_id=1, source_target_pairs={{0,1},{1,0},{2,3},{3,2},{4,5},{5,4},{6,7},{7,6},{8,9},{9,8},{10,11... | collective-permute-start | bytes 196616 | tf_op jit(solution)/shard_map/ppermute | solution.py:576
  56.9 9.6 %collective-permute-start.14 = (f32[128,256]{1,0:T(8,128)S(1)}, f32[128,256]{1,0:T(8,128)S(1)}, u32[]{:S(2)}, u32[]{:S(2)}) collective-permute-start(f32[128,256]{1,0:T(8,128)S(1)} %pad_maximum_fusion.1), channel_id=1, source_target_pairs={{0,8},{4,12},{8,0},{12,4},{1,9},{5,13},{9,1},{13,5},{2,10},{6,14},... | collective-permute-start | bytes 393224 | tf_op jit(solution)/shard_map/ppermute | solution.py:576
  59.6 4.3 %collective-permute-start.7 = (f32[64,256]{1,0:T(8,128)S(1)}, f32[64,256]{1,0:T(8,128)S(1)}, u32[]{:S(2)}, u32[]{:S(2)}) collective-permute-start(f32[64,256]{1,0:T(8,128)S(1)} %add.19), channel_id=1, source_target_pairs={{0,2},{1,3},{2,0},{3,1},{4,6},{5,7},{6,4},{7,5},{8,10},{9,11},{10,... | collective-permute-start | bytes 196616 | tf_op jit(solution)/shard_map/ppermute | solution.py:576
  63.9 4.3 %collective-permute-start.8 = (f32[64,256]{1,0:T(8,128)S(1)}, f32[64,256]{1,0:T(8,128)S(1)}, u32[]{:S(2)}, u32[]{:S(2)}) collective-permute-start(f32[64,256]{1,0:T(8,128)S(1)} %add.20), channel_id=1, source_target_pairs={{0,16},{16,0},{1,17},{17,1},{2,18},{18,2},{3,19},{19,3},{4,20},{20... | collective-permute-start | bytes 196616 | tf_op jit(solution)/shard_map/ppermute | solution.py:576
  66.5 12.1 %collective-permute-start.15 = (f32[256,256]{1,0:T(8,128)S(1)}, f32[256,256]{1,0:T(8,128)S(1)}, u32[]{:S(2)}, u32[]{:S(2)}) collective-permute-start(f32[256,256]{1,0:T(8,128)S(1)} %pad_maximum_fusion), channel_id=1, source_target_pairs={{0,1},{1,0},{2,3},{3,2},{4,5},{5,4},{6,7},{7,6},{8,9},{9,8},{10,11... | collective-permute-start | bytes 786440 | tf_op jit(solution)/shard_map/ppermute | solution.py:576
  68.3 4.3 %collective-permute-start.9 = (f32[64,256]{1,0:T(8,128)S(1)}, f32[64,256]{1,0:T(8,128)S(1)}, u32[]{:S(2)}, u32[]{:S(2)}) collective-permute-start(f32[64,256]{1,0:T(8,128)S(1)} %add.21), channel_id=1, source_target_pairs={{0,4},{4,0},{8,12},{12,8},{1,5},{5,1},{9,13},{13,9},{2,6},{6,2},{1... | collective-permute-start | bytes 196616 | tf_op jit(solution)/shard_map/ppermute | solution.py:576
  72.6 5.9 %collective-permute-start.10 = (f32[64,256]{1,0:T(8,128)S(1)}, f32[64,256]{1,0:T(8,128)S(1)}, u32[]{:S(2)}, u32[]{:S(2)}) collective-permute-start(f32[64,256]{1,0:T(8,128)S(1)} %add.22), channel_id=1, source_target_pairs={{0,8},{4,12},{8,0},{12,4},{1,9},{5,13},{9,1},{13,5},{2,10},{6,14},... | collective-permute-start | bytes 196616 | tf_op jit(solution)/shard_map/ppermute | solution.py:576
  78.6 8.1 %collective-permute-start.11 = (f32[64,256]{1,0:T(8,128)S(1)}, f32[64,256]{1,0:T(8,128)S(1)}, u32[]{:S(2)}, u32[]{:S(2)}) collective-permute-start(f32[64,256]{1,0:T(8,128)S(1)} %add.23.refs_0_), channel_id=1, source_target_pairs={{0,1},{1,0},{2,3},{3,2},{4,5},{5,4},{6,7},{7,6},{8,9},{9,8},{10,11... | collective-permute-start | bytes 196616 | tf_op jit(solution)/shard_map/ppermute | solution.py:576

commit v2 on v1

v2 whole, which is shorter than its diff:
```python
import math

import jax
import jax.numpy as jnp
from jax import lax
from jax.experimental import pallas as pl
from jax.experimental.pallas import tpu as pltpu
from jax.sharding import PartitionSpec as P

STEPS = 8
NLEV = 50
PH = 8
PW = 16
HALO = 8
PAD = 16

GRAVITY = 0.45
DRAG_RATE = 0.02
CORI_BASE = 0.05
CORI_SLOPE = 0.1
WIND_SCALE = 0.05
EPSILON = 1e-06
PRECISE = lax.Precision.HIGHEST
F32 = jnp.float32
BF16 = jnp.bfloat16
LANES = 128
MEBI = 2**20


def vmem():
    return pl.BlockSpec(memory_space=pltpu.VMEM)


def smem():
    return pl.BlockSpec(memory_space=pltpu.SMEM)


def params_of(mebi, **rest):
    return pltpu.CompilerParams(vmem_limit_bytes=mebi * MEBI, **rest)


def lane_ids(rows):
    return lax.broadcasted_iota(jnp.int32, (rows, LANES), 1)


def plane_matrix(cols, inverse=False):
    patches = cols // PW
    src = lax.broadcasted_iota(jnp.int32, (cols, cols), 1 if inverse else 0)
    dst = lax.broadcasted_iota(jnp.int32, (cols, cols), 0 if inverse else 1)
    return jnp.where(src == (dst % patches) * PW + dst // patches, 1.0, 0.0).astype(BF16)


def moved(value, matrix):
    high = value.astype(BF16)
    rest = (value - high.astype(F32)).astype(BF16)
    return jnp.dot(high, matrix, preferred_element_type=F32) + jnp.dot(
        rest, matrix, preferred_element_type=F32
    )


def by_segment(pieces, segment):
    out = pieces[-1]
    for index in range(len(pieces) - 2, -1, -1):
        out = jnp.where(segment == index, pieces[index], out)
    return out


def turned(value, shift):
    shift = shift % LANES
    return value if shift == 0 else pltpu.roll(value, shift, 1)


def planes_from(parts, patches):
    rows = parts[0].shape[0]
    per = LANES // patches
    segment = lane_ids(rows) // patches
    planes = []
    for k in range(PW):
        group, place = divmod(k, per)
        block = slice(group * LANES, (group + 1) * LANES)
        planes.append(
            by_segment(
                [turned(part[:, block], (m - place) * patches) for m, part in enumerate(parts)],
                segment,
            )
        )
    return planes


def edges_of(firsts, lasts, patches):
    rows = firsts[0].shape[0]
    lane = lane_ids(rows)
    out = jnp.zeros((rows, LANES), F32)
    for m, (first, last) in enumerate(zip(firsts, lasts)):
        both = jnp.where(lane < HALO, first, turned(last, 2 * HALO))
        here = (lane >= m * patches) & (lane < m * patches + 2 * HALO)
        out = jnp.where(here, turned(both, m * patches), out)
    return out


def forcing_rows(coeff, basis, members):
    acc = [None] * members
    for k in range(basis.shape[0]):
        value = basis[k].astype(F32)
        for m in range(members):
            term = coeff[m][:, k : k + 1] * value
            acc[m] = term if acc[m] is None else acc[m] + term
    return acc


def coefficients(members, ids, props):
    base = lax.axis_index("grp") * members
    return [
        props[pl.ds(ids[base + m], 1), :].astype(BF16).astype(F32) * WIND_SCALE
        for m in range(members)
    ]


def pack_kernel(
    members, ids_in, sea, vel, levels, wind, props_in, low, high, ids, cells, depth, basis, props, sems
):
    rows, cols = levels.shape
    copies = [(ids_in, ids), (props_in, props)]
    ends = ((0, 0), (rows - HALO, rows - 16))
    for side, (r0, w0) in enumerate(ends):
        rs = pl.ds(r0, HALO)
        copies.append((sea.at[:, rs, :], cells.at[side, 0]))
        copies.append((vel.at[0, :, rs, :], cells.at[side, 1]))
        copies.append((vel.at[1, :, rs, :], cells.at[side, 2]))
        copies.append((levels.at[rs, :], depth.at[side]))
        copies.append((wind.at[:, pl.ds(w0, 16), :], basis.at[side]))
    started = [pltpu.make_async_copy(a, b, sems.at[n]) for n, (a, b) in enumerate(copies)]
    for copy in started:
        copy.start()
    for copy in started:
        copy.wait()
    coeff = coefficients(members, ids, props)
    for side, out in ((0, low), (1, high)):
        force = forcing_rows(coeff, basis.at[side], members)
        keep = slice(0, HALO) if side == 0 else slice(16 - HALO, 16)
        blocks = [cells[side, i, m] for i in range(3) for m in range(members)]
        blocks += [force[m][keep] for m in range(members)]
        blocks += [depth[side].astype(F32), jnp.zeros((HALO, cols), F32)]
        for g in range(0, len(blocks), 2):
            pair = jnp.concatenate(blocks[g : g + 2], axis=0)
            out[g * HALO : (g + 2) * HALO, :] = pair.astype(BF16)


def planar_kernel(members, ids, sea, vel, levels, wind, props, out, side):
    rows, cols = levels.shape
    patches = cols // PW
    coeff = coefficients(members, ids, props)
    strips = [
        forcing_rows(coeff, wind.at[:, pl.ds(r0, 16), :], members) for r0 in range(0, rows, 16)
    ]
    force = jnp.concatenate([strip[m] for m in range(members) for strip in strips], axis=0)
    depth = levels[...].astype(F32)
    matrix = plane_matrix(cols)
    scale = 1.0 / GRAVITY
    full = (members * rows, cols)
    fields = [sea[...].reshape(full), vel[0].reshape(full), vel[1].reshape(full), force, depth]
    for i, value in enumerate(fields):
        starts = [m * rows if i < 4 else 0 for m in range(members)]
        edge = edges_of(
            [value[r : r + rows, :LANES] for r in starts],
            [value[r : r + rows, cols - LANES :] for r in starts],
            patches,
        )
        side[i * rows : (i + 1) * rows, :] = edge.astype(BF16)
        if i < 4:
            spread = moved(value if i == 0 else value * scale, matrix)
        else:
            spread = jnp.dot(value.astype(BF16), matrix, preferred_element_type=F32)
        parts = [spread[r : r + rows] for r in starts]
        for k, plane in enumerate(planes_from(parts, patches)):
            out[i, k] = plane


def starts_of(i, members):
    if i < 4:
        return [(i * members + m) * HALO for m in range(members)]
    return [4 * members * HALO] * members


def rim_kernel(members, patches, south, north, side, out):
    rows = side.shape[0] // 5
    cols = south.shape[1]
    low, high = south[...].astype(F32), north[...].astype(F32)
    for i in range(5):
        ends = [
            edges_of(
                [plain[s : s + HALO, :LANES] for s in starts_of(i, members)],
                [plain[s : s + HALO, cols - LANES :] for s in starts_of(i, members)],
                patches,
            )
            for plain in (low, high)
        ]
        own = side[i * rows : (i + 1) * rows, :].astype(F32)
        whole = jnp.concatenate([ends[0], own, ends[1]], axis=0)
        out[i * whole.shape[0] : (i + 1) * whole.shape[0], :] = whole.astype(BF16)


def halo_kernel(members, south, north, out):
    cols = south.shape[1]
    matrix = plane_matrix(cols)
    for end, got in enumerate((south, north)):
        spread = jnp.dot(got[...], matrix, preferred_element_type=F32)
        for i in range(5):
            parts = [spread[s : s + HALO] for s in starts_of(i, members)]
            for k, plane in enumerate(planes_from(parts, cols // PW)):
                out[end, i, k] = plane if i in (0, 4) else plane * (1.0 / GRAVITY)


def back_kernel(members, state, sea, vel):
    rows, cols = sea.shape[1:]
    patches = cols // PW
    per = LANES // patches
    matrix = plane_matrix(cols, inverse=True)
    segment = lane_ids(rows) // patches
    for i in range(3):
        parts = []
        for m in range(members):
            groups = []
            for g in range(PW // per):
                pieces = [
                    turned(state[i, g * per + j, PAD : PAD + rows, :], (j - m) * patches)
                    for j in range(per)
                ]
                groups.append(by_segment(pieces, segment))
            parts.append(jnp.concatenate(groups, axis=1))
        value = moved(jnp.concatenate(parts, axis=0), matrix)
        for m in range(members):
            part = value[m * rows : (m + 1) * rows]
            if i == 0:
                sea[m] = part
            else:
                vel[i - 1, m] = part * GRAVITY


def flow_step(src, src_rim, dst, dst_rim, force, force_rim, hu, hv, hvu, cu, cv, last_mask, rows, patches):
    strip = PW
    end = PAD + rows + HALO
    half = (rows + 2 * HALO) // 2
    keep = 1.0 - DRAG_RATE
    for r0 in range(PAD - HALO, end, half):
        here, up, down = pl.ds(r0, half), pl.ds(r0 + 1, half), pl.ds(r0 - 1, half)
        last = lane_ids(half) % patches == patches - 1

        def wrap_left(plane, rim):
            return pltpu.roll(jnp.where(last, rim, plane), 1, 1)

        def wrap_right(plane, rim):
            return jnp.where(last, pltpu.roll(rim, PW - 1, 1), pltpu.roll(plane, LANES - 1, 1))

        def of(planes, rim, i, p):
            return rim.at[i] if p == strip else planes.at[i, p]

        def new_level(p, fx, fx_right):
            n_up = of(src, src_rim, 2, p)[up, :]
            n = of(src, src_rim, 2, p)[here, :]
            fy = hvu[p, here, :] * n_up - hv[p, here, :] * n
            level = of(src, src_rim, 0, p)[here, :] - ((fx_right - fx) + fy)
            of(dst, dst_rim, 0, p)[here, :] = level
            return level, n, n + n_up

        def new_flow(p, e, e_right, em, em_right, n, v, level, level_left):
            u = (e + e_right) + (em + em_right)
            push = force_rim[here, :] if p == strip else force[p, here, :]
            of(dst, dst_rim, 1, p)[here, :] = (
                keep * e + cu[here, :] * v - (level - level_left) + push
            )
            level_down = of(dst, dst_rim, 0, p)[down, :]
            north = keep * n - cv[here, :] * u - (level - level_down)
            home = of(dst, dst_rim, 2, p)
            if r0 + half == end:
                home[pl.ds(r0, half - HALO), :] = north[: half - HALO]
                home[pl.ds(end - HALO, HALO), :] = north[half - HALO :] * last_mask
            else:
                home[here, :] = north

        e_rim = src_rim[1, here, :]
        em_rim = src_rim[1, down, :]
        fx_rim = hu[strip, here, :] * e_rim
        level_rim, n_rim, vs_rim = new_level(strip, fx_rim, pltpu.roll(fx_rim, LANES - 1, 1))
        new_flow(
            strip,
            e_rim,
            pltpu.roll(e_rim, LANES - 1, 1),
            em_rim,
            pltpu.roll(em_rim, LANES - 1, 1),
            n_rim,
            vs_rim + pltpu.roll(vs_rim, 1, 1),
            level_rim,
            pltpu.roll(level_rim, 1, 1),
        )
        e_end = wrap_right(src[1, 0, here, :], e_rim)
        em_end = wrap_right(src[1, 0, down, :], em_rim)
        e_last = src[1, PW - 1, here, :]
        level_last, n_last, vs_last = new_level(
            PW - 1, hu[PW - 1, here, :] * e_last, hu[PW + 1, here, :] * e_end
        )
        level_left = wrap_left(level_last, level_rim)
        vs_left = wrap_left(vs_last, vs_rim)
        e = src[1, 0, here, :]
        em = src[1, 0, down, :]
        fx = hu[0, here, :] * e
        for p in range(PW):
            if p < PW - 1:
                e_right = src[1, p + 1, here, :]
                em_right = src[1, p + 1, down, :]
                fx_right = hu[p + 1, here, :] * e_right
                level, n, vs = new_level(p, fx, fx_right)
            else:
                e_right, em_right, fx_right = e_end, em_end, None
                level, n, vs = level_last, n_last, vs_last
            new_flow(p, e, e_right, em, em_right, n, vs + vs_left, level, level_left)
            level_left, vs_left, e, em, fx = level, vs, e_right, em_right, fx_right


def flow_kernel(
    members,
    rows,
    cols,
    lat_count,
    planes,
    halo,
    side,
    east,
    west,
    weight,
    partial,
    gram,
    state_a,
    state_b,
    force,
    depth,
    rim_a,
    rim_b,
    force_rim,
    depth_rim,
    hu,
    hv,
    hvu,
    cu,
    cv,
    w_rows,
    w_planes,
    patch_t,
    slope,
):
    patches = cols // PW
    lat = lax.axis_index("lat")
    strip = PW
    height = rows + 2 * PAD
    wide = rows + 2 * HALO
    scale = 1.0 / GRAVITY
    edge_rows = (slice(0, HALO), slice(height - HALO, height))
    for i in range(3):
        for rs in edge_rows:
            rim_a[i, rs, :] = jnp.zeros((HALO, LANES), F32)
            rim_b[i, rs, :] = jnp.zeros((HALO, LANES), F32)
            for p in range(PW):
                state_a[i, p, rs, :] = jnp.zeros((HALO, LANES), F32)
                state_b[i, p, rs, :] = jnp.zeros((HALO, LANES), F32)
    homes = (state_a.at[0], state_a.at[1], state_a.at[2], force, depth)
    for i, home in enumerate(homes):
        home[:, PAD : PAD + rows, :] = planes[i]
        home[:, PAD - HALO : PAD, :] = halo[0, i]
        home[:, PAD + rows : PAD + rows + HALO, :] = halo[1, i]
    for rs in edge_rows:
        depth_rim[rs, :] = jnp.zeros((HALO, LANES), F32)
        for p in range(PW):
            depth[p, rs, :] = jnp.zeros((HALO, LANES), F32)
    place = lane_ids(wide) % patches
    rim_homes = (rim_a.at[0], rim_a.at[1], rim_a.at[2], force_rim, depth_rim)
    for i, home in enumerate(rim_homes):
        rs = slice(i * wide, (i + 1) * wide)
        rim = jnp.where(
            place < 2 * HALO,
            side[rs, :].astype(F32),
            jnp.where(
                place < 3 * HALO,
                pltpu.roll(east[rs, :].astype(F32), 2 * HALO, 1),
                pltpu.roll(west[rs, :].astype(F32), LANES - 2 * HALO, 1),
            ),
        )
        home[PAD - HALO : PAD + rows + HALO, :] = rim * (1.0 if i in (0, 4) else scale)
    for h in range(w_rows.shape[0]):
        cs = slice(h * LANES, (h + 1) * LANES)
        w_rows[h] = weight[:, cs].astype(F32)
        w_planes[:, cs] = jnp.concatenate(
            [w_rows[h, pl.ds(k, PH, stride=PW), :] for k in range(PW)], axis=0
        ).astype(BF16)
    span = slice(PAD - HALO, PAD + rows + HALO)
    row = lax.broadcasted_iota(jnp.int32, (wide, LANES), 0) + (lat * rows - HALO)
    inside = (row >= 0) & (row < lat_count * rows)
    place = row.astype(F32)
    total = lat_count * rows
    cu[span, :] = jnp.where(
        inside, 0.25 * (CORI_BASE + CORI_SLOPE * (place + 0.5) / total), 0.0
    )
    cv[span, :] = jnp.where(inside, 0.25 * (CORI_BASE + CORI_SLOPE * place / total), 0.0)
    half_depth = 0.5 * GRAVITY / NLEV
    last = lane_ids(wide) % patches == patches - 1
    for p in range(PW + 1):
        home = depth_rim if p == strip else depth.at[p]
        here = home[span, :]
        if p == 0:
            left = pltpu.roll(jnp.where(last, depth_rim[span, :], depth[PW - 1, span, :]), 1, 1)
        elif p == strip:
            left = pltpu.roll(here, 1, 1)
        else:
            left = depth[p - 1, span, :]
        below = home[PAD - HALO - 1 : PAD + rows + HALO - 1, :]
        above = home[PAD - HALO + 1 : PAD + rows + HALO + 1, :]
        hu[p, span, :] = half_depth * (here + left)
        hv[p, span, :] = half_depth * (here + below)
        hvu[p, span, :] = jnp.where(inside, half_depth * (here + above), 0.0)
    hu[PW + 1, span, :] = jnp.where(
        last,
        pltpu.roll(hu[strip, span, :], PW - 1, 1),
        pltpu.roll(hu[0, span, :], LANES - 1, 1),
    )

    last_mask = jnp.where(lat < lat_count - 1, 1.0, 0.0)
    count = rows // PH

    def two_steps(turn, carry):
        for sub, (src, src_rim, dst, dst_rim) in enumerate(
            ((state_a, rim_a, state_b, rim_b), (state_b, rim_b, state_a, rim_a))
        ):
            flow_step(
                src, src_rim, dst, dst_rim, force, force_rim, hu, hv, hvu, cu, cv, last_mask, rows, patches
            )
            total = None
            for b in range(count):
                cells = dst[0, :, PAD + b * PH : PAD + (b + 1) * PH, :].reshape(PW * PH, LANES)
                cells_t = cells.T.astype(BF16)
                act = jnp.tanh(jnp.dot(cells_t, w_planes[...], preferred_element_type=F32))
                total = act if total is None else total + act
                fall = (1.0 - act * act).astype(BF16)
                for m in range(members):
                    rs = slice(m * patches, (m + 1) * patches)
                    to = slice(b * patches, (b + 1) * patches)
                    patch_t[m, to, :] = cells_t[rs]
                    slope[m, to, :] = fall[rs]
            sums = jnp.sum(total.reshape(members, patches, total.shape[1]), axis=1)
            partial[turn, sub * members : (sub + 1) * members, :] = sums
            for m in range(members):
                gram[(2 * turn + sub) * members + m] = lax.dot_general(
                    patch_t[m], slope[m], (((0,), (0,)), ((), ())), preferred_element_type=F32
                )
        return carry

    lax.fori_loop(0, STEPS // 2, two_steps, 0)


def split(value):
    high = value.astype(BF16)
    return high, (value - high.astype(F32)).astype(BF16)


def dot(a, b, ca=1, cb=0):
    return lax.dot_general(a, b, (((ca,), (cb,)), ((), ())), preferred_element_type=F32)


def mm(a, b, ca=1, cb=0):
    return dot(a[0], b[0], ca, cb) + (dot(a[0], b[1], ca, cb) + dot(a[1], b[0], ca, cb))


def member_params(ids_col, props):
    count = props.shape[0]
    hot = jnp.where(ids_col[...] == lax.broadcasted_iota(jnp.int32, (count, count), 1), 1.0, 0.0)
    return jnp.dot(hot, props[...], precision=PRECISE, preferred_element_type=F32)


def repeated(rows, count):
    return jnp.concatenate([rows] * count, axis=0)


def flow_grads(lower_in, upper, summary, w_in, w_out, b_out):
    half = upper.shape[1]
    width = 2 * half
    sums = split(summary)
    w_sum = split(w_in[half:, :])
    hidden = jnp.tanh(mm(sums, w_sum) + lower_in)
    hid = split(hidden)
    out_w = split(w_out[...])
    both = dot(hid[0], jnp.concatenate(out_w, axis=1))
    raw = both[:, :width] + both[:, width:] + dot(hid[1], out_w[0]) + b_out[...]
    log_scale = jnp.tanh(raw[:, :half])
    grown = upper * jnp.exp(log_scale)
    latent = grown + raw[:, half:]
    d_scale = (latent * grown - 1.0) * (1.0 - log_scale * log_scale)
    d_raw = jnp.concatenate([d_scale, latent], axis=1)
    d_r = split(d_raw)
    d_hidden = dot(
        jnp.concatenate([d_r[0], d_r[1], d_r[0]], axis=1),
        jnp.concatenate([out_w[0], out_w[0], out_w[1]], axis=1),
        1,
        1,
    )
    d_hidden = d_hidden * (1.0 - hidden * hidden)
    return sums, hid, d_raw, d_r, d_hidden, w_sum


def local_kernel(
    members, inv_root, mine, theirs, ids, props, w_in, b_in, w_out, b_out, gram, kept, sent, total
):
    sums = (mine[...] + theirs[...]) * inv_root
    count = sums.shape[0]
    params = member_params(ids, props)
    half = params.shape[1] // 2
    low = split(params[:, :half])
    low_in = mm(low, split(w_in[:half, :])) + b_in[...]
    slot = lax.broadcasted_iota(jnp.int32, (count, params.shape[0]), 1)
    row = lax.broadcasted_iota(jnp.int32, (count, params.shape[0]), 0)
    hot = jnp.where(slot == lax.axis_index("grp") * members + row % members, 1.0, 0.0)
    low_in = jnp.dot(hot, low_in, precision=PRECISE, preferred_element_type=F32)
    upper = jnp.dot(hot, params[:, half:], precision=PRECISE, preferred_element_type=F32)
    _, _, _, _, d_hidden, w_sum = flow_grads(low_in, upper, sums, w_in, w_out, b_out)
    d_summary = mm(split(d_hidden), w_sum, 1, 1) * inv_root
    acc = gram[0] * d_summary[0:1, :]
    for i in range(1, count):
        acc = acc + gram[i] * d_summary[i : i + 1, :]
    total[...] = acc
    cells = acc.shape[0] // 2
    core = lax.axis_index("grp") % 2
    kept[...] = total[pl.ds(pl.multiple_of(core * cells, 8), cells), :]
    sent[...] = total[pl.ds(pl.multiple_of((1 - core) * cells, 8), cells), :]


def couple_kernel(
    members, lat_count, grp_count, order, summary, ids, props, w_in, b_in, w_out, b_out, rows, square, sorted_sums, staged
):
    per = summary.shape[0] // len(order)
    for index, (lat_flip, grp_flip) in enumerate(order):
        block = (lax.axis_index("lat") ^ lat_flip) * grp_count + (lax.axis_index("grp") ^ grp_flip)
        sorted_sums[pl.ds(pl.multiple_of(block * per, per), per), :] = summary[
            index * per : (index + 1) * per, :
        ]
    params = member_params(ids, props)
    half = params.shape[1] // 2
    low_in = mm(split(params[:, :half]), split(w_in[:half, :])) + b_in[...]
    groups = [slice(g * members, (g + 1) * members) for g in range(grp_count)]
    steps = per // members
    spread = lambda value: jnp.concatenate(
        [repeated(value[rs], steps) for rs in groups] * lat_count, axis=0
    )
    lower = spread(params[:, :half])
    sums, hid, d_raw, d_r, d_hidden, _ = flow_grads(
        spread(low_in), spread(params[:, half:]), sorted_sums[...], w_in, w_out, b_out
    )
    low = split(lower)
    context = [jnp.concatenate([sums[n], low[n]], axis=1) for n in range(2)]
    g_in = mm(context, split(d_hidden), 0, 0)
    width = 2 * half
    both = dot(hid[0], jnp.concatenate(d_r, axis=1), 0, 0)
    g_out = both[:, :width] + both[:, width:] + dot(hid[1], d_r[0], 0, 0)
    g_in_b = jnp.sum(d_hidden, axis=0, keepdims=True)
    g_out_b = jnp.sum(d_raw, axis=0, keepdims=True)
    hidden = d_hidden.shape[1]
    per_row = hidden // LANES
    feats = summary.shape[1]
    fold = LANES // width
    base = (half + feats) * per_row
    after = base + per_row
    tail = after + hidden // fold
    rows[base:, :] = jnp.zeros((rows.shape[0] - base, LANES), F32)
    for q in range(per_row):
        cs = slice(q * LANES, (q + 1) * LANES)
        rows[pl.ds(q, half, stride=per_row), :] = g_in[feats:, cs]
        rows[pl.ds(half * per_row + q, feats, stride=per_row), :] = g_in[:feats, cs]
        rows[base + q : base + q + 1, :] = g_in_b[:, cs]
    staged[...] = jnp.concatenate([g_out, jnp.zeros((hidden, LANES - width), F32)], axis=1)
    packed = jnp.zeros((hidden // fold, LANES), F32)
    for j in range(fold):
        packed = packed + turned(staged[pl.ds(j, hidden // fold, stride=fold), :], j * width)
    rows[after:tail, :] = packed
    rows[tail : tail + 1, :] = jnp.concatenate(
        [g_out_b, jnp.zeros((1, LANES - width), F32)], axis=1
    )
    whole = rows[...]
    square[...] = jnp.sum(whole * whole, axis=0, keepdims=True)


def finish_kernel(count, mine, theirs, couple, square, out, whole):
    core = lax.axis_index("grp") % 2
    cells = mine.shape[0]
    per_row = mine.shape[1] // LANES
    for h in range(per_row):
        cs = slice(h * LANES, (h + 1) * LANES)
        whole[h, pl.ds(pl.multiple_of(core * cells, 8), cells), :] = mine[:, cs]
        whole[h, pl.ds(pl.multiple_of((1 - core) * cells, 8), cells), :] = theirs[:, cs]
    conv = whole[...]
    squares = jnp.sum(conv * conv) + jnp.sum(square[...])
    scale = -lax.rsqrt(jnp.full((1, 1), squares, F32) / count + EPSILON)
    for r in range(PH):
        for h in range(per_row):
            part = whole[h, pl.ds(r, PW, stride=PH), :]
            out[pl.ds(r * PW * per_row + h, PW, stride=per_row), :] = part * scale
    used = 2 * cells * per_row
    out[used : used + couple.shape[0], :] = couple[...] * scale


def neighbour(value, axis, step):
    count = lax.axis_size(axis)
    pairs = [(i, (i + step) % count) for i in range(count)]
    return lax.ppermute(value, axis, pairs)


def from_lat(value, step):
    count = lax.axis_size("lat")
    return lax.ppermute(value, "lat", [(i, i + step) for i in range(count) if 0 <= i + step < count])


def swapped(value, axis, flip):
    count = lax.axis_size(axis)
    return lax.ppermute(value, axis, [(i, i ^ flip) for i in range(count)])


def flips(axis):
    count = lax.axis_size(axis)
    return [1 << i for i in range(count.bit_length() - 1)]


def shape(*dims, dtype=F32):
    return jax.ShapeDtypeStruct(dims, dtype)


def shards(
    sea_surface,
    velocity,
    levels,
    wind_basis,
    proposals,
    member_ids,
    conv_weight,
    couple_in,
    couple_in_bias,
    couple_out,
    couple_out_bias,
):
    members, rows, cols = sea_surface.shape
    lat_count, lon_count = lax.axis_size("lat"), lax.axis_size("lon")
    grp_count = lax.axis_size("grp")
    cells, feats = conv_weight.shape
    hid, width = couple_out.shape
    patches = cols // PW
    samples = STEPS * members
    groups = (4 * members + 2) * HALO
    height = rows + 2 * PAD
    inv_root = 1.0 / math.sqrt(rows // PH * (cols * lon_count // PW))

    anywhere = pl.BlockSpec(memory_space=pl.ANY)
    low, high = pl.pallas_call(
        lambda *refs: pack_kernel(members, *refs),
        out_shape=(shape(groups, cols, dtype=BF16), shape(groups, cols, dtype=BF16)),
        in_specs=[anywhere] * 6,
        out_specs=(vmem(), vmem()),
        scratch_shapes=[
            pltpu.SMEM(member_ids.shape, jnp.int32),
            pltpu.VMEM((2, 3, members, HALO, cols), F32),
            pltpu.VMEM((2, HALO, cols), jnp.int32),
            pltpu.VMEM((2, wind_basis.shape[0], 16, cols), BF16),
            pltpu.VMEM(proposals.shape, F32),
            pltpu.SemaphoreType.DMA((12,)),
        ],
        compiler_params=params_of(60),
        name="pack_rows",
    )(member_ids, sea_surface, velocity, levels, wind_basis, proposals)

    south = from_lat(high, 1)
    north = from_lat(low, -1)

    planes, side = pl.pallas_call(
        lambda *refs: planar_kernel(members, *refs),
        out_shape=(shape(5, PW, rows, LANES), shape(5 * rows, LANES, dtype=BF16)),
        in_specs=[smem()] + [vmem()] * 5,
        out_specs=(vmem(), vmem()),
        compiler_params=params_of(32),
        cost_estimate=pl.CostEstimate(flops=2 * 10**9, bytes_accessed=6 * MEBI, transcendentals=0),
        name="to_planes",
    )(member_ids, sea_surface, velocity, levels, wind_basis, proposals)

    wide = rows + 2 * HALO
    rim = pl.pallas_call(
        lambda *refs: rim_kernel(members, patches, *refs),
        out_shape=shape(5 * wide, LANES, dtype=BF16),
        in_specs=[vmem()] * 3,
        out_specs=vmem(),
        compiler_params=params_of(16),
        name="rim",
    )(south, north, side)
    west = neighbour(rim, "lon", 1)
    east = west if lon_count == 2 else neighbour(rim, "lon", -1)

    halo = pl.pallas_call(
        lambda *refs: halo_kernel(members, *refs),
        out_shape=shape(2, 5, PW, HALO, LANES),
        in_specs=[vmem()] * 2,
        out_specs=vmem(),
        compiler_params=params_of(16),
        cost_estimate=pl.CostEstimate(flops=10**9, bytes_accessed=4 * MEBI, transcendentals=0),
        name="halo_planes",
    )(south, north)

    partial, gram, final = pl.pallas_call(
        lambda *refs: flow_kernel(members, rows, cols, lat_count, *refs),
        out_shape=(
            shape(STEPS // 2, 2 * members, feats),
            shape(samples, cells, feats),
            shape(3, PW, height, LANES),
        ),
        in_specs=[vmem()] * 6,
        out_specs=(vmem(),) * 3,
        scratch_shapes=[
            pltpu.VMEM((3, PW, height, LANES), F32),
            pltpu.VMEM((PW, height, LANES), F32),
            pltpu.VMEM((PW, height, LANES), F32),
            pltpu.VMEM((3, height, LANES), F32),
            pltpu.VMEM((3, height, LANES), F32),
            pltpu.VMEM((height, LANES), F32),
            pltpu.VMEM((height, LANES), F32),
            pltpu.VMEM((PW + 2, height, LANES), F32),
            pltpu.VMEM((PW + 1, height, LANES), F32),
            pltpu.VMEM((PW + 1, height, LANES), F32),
            pltpu.VMEM((height, LANES), F32),
            pltpu.VMEM((height, LANES), F32),
            pltpu.VMEM((feats // LANES, cells, LANES), F32),
            pltpu.VMEM((cells, feats), BF16),
            pltpu.VMEM((members, rows // PH * patches, cells), BF16),
            pltpu.VMEM((members, rows // PH * patches, feats), BF16),
        ],
        compiler_params=params_of(32),
        name="flow_embed",
    )(planes, halo, rim, east, west, conv_weight)
    partial = partial.reshape(samples, feats)

    if lon_count == 2:
        others = swapped(partial, "lon", 1)
    else:
        others = lax.psum(partial, "lon") - partial
    summaries = (partial + others) * inv_root

    ids_col = member_ids.reshape(-1, 1)
    b_in = couple_in_bias.reshape(1, -1)
    b_out = couple_out_bias.reshape(1, -1)
    kept, sent = pl.pallas_call(
        lambda *refs: local_kernel(members, inv_root, *refs),
        out_shape=(shape(cells // 2, feats), shape(cells // 2, feats)),
        in_specs=[vmem()] * 9,
        out_specs=(vmem(),) * 2,
        scratch_shapes=[pltpu.VMEM((cells, feats), F32)],
        compiler_params=params_of(16),
        name="local_loss",
    )(partial, others, ids_col, proposals, couple_in, b_in, couple_out, b_out, gram)

    conv = kept + swapped(sent, "grp", 1)
    if lon_count == 2:
        corner = lax.ppermute(
            conv,
            ("lon", "grp"),
            [(i, (i // grp_count ^ 1) * grp_count + (i % grp_count ^ 2)) for i in range(2 * grp_count)],
        )
        conv = (conv + swapped(conv, "lon", 1)) + (swapped(conv, "grp", 2) + corner)
    else:
        conv = conv + swapped(conv, "grp", 2)
        for flip in flips("lon"):
            conv = conv + swapped(conv, "lon", flip)
    for flip in reversed(flips("lat")):
        conv = conv + swapped(conv, "lat", flip)
    conv_other = swapped(conv, "grp", 1)

    gathered = summaries.astype(jnp.float16)
    order = [(0, 0)]
    for axis, flip in [("grp", 2)] + [("lat", f) for f in reversed(flips("lat"))] + [("grp", 1)]:
        gathered = jnp.concatenate([gathered, swapped(gathered, axis, flip)], axis=0)
        order = order + [(a ^ flip, b) if axis == "lat" else (a, b ^ flip) for a, b in order]

    low_rows = (couple_in.size + hid + couple_out.size) // LANES + 1
    low_rows = -(-low_rows // 8) * 8
    count = cells * feats + couple_in.size + hid + couple_out.size + width
    couple, square = pl.pallas_call(
        lambda *refs: couple_kernel(members, lat_count, grp_count, order, *refs),
        out_shape=(shape(low_rows, LANES), shape(1, LANES)),
        in_specs=[vmem()] * 7,
        out_specs=(vmem(), vmem()),
        scratch_shapes=[
            pltpu.VMEM((len(order) * samples, feats), F32),
            pltpu.VMEM((hid, LANES), F32),
        ],
        compiler_params=params_of(24),
        cost_estimate=pl.CostEstimate(flops=3 * 10**9, bytes_accessed=3 * MEBI, transcendentals=0),
        name="couple_grads",
    )(gathered.astype(F32), ids_col, proposals, couple_in, b_in, couple_out, b_out)

    surface_out, velocity_out = pl.pallas_call(
        lambda *refs: back_kernel(members, *refs),
        out_shape=(shape(members, rows, cols), shape(2, members, rows, cols)),
        in_specs=[vmem()],
        out_specs=(vmem(), vmem()),
        compiler_params=params_of(24),
        cost_estimate=pl.CostEstimate(flops=2 * 10**9, bytes_accessed=6 * MEBI, transcendentals=0),
        name="from_planes",
    )(final)

    stepped = pl.pallas_call(
        lambda *refs: finish_kernel(count, *refs),
        out_shape=shape(cells * feats // LANES + low_rows, LANES),
        in_specs=[vmem()] * 4,
        out_specs=vmem(),
        scratch_shapes=[pltpu.VMEM((feats // LANES, cells, LANES), F32)],
        compiler_params=params_of(16),
        name="finish",
    )(conv, conv_other, couple, square)
    weight_step = stepped.reshape(-1)[:count]

    items = samples // lon_count
    own = lax.dynamic_slice_in_dim(summaries, lax.axis_index("lon") * items, items, axis=0)
    return (surface_out, velocity_out, own.reshape(1, 1, 1, items, feats), weight_step)


def solution(mesh):
    in_specs = (
        P("grp", "lat", "lon"),
        P(None, "grp", "lat", "lon"),
        P("lat", "lon"),
        P(None, "lat", "lon"),
        P(),
        P(),
        P(),
        P(),
        P(),
        P(),
        P(),
    )
    out_specs = (
        P("grp", "lat", "lon"),
        P(None, "grp", "lat", "lon"),
        P("lon", "lat", "grp", None, None),
        P(),
    )
    return jax.shard_map(shards, mesh=mesh, in_specs=in_specs, out_specs=out_specs, check_vma=False)
```

time: 88.2 us -> 69.7 us (0.79)
  local copies, waits for them, and re-layouts: 8.83 us -> 3.36 us
  waiting for transfers between devices: 20.6 us -> 15.4 us
  Pallas kernels: 31.4 us -> 26.4 us
  starting transfers between devices: 25.8 us -> 23.2 us
    ppermute x11, waiting for transfers between devices: 18 us -> 11.1 us  [swapped(): return lax.ppermute(value, axis, [(i, i ^ flip) for i in range(count)])]
    unnamed x39 -> x26, local copies, waits for them, and re-layouts: 8.12 us -> 2.63 us
    ppermute x2 -> x1, starting transfers between devices: 5.81 us -> 1.05 us  [shards(): lax.ppermute(conv, ('lon', 'grp'), [(i, (i // grp_count ^ 1) * grp_count...]
    pallas_call x2 -> x4, Pallas kernels: 10.4 us -> 7.59 us  [the longest x1 4.06 us: shards(): pl.pallas_call(lambda *refs: planar_kernel(members, *refs), out_shape=(sh...]
    ppermute x1, waiting for transfers between devices: 0.01 us -> 2.19 us  [neighbour(): return lax.ppermute(value, axis, pairs)]
    ppermute x11, starting transfers between devices: 12.2 us -> 14.4 us  [swapped(): return lax.ppermute(value, axis, [(i, i ^ flip) for i in range(count)])]
    pallas_call x1, Pallas kernels: 12.9 us -> 10.8 us  [shards(): pl.pallas_call(lambda *refs: flow_kernel(members, rows, cols, lat_count,...]
    ppermute x2, starting transfers between devices: 4.77 us -> 6.23 us  [from_lat(): lax.ppermute(value, 'lat', [(i, i + step) for i in range(count) if 0 <= i...]
  transfers between devices with their start and end apart: 16 -> 15, of which waited for: 8 -> 7; matrix products, arithmetic and copies ran while one was open for 1% -> 1% of each run, Pallas kernels for 15% -> 17%
where the time goes in v2:
time: 69.7 us; the launch traced here: 69.4 us
  Pallas kernels  26.4 us (38%)
  starting transfers between devices  23.2 us (33%)
  waiting for transfers between devices  15.4 us (22%)
  local copies, waits for them, and re-layouts  3.36 us (5%)
  between operations  0.92 us (1%)
    ppermute x11, starting transfers between devices, swapped(): return lax.ppermute(value, axis, [(i, i ^ flip) for i in range(count)])  14.4 us
    ppermute x11, waiting for transfers between devices, swapped(): return lax.ppermute(value, axis, [(i, i ^ flip) for i in range(count)])  11.1 us
    pallas_call x1, Pallas kernels, shards(): pl.pallas_call(lambda *refs: flow_kernel(members, rows, cols, lat_count,...  10.8 us
    ppermute x2, starting transfers between devices, from_lat(): lax.ppermute(value, 'lat', [(i, i + step) for i in range(count) if 0 <= i...  6.23 us
    pallas_call x1, Pallas kernels, shards(): pl.pallas_call(lambda *refs: planar_kernel(members, *refs), out_shape=(sh...  4.06 us
    pallas_call x1, Pallas kernels, shards(): pl.pallas_call(lambda *refs: back_kernel(members, *refs), out_shape=(shap...  2.69 us
    unnamed x26, local copies, waits for them, and re-layouts  2.63 us
    pallas_call x1, Pallas kernels, shards(): pl.pallas_call(lambda *refs: couple_kernel(members, lat_count, grp_count,...  2.62 us
  transfers between devices with their start and end apart: 15, of which 7 were waited for; matrix products, arithmetic and copies ran while one was open for 1% of the time, Pallas kernels for 17%

profile of v2, /device:TPU:0, one launch (start us, length us, event | category | flops | bytes accessed | tf_op | source)
XLA Modules:
  0.0 69.4 jit_solution(14794464780016718071)
XLA Ops:
  0.6 0.0 copy-start.3
  0.7 2.4 %pack_rows.1 = (bf16[144,512]{1,0:T(8,128)(2,1)}, bf16[144,512]{1,0:T(8,128)(2,1)}) custom-call(s32[16]{0:T(128)} %refs_0_.3, f32[4,64,512]{2,1,0:T(8,128)} %refs_1_.3, f32[2,4,64,512]{3,2,1,0:T(8,128)} %refs_2_.4, s32[64,512]{1,0:T(8,128)} %refs_3_.5, bf16[16,64,512]{2,1,0:T(8,128)(2,1)} %refs_4_.4, f32[16,16]{1,0:T(8,128)} %refs_2_.5), custom_call_target="tpu_custom_call" | custom-call | tf_op jit(solution)/shard_map/pack_rows/pallas_call | solution.py:656
  3.1 4.9 %collective-permute-start = (bf16[144,512]{1,0:T(8,128)(2,1)}, bf16[144,512]{1,0:T(8,128)(2,1)S(1)}, u32[]{:S(2)}, u32[]{:S(2)}) collective-permute-start(bf16[144,512]{1,0:T(8,128)(2,1)} %get-tuple-element.18), channel_id=1, source_target_pairs={{0,4},{4,8},{8,12},{1,5},{5,9},{9,13},{2,6},{6,10},{10,14},{3,7},{... | collective-permute-start | bytes 442376 | tf_op jit(solution)/shard_map/ppermute | solution.py:614
  8.0 1.3 %collective-permute-start.1 = (bf16[144,512]{1,0:T(8,128)(2,1)}, bf16[144,512]{1,0:T(8,128)(2,1)S(1)}, u32[]{:S(2)}, u32[]{:S(2)}) collective-permute-start(bf16[144,512]{1,0:T(8,128)(2,1)} %get-tuple-element.19), channel_id=1, source_target_pairs={{4,0},{8,4},{12,8},{5,1},{9,5},{13,9},{6,2},{10,6},{14,10},{7,3},{... | collective-permute-start | bytes 442376 | tf_op jit(solution)/shard_map/ppermute | solution.py:614
  9.3 0.0 copy-start
  9.4 1.2 %copy-done = f32[2,4,64,512]{3,2,1,0:T(8,128)S(1)} copy-done((f32[2,4,64,512]{3,2,1,0:T(8,128)S(1)}, f32[2,4,64,512]{3,2,1,0:T(8,128)}, u32[]{:S(2)}) %copy-start) | copy-done | bytes 1048600
  10.6 1.2 %copy-done.1 = bf16[16,64,512]{2,1,0:T(8,128)(2,1)S(1)} copy-done((bf16[16,64,512]{2,1,0:T(8,128)(2,1)S(1)}, bf16[16,64,512]{2,1,0:T(8,128)(2,1)}, u32[]{:S(2)}) %copy-start.1) | copy-done | bytes 1048600
  11.8 4.1 %to_planes.1 = (f32[5,16,64,128]{3,2,1,0:T(8,128)S(1)}, bf16[320,128]{1,0:T(8,128)(2,1)S(1)}) custom-call(s32[16]{0:T(128)S(1)} %copy-done.8, f32[4,64,512]{2,1,0:T(8,128)S(1)} %copy-done.3, f32[2,4,64,512]{3,2,1,0:T(8,128)S(1)} %copy-done, s32[64,512]{1,0:T(8,128)S(1)} %copy-done.4, bf16[16,64,512]{2,1,0:T(8,128)(2,1)S(1)} %copy-done.1, f32[16,16]{1,0:T(8,128)S(1)} %copy-done.6), custom_call_target="tpu_custom_call" | custom-call | flops 2000000000 | bytes 6291456 | tf_op jit(solution)/shard_map/to_planes/pallas_call | solution.py:676
  15.9 0.0 copy-start.5
  15.9 0.0 collective-permute-done.refs_0_
  15.9 0.0 collective-permute-done.1.refs_1_
  15.9 0.2 rim.1.refs_2_
  16.1 1.6 %collective-permute-start.2 = (bf16[400,128]{1,0:T(8,128)(2,1)S(1)}, bf16[400,128]{1,0:T(8,128)(2,1)S(1)}, u32[]{:S(2)}, u32[]{:S(2)}) collective-permute-start(bf16[400,128]{1,0:T(8,128)(2,1)S(1)} %rim.1.refs_2_), channel_id=1, source_target_pairs={{0,16},{16,0},{1,17},{17,1},{2,18},{18,2},{3,19},{19,3},{4,20},{20... | collective-permute-start | bytes 307208 | tf_op jit(solution)/shard_map/ppermute | solution.py:609
  17.6 0.1 copy.16.refs_6_.refs_5_
  17.8 0.1 copy.15.refs_2_.refs_1_
  17.8 0.8 %halo_planes.1.refs_1_ = f32[2,5,16,8,128]{4,3,2,1,0:T(8,128)S(1)} custom-call(bf16[144,512]{1,0:T(8,128)(2,1)S(1)} %collective-permute-done.refs_0_, bf16[144,512]{1,0:T(8,128)(2,1)S(1)} %collective-permute-done.1.refs_1_), custom_call_target="tpu_custom_call" | custom-call | flops 1000000000 | bytes 4194304 | tf_op jit(solution)/shard_map/halo_planes/pallas_call | solution.py:698
  18.6 2.2 %collective-permute-done.2.refs_3_.refs_4_ = bf16[400,128]{1,0:T(8,128)(2,1)S(1)} collective-permute-done((bf16[400,128]{1,0:T(8,128)(2,1)S(1)}, bf16[400,128]{1,0:T(8,128)(2,1)S(1)}, u32[]{:S(2)}, u32[]{:S(2)}) %collective-permute-start.2) | collective-permute-done | bytes 102432 | tf_op jit(solution)/shard_map/ppermute | solution.py:609
  20.8 10.8 %flow_embed.1 = (f32[4,8,256]{2,1,0:T(8,128)S(1)}, f32[32,128,256]{2,1,0:T(8,128)S(1)}, f32[3,16,96,128]{3,2,1,0:T(8,128)S(1)}) custom-call(f32[5,16,64,128]{3,2,1,0:T(8,128)S(1)} %get-tuple-element.17.refs_0_, f32[2,5,16,8,128]{4,3,2,1,0:T(8,128)S(1)} %halo_planes.1.refs_1_, bf16[400,128]{1,0:T(8,128)(2,1)S(1)} %rim.1.refs_2_, ...), custom_call_target="tpu_custom_call" | custom-call | tf_op jit(solution)/shard_map/flow_embed/pallas_call | solution.py:708
  31.6 1.6 %collective-permute-start.3 = (f32[32,256]{1,0:T(8,128)S(1)}, f32[32,256]{1,0:T(8,128)S(1)}, u32[]{:S(2)}, u32[]{:S(2)}) collective-permute-start(f32[32,256]{1,0:T(8,128)S(1)} %bitcast.10), channel_id=1, source_target_pairs={{0,16},{16,0},{1,17},{17,1},{2,18},{18,2},{3,19},{19,3},{4,20},{20... | collective-permute-start | bytes 98312 | tf_op jit(solution)/shard_map/ppermute | solution.py:619
  33.2 2.7 %from_planes.1 = (f32[4,64,512]{2,1,0:T(8,128)}, f32[2,4,64,512]{3,2,1,0:T(8,128)}) custom-call(f32[3,16,96,128]{3,2,1,0:T(8,128)S(1)} %get-tuple-element.21.refs_0_), custom_call_target="tpu_custom_call" | custom-call | flops 2000000000 | bytes 6291456 | tf_op jit(solution)/shard_map/from_planes/pallas_call | solution.py:798
  35.9 0.0 collective-permute-done.3.refs_1_
  35.9 1.6 %collective-permute-start.11 = (f16[32,256]{1,0:T(8,128)(2,1)S(1)}, f16[32,256]{1,0:T(8,128)(2,1)S(1)}, u32[]{:S(2)}, u32[]{:S(2)}) collective-permute-start(f16[32,256]{1,0:T(8,128)(2,1)S(1)} %get-tuple-element.31), channel_id=1, source_target_pairs={{0,2},{1,3},{2,0},{3,1},{4,6},{5,7},{6,4},{7,5},{8,10},{9,11},{10,... | collective-permute-start | bytes 49160 | tf_op jit(solution)/shard_map/ppermute | solution.py:619
  37.5 0.0 copy-done.9
  37.5 1.8 %local_loss.1 = (f32[64,256]{1,0:T(8,128)S(1)}, f32[64,256]{1,0:T(8,128)S(1)}) custom-call(f32[32,256]{1,0:T(8,128)S(1)} %bitcast.11, f32[32,256]{1,0:T(8,128)S(1)} %collective-permute-done.3.refs_1_, s32[16,1]{1,0:T(8,128)S(1)} %copy.15.refs_2_.refs_1_, f32[16,16]{1,0:T(8,128)S(1)} %copy-done.6, f32[264,512]{1,0:T(8,128)S(1)} %copy-done.2, ...), custom_call_target="tpu_custom_call" | custom-call | tf_op jit(solution)/shard_map/local_loss/pallas_call | solution.py:749
  39.3 0.1 collective-permute-start.4
  39.4 0.6 dynamic-slice_bitcast_fusion
  40.0 0.0 collective-permute-done.11
  40.0 3.7 %collective-permute-start.12 = (f16[64,256]{1,0:T(8,128)(2,1)S(1)}, f16[64,256]{1,0:T(8,128)(2,1)S(1)}, u32[]{:S(2)}, u32[]{:S(2)}) collective-permute-start(f16[64,256]{1,0:T(8,128)(2,1)S(1)} %pad_maximum_fusion.2), channel_id=1, source_target_pairs={{0,8},{4,12},{8,0},{12,4},{1,9},{5,13},{9,1},{13,5},{2,10},{6,14},... | collective-permute-start | bytes 98312 | tf_op jit(solution)/shard_map/ppermute | solution.py:619
  43.7 2.0 %collective-permute-done.12 = f16[64,256]{1,0:T(8,128)(2,1)S(1)} collective-permute-done((f16[64,256]{1,0:T(8,128)(2,1)S(1)}, f16[64,256]{1,0:T(8,128)(2,1)S(1)}, u32[]{:S(2)}, u32[]{:S(2)}) %collective-permute-start.12) | collective-permute-done | bytes 32800 | tf_op jit(solution)/shard_map/ppermute | solution.py:619
  45.8 1.8 %collective-permute-start.13 = (f16[128,256]{1,0:T(8,128)(2,1)S(1)}, f16[128,256]{1,0:T(8,128)(2,1)S(1)}, u32[]{:S(2)}, u32[]{:S(2)}) collective-permute-start(f16[128,256]{1,0:T(8,128)(2,1)S(1)} %pad_maximum_fusion.1), channel_id=1, source_target_pairs={{0,4},{4,0},{8,12},{12,8},{1,5},{5,1},{9,13},{13,9},{2,6},{6,2},{1... | collective-permute-start | bytes 196616 | tf_op jit(solution)/shard_map/ppermute | solution.py:619
  47.6 0.0 collective-permute-done.4
  47.6 1.3 %collective-permute-start.5 = (f32[64,256]{1,0:T(8,128)S(1)}, f32[64,256]{1,0:T(8,128)S(1)}, u32[]{:S(2)}, u32[]{:S(2)}) collective-permute-start(f32[64,256]{1,0:T(8,128)S(1)} %add.26), channel_id=1, source_target_pairs={{0,16},{16,0},{1,17},{17,1},{2,18},{18,2},{3,19},{19,3},{4,20},{20... | collective-permute-start | bytes 196616 | tf_op jit(solution)/shard_map/ppermute | solution.py:619
  48.9 1.2 %collective-permute-start.6 = (f32[64,256]{1,0:T(8,128)S(1)}, f32[64,256]{1,0:T(8,128)S(1)}, u32[]{:S(2)}, u32[]{:S(2)}) collective-permute-start(f32[64,256]{1,0:T(8,128)S(1)} %add.26), channel_id=1, source_target_pairs={{0,2},{1,3},{2,0},{3,1},{4,6},{5,7},{6,4},{7,5},{8,10},{9,11},{10,... | collective-permute-start | bytes 196616 | tf_op jit(solution)/shard_map/ppermute | solution.py:619
  50.2 1.1 %collective-permute-start.7 = (f32[64,256]{1,0:T(8,128)S(1)}, f32[64,256]{1,0:T(8,128)S(1)}, u32[]{:S(2)}, u32[]{:S(2)}) collective-permute-start(f32[64,256]{1,0:T(8,128)S(1)} %add.26), channel_id=1, source_target_pairs={{0,18},{1,19},{2,16},{3,17},{16,2},{17,3},{18,0},{19,1},{4,22},{5,... | collective-permute-start | bytes 196616 | tf_op jit(solution)/shard_map/ppermute | solution.py:761
  51.2 0.0 collective-permute-done.13
  51.3 0.1 collective-permute-start.14
  51.3 1.1 %collective-permute-done.5 = f32[64,256]{1,0:T(8,128)S(1)} collective-permute-done((f32[64,256]{1,0:T(8,128)S(1)}, f32[64,256]{1,0:T(8,128)S(1)}, u32[]{:S(2)}, u32[]{:S(2)}) %collective-permute-start.5) | collective-permute-done | bytes 65568 | tf_op jit(solution)/shard_map/ppermute | solution.py:619
  52.4 0.9 %collective-permute-done.6 = f32[64,256]{1,0:T(8,128)S(1)} collective-permute-done((f32[64,256]{1,0:T(8,128)S(1)}, f32[64,256]{1,0:T(8,128)S(1)}, u32[]{:S(2)}, u32[]{:S(2)}) %collective-permute-start.6) | collective-permute-done | bytes 65568 | tf_op jit(solution)/shard_map/ppermute | solution.py:619
  53.3 2.1 %collective-permute-done.7 = f32[64,256]{1,0:T(8,128)S(1)} collective-permute-done((f32[64,256]{1,0:T(8,128)S(1)}, f32[64,256]{1,0:T(8,128)S(1)}, u32[]{:S(2)}, u32[]{:S(2)}) %collective-permute-start.7) | collective-permute-done | bytes 65568 | tf_op jit(solution)/shard_map/ppermute | solution.py:761
  55.3 2.9 %collective-permute-start.8 = (f32[64,256]{1,0:T(8,128)S(1)}, f32[64,256]{1,0:T(8,128)S(1)}, u32[]{:S(2)}, u32[]{:S(2)}) collective-permute-start(f32[64,256]{1,0:T(8,128)S(1)} %add_add_fusion), channel_id=1, source_target_pairs={{0,8},{4,12},{8,0},{12,4},{1,9},{5,13},{9,1},{13,5},{2,10},{6,14},... | collective-permute-start | bytes 196616 | tf_op jit(solution)/shard_map/ppermute | solution.py:619
  58.2 3.0 %collective-permute-done.8 = f32[64,256]{1,0:T(8,128)S(1)} collective-permute-done((f32[64,256]{1,0:T(8,128)S(1)}, f32[64,256]{1,0:T(8,128)S(1)}, u32[]{:S(2)}, u32[]{:S(2)}) %collective-permute-start.8) | collective-permute-done | bytes 65568 | tf_op jit(solution)/shard_map/ppermute | solution.py:619
  61.2 0.1 collective-permute-start.9
  61.3 0.0 collective-permute-done.14
  61.4 4.2 %collective-permute-done.9 = f32[64,256]{1,0:T(8,128)S(1)} collective-permute-done((f32[64,256]{1,0:T(8,128)S(1)}, f32[64,256]{1,0:T(8,128)S(1)}, u32[]{:S(2)}, u32[]{:S(2)}) %collective-permute-start.9) | collective-permute-done | bytes 65568 | tf_op jit(solution)/shard_map/ppermute | solution.py:619
  65.6 0.1 collective-permute-start.10
  65.7 2.6 %couple_grads.1 = (f32[1128,128]{1,0:T(8,128)S(1)}, f32[1,128]{1,0:T(1,128)S(1)}) custom-call(f32[512,256]{1,0:T(8,128)S(1)} %convert_element_type.7.refs_0_, s32[16,1]{1,0:T(8,128)S(1)} %copy.15.refs_2_.refs_1_, f32[16,16]{1,0:T(8,128)S(1)} %copy-done.6, f32[264,512]{1,0:T(8,128)S(1)} %copy-done.2, f32[1,512]{1,0:T(1,128)S(1)} %bitcast.13, ...), custom_call_target="tpu_custom_call" | custom-call | flops 3000000000 | bytes 3145728 | tf_op jit(solution)/shard_map/couple_grads/pallas_call | solution.py:784
  68.3 0.0 collective-permute-done.10.refs_1_
  68.3 1.1 %finish.1 = f32[1384,128]{1,0:T(8,128)} custom-call(f32[64,256]{1,0:T(8,128)S(1)} %add.31.refs_0_, f32[64,256]{1,0:T(8,128)S(1)} %collective-permute-done.10.refs_1_, f32[1128,128]{1,0:T(8,128)S(1)} %get-tuple-element.28.refs_2_, f32[1,128]{1,0:T(1,128)S(1)} %get-tuple-element.29.refs_3_), custom_call_target="tpu_custom_call" | custom-call | tf_op jit(solution)/shard_map/finish/pallas_call | solution.py:808
  (29 shorter events, 0.3 us)
Async XLA Ops:
  0.6 8.7 %copy-start.3 = (f32[4,64,512]{2,1,0:T(8,128)S(1)}, f32[4,64,512]{2,1,0:T(8,128)}, u32[]{:S(2)}) copy-start(f32[4,64,512]{2,1,0:T(8,128)} %refs_1_.3) | copy-start | bytes 1572868
  0.6 8.7 %copy-start.4 = (s32[64,512]{1,0:T(8,128)S(1)}, s32[64,512]{1,0:T(8,128)}, u32[]{:S(2)}) copy-start(s32[64,512]{1,0:T(8,128)} %refs_3_.5) | copy-start | bytes 393220
  0.7 8.7 %copy-start.6 = (f32[16,16]{1,0:T(8,128)S(1)}, f32[16,16]{1,0:T(8,128)}, u32[]{:S(2)}) copy-start(f32[16,16]{1,0:T(8,128)} %refs_2_.5) | copy-start | bytes 3076
  0.7 8.7 %copy-start.8 = (s32[16]{0:T(128)S(1)}, s32[16]{0:T(128)}, u32[]{:S(2)}) copy-start(s32[16]{0:T(128)} %refs_0_.3) | copy-start | bytes 196
  3.1 12.8 %collective-permute-start = (bf16[144,512]{1,0:T(8,128)(2,1)}, bf16[144,512]{1,0:T(8,128)(2,1)S(1)}, u32[]{:S(2)}, u32[]{:S(2)}) collective-permute-start(bf16[144,512]{1,0:T(8,128)(2,1)} %get-tuple-element.18), channel_id=1, source_target_pairs={{0,4},{4,8},{8,12},{1,5},{5,9},{9,13},{2,6},{6,10},{10,14},{3,7},{... | collective-permute-start | bytes 442376 | tf_op jit(solution)/shard_map/ppermute | solution.py:614
  8.0 7.9 %collective-permute-start.1 = (bf16[144,512]{1,0:T(8,128)(2,1)}, bf16[144,512]{1,0:T(8,128)(2,1)S(1)}, u32[]{:S(2)}, u32[]{:S(2)}) collective-permute-start(bf16[144,512]{1,0:T(8,128)(2,1)} %get-tuple-element.19), channel_id=1, source_target_pairs={{4,0},{8,4},{12,8},{5,1},{9,5},{13,9},{6,2},{10,6},{14,10},{7,3},{... | collective-permute-start | bytes 442376 | tf_op jit(solution)/shard_map/ppermute | solution.py:614
  9.3 1.2 %copy-start = (f32[2,4,64,512]{3,2,1,0:T(8,128)S(1)}, f32[2,4,64,512]{3,2,1,0:T(8,128)}, u32[]{:S(2)}) copy-start(f32[2,4,64,512]{3,2,1,0:T(8,128)} %refs_2_.4) | copy-start | bytes 3145732
  10.6 1.2 %copy-start.1 = (bf16[16,64,512]{2,1,0:T(8,128)(2,1)S(1)}, bf16[16,64,512]{2,1,0:T(8,128)(2,1)}, u32[]{:S(2)}) copy-start(bf16[16,64,512]{2,1,0:T(8,128)(2,1)} %refs_4_.4) | copy-start | bytes 3145732
  11.8 5.8 %copy-start.10 = (f32[512,16]{0,1:T(8,128)S(1)}, f32[512,16]{0,1:T(8,128)}, u32[]{:S(2)}) copy-start(f32[512,16]{0,1:T(8,128)} %param.20) | copy-start | bytes 98308
  15.9 4.9 %copy-start.5 = (bf16[128,256]{1,0:T(8,128)(2,1)S(1)}, bf16[128,256]{1,0:T(8,128)(2,1)}, u32[]{:S(2)}) copy-start(bf16[128,256]{1,0:T(8,128)(2,1)} %refs_5_.6) | copy-start | bytes 196612
  16.1 4.7 %collective-permute-start.2 = (bf16[400,128]{1,0:T(8,128)(2,1)S(1)}, bf16[400,128]{1,0:T(8,128)(2,1)S(1)}, u32[]{:S(2)}, u32[]{:S(2)}) collective-permute-start(bf16[400,128]{1,0:T(8,128)(2,1)S(1)} %rim.1.refs_2_), channel_id=1, source_target_pairs={{0,16},{16,0},{1,17},{17,1},{2,18},{18,2},{3,19},{19,3},{4,20},{20... | collective-permute-start | bytes 307208 | tf_op jit(solution)/shard_map/ppermute | solution.py:609
  31.6 4.3 %collective-permute-start.3 = (f32[32,256]{1,0:T(8,128)S(1)}, f32[32,256]{1,0:T(8,128)S(1)}, u32[]{:S(2)}, u32[]{:S(2)}) collective-permute-start(f32[32,256]{1,0:T(8,128)S(1)} %bitcast.10), channel_id=1, source_target_pairs={{0,16},{16,0},{1,17},{17,1},{2,18},{18,2},{3,19},{19,3},{4,20},{20... | collective-permute-start | bytes 98312 | tf_op jit(solution)/shard_map/ppermute | solution.py:619
  33.2 4.3 %copy-start.2 = (f32[264,512]{1,0:T(8,128)S(1)}, f32[264,512]{1,0:T(8,128)}, u32[]{:S(2)}) copy-start(f32[264,512]{1,0:T(8,128)} %refs_3_.7) | copy-start | bytes 1622020
  33.2 4.3 %copy-start.7 = (f32[512]{0:T(512)S(1)}, f32[512]{0:T(512)}, u32[]{:S(2)}) copy-start(f32[512]{0:T(512)} %param.19) | copy-start | bytes 6148
  33.2 4.3 %copy-start.9 = (f32[16]{0:T(128)S(1)}, f32[16]{0:T(128)}, u32[]{:S(2)}) copy-start(f32[16]{0:T(128)} %param.21) | copy-start | bytes 196
  35.9 4.1 %collective-permute-start.11 = (f16[32,256]{1,0:T(8,128)(2,1)S(1)}, f16[32,256]{1,0:T(8,128)(2,1)S(1)}, u32[]{:S(2)}, u32[]{:S(2)}) collective-permute-start(f16[32,256]{1,0:T(8,128)(2,1)S(1)} %get-tuple-element.31), channel_id=1, source_target_pairs={{0,2},{1,3},{2,0},{3,1},{4,6},{5,7},{6,4},{7,5},{8,10},{9,11},{10,... | collective-permute-start | bytes 49160 | tf_op jit(solution)/shard_map/ppermute | solution.py:619
  39.3 8.4 %collective-permute-start.4 = (f32[64,256]{1,0:T(8,128)S(1)}, f32[64,256]{1,0:T(8,128)S(1)}, u32[]{:S(2)}, u32[]{:S(2)}) collective-permute-start(f32[64,256]{1,0:T(8,128)S(1)} %get-tuple-element.27), channel_id=1, source_target_pairs={{0,1},{1,0},{2,3},{3,2},{4,5},{5,4},{6,7},{7,6},{8,9},{9,8},{10,11... | collective-permute-start | bytes 196616 | tf_op jit(solution)/shard_map/ppermute | solution.py:619
  40.0 5.8 %collective-permute-start.12 = (f16[64,256]{1,0:T(8,128)(2,1)S(1)}, f16[64,256]{1,0:T(8,128)(2,1)S(1)}, u32[]{:S(2)}, u32[]{:S(2)}) collective-permute-start(f16[64,256]{1,0:T(8,128)(2,1)S(1)} %pad_maximum_fusion.2), channel_id=1, source_target_pairs={{0,8},{4,12},{8,0},{12,4},{1,9},{5,13},{9,1},{13,5},{2,10},{6,14},... | collective-permute-start | bytes 98312 | tf_op jit(solution)/shard_map/ppermute | solution.py:619
  45.8 5.4 %collective-permute-start.13 = (f16[128,256]{1,0:T(8,128)(2,1)S(1)}, f16[128,256]{1,0:T(8,128)(2,1)S(1)}, u32[]{:S(2)}, u32[]{:S(2)}) collective-permute-start(f16[128,256]{1,0:T(8,128)(2,1)S(1)} %pad_maximum_fusion.1), channel_id=1, source_target_pairs={{0,4},{4,0},{8,12},{12,8},{1,5},{5,1},{9,13},{13,9},{2,6},{6,2},{1... | collective-permute-start | bytes 196616 | tf_op jit(solution)/shard_map/ppermute | solution.py:619
  47.6 4.7 %collective-permute-start.5 = (f32[64,256]{1,0:T(8,128)S(1)}, f32[64,256]{1,0:T(8,128)S(1)}, u32[]{:S(2)}, u32[]{:S(2)}) collective-permute-start(f32[64,256]{1,0:T(8,128)S(1)} %add.26), channel_id=1, source_target_pairs={{0,16},{16,0},{1,17},{17,1},{2,18},{18,2},{3,19},{19,3},{4,20},{20... | collective-permute-start | bytes 196616 | tf_op jit(solution)/shard_map/ppermute | solution.py:619
  48.9 4.3 %collective-permute-start.6 = (f32[64,256]{1,0:T(8,128)S(1)}, f32[64,256]{1,0:T(8,128)S(1)}, u32[]{:S(2)}, u32[]{:S(2)}) collective-permute-start(f32[64,256]{1,0:T(8,128)S(1)} %add.26), channel_id=1, source_target_pairs={{0,2},{1,3},{2,0},{3,1},{4,6},{5,7},{6,4},{7,5},{8,10},{9,11},{10,... | collective-permute-start | bytes 196616 | tf_op jit(solution)/shard_map/ppermute | solution.py:619
  50.2 5.2 %collective-permute-start.7 = (f32[64,256]{1,0:T(8,128)S(1)}, f32[64,256]{1,0:T(8,128)S(1)}, u32[]{:S(2)}, u32[]{:S(2)}) collective-permute-start(f32[64,256]{1,0:T(8,128)S(1)} %add.26), channel_id=1, source_target_pairs={{0,18},{1,19},{2,16},{3,17},{16,2},{17,3},{18,0},{19,1},{4,22},{5,... | collective-permute-start | bytes 196616 | tf_op jit(solution)/shard_map/ppermute | solution.py:761
  51.3 10.1 %collective-permute-start.14 = (f16[256,256]{1,0:T(8,128)(2,1)S(1)}, f16[256,256]{1,0:T(8,128)(2,1)S(1)}, u32[]{:S(2)}, u32[]{:S(2)}) collective-permute-start(f16[256,256]{1,0:T(8,128)(2,1)S(1)} %pad_maximum_fusion), channel_id=1, source_target_pairs={{0,1},{1,0},{2,3},{3,2},{4,5},{5,4},{6,7},{7,6},{8,9},{9,8},{10,11... | collective-permute-start | bytes 393224 | tf_op jit(solution)/shard_map/ppermute | solution.py:619
  55.3 5.9 %collective-permute-start.8 = (f32[64,256]{1,0:T(8,128)S(1)}, f32[64,256]{1,0:T(8,128)S(1)}, u32[]{:S(2)}, u32[]{:S(2)}) collective-permute-start(f32[64,256]{1,0:T(8,128)S(1)} %add_add_fusion), channel_id=1, source_target_pairs={{0,8},{4,12},{8,0},{12,4},{1,9},{5,13},{9,1},{13,5},{2,10},{6,14},... | collective-permute-start | bytes 196616 | tf_op jit(solution)/shard_map/ppermute | solution.py:619
  61.2 4.3 %collective-permute-start.9 = (f32[64,256]{1,0:T(8,128)S(1)}, f32[64,256]{1,0:T(8,128)S(1)}, u32[]{:S(2)}, u32[]{:S(2)}) collective-permute-start(f32[64,256]{1,0:T(8,128)S(1)} %add.30), channel_id=1, source_target_pairs={{0,4},{4,0},{8,12},{12,8},{1,5},{5,1},{9,13},{13,9},{2,6},{6,2},{1... | collective-permute-start | bytes 196616 | tf_op jit(solution)/shard_map/ppermute | solution.py:619
  65.6 2.7 %collective-permute-start.10 = (f32[64,256]{1,0:T(8,128)S(1)}, f32[64,256]{1,0:T(8,128)S(1)}, u32[]{:S(2)}, u32[]{:S(2)}) collective-permute-start(f32[64,256]{1,0:T(8,128)S(1)} %add.31.refs_0_), channel_id=1, source_target_pairs={{0,1},{1,0},{2,3},{3,2},{4,5},{5,4},{6,7},{7,6},{8,9},{9,8},{10,11... | collective-permute-start | bytes 196616 | tf_op jit(solution)/shard_map/ppermute | solution.py:619

commit v3 on v2

--- a/solution.py
+++ b/solution.py
@@ -98,10 +98,10 @@
     return out
 
 
-def forcing_rows(coeff, basis, members):
+def forcing_rows(coeff, basis, members, keep=slice(None)):
     acc = [None] * members
     for k in range(basis.shape[0]):
-        value = basis[k].astype(F32)
+        value = basis[k].astype(F32)[keep]
         for m in range(members):
             term = coeff[m][:, k : k + 1] * value
             acc[m] = term if acc[m] is None else acc[m] + term
@@ -136,10 +136,10 @@
         copy.wait()
     coeff = coefficients(members, ids, props)
     for side, out in ((0, low), (1, high)):
-        force = forcing_rows(coeff, basis.at[side], members)
         keep = slice(0, HALO) if side == 0 else slice(16 - HALO, 16)
+        force = forcing_rows(coeff, basis.at[side], members, keep)
         blocks = [cells[side, i, m] for i in range(3) for m in range(members)]
-        blocks += [force[m][keep] for m in range(members)]
+        blocks += force
         blocks += [depth[side].astype(F32), jnp.zeros((HALO, cols), F32)]
         for g in range(0, len(blocks), 2):
             pair = jnp.concatenate(blocks[g : g + 2], axis=0)
@@ -505,10 +505,17 @@
 
 
 def local_kernel(
-    members, inv_root, mine, theirs, ids, props, w_in, b_in, w_out, b_out, gram, kept, sent, total
+    members, inv_root, mine, theirs, ids, props, w_in, b_in, w_out, b_out, gram, kept, sent, own, total
 ):
     sums = (mine[...] + theirs[...]) * inv_root
     count = sums.shape[0]
+    items = own.shape[0]
+    for part in range(count // items):
+
+        @pl.when(lax.axis_index("lon") == part)
+        def _():
+            own[...] = sums[part * items : (part + 1) * items, :]
+
     params = member_params(ids, props)
     half = params.shape[1] // 2
     low = split(params[:, :half])
@@ -741,21 +748,42 @@
         others = swapped(partial, "lon", 1)
     else:
         others = lax.psum(partial, "lon") - partial
+    surface_out, velocity_out = pl.pallas_call(
+        lambda *refs: back_kernel(members, *refs),
+        out_shape=(shape(members, rows, cols), shape(2, members, rows, cols)),
+        in_specs=[vmem()],
+        out_specs=(vmem(), vmem()),
+        compiler_params=params_of(24),
+        cost_estimate=pl.CostEstimate(flops=2 * 10**9, bytes_accessed=6 * MEBI, transcendentals=0),
+        name="from_planes",
+    )(final)
+
+    others, surface_out, velocity_out = lax.optimization_barrier((others, surface_out, velocity_out))
     summaries = (partial + others) * inv_root
 
     ids_col = member_ids.reshape(-1, 1)
     b_in = couple_in_bias.reshape(1, -1)
     b_out = couple_out_bias.reshape(1, -1)
-    kept, sent = pl.pallas_call(
+    items = samples // lon_count
+    kept, sent, own = pl.pallas_call(
         lambda *refs: local_kernel(members, inv_root, *refs),
-        out_shape=(shape(cells // 2, feats), shape(cells // 2, feats)),
+        out_shape=(shape(cells // 2, feats), shape(cells // 2, feats), shape(items, feats)),
         in_specs=[vmem()] * 9,
-        out_specs=(vmem(),) * 2,
+        out_specs=(vmem(),) * 3,
         scratch_shapes=[pltpu.VMEM((cells, feats), F32)],
         compiler_params=params_of(16),
         name="local_loss",
     )(partial, others, ids_col, proposals, couple_in, b_in, couple_out, b_out, gram)
 
+    def after(value, *others):
+        return lax.optimization_barrier((value,) + others)[0]
+
+    def gather(axis, flip):
+        both = jnp.concatenate([gathered, swapped(gathered, axis, flip)], axis=0)
+        return both, order + [(a ^ flip, b) if axis == "lat" else (a, b ^ flip) for a, b in order]
+
+    gathered, order = summaries.astype(jnp.float16), [(0, 0)]
+    gathered, order = gather("grp", 2)
     conv = kept + swapped(sent, "grp", 1)
     if lon_count == 2:
         corner = lax.ppermute(
@@ -763,20 +791,22 @@
             ("lon", "grp"),
             [(i, (i // grp_count ^ 1) * grp_count + (i % grp_count ^ 2)) for i in range(2 * grp_count)],
         )
-        conv = (conv + swapped(conv, "lon", 1)) + (swapped(conv, "grp", 2) + corner)
+        by_lon = swapped(conv, "lon", 1)
+        gathered = after(gathered, by_lon)
+        conv = (conv + by_lon) + (swapped(conv, "grp", 2) + corner)
     else:
         conv = conv + swapped(conv, "grp", 2)
         for flip in flips("lon"):
             conv = conv + swapped(conv, "lon", flip)
     for flip in reversed(flips("lat")):
-        conv = conv + swapped(conv, "lat", flip)
-    conv_other = swapped(conv, "grp", 1)
-
-    gathered = summaries.astype(jnp.float16)
-    order = [(0, 0)]
-    for axis, flip in [("grp", 2)] + [("lat", f) for f in reversed(flips("lat"))] + [("grp", 1)]:
-        gathered = jnp.concatenate([gathered, swapped(gathered, axis, flip)], axis=0)
-        order = order + [(a ^ flip, b) if axis == "lat" else (a, b ^ flip) for a, b in order]
+        by_lat = swapped(conv, "lat", flip)
+        if flip > 1:
+            gathered, order = gather("lat", flip)
+            gathered = after(gathered, conv)
+            conv = conv + by_lat
+    gathered, order = gather("lat", 1)
+    gathered = after(gathered, conv)
+    gathered, order = gather("grp", 1)
 
     low_rows = (couple_in.size + hid + couple_out.size) // LANES + 1
     low_rows = -(-low_rows // 8) * 8
@@ -795,15 +825,8 @@
         name="couple_grads",
     )(gathered.astype(F32), ids_col, proposals, couple_in, b_in, couple_out, b_out)
 
-    surface_out, velocity_out = pl.pallas_call(
-        lambda *refs: back_kernel(members, *refs),
-        out_shape=(shape(members, rows, cols), shape(2, members, rows, cols)),
-        in_specs=[vmem()],
-        out_specs=(vmem(), vmem()),
-        compiler_params=params_of(24),
-        cost_estimate=pl.CostEstimate(flops=2 * 10**9, bytes_accessed=6 * MEBI, transcendentals=0),
-        name="from_planes",
-    )(final)
+    conv = conv + after(by_lat, couple, square)
+    conv_other = swapped(conv, "grp", 1)
 
     stepped = pl.pallas_call(
         lambda *refs: finish_kernel(count, *refs),
@@ -816,8 +839,6 @@
     )(conv, conv_other, couple, square)
     weight_step = stepped.reshape(-1)[:count]
 
-    items = samples // lon_count
-    own = lax.dynamic_slice_in_dim(summaries, lax.axis_index("lon") * items, items, axis=0)
     return (surface_out, velocity_out, own.reshape(1, 1, 1, items, feats), weight_step)
 
 

time: 69.7 us -> 62.4 us (0.90)
  waiting for transfers between devices: 15.4 us -> 7.08 us
  starting transfers between devices: 23.2 us -> 25 us
    ppermute x11, waiting for transfers between devices: 11.1 us -> 4.89 us  [swapped(): return lax.ppermute(value, axis, [(i, i ^ flip) for i in range(count)])]
    ppermute x1, waiting for transfers between devices: 2.06 us -> 0.01 us  [shards(): lax.ppermute(conv, ('lon', 'grp'), [(i, (i // grp_count ^ 1) * grp_count...]
    ppermute x11, starting transfers between devices: 14.4 us -> 16 us  [swapped(): return lax.ppermute(value, axis, [(i, i ^ flip) for i in range(count)])]
    unnamed x26 -> x23, local copies, waits for them, and re-layouts: 2.63 us -> 2.6 us
  transfers between devices with their start and end apart: 15 -> 15, of which waited for: 7 -> 6; matrix products, arithmetic and copies ran while one was open for 1% -> 1% of each run, Pallas kernels for 17% -> 16%
where the time goes in v3:
time: 62.4 us; the launch traced here: 62.1 us
  Pallas kernels  26.4 us (42%)
  starting transfers between devices  25 us (40%)
  waiting for transfers between devices  7.08 us (11%)
  local copies, waits for them, and re-layouts  2.69 us (4%)
  between operations  0.89 us (1%)
    ppermute x11, starting transfers between devices, swapped(): return lax.ppermute(value, axis, [(i, i ^ flip) for i in range(count)])  16 us
    pallas_call x1, Pallas kernels, shards(): pl.pallas_call(lambda *refs: flow_kernel(members, rows, cols, lat_count,...  10.6 us
    ppermute x2, starting transfers between devices, from_lat(): lax.ppermute(value, 'lat', [(i, i + step) for i in range(count) if 0 <= i...  6.23 us
    ppermute x11, waiting for transfers between devices, swapped(): return lax.ppermute(value, axis, [(i, i ^ flip) for i in range(count)])  4.89 us
    pallas_call x1, Pallas kernels, shards(): pl.pallas_call(lambda *refs: planar_kernel(members, *refs), out_shape=(sh...  4.06 us
    pallas_call x1, Pallas kernels, shards(): pl.pallas_call(lambda *refs: back_kernel(members, *refs), out_shape=(shap...  2.69 us
    pallas_call x1, Pallas kernels, shards(): pl.pallas_call(lambda *refs: couple_kernel(members, lat_count, grp_count,...  2.62 us
    unnamed x23, local copies, waits for them, and re-layouts  2.6 us
  transfers between devices with their start and end apart: 15, of which 6 were waited for; matrix products, arithmetic and copies ran while one was open for 1% of the time, Pallas kernels for 16%

profile of v3, /device:TPU:0, one launch (start us, length us, event | category | flops | bytes accessed | tf_op | source)
XLA Modules:
  0.0 62.1 jit_solution(4675044220905591791)
XLA Ops:
  0.6 0.0 copy-start.3
  0.7 2.4 %pack_rows.1 = (bf16[144,512]{1,0:T(8,128)(2,1)}, bf16[144,512]{1,0:T(8,128)(2,1)}) custom-call(s32[16]{0:T(128)} %refs_0_.3, f32[4,64,512]{2,1,0:T(8,128)} %refs_1_.3, f32[2,4,64,512]{3,2,1,0:T(8,128)} %refs_2_.4, s32[64,512]{1,0:T(8,128)} %refs_3_.5, bf16[16,64,512]{2,1,0:T(8,128)(2,1)} %refs_4_.4, f32[16,16]{1,0:T(8,128)} %refs_2_.5), custom_call_target="tpu_custom_call" | custom-call | tf_op jit(solution)/shard_map/pack_rows/pallas_call | solution.py:663
  3.1 4.9 %collective-permute-start = (bf16[144,512]{1,0:T(8,128)(2,1)}, bf16[144,512]{1,0:T(8,128)(2,1)S(1)}, u32[]{:S(2)}, u32[]{:S(2)}) collective-permute-start(bf16[144,512]{1,0:T(8,128)(2,1)} %get-tuple-element.26), channel_id=1, source_target_pairs={{0,4},{4,8},{8,12},{1,5},{5,9},{9,13},{2,6},{6,10},{10,14},{3,7},{... | collective-permute-start | bytes 442376 | tf_op jit(solution)/shard_map/ppermute | solution.py:621
  8.0 1.3 %collective-permute-start.1 = (bf16[144,512]{1,0:T(8,128)(2,1)}, bf16[144,512]{1,0:T(8,128)(2,1)S(1)}, u32[]{:S(2)}, u32[]{:S(2)}) collective-permute-start(bf16[144,512]{1,0:T(8,128)(2,1)} %get-tuple-element.27), channel_id=1, source_target_pairs={{4,0},{8,4},{12,8},{5,1},{9,5},{13,9},{6,2},{10,6},{14,10},{7,3},{... | collective-permute-start | bytes 442376 | tf_op jit(solution)/shard_map/ppermute | solution.py:621
  9.3 0.0 copy-start
  9.4 1.2 %copy-done = f32[2,4,64,512]{3,2,1,0:T(8,128)S(1)} copy-done((f32[2,4,64,512]{3,2,1,0:T(8,128)S(1)}, f32[2,4,64,512]{3,2,1,0:T(8,128)}, u32[]{:S(2)}) %copy-start) | copy-done | bytes 1048600
  10.6 1.2 %copy-done.1 = bf16[16,64,512]{2,1,0:T(8,128)(2,1)S(1)} copy-done((bf16[16,64,512]{2,1,0:T(8,128)(2,1)S(1)}, bf16[16,64,512]{2,1,0:T(8,128)(2,1)}, u32[]{:S(2)}) %copy-start.1) | copy-done | bytes 1048600
  11.8 4.1 %to_planes.1 = (f32[5,16,64,128]{3,2,1,0:T(8,128)S(1)}, bf16[320,128]{1,0:T(8,128)(2,1)S(1)}) custom-call(s32[16]{0:T(128)S(1)} %copy-done.8, f32[4,64,512]{2,1,0:T(8,128)S(1)} %copy-done.3, f32[2,4,64,512]{3,2,1,0:T(8,128)S(1)} %copy-done, s32[64,512]{1,0:T(8,128)S(1)} %copy-done.4, bf16[16,64,512]{2,1,0:T(8,128)(2,1)S(1)} %copy-done.1, f32[16,16]{1,0:T(8,128)S(1)} %copy-done.6), custom_call_target="tpu_custom_call" | custom-call | flops 2000000000 | bytes 6291456 | tf_op jit(solution)/shard_map/to_planes/pallas_call | solution.py:683
  15.9 0.0 copy-start.5
  15.9 0.0 collective-permute-done.refs_0_
  15.9 0.0 collective-permute-done.1.refs_1_
  15.9 0.2 rim.1.refs_2_
  16.1 1.6 %collective-permute-start.2 = (bf16[400,128]{1,0:T(8,128)(2,1)S(1)}, bf16[400,128]{1,0:T(8,128)(2,1)S(1)}, u32[]{:S(2)}, u32[]{:S(2)}) collective-permute-start(bf16[400,128]{1,0:T(8,128)(2,1)S(1)} %rim.1.refs_2_), channel_id=1, source_target_pairs={{0,16},{16,0},{1,17},{17,1},{2,18},{18,2},{3,19},{19,3},{4,20},{20... | collective-permute-start | bytes 307208 | tf_op jit(solution)/shard_map/ppermute | solution.py:616
  17.6 0.1 copy.16.refs_6_.refs_5_
  17.8 0.1 copy.15.refs_2_.refs_1_
  17.8 0.8 %halo_planes.1.refs_1_ = f32[2,5,16,8,128]{4,3,2,1,0:T(8,128)S(1)} custom-call(bf16[144,512]{1,0:T(8,128)(2,1)S(1)} %collective-permute-done.refs_0_, bf16[144,512]{1,0:T(8,128)(2,1)S(1)} %collective-permute-done.1.refs_1_), custom_call_target="tpu_custom_call" | custom-call | flops 1000000000 | bytes 4194304 | tf_op jit(solution)/shard_map/halo_planes/pallas_call | solution.py:705
  18.6 2.2 %collective-permute-done.2.refs_3_.refs_4_ = bf16[400,128]{1,0:T(8,128)(2,1)S(1)} collective-permute-done((bf16[400,128]{1,0:T(8,128)(2,1)S(1)}, bf16[400,128]{1,0:T(8,128)(2,1)S(1)}, u32[]{:S(2)}, u32[]{:S(2)}) %collective-permute-start.2) | collective-permute-done | bytes 102432 | tf_op jit(solution)/shard_map/ppermute | solution.py:616
  20.8 10.6 %flow_embed.1 = (f32[4,8,256]{2,1,0:T(8,128)S(1)}, f32[32,128,256]{2,1,0:T(8,128)S(1)}, f32[3,16,96,128]{3,2,1,0:T(8,128)S(1)}) custom-call(f32[5,16,64,128]{3,2,1,0:T(8,128)S(1)} %get-tuple-element.25.refs_0_, f32[2,5,16,8,128]{4,3,2,1,0:T(8,128)S(1)} %halo_planes.1.refs_1_, bf16[400,128]{1,0:T(8,128)(2,1)S(1)} %rim.1.refs_2_, ...), custom_call_target="tpu_custom_call" | custom-call | tf_op jit(solution)/shard_map/flow_embed/pallas_call | solution.py:715
  31.4 1.6 %collective-permute-start.3 = (f32[32,256]{1,0:T(8,128)S(1)}, f32[32,256]{1,0:T(8,128)S(1)}, u32[]{:S(2)}, u32[]{:S(2)}) collective-permute-start(f32[32,256]{1,0:T(8,128)S(1)} %bitcast.8), channel_id=1, source_target_pairs={{0,16},{16,0},{1,17},{17,1},{2,18},{18,2},{3,19},{19,3},{4,20},{20... | collective-permute-start | bytes 98312 | tf_op jit(solution)/shard_map/ppermute | solution.py:626
  33.0 2.7 %from_planes.1 = (f32[4,64,512]{2,1,0:T(8,128)}, f32[2,4,64,512]{3,2,1,0:T(8,128)}) custom-call(f32[3,16,96,128]{3,2,1,0:T(8,128)S(1)} %get-tuple-element.30.refs_0_), custom_call_target="tpu_custom_call" | custom-call | flops 2000000000 | bytes 6291456 | tf_op jit(solution)/shard_map/from_planes/pallas_call | solution.py:751
  35.7 0.0 collective-permute-done.3.refs_1_
  35.7 0.0 copy-done.7
  35.7 0.0 copy-done.9
  35.7 2.0 %local_loss.1 = (f32[64,256]{1,0:T(8,128)S(1)}, f32[64,256]{1,0:T(8,128)S(1)}, f32[16,256]{1,0:T(8,128)}) custom-call(f32[32,256]{1,0:T(8,128)S(1)} %bitcast.9, f32[32,256]{1,0:T(8,128)S(1)} %collective-permute-done.3.refs_1_, s32[16,1]{1,0:T(8,128)S(1)} %copy.15.refs_2_.refs_1_, f32[16,16]{1,0:T(8,128)S(1)} %copy-done.6, f32[264,512]{1,0:T(8,128)S(1)} %copy-done.2, ...), custom_call_target="tpu_custom_call" | custom-call | tf_op jit(solution)/shard_map/local_loss/pallas_call | solution.py:768
  37.7 0.1 collective-permute-start.4
  37.8 1.6 %collective-permute-start.10 = (f16[32,256]{1,0:T(8,128)(2,1)S(1)}, f16[32,256]{1,0:T(8,128)(2,1)S(1)}, u32[]{:S(2)}, u32[]{:S(2)}) collective-permute-start(f16[32,256]{1,0:T(8,128)(2,1)S(1)} %multiply_convert_fusion), channel_id=1, source_target_pairs={{0,2},{1,3},{2,0},{3,1},{4,6},{5,7},{6,4},{7,5},{8,10},{9,11},{10,... | collective-permute-start | bytes 49160 | tf_op jit(solution)/shard_map/ppermute | solution.py:626
  39.4 0.0 collective-permute-done.4
  39.4 1.3 %collective-permute-start.5 = (f32[64,256]{1,0:T(8,128)S(1)}, f32[64,256]{1,0:T(8,128)S(1)}, u32[]{:S(2)}, u32[]{:S(2)}) collective-permute-start(f32[64,256]{1,0:T(8,128)S(1)} %add.21), channel_id=1, source_target_pairs={{0,16},{16,0},{1,17},{17,1},{2,18},{18,2},{3,19},{19,3},{4,20},{20... | collective-permute-start | bytes 196616 | tf_op jit(solution)/shard_map/ppermute | solution.py:626
  40.7 1.2 %collective-permute-start.6 = (f32[64,256]{1,0:T(8,128)S(1)}, f32[64,256]{1,0:T(8,128)S(1)}, u32[]{:S(2)}, u32[]{:S(2)}) collective-permute-start(f32[64,256]{1,0:T(8,128)S(1)} %add.21), channel_id=1, source_target_pairs={{0,2},{1,3},{2,0},{3,1},{4,6},{5,7},{6,4},{7,5},{8,10},{9,11},{10,... | collective-permute-start | bytes 196616 | tf_op jit(solution)/shard_map/ppermute | solution.py:626
  41.8 1.1 %collective-permute-start.7 = (f32[64,256]{1,0:T(8,128)S(1)}, f32[64,256]{1,0:T(8,128)S(1)}, u32[]{:S(2)}, u32[]{:S(2)}) collective-permute-start(f32[64,256]{1,0:T(8,128)S(1)} %add.21), channel_id=1, source_target_pairs={{0,18},{1,19},{2,16},{3,17},{16,2},{17,3},{18,0},{19,1},{4,22},{5,... | collective-permute-start | bytes 196616 | tf_op jit(solution)/shard_map/ppermute | solution.py:789
  43.0 0.0 collective-permute-done.10
  43.0 0.8 %collective-permute-done.5 = f32[64,256]{1,0:T(8,128)S(1)} collective-permute-done((f32[64,256]{1,0:T(8,128)S(1)}, f32[64,256]{1,0:T(8,128)S(1)}, u32[]{:S(2)}, u32[]{:S(2)}) %collective-permute-start.5) | collective-permute-done | bytes 65568 | tf_op jit(solution)/shard_map/ppermute | solution.py:626
  43.7 3.7 %collective-permute-start.11 = (f16[64,256]{1,0:T(8,128)(2,1)S(1)}, f16[64,256]{1,0:T(8,128)(2,1)S(1)}, u32[]{:S(2)}, u32[]{:S(2)}) collective-permute-start(f16[64,256]{1,0:T(8,128)(2,1)S(1)} %pad_maximum_fusion.2), channel_id=1, source_target_pairs={{0,8},{4,12},{8,0},{12,4},{1,9},{5,13},{9,1},{13,5},{2,10},{6,14},... | collective-permute-start | bytes 98312 | tf_op jit(solution)/shard_map/ppermute | solution.py:626
  47.4 0.0 collective-permute-done.6
  47.4 0.0 collective-permute-done.7
  47.4 3.3 %collective-permute-start.8 = (f32[64,256]{1,0:T(8,128)S(1)}, f32[64,256]{1,0:T(8,128)S(1)}, u32[]{:S(2)}, u32[]{:S(2)}) collective-permute-start(f32[64,256]{1,0:T(8,128)S(1)} %add_add_fusion), channel_id=1, source_target_pairs={{0,8},{4,12},{8,0},{12,4},{1,9},{5,13},{9,1},{13,5},{2,10},{6,14},... | collective-permute-start | bytes 196616 | tf_op jit(solution)/shard_map/ppermute | solution.py:626
  50.7 0.0 collective-permute-done.11
  50.8 1.6 %collective-permute-start.12 = (f16[128,256]{1,0:T(8,128)(2,1)S(1)}, f16[128,256]{1,0:T(8,128)(2,1)S(1)}, u32[]{:S(2)}, u32[]{:S(2)}) collective-permute-start(f16[128,256]{1,0:T(8,128)(2,1)S(1)} %pad_maximum_fusion.1), channel_id=1, source_target_pairs={{0,4},{4,0},{8,12},{12,8},{1,5},{5,1},{9,13},{13,9},{2,6},{6,2},{1... | collective-permute-start | bytes 196616 | tf_op jit(solution)/shard_map/ppermute | solution.py:626
  52.4 0.6 collective-permute-done.8
  53.0 2.1 %collective-permute-done.12 = f16[128,256]{1,0:T(8,128)(2,1)S(1)} collective-permute-done((f16[128,256]{1,0:T(8,128)(2,1)S(1)}, f16[128,256]{1,0:T(8,128)(2,1)S(1)}, u32[]{:S(2)}, u32[]{:S(2)}) %collective-permute-start.12) | collective-permute-done | bytes 65568 | tf_op jit(solution)/shard_map/ppermute | solution.py:626
  55.1 0.1 collective-permute-start.13
  55.2 1.6 %collective-permute-start.9 = (f32[64,256]{1,0:T(8,128)S(1)}, f32[64,256]{1,0:T(8,128)S(1)}, u32[]{:S(2)}, u32[]{:S(2)}) collective-permute-start(f32[64,256]{1,0:T(8,128)S(1)} %add.25), channel_id=1, source_target_pairs={{0,4},{4,0},{8,12},{12,8},{1,5},{5,1},{9,13},{13,9},{2,6},{6,2},{1... | collective-permute-start | bytes 196616 | tf_op jit(solution)/shard_map/ppermute | solution.py:626
  56.9 0.0 collective-permute-done.13
  56.9 2.6 %couple_grads.1 = (f32[1128,128]{1,0:T(8,128)S(1)}, f32[1,128]{1,0:T(1,128)S(1)}) custom-call(f32[512,256]{1,0:T(8,128)S(1)} %maximum_convert_fusion.refs_0_, s32[16,1]{1,0:T(8,128)S(1)} %copy.15.refs_2_.refs_1_, f32[16,16]{1,0:T(8,128)S(1)} %copy-done.6, f32[264,512]{1,0:T(8,128)S(1)} %copy-done.2, f32[1,512]{1,0:T(1,128)S(1)} %bitcast.11, ...), custom_call_target="tpu_custom_call" | custom-call | flops 3000000000 | bytes 3145728 | tf_op jit(solution)/shard_map/couple_grads/pallas_call | solution.py:814
  59.5 0.2 collective-permute-done.9
  59.7 0.1 collective-permute-start.14
  59.8 1.2 %collective-permute-done.14.refs_1_ = f32[64,256]{1,0:T(8,128)S(1)} collective-permute-done((f32[64,256]{1,0:T(8,128)S(1)}, f32[64,256]{1,0:T(8,128)S(1)}, u32[]{:S(2)}, u32[]{:S(2)}) %collective-permute-start.14) | collective-permute-done | bytes 65568 | tf_op jit(solution)/shard_map/ppermute | solution.py:626
  61.1 1.1 %finish.1 = f32[1384,128]{1,0:T(8,128)} custom-call(f32[64,256]{1,0:T(8,128)S(1)} %add.27.refs_0_, f32[64,256]{1,0:T(8,128)S(1)} %collective-permute-done.14.refs_1_, f32[1128,128]{1,0:T(8,128)S(1)} %get-tuple-element.43.refs_2_, f32[1,128]{1,0:T(1,128)S(1)} %get-tuple-element.44.refs_3_), custom_call_target="tpu_custom_call" | custom-call | tf_op jit(solution)/shard_map/finish/pallas_call | solution.py:831
  (24 shorter events, 0.2 us)
Async XLA Ops:
  0.6 8.7 %copy-start.3 = (f32[4,64,512]{2,1,0:T(8,128)S(1)}, f32[4,64,512]{2,1,0:T(8,128)}, u32[]{:S(2)}) copy-start(f32[4,64,512]{2,1,0:T(8,128)} %refs_1_.3) | copy-start | bytes 1572868
  0.6 8.7 %copy-start.4 = (s32[64,512]{1,0:T(8,128)S(1)}, s32[64,512]{1,0:T(8,128)}, u32[]{:S(2)}) copy-start(s32[64,512]{1,0:T(8,128)} %refs_3_.5) | copy-start | bytes 393220
  0.7 8.7 %copy-start.6 = (f32[16,16]{1,0:T(8,128)S(1)}, f32[16,16]{1,0:T(8,128)}, u32[]{:S(2)}) copy-start(f32[16,16]{1,0:T(8,128)} %refs_2_.5) | copy-start | bytes 3076
  0.7 8.7 %copy-start.8 = (s32[16]{0:T(128)S(1)}, s32[16]{0:T(128)}, u32[]{:S(2)}) copy-start(s32[16]{0:T(128)} %refs_0_.3) | copy-start | bytes 196
  3.1 12.8 %collective-permute-start = (bf16[144,512]{1,0:T(8,128)(2,1)}, bf16[144,512]{1,0:T(8,128)(2,1)S(1)}, u32[]{:S(2)}, u32[]{:S(2)}) collective-permute-start(bf16[144,512]{1,0:T(8,128)(2,1)} %get-tuple-element.26), channel_id=1, source_target_pairs={{0,4},{4,8},{8,12},{1,5},{5,9},{9,13},{2,6},{6,10},{10,14},{3,7},{... | collective-permute-start | bytes 442376 | tf_op jit(solution)/shard_map/ppermute | solution.py:621
  8.0 7.9 %collective-permute-start.1 = (bf16[144,512]{1,0:T(8,128)(2,1)}, bf16[144,512]{1,0:T(8,128)(2,1)S(1)}, u32[]{:S(2)}, u32[]{:S(2)}) collective-permute-start(bf16[144,512]{1,0:T(8,128)(2,1)} %get-tuple-element.27), channel_id=1, source_target_pairs={{4,0},{8,4},{12,8},{5,1},{9,5},{13,9},{6,2},{10,6},{14,10},{7,3},{... | collective-permute-start | bytes 442376 | tf_op jit(solution)/shard_map/ppermute | solution.py:621
  9.3 1.2 %copy-start = (f32[2,4,64,512]{3,2,1,0:T(8,128)S(1)}, f32[2,4,64,512]{3,2,1,0:T(8,128)}, u32[]{:S(2)}) copy-start(f32[2,4,64,512]{3,2,1,0:T(8,128)} %refs_2_.4) | copy-start | bytes 3145732
  10.6 1.2 %copy-start.1 = (bf16[16,64,512]{2,1,0:T(8,128)(2,1)S(1)}, bf16[16,64,512]{2,1,0:T(8,128)(2,1)}, u32[]{:S(2)}) copy-start(bf16[16,64,512]{2,1,0:T(8,128)(2,1)} %refs_4_.4) | copy-start | bytes 3145732
  11.8 5.8 %copy-start.10 = (f32[512,16]{0,1:T(8,128)S(1)}, f32[512,16]{0,1:T(8,128)}, u32[]{:S(2)}) copy-start(f32[512,16]{0,1:T(8,128)} %param.20) | copy-start | bytes 98308
  15.9 4.9 %copy-start.5 = (bf16[128,256]{1,0:T(8,128)(2,1)S(1)}, bf16[128,256]{1,0:T(8,128)(2,1)}, u32[]{:S(2)}) copy-start(bf16[128,256]{1,0:T(8,128)(2,1)} %refs_5_.6) | copy-start | bytes 196612
  16.1 4.7 %collective-permute-start.2 = (bf16[400,128]{1,0:T(8,128)(2,1)S(1)}, bf16[400,128]{1,0:T(8,128)(2,1)S(1)}, u32[]{:S(2)}, u32[]{:S(2)}) collective-permute-start(bf16[400,128]{1,0:T(8,128)(2,1)S(1)} %rim.1.refs_2_), channel_id=1, source_target_pairs={{0,16},{16,0},{1,17},{17,1},{2,18},{18,2},{3,19},{19,3},{4,20},{20... | collective-permute-start | bytes 307208 | tf_op jit(solution)/shard_map/ppermute | solution.py:616
  31.4 4.3 %collective-permute-start.3 = (f32[32,256]{1,0:T(8,128)S(1)}, f32[32,256]{1,0:T(8,128)S(1)}, u32[]{:S(2)}, u32[]{:S(2)}) collective-permute-start(f32[32,256]{1,0:T(8,128)S(1)} %bitcast.8), channel_id=1, source_target_pairs={{0,16},{16,0},{1,17},{17,1},{2,18},{18,2},{3,19},{19,3},{4,20},{20... | collective-permute-start | bytes 98312 | tf_op jit(solution)/shard_map/ppermute | solution.py:626
  33.0 2.7 %copy-start.2 = (f32[264,512]{1,0:T(8,128)S(1)}, f32[264,512]{1,0:T(8,128)}, u32[]{:S(2)}) copy-start(f32[264,512]{1,0:T(8,128)} %refs_3_.7) | copy-start | bytes 1622020
  33.0 2.7 %copy-start.7 = (f32[512]{0:T(512)S(1)}, f32[512]{0:T(512)}, u32[]{:S(2)}) copy-start(f32[512]{0:T(512)} %param.19) | copy-start | bytes 6148
  33.0 2.7 %copy-start.9 = (f32[16]{0:T(128)S(1)}, f32[16]{0:T(128)}, u32[]{:S(2)}) copy-start(f32[16]{0:T(128)} %param.21) | copy-start | bytes 196
  37.7 1.7 %collective-permute-start.4 = (f32[64,256]{1,0:T(8,128)S(1)}, f32[64,256]{1,0:T(8,128)S(1)}, u32[]{:S(2)}, u32[]{:S(2)}) collective-permute-start(f32[64,256]{1,0:T(8,128)S(1)} %get-tuple-element.39), channel_id=1, source_target_pairs={{0,1},{1,0},{2,3},{3,2},{4,5},{5,4},{6,7},{7,6},{8,9},{9,8},{10,11... | collective-permute-start | bytes 196616 | tf_op jit(solution)/shard_map/ppermute | solution.py:626
  37.8 5.1 %collective-permute-start.10 = (f16[32,256]{1,0:T(8,128)(2,1)S(1)}, f16[32,256]{1,0:T(8,128)(2,1)S(1)}, u32[]{:S(2)}, u32[]{:S(2)}) collective-permute-start(f16[32,256]{1,0:T(8,128)(2,1)S(1)} %multiply_convert_fusion), channel_id=1, source_target_pairs={{0,2},{1,3},{2,0},{3,1},{4,6},{5,7},{6,4},{7,5},{8,10},{9,11},{10,... | collective-permute-start | bytes 49160 | tf_op jit(solution)/shard_map/ppermute | solution.py:626
  39.4 4.3 %collective-permute-start.5 = (f32[64,256]{1,0:T(8,128)S(1)}, f32[64,256]{1,0:T(8,128)S(1)}, u32[]{:S(2)}, u32[]{:S(2)}) collective-permute-start(f32[64,256]{1,0:T(8,128)S(1)} %add.21), channel_id=1, source_target_pairs={{0,16},{16,0},{1,17},{17,1},{2,18},{18,2},{3,19},{19,3},{4,20},{20... | collective-permute-start | bytes 196616 | tf_op jit(solution)/shard_map/ppermute | solution.py:626
  40.7 6.7 %collective-permute-start.6 = (f32[64,256]{1,0:T(8,128)S(1)}, f32[64,256]{1,0:T(8,128)S(1)}, u32[]{:S(2)}, u32[]{:S(2)}) collective-permute-start(f32[64,256]{1,0:T(8,128)S(1)} %add.21), channel_id=1, source_target_pairs={{0,2},{1,3},{2,0},{3,1},{4,6},{5,7},{6,4},{7,5},{8,10},{9,11},{10,... | collective-permute-start | bytes 196616 | tf_op jit(solution)/shard_map/ppermute | solution.py:626
  41.8 5.6 %collective-permute-start.7 = (f32[64,256]{1,0:T(8,128)S(1)}, f32[64,256]{1,0:T(8,128)S(1)}, u32[]{:S(2)}, u32[]{:S(2)}) collective-permute-start(f32[64,256]{1,0:T(8,128)S(1)} %add.21), channel_id=1, source_target_pairs={{0,18},{1,19},{2,16},{3,17},{16,2},{17,3},{18,0},{19,1},{4,22},{5,... | collective-permute-start | bytes 196616 | tf_op jit(solution)/shard_map/ppermute | solution.py:789
  43.7 7.0 %collective-permute-start.11 = (f16[64,256]{1,0:T(8,128)(2,1)S(1)}, f16[64,256]{1,0:T(8,128)(2,1)S(1)}, u32[]{:S(2)}, u32[]{:S(2)}) collective-permute-start(f16[64,256]{1,0:T(8,128)(2,1)S(1)} %pad_maximum_fusion.2), channel_id=1, source_target_pairs={{0,8},{4,12},{8,0},{12,4},{1,9},{5,13},{9,1},{13,5},{2,10},{6,14},... | collective-permute-start | bytes 98312 | tf_op jit(solution)/shard_map/ppermute | solution.py:626
  47.4 5.6 %collective-permute-start.8 = (f32[64,256]{1,0:T(8,128)S(1)}, f32[64,256]{1,0:T(8,128)S(1)}, u32[]{:S(2)}, u32[]{:S(2)}) collective-permute-start(f32[64,256]{1,0:T(8,128)S(1)} %add_add_fusion), channel_id=1, source_target_pairs={{0,8},{4,12},{8,0},{12,4},{1,9},{5,13},{9,1},{13,5},{2,10},{6,14},... | collective-permute-start | bytes 196616 | tf_op jit(solution)/shard_map/ppermute | solution.py:626
  50.8 4.3 %collective-permute-start.12 = (f16[128,256]{1,0:T(8,128)(2,1)S(1)}, f16[128,256]{1,0:T(8,128)(2,1)S(1)}, u32[]{:S(2)}, u32[]{:S(2)}) collective-permute-start(f16[128,256]{1,0:T(8,128)(2,1)S(1)} %pad_maximum_fusion.1), channel_id=1, source_target_pairs={{0,4},{4,0},{8,12},{12,8},{1,5},{5,1},{9,13},{13,9},{2,6},{6,2},{1... | collective-permute-start | bytes 196616 | tf_op jit(solution)/shard_map/ppermute | solution.py:626
  55.1 1.7 %collective-permute-start.13 = (f16[256,256]{1,0:T(8,128)(2,1)S(1)}, f16[256,256]{1,0:T(8,128)(2,1)S(1)}, u32[]{:S(2)}, u32[]{:S(2)}) collective-permute-start(f16[256,256]{1,0:T(8,128)(2,1)S(1)} %pad_maximum_fusion), channel_id=1, source_target_pairs={{0,1},{1,0},{2,3},{3,2},{4,5},{5,4},{6,7},{7,6},{8,9},{9,8},{10,11... | collective-permute-start | bytes 393224 | tf_op jit(solution)/shard_map/ppermute | solution.py:626
  55.2 4.5 %collective-permute-start.9 = (f32[64,256]{1,0:T(8,128)S(1)}, f32[64,256]{1,0:T(8,128)S(1)}, u32[]{:S(2)}, u32[]{:S(2)}) collective-permute-start(f32[64,256]{1,0:T(8,128)S(1)} %add.25), channel_id=1, source_target_pairs={{0,4},{4,0},{8,12},{12,8},{1,5},{5,1},{9,13},{13,9},{2,6},{6,2},{1... | collective-permute-start | bytes 196616 | tf_op jit(solution)/shard_map/ppermute | solution.py:626
  59.7 1.3 %collective-permute-start.14 = (f32[64,256]{1,0:T(8,128)S(1)}, f32[64,256]{1,0:T(8,128)S(1)}, u32[]{:S(2)}, u32[]{:S(2)}) collective-permute-start(f32[64,256]{1,0:T(8,128)S(1)} %add.27.refs_0_), channel_id=1, source_target_pairs={{0,1},{1,0},{2,3},{3,2},{4,5},{5,4},{6,7},{7,6},{8,9},{9,8},{10,11... | collective-permute-start | bytes 196616 | tf_op jit(solution)/shard_map/ppermute | solution.py:626

commit v4 on v3

--- a/solution.py
+++ b/solution.py
@@ -25,6 +25,7 @@
 BF16 = jnp.bfloat16
 LANES = 128
 MEBI = 2**20
+HALF_DEPTH = 0.5 * GRAVITY / NLEV
 
 
 def vmem():
@@ -186,6 +187,7 @@
     rows = side.shape[0] // 5
     cols = south.shape[1]
     low, high = south[...].astype(F32), north[...].astype(F32)
+    wholes = []
     for i in range(5):
         ends = [
             edges_of(
@@ -196,19 +198,88 @@
             for plain in (low, high)
         ]
         own = side[i * rows : (i + 1) * rows, :].astype(F32)
-        whole = jnp.concatenate([ends[0], own, ends[1]], axis=0)
-        out[i * whole.shape[0] : (i + 1) * whole.shape[0], :] = whole.astype(BF16)
-
-
-def halo_kernel(members, south, north, out):
-    cols = south.shape[1]
+        wholes.append(jnp.concatenate([ends[0], own, ends[1]], axis=0))
+    wide = rows + 2 * HALO
+    for n, i in enumerate((0, 2, 4)):
+        pair = wholes[i]
+        if i + 1 < len(wholes):
+            pair = pair + pltpu.roll(wholes[i + 1], 2 * HALO, 1)
+        out[n * wide : (n + 1) * wide, :] = pair.astype(BF16)
+
+
+def rims_of(own, from_east, from_west, patches):
+    place = lane_ids(own.shape[0]) % patches
+    out = []
+    for shift in (0, 2 * HALO):
+        out.append(
+            jnp.where(
+                place < 2 * HALO,
+                turned(own, -shift),
+                jnp.where(
+                    place < 3 * HALO,
+                    turned(from_east, 2 * HALO - shift),
+                    turned(from_west, -2 * HALO - shift),
+                ),
+            )
+        )
+    return out
+
+
+def prepare_kernel(
+    members, rows, cols, lat_count, south, north, planes, weight, state, force, ends, hu, hv, hvu, cu, cv, w_planes, depth, w_rows
+):
+    patches = cols // PW
+    height = rows + 2 * PAD
+    wide = rows + 2 * HALO
+    edge_rows = (slice(0, HALO), slice(height - HALO, height))
+    homes = (state.at[0], state.at[1], state.at[2], force, depth)
+    for i, home in enumerate(homes):
+        home[:, PAD : PAD + rows, :] = planes[i]
+        if i != 3:
+            for p in range(PW):
+                for rs in edge_rows:
+                    home[p, rs, :] = jnp.zeros((HALO, LANES), F32)
     matrix = plane_matrix(cols)
-    for end, got in enumerate((south, north)):
+    for got, r0 in ((south, PAD - HALO), (north, PAD + rows)):
         spread = jnp.dot(got[...], matrix, preferred_element_type=F32)
-        for i in range(5):
+        for i, home in enumerate(homes):
             parts = [spread[s : s + HALO] for s in starts_of(i, members)]
-            for k, plane in enumerate(planes_from(parts, cols // PW)):
-                out[end, i, k] = plane if i in (0, 4) else plane * (1.0 / GRAVITY)
+            for k, plane in enumerate(planes_from(parts, patches)):
+                home[k, r0 : r0 + HALO, :] = plane if i in (0, 4) else plane * (1.0 / GRAVITY)
+    span = slice(PAD - HALO, PAD + rows + HALO)
+    row, inside = row_ids(rows, lat_count)
+    place = row.astype(F32)
+    total = lat_count * rows
+    cu[span, :] = jnp.where(inside, 0.25 * (CORI_BASE + CORI_SLOPE * (place + 0.5) / total), 0.0)
+    cv[span, :] = jnp.where(inside, 0.25 * (CORI_BASE + CORI_SLOPE * place / total), 0.0)
+    for p in range(PW):
+        here = depth[p, span, :]
+        if p > 0:
+            hu[p, span, :] = HALF_DEPTH * (here + depth[p - 1, span, :])
+        vertical(depth.at[p], hv.at[p], hvu.at[p], inside, rows)
+    ends[0] = depth[0]
+    ends[1] = depth[PW - 1]
+    for h in range(w_rows.shape[0]):
+        cs = slice(h * LANES, (h + 1) * LANES)
+        w_rows[h] = weight[:, cs].astype(F32)
+        w_planes[:, cs] = jnp.concatenate(
+            [w_rows[h, pl.ds(k, PH, stride=PW), :] for k in range(PW)], axis=0
+        ).astype(BF16)
+
+
+def row_ids(rows, lat_count):
+    wide = rows + 2 * HALO
+    row = lax.broadcasted_iota(jnp.int32, (wide, LANES), 0) + (lax.axis_index("lat") * rows - HALO)
+    return row, (row >= 0) & (row < lat_count * rows)
+
+
+def vertical(depth, hv, hvu, inside, rows):
+    span = slice(PAD - HALO, PAD + rows + HALO)
+    here = depth[span, :]
+    below = depth[PAD - HALO - 1 : PAD + rows + HALO - 1, :]
+    above = depth[PAD - HALO + 1 : PAD + rows + HALO + 1, :]
+    hv[span, :] = HALF_DEPTH * (here + below)
+    hvu[span, :] = jnp.where(inside, HALF_DEPTH * (here + above), 0.0)
 
 
 def back_kernel(members, state, sea, vel):
@@ -237,7 +308,7 @@
                 vel[i - 1, m] = part * GRAVITY
 
 
-def flow_step(src, src_rim, dst, dst_rim, force, force_rim, hu, hv, hvu, cu, cv, last_mask, rows, patches):
+def flow_step(src, src_rim, dst, dst_rim, force, force_rim, hus, hvs, hvus, cu, cv, last_mask, rows, patches):
     strip = PW
     end = PAD + rows + HALO
     half = (rows + 2 * HALO) // 2
@@ -258,7 +329,7 @@
         def new_level(p, fx, fx_right):
             n_up = of(src, src_rim, 2, p)[up, :]
             n = of(src, src_rim, 2, p)[here, :]
-            fy = hvu[p, here, :] * n_up - hv[p, here, :] * n
+            fy = hvus[p][here, :] * n_up - hvs[p][here, :] * n
             level = of(src, src_rim, 0, p)[here, :] - ((fx_right - fx) + fy)
             of(dst, dst_rim, 0, p)[here, :] = level
             return level, n, n + n_up
@@ -280,7 +351,7 @@
 
         e_rim = src_rim[1, here, :]
         em_rim = src_rim[1, down, :]
-        fx_rim = hu[strip, here, :] * e_rim
+        fx_rim = hus[strip][here, :] * e_rim
         level_rim, n_rim, vs_rim = new_level(strip, fx_rim, pltpu.roll(fx_rim, LANES - 1, 1))
         new_flow(
             strip,
@@ -297,24 +368,25 @@
         em_end = wrap_right(src[1, 0, down, :], em_rim)
         e_last = src[1, PW - 1, here, :]
         level_last, n_last, vs_last = new_level(
-            PW - 1, hu[PW - 1, here, :] * e_last, hu[PW + 1, here, :] * e_end
+            PW - 1, hus[PW - 1][here, :] * e_last, hus[PW + 1][here, :] * e_end
         )
         level_left = wrap_left(level_last, level_rim)
         vs_left = wrap_left(vs_last, vs_rim)
         e = src[1, 0, here, :]
         em = src[1, 0, down, :]
-        fx = hu[0, here, :] * e
+        fx = hus[0][here, :] * e
         for p in range(PW):
             if p < PW - 1:
                 e_right = src[1, p + 1, here, :]
                 em_right = src[1, p + 1, down, :]
-                fx_right = hu[p + 1, here, :] * e_right
+                fx_right = hus[p + 1][here, :] * e_right
                 level, n, vs = new_level(p, fx, fx_right)
             else:
                 e_right, em_right, fx_right = e_end, em_end, None
                 level, n, vs = level_last, n_last, vs_last
             new_flow(p, e, e_right, em, em_right, n, vs + vs_left, level, level_left)
             level_left, vs_left, e, em, fx = level, vs, e_right, em_right, fx_right
+            yield
 
 
 def flow_kernel(
@@ -322,137 +394,119 @@
     rows,
     cols,
     lat_count,
-    planes,
-    halo,
-    side,
-    east,
-    west,
-    weight,
-    partial,
-    gram,
-    state_a,
-    state_b,
+    state,
     force,
-    depth,
-    rim_a,
-    rim_b,
-    force_rim,
-    depth_rim,
+    ends,
     hu,
     hv,
     hvu,
     cu,
     cv,
-    w_rows,
     w_planes,
+    side,
+    east,
+    west,
+    partial,
+    gram,
+    final,
+    state_b,
+    rim_a,
+    rim_b,
+    force_rim,
+    depth_rim,
+    hu_rim,
+    hv_rim,
+    hvu_rim,
     patch_t,
     slope,
+    state_a,
 ):
     patches = cols // PW
     lat = lax.axis_index("lat")
-    strip = PW
     height = rows + 2 * PAD
     wide = rows + 2 * HALO
-    scale = 1.0 / GRAVITY
-    edge_rows = (slice(0, HALO), slice(height - HALO, height))
-    for i in range(3):
-        for rs in edge_rows:
+    span = slice(PAD - HALO, PAD + rows + HALO)
+    state_a[...] = state[...]
+    for rs in (slice(0, HALO), slice(height - HALO, height)):
+        depth_rim[rs, :] = jnp.zeros((HALO, LANES), F32)
+        for i in range(3):
             rim_a[i, rs, :] = jnp.zeros((HALO, LANES), F32)
             rim_b[i, rs, :] = jnp.zeros((HALO, LANES), F32)
             for p in range(PW):
-                state_a[i, p, rs, :] = jnp.zeros((HALO, LANES), F32)
                 state_b[i, p, rs, :] = jnp.zeros((HALO, LANES), F32)
-    homes = (state_a.at[0], state_a.at[1], state_a.at[2], force, depth)
-    for i, home in enumerate(homes):
-        home[:, PAD : PAD + rows, :] = planes[i]
-        home[:, PAD - HALO : PAD, :] = halo[0, i]
-        home[:, PAD + rows : PAD + rows + HALO, :] = halo[1, i]
-    for rs in edge_rows:
-        depth_rim[rs, :] = jnp.zeros((HALO, LANES), F32)
-        for p in range(PW):
-            depth[p, rs, :] = jnp.zeros((HALO, LANES), F32)
-    place = lane_ids(wide) % patches
     rim_homes = (rim_a.at[0], rim_a.at[1], rim_a.at[2], force_rim, depth_rim)
-    for i, home in enumerate(rim_homes):
-        rs = slice(i * wide, (i + 1) * wide)
-        rim = jnp.where(
-            place < 2 * HALO,
-            side[rs, :].astype(F32),
-            jnp.where(
-                place < 3 * HALO,
-                pltpu.roll(east[rs, :].astype(F32), 2 * HALO, 1),
-                pltpu.roll(west[rs, :].astype(F32), LANES - 2 * HALO, 1),
-            ),
-        )
-        home[PAD - HALO : PAD + rows + HALO, :] = rim * (1.0 if i in (0, 4) else scale)
-    for h in range(w_rows.shape[0]):
-        cs = slice(h * LANES, (h + 1) * LANES)
-        w_rows[h] = weight[:, cs].astype(F32)
-        w_planes[:, cs] = jnp.concatenate(
-            [w_rows[h, pl.ds(k, PH, stride=PW), :] for k in range(PW)], axis=0
-        ).astype(BF16)
-    span = slice(PAD - HALO, PAD + rows + HALO)
-    row = lax.broadcasted_iota(jnp.int32, (wide, LANES), 0) + (lat * rows - HALO)
-    inside = (row >= 0) & (row < lat_count * rows)
-    place = row.astype(F32)
-    total = lat_count * rows
-    cu[span, :] = jnp.where(
-        inside, 0.25 * (CORI_BASE + CORI_SLOPE * (place + 0.5) / total), 0.0
+    for n in range(3):
+        rs = slice(n * wide, (n + 1) * wide)
+        got = [ref[rs, :].astype(F32) for ref in (side, east, west)]
+        for i, rim in zip((2 * n, 2 * n + 1), rims_of(*got, patches)):
+            if i < len(rim_homes):
+                rim_homes[i][span, :] = rim if i in (0, 4) else rim * (1.0 / GRAVITY)
+    _, inside = row_ids(rows, lat_count)
+    last = lane_ids(wide) % patches == patches - 1
+    rim = depth_rim[span, :]
+    left = pltpu.roll(jnp.where(last, rim, ends[1, span, :]), 1, 1)
+    first = HALF_DEPTH * (ends[0, span, :] + left)
+    rim = HALF_DEPTH * (rim + pltpu.roll(rim, 1, 1))
+    hu_rim[0, span, :] = first
+    hu_rim[1, span, :] = rim
+    hu_rim[2, span, :] = jnp.where(
+        last, pltpu.roll(rim, PW - 1, 1), pltpu.roll(first, LANES - 1, 1)
     )
-    cv[span, :] = jnp.where(inside, 0.25 * (CORI_BASE + CORI_SLOPE * place / total), 0.0)
-    half_depth = 0.5 * GRAVITY / NLEV
-    last = lane_ids(wide) % patches == patches - 1
-    for p in range(PW + 1):
-        home = depth_rim if p == strip else depth.at[p]
-        here = home[span, :]
-        if p == 0:
-            left = pltpu.roll(jnp.where(last, depth_rim[span, :], depth[PW - 1, span, :]), 1, 1)
-        elif p == strip:
-            left = pltpu.roll(here, 1, 1)
-        else:
-            left = depth[p - 1, span, :]
-        below = home[PAD - HALO - 1 : PAD + rows + HALO - 1, :]
-        above = home[PAD - HALO + 1 : PAD + rows + HALO + 1, :]
-        hu[p, span, :] = half_depth * (here + left)
-        hv[p, span, :] = half_depth * (here + below)
-        hvu[p, span, :] = jnp.where(inside, half_depth * (here + above), 0.0)
-    hu[PW + 1, span, :] = jnp.where(
-        last,
-        pltpu.roll(hu[strip, span, :], PW - 1, 1),
-        pltpu.roll(hu[0, span, :], LANES - 1, 1),
-    )
+    vertical(depth_rim, hv_rim, hvu_rim, inside, rows)
+    hus = [hu_rim.at[0]] + [hu.at[p] for p in range(1, PW)] + [hu_rim.at[1], hu_rim.at[2]]
+    hvs = [hv.at[p] for p in range(PW)] + [hv_rim]
+    hvus = [hvu.at[p] for p in range(PW)] + [hvu_rim]
 
     last_mask = jnp.where(lat < lat_count - 1, 1.0, 0.0)
     count = rows // PH
 
+    def embed_step(state, turn, sub):
+        step = 2 * turn + sub
+        total = None
+        for b in range(count):
+            cells = state[0, :, PAD + b * PH : PAD + (b + 1) * PH, :].reshape(PW * PH, LANES)
+            cells_t = cells.T.astype(BF16)
+            act = jnp.tanh(jnp.dot(cells_t, w_planes[...], preferred_element_type=F32))
+            total = act if total is None else total + act
+            fall = (1.0 - act * act).astype(BF16)
+            for m in range(members):
+                rs = slice(m * patches, (m + 1) * patches)
+                to = slice(b * patches, (b + 1) * patches)
+                patch_t[m, to, :] = cells_t[rs]
+                slope[m, to, :] = fall[rs]
+            yield
+        sums = jnp.sum(total.reshape(members, patches, total.shape[1]), axis=1)
+        partial[turn, sub * members : (sub + 1) * members, :] = sums
+        for m in range(members):
+            gram[step * members + m] = lax.dot_general(
+                patch_t[m], slope[m], (((0,), (0,)), ((), ())), preferred_element_type=F32
+            )
+            yield
+
+    def beside(flow, embed):
+        for n, _ in enumerate(flow):
+            if n % 3 == 2:
+                next(embed, None)
+        for _ in embed:
+            pass
+
+    def step_of(src, src_rim, dst, dst_rim):
+        return flow_step(
+            src, src_rim, dst, dst_rim, force, force_rim, hus, hvs, hvus, cu, cv, last_mask, rows, patches
+        )
+
     def two_steps(turn, carry):
-        for sub, (src, src_rim, dst, dst_rim) in enumerate(
-            ((state_a, rim_a, state_b, rim_b), (state_b, rim_b, state_a, rim_a))
-        ):
-            flow_step(
-                src, src_rim, dst, dst_rim, force, force_rim, hu, hv, hvu, cu, cv, last_mask, rows, patches
-            )
-            total = None
-            for b in range(count):
-                cells = dst[0, :, PAD + b * PH : PAD + (b + 1) * PH, :].reshape(PW * PH, LANES)
-                cells_t = cells.T.astype(BF16)
-                act = jnp.tanh(jnp.dot(cells_t, w_planes[...], preferred_element_type=F32))
-                total = act if total is None else total + act
-                fall = (1.0 - act * act).astype(BF16)
-                for m in range(members):
-                    rs = slice(m * patches, (m + 1) * patches)
-                    to = slice(b * patches, (b + 1) * patches)
-                    patch_t[m, to, :] = cells_t[rs]
-                    slope[m, to, :] = fall[rs]
-            sums = jnp.sum(total.reshape(members, patches, total.shape[1]), axis=1)
-            partial[turn, sub * members : (sub + 1) * members, :] = sums
-            for m in range(members):
-                gram[(2 * turn + sub) * members + m] = lax.dot_general(
-                    patch_t[m], slope[m], (((0,), (0,)), ((), ())), preferred_element_type=F32
-                )
+        beside(
+            step_of(state_a, rim_a, state_b, rim_b),
+            embed_step(state_a, jnp.maximum(turn - 1, 0), 1),
+        )
+        beside(step_of(state_b, rim_b, state_a, rim_a), embed_step(state_b, turn, 0))
         return carry
 
     lax.fori_loop(0, STEPS // 2, two_steps, 0)
+    final[...] = state_a[...]
+    for _ in embed_step(state_a, STEPS // 2 - 1, 1):
+        pass
 
 
 def split(value):
@@ -693,7 +747,7 @@
     wide = rows + 2 * HALO
     rim = pl.pallas_call(
         lambda *refs: rim_kernel(members, patches, *refs),
-        out_shape=shape(5 * wide, LANES, dtype=BF16),
+        out_shape=shape(3 * wide, LANES, dtype=BF16),
         in_specs=[vmem()] * 3,
         out_specs=vmem(),
         compiler_params=params_of(16),
@@ -702,46 +756,56 @@
     west = neighbour(rim, "lon", 1)
     east = west if lon_count == 2 else neighbour(rim, "lon", -1)
 
-    halo = pl.pallas_call(
-        lambda *refs: halo_kernel(members, *refs),
-        out_shape=shape(2, 5, PW, HALO, LANES),
-        in_specs=[vmem()] * 2,
-        out_specs=vmem(),
+    plane = (PW, height, LANES)
+    prepared = pl.pallas_call(
+        lambda *refs: prepare_kernel(members, rows, cols, lat_count, *refs),
+        out_shape=(
+            shape(3, *plane),
+            shape(*plane),
+            shape(2, height, LANES),
+            shape(*plane),
+            shape(*plane),
+            shape(*plane),
+            shape(height, LANES),
+            shape(height, LANES),
+            shape(cells, feats, dtype=BF16),
+        ),
+        in_specs=[vmem()] * 4,
+        out_specs=(vmem(),) * 9,
+        scratch_shapes=[
+            pltpu.VMEM(plane, F32),
+            pltpu.VMEM((feats // LANES, cells, LANES), F32),
+        ],
         compiler_params=params_of(16),
         cost_estimate=pl.CostEstimate(flops=10**9, bytes_accessed=4 * MEBI, transcendentals=0),
-        name="halo_planes",
-    )(south, north)
+        name="prepare",
+    )(south, north, planes, conv_weight)
 
     partial, gram, final = pl.pallas_call(
         lambda *refs: flow_kernel(members, rows, cols, lat_count, *refs),
         out_shape=(
             shape(STEPS // 2, 2 * members, feats),
             shape(samples, cells, feats),
-            shape(3, PW, height, LANES),
+            shape(3, *plane),
         ),
-        in_specs=[vmem()] * 6,
+        in_specs=[vmem()] * 12,
         out_specs=(vmem(),) * 3,
         scratch_shapes=[
-            pltpu.VMEM((3, PW, height, LANES), F32),
-            pltpu.VMEM((PW, height, LANES), F32),
-            pltpu.VMEM((PW, height, LANES), F32),
+            pltpu.VMEM((3, *plane), F32),
             pltpu.VMEM((3, height, LANES), F32),
             pltpu.VMEM((3, height, LANES), F32),
             pltpu.VMEM((height, LANES), F32),
             pltpu.VMEM((height, LANES), F32),
-            pltpu.VMEM((PW + 2, height, LANES), F32),
-            pltpu.VMEM((PW + 1, height, LANES), F32),
-            pltpu.VMEM((PW + 1, height, LANES), F32),
+            pltpu.VMEM((3, height, LANES), F32),
             pltpu.VMEM((height, LANES), F32),
             pltpu.VMEM((height, LANES), F32),
-            pltpu.VMEM((feats // LANES, cells, LANES), F32),
-            pltpu.VMEM((cells, feats), BF16),
             pltpu.VMEM((members, rows // PH * patches, cells), BF16),
             pltpu.VMEM((members, rows // PH * patches, feats), BF16),
+            pltpu.VMEM((3, *plane), F32),
         ],
         compiler_params=params_of(32),
         name="flow_embed",
-    )(planes, halo, rim, east, west, conv_weight)
+    )(*prepared, rim, east, west)
     partial = partial.reshape(samples, feats)
 
     if lon_count == 2:

time: 62.4 us -> 60 us (0.962)
  starting transfers between devices: 25 us -> 23.1 us
  local copies, waits for them, and re-layouts: 2.69 us -> 1.01 us
  waiting for transfers between devices: 7.08 us -> 8.29 us
    ppermute x11, starting transfers between devices: 16 us -> 14.2 us  [swapped(): return lax.ppermute(value, axis, [(i, i ^ flip) for i in range(count)])]
    unnamed x23 -> x21, local copies, waits for them, and re-layouts: 2.6 us -> 0.92 us
    ppermute x2, waiting for transfers between devices: 0.01 us -> 1.12 us  [from_lat(): lax.ppermute(value, 'lat', [(i, i + step) for i in range(count) if 0 <= i...]
    ppermute x1, waiting for transfers between devices: 0.01 us -> 0.63 us  [shards(): lax.ppermute(conv, ('lon', 'grp'), [(i, (i // grp_count ^ 1) * grp_count...]
  transfers between devices with their start and end apart: 15 -> 15, of which waited for: 6 -> 8; matrix products, arithmetic and copies ran while one was open for 1% -> 2% of each run, Pallas kernels for 16% -> 18%
where the time goes in v4:
time: 60 us; the launch traced here: 59.7 us
  Pallas kernels  26.3 us (44%)
  starting transfers between devices  23.1 us (38%)
  waiting for transfers between devices  8.29 us (14%)
  local copies, waits for them, and re-layouts  1.01 us (2%)
  between operations  0.87 us (1%)
    ppermute x11, starting transfers between devices, swapped(): return lax.ppermute(value, axis, [(i, i ^ flip) for i in range(count)])  14.2 us
    pallas_call x1, Pallas kernels, shards(): pl.pallas_call(lambda *refs: flow_kernel(members, rows, cols, lat_count,...  10.1 us
    ppermute x2, starting transfers between devices, from_lat(): lax.ppermute(value, 'lat', [(i, i + step) for i in range(count) if 0 <= i...  6.23 us
    ppermute x11, waiting for transfers between devices, swapped(): return lax.ppermute(value, axis, [(i, i ^ flip) for i in range(count)])  4.98 us
    pallas_call x1, Pallas kernels, shards(): pl.pallas_call(lambda *refs: planar_kernel(members, *refs), out_shape=(sh...  3.96 us
    pallas_call x1, Pallas kernels, shards(): pl.pallas_call(lambda *refs: back_kernel(members, *refs), out_shape=(shap...  2.74 us
    pallas_call x1, Pallas kernels, shards(): pl.pallas_call(lambda *refs: couple_kernel(members, lat_count, grp_count,...  2.62 us
    pallas_call x1, Pallas kernels, shards(): pl.pallas_call(lambda *refs: pack_kernel(members, *refs), out_shape=(shap...  2.48 us
  transfers between devices with their start and end apart: 15, of which 8 were waited for; matrix products, arithmetic and copies ran while one was open for 2% of the time, Pallas kernels for 18%

profile of v4, /device:TPU:0, one launch (start us, length us, event | category | flops | bytes accessed | tf_op | source)
XLA Modules:
  0.0 59.7 jit_solution(10799295255388854260)
XLA Ops:
  0.6 0.0 copy-start.3
  0.6 0.0 copy-start
  0.7 0.0 copy-start.4
  0.7 0.0 copy-start.1
  0.7 2.5 %pack_rows.1 = (bf16[144,512]{1,0:T(8,128)(2,1)}, bf16[144,512]{1,0:T(8,128)(2,1)}) custom-call(s32[16]{0:T(128)} %refs_0_.3, f32[4,64,512]{2,1,0:T(8,128)} %refs_1_.3, f32[2,4,64,512]{3,2,1,0:T(8,128)} %refs_2_.4, s32[64,512]{1,0:T(8,128)} %refs_3_.6, bf16[16,64,512]{2,1,0:T(8,128)(2,1)} %refs_4_.4, f32[16,16]{1,0:T(8,128)} %refs_2_.5), custom_call_target="tpu_custom_call" | custom-call | tf_op jit(solution)/shard_map/pack_rows/pallas_call | solution.py:717
  3.2 4.9 %collective-permute-start = (bf16[144,512]{1,0:T(8,128)(2,1)}, bf16[144,512]{1,0:T(8,128)(2,1)S(1)}, u32[]{:S(2)}, u32[]{:S(2)}) collective-permute-start(bf16[144,512]{1,0:T(8,128)(2,1)} %get-tuple-element.34), channel_id=1, source_target_pairs={{0,4},{4,8},{8,12},{1,5},{5,9},{9,13},{2,6},{6,10},{10,14},{3,7},{... | collective-permute-start | bytes 442376 | tf_op jit(solution)/shard_map/ppermute | solution.py:675
  8.1 1.3 %collective-permute-start.1 = (bf16[144,512]{1,0:T(8,128)(2,1)}, bf16[144,512]{1,0:T(8,128)(2,1)S(1)}, u32[]{:S(2)}, u32[]{:S(2)}) collective-permute-start(bf16[144,512]{1,0:T(8,128)(2,1)} %get-tuple-element.35), channel_id=1, source_target_pairs={{4,0},{8,4},{12,8},{5,1},{9,5},{13,9},{6,2},{10,6},{14,10},{7,3},{... | collective-permute-start | bytes 442376 | tf_op jit(solution)/shard_map/ppermute | solution.py:675
  9.4 0.9 %copy.16.refs_6_.refs_5_ = f32[512,16]{1,0:T(8,128)S(1)} copy(f32[512,16]{0,1:T(8,128)} %param.20) | data formatting | bytes 65536 | tf_op args[9]
  10.3 0.1 copy.15.refs_2_.refs_1_
  10.4 0.0 copy-done
  10.4 0.0 copy-start.9
  10.4 4.0 %to_planes.1 = (f32[5,16,64,128]{3,2,1,0:T(8,128)S(1)}, bf16[320,128]{1,0:T(8,128)(2,1)S(1)}) custom-call(s32[16]{0:T(128)S(1)} %copy-done.7, f32[4,64,512]{2,1,0:T(8,128)S(1)} %copy-done.3, f32[2,4,64,512]{3,2,1,0:T(8,128)S(1)} %copy-done, s32[64,512]{1,0:T(8,128)S(1)} %copy-done.4, bf16[16,64,512]{2,1,0:T(8,128)(2,1)S(1)} %copy-done.1, f32[16,16]{1,0:T(8,128)S(1)} %copy-done.5), custom_call_target="tpu_custom_call" | custom-call | flops 2000000000 | bytes 6291456 | tf_op jit(solution)/shard_map/to_planes/pallas_call | solution.py:737
  14.4 0.0 collective-permute-done.refs_0_
  14.4 1.1 %collective-permute-done.1.refs_1_ = bf16[144,512]{1,0:T(8,128)(2,1)S(1)} collective-permute-done((bf16[144,512]{1,0:T(8,128)(2,1)}, bf16[144,512]{1,0:T(8,128)(2,1)S(1)}, u32[]{:S(2)}, u32[]{:S(2)}) %collective-permute-start.1) | collective-permute-done | bytes 147488 | tf_op jit(solution)/shard_map/ppermute | solution.py:675
  15.5 0.2 rim.1.refs_9_
  15.8 1.5 %collective-permute-start.2 = (bf16[240,128]{1,0:T(8,128)(2,1)S(1)}, bf16[240,128]{1,0:T(8,128)(2,1)S(1)}, u32[]{:S(2)}, u32[]{:S(2)}) collective-permute-start(bf16[240,128]{1,0:T(8,128)(2,1)S(1)} %rim.1.refs_9_), channel_id=1, source_target_pairs={{0,16},{16,0},{1,17},{17,1},{2,18},{18,2},{3,19},{19,3},{4,20},{20... | collective-permute-start | bytes 184328 | tf_op jit(solution)/shard_map/ppermute | solution.py:670
  17.3 1.1 %prepare.1 = (f32[3,16,96,128]{3,2,1,0:T(8,128)S(1)}, f32[16,96,128]{2,1,0:T(8,128)S(1)}, f32[2,96,128]{2,1,0:T(8,128)S(1)}, f32[16,96,128]{2,1,0:T(8,128)S(1)},...) custom-call(bf16[144,512]{1,0:T(8,128)(2,1)S(1)} %collective-permute, ...), custom_call_target="tpu_custom_call" | custom-call | flops 1000000000 | bytes 4194304 | tf_op jit(solution)/shard_map/prepare/pallas_call | solution.py:760
  18.4 1.6 %collective-permute-done.2.refs_10_.refs_11_ = bf16[240,128]{1,0:T(8,128)(2,1)S(1)} collective-permute-done((bf16[240,128]{1,0:T(8,128)(2,1)S(1)}, bf16[240,128]{1,0:T(8,128)(2,1)S(1)}, u32[]{:S(2)}, u32[]{:S(2)}) %collective-permute-start.2) | collective-permute-done | bytes 61472 | tf_op jit(solution)/shard_map/ppermute | solution.py:670
  20.0 10.1 %flow_embed.1 = (f32[4,8,256]{2,1,0:T(8,128)S(1)}, f32[32,128,256]{2,1,0:T(8,128)S(1)}, f32[3,16,96,128]{3,2,1,0:T(8,128)S(1)}) custom-call(f32[3,16,96,128]{3,2,1,0:T(8,128)S(1)} %get-tuple-element.37.refs_0_, f32[16,96,128]{2,1,0:T(8,128)S(1)} %get-tuple-element.38.refs_1_, f32[2,96,128]{2,1,0:T(8,128)S(1)} %get-tuple-element.39.refs_2_, ...), custom_call_target="tpu_custom_call" | custom-call | tf_op jit(solution)/shard_map/flow_embed/pallas_call | solution.py:784
  30.1 1.6 %collective-permute-start.3 = (f32[32,256]{1,0:T(8,128)S(1)}, f32[32,256]{1,0:T(8,128)S(1)}, u32[]{:S(2)}, u32[]{:S(2)}) collective-permute-start(f32[32,256]{1,0:T(8,128)S(1)} %bitcast.8), channel_id=1, source_target_pairs={{0,16},{16,0},{1,17},{17,1},{2,18},{18,2},{3,19},{19,3},{4,20},{20... | collective-permute-start | bytes 98312 | tf_op jit(solution)/shard_map/ppermute | solution.py:680
  31.7 2.7 %from_planes.1 = (f32[4,64,512]{2,1,0:T(8,128)}, f32[2,4,64,512]{3,2,1,0:T(8,128)}) custom-call(f32[3,16,96,128]{3,2,1,0:T(8,128)S(1)} %get-tuple-element.48.refs_0_), custom_call_target="tpu_custom_call" | custom-call | flops 2000000000 | bytes 6291456 | tf_op jit(solution)/shard_map/from_planes/pallas_call | solution.py:815
  34.4 0.0 collective-permute-done.3.refs_1_
  34.4 0.0 copy-done.6
  34.4 2.0 %local_loss.1 = (f32[64,256]{1,0:T(8,128)S(1)}, f32[64,256]{1,0:T(8,128)S(1)}, f32[16,256]{1,0:T(8,128)}) custom-call(f32[32,256]{1,0:T(8,128)S(1)} %bitcast.9, f32[32,256]{1,0:T(8,128)S(1)} %collective-permute-done.3.refs_1_, s32[16,1]{1,0:T(8,128)S(1)} %copy.15.refs_2_.refs_1_, f32[16,16]{1,0:T(8,128)S(1)} %copy-done.5, f32[264,512]{1,0:T(8,128)S(1)} %copy-done.2, ...), custom_call_target="tpu_custom_call" | custom-call | tf_op jit(solution)/shard_map/local_loss/pallas_call | solution.py:832
  36.4 0.1 collective-permute-start.4
  36.5 1.6 %collective-permute-start.10 = (f16[32,256]{1,0:T(8,128)(2,1)S(1)}, f16[32,256]{1,0:T(8,128)(2,1)S(1)}, u32[]{:S(2)}, u32[]{:S(2)}) collective-permute-start(f16[32,256]{1,0:T(8,128)(2,1)S(1)} %multiply_convert_fusion), channel_id=1, source_target_pairs={{0,2},{1,3},{2,0},{3,1},{4,6},{5,7},{6,4},{7,5},{8,10},{9,11},{10,... | collective-permute-start | bytes 49160 | tf_op jit(solution)/shard_map/ppermute | solution.py:680
  38.1 0.0 collective-permute-done.4
  38.1 1.2 %collective-permute-start.5 = (f32[64,256]{1,0:T(8,128)S(1)}, f32[64,256]{1,0:T(8,128)S(1)}, u32[]{:S(2)}, u32[]{:S(2)}) collective-permute-start(f32[64,256]{1,0:T(8,128)S(1)} %add.21), channel_id=1, source_target_pairs={{0,16},{16,0},{1,17},{17,1},{2,18},{18,2},{3,19},{19,3},{4,20},{20... | collective-permute-start | bytes 196616 | tf_op jit(solution)/shard_map/ppermute | solution.py:680
  39.4 1.2 %collective-permute-start.6 = (f32[64,256]{1,0:T(8,128)S(1)}, f32[64,256]{1,0:T(8,128)S(1)}, u32[]{:S(2)}, u32[]{:S(2)}) collective-permute-start(f32[64,256]{1,0:T(8,128)S(1)} %add.21), channel_id=1, source_target_pairs={{0,2},{1,3},{2,0},{3,1},{4,6},{5,7},{6,4},{7,5},{8,10},{9,11},{10,... | collective-permute-start | bytes 196616 | tf_op jit(solution)/shard_map/ppermute | solution.py:680
  40.5 1.2 %collective-permute-start.7 = (f32[64,256]{1,0:T(8,128)S(1)}, f32[64,256]{1,0:T(8,128)S(1)}, u32[]{:S(2)}, u32[]{:S(2)}) collective-permute-start(f32[64,256]{1,0:T(8,128)S(1)} %add.21), channel_id=1, source_target_pairs={{0,18},{1,19},{2,16},{3,17},{16,2},{17,3},{18,0},{19,1},{4,22},{5,... | collective-permute-start | bytes 196616 | tf_op jit(solution)/shard_map/ppermute | solution.py:853
  41.7 0.0 collective-permute-done.10
  41.7 0.8 %collective-permute-done.5 = f32[64,256]{1,0:T(8,128)S(1)} collective-permute-done((f32[64,256]{1,0:T(8,128)S(1)}, f32[64,256]{1,0:T(8,128)S(1)}, u32[]{:S(2)}, u32[]{:S(2)}) %collective-permute-start.5) | collective-permute-done | bytes 65568 | tf_op jit(solution)/shard_map/ppermute | solution.py:680
  42.5 2.6 %collective-permute-start.11 = (f16[64,256]{1,0:T(8,128)(2,1)S(1)}, f16[64,256]{1,0:T(8,128)(2,1)S(1)}, u32[]{:S(2)}, u32[]{:S(2)}) collective-permute-start(f16[64,256]{1,0:T(8,128)(2,1)S(1)} %pad_maximum_fusion.2), channel_id=1, source_target_pairs={{0,8},{4,12},{8,0},{12,4},{1,9},{5,13},{9,1},{13,5},{2,10},{6,14},... | collective-permute-start | bytes 98312 | tf_op jit(solution)/shard_map/ppermute | solution.py:680
  45.0 0.0 collective-permute-done.6
  45.1 0.6 %collective-permute-done.7 = f32[64,256]{1,0:T(8,128)S(1)} collective-permute-done((f32[64,256]{1,0:T(8,128)S(1)}, f32[64,256]{1,0:T(8,128)S(1)}, u32[]{:S(2)}, u32[]{:S(2)}) %collective-permute-start.7) | collective-permute-done | bytes 65568 | tf_op jit(solution)/shard_map/ppermute | solution.py:853
  45.7 2.6 %collective-permute-start.8 = (f32[64,256]{1,0:T(8,128)S(1)}, f32[64,256]{1,0:T(8,128)S(1)}, u32[]{:S(2)}, u32[]{:S(2)}) collective-permute-start(f32[64,256]{1,0:T(8,128)S(1)} %add_add_fusion), channel_id=1, source_target_pairs={{0,8},{4,12},{8,0},{12,4},{1,9},{5,13},{9,1},{13,5},{2,10},{6,14},... | collective-permute-start | bytes 196616 | tf_op jit(solution)/shard_map/ppermute | solution.py:680
  48.3 0.0 collective-permute-done.11
  48.4 1.6 %collective-permute-start.12 = (f16[128,256]{1,0:T(8,128)(2,1)S(1)}, f16[128,256]{1,0:T(8,128)(2,1)S(1)}, u32[]{:S(2)}, u32[]{:S(2)}) collective-permute-start(f16[128,256]{1,0:T(8,128)(2,1)S(1)} %pad_maximum_fusion.1), channel_id=1, source_target_pairs={{0,4},{4,0},{8,12},{12,8},{1,5},{5,1},{9,13},{13,9},{2,6},{6,2},{1... | collective-permute-start | bytes 196616 | tf_op jit(solution)/shard_map/ppermute | solution.py:680
  50.0 1.0 %collective-permute-done.8 = f32[64,256]{1,0:T(8,128)S(1)} collective-permute-done((f32[64,256]{1,0:T(8,128)S(1)}, f32[64,256]{1,0:T(8,128)S(1)}, u32[]{:S(2)}, u32[]{:S(2)}) %collective-permute-start.8) | collective-permute-done | bytes 65568 | tf_op jit(solution)/shard_map/ppermute | solution.py:680
  50.9 1.8 %collective-permute-done.12 = f16[128,256]{1,0:T(8,128)(2,1)S(1)} collective-permute-done((f16[128,256]{1,0:T(8,128)(2,1)S(1)}, f16[128,256]{1,0:T(8,128)(2,1)S(1)}, u32[]{:S(2)}, u32[]{:S(2)}) %collective-permute-start.12) | collective-permute-done | bytes 65568 | tf_op jit(solution)/shard_map/ppermute | solution.py:680
  52.7 0.1 collective-permute-start.13
  52.8 1.6 %collective-permute-start.9 = (f32[64,256]{1,0:T(8,128)S(1)}, f32[64,256]{1,0:T(8,128)S(1)}, u32[]{:S(2)}, u32[]{:S(2)}) collective-permute-start(f32[64,256]{1,0:T(8,128)S(1)} %add.25), channel_id=1, source_target_pairs={{0,4},{4,0},{8,12},{12,8},{1,5},{5,1},{9,13},{13,9},{2,6},{6,2},{1... | collective-permute-start | bytes 196616 | tf_op jit(solution)/shard_map/ppermute | solution.py:680
  54.4 0.0 collective-permute-done.13
  54.5 2.6 %couple_grads.1 = (f32[1128,128]{1,0:T(8,128)S(1)}, f32[1,128]{1,0:T(1,128)S(1)}) custom-call(f32[512,256]{1,0:T(8,128)S(1)} %maximum_convert_fusion.refs_0_, s32[16,1]{1,0:T(8,128)S(1)} %copy.15.refs_2_.refs_1_, f32[16,16]{1,0:T(8,128)S(1)} %copy-done.5, f32[264,512]{1,0:T(8,128)S(1)} %copy-done.2, f32[1,512]{1,0:T(1,128)S(1)} %bitcast.11, ...), custom_call_target="tpu_custom_call" | custom-call | flops 3000000000 | bytes 3145728 | tf_op jit(solution)/shard_map/couple_grads/pallas_call | solution.py:878
  57.1 0.2 collective-permute-done.9
  57.3 0.1 collective-permute-start.14
  57.4 1.2 %collective-permute-done.14.refs_1_ = f32[64,256]{1,0:T(8,128)S(1)} collective-permute-done((f32[64,256]{1,0:T(8,128)S(1)}, f32[64,256]{1,0:T(8,128)S(1)}, u32[]{:S(2)}, u32[]{:S(2)}) %collective-permute-start.14) | collective-permute-done | bytes 65568 | tf_op jit(solution)/shard_map/ppermute | solution.py:680
  58.7 1.1 %finish.1 = f32[1384,128]{1,0:T(8,128)} custom-call(f32[64,256]{1,0:T(8,128)S(1)} %add.27.refs_0_, f32[64,256]{1,0:T(8,128)S(1)} %collective-permute-done.14.refs_1_, f32[1128,128]{1,0:T(8,128)S(1)} %get-tuple-element.61.refs_2_, f32[1,128]{1,0:T(1,128)S(1)} %get-tuple-element.62.refs_3_), custom_call_target="tpu_custom_call" | custom-call | tf_op jit(solution)/shard_map/finish/pallas_call | solution.py:895
  (22 shorter events, 0.2 us)
Async XLA Ops:
  0.6 9.8 %copy-start.3 = (f32[4,64,512]{2,1,0:T(8,128)S(1)}, f32[4,64,512]{2,1,0:T(8,128)}, u32[]{:S(2)}) copy-start(f32[4,64,512]{2,1,0:T(8,128)} %refs_1_.3) | copy-start | bytes 1572868
  0.6 9.8 %copy-start = (f32[2,4,64,512]{3,2,1,0:T(8,128)S(1)}, f32[2,4,64,512]{3,2,1,0:T(8,128)}, u32[]{:S(2)}) copy-start(f32[2,4,64,512]{3,2,1,0:T(8,128)} %refs_2_.4) | copy-start | bytes 3145732
  0.7 9.8 %copy-start.4 = (s32[64,512]{1,0:T(8,128)S(1)}, s32[64,512]{1,0:T(8,128)}, u32[]{:S(2)}) copy-start(s32[64,512]{1,0:T(8,128)} %refs_3_.6) | copy-start | bytes 393220
  0.7 9.8 %copy-start.1 = (bf16[16,64,512]{2,1,0:T(8,128)(2,1)S(1)}, bf16[16,64,512]{2,1,0:T(8,128)(2,1)}, u32[]{:S(2)}) copy-start(bf16[16,64,512]{2,1,0:T(8,128)(2,1)} %refs_4_.4) | copy-start | bytes 3145732
  0.7 9.8 %copy-start.5 = (f32[16,16]{1,0:T(8,128)S(1)}, f32[16,16]{1,0:T(8,128)}, u32[]{:S(2)}) copy-start(f32[16,16]{1,0:T(8,128)} %refs_2_.5) | copy-start | bytes 3076
  0.7 9.6 %copy-start.7 = (s32[16]{0:T(128)S(1)}, s32[16]{0:T(128)}, u32[]{:S(2)}) copy-start(s32[16]{0:T(128)} %refs_0_.3) | copy-start | bytes 196
  3.2 11.2 %collective-permute-start = (bf16[144,512]{1,0:T(8,128)(2,1)}, bf16[144,512]{1,0:T(8,128)(2,1)S(1)}, u32[]{:S(2)}, u32[]{:S(2)}) collective-permute-start(bf16[144,512]{1,0:T(8,128)(2,1)} %get-tuple-element.34), channel_id=1, source_target_pairs={{0,4},{4,8},{8,12},{1,5},{5,9},{9,13},{2,6},{6,10},{10,14},{3,7},{... | collective-permute-start | bytes 442376 | tf_op jit(solution)/shard_map/ppermute | solution.py:675
  8.1 7.4 %collective-permute-start.1 = (bf16[144,512]{1,0:T(8,128)(2,1)}, bf16[144,512]{1,0:T(8,128)(2,1)S(1)}, u32[]{:S(2)}, u32[]{:S(2)}) collective-permute-start(bf16[144,512]{1,0:T(8,128)(2,1)} %get-tuple-element.35), channel_id=1, source_target_pairs={{4,0},{8,4},{12,8},{5,1},{9,5},{13,9},{6,2},{10,6},{14,10},{7,3},{... | collective-permute-start | bytes 442376 | tf_op jit(solution)/shard_map/ppermute | solution.py:675
  10.4 6.9 %copy-start.9 = (bf16[128,256]{1,0:T(8,128)(2,1)S(1)}, bf16[128,256]{1,0:T(8,128)(2,1)}, u32[]{:S(2)}) copy-start(bf16[128,256]{1,0:T(8,128)(2,1)} %refs_3_.7) | copy-start | bytes 196612
  15.8 4.3 %collective-permute-start.2 = (bf16[240,128]{1,0:T(8,128)(2,1)S(1)}, bf16[240,128]{1,0:T(8,128)(2,1)S(1)}, u32[]{:S(2)}, u32[]{:S(2)}) collective-permute-start(bf16[240,128]{1,0:T(8,128)(2,1)S(1)} %rim.1.refs_9_), channel_id=1, source_target_pairs={{0,16},{16,0},{1,17},{17,1},{2,18},{18,2},{3,19},{19,3},{4,20},{20... | collective-permute-start | bytes 184328 | tf_op jit(solution)/shard_map/ppermute | solution.py:670
  30.1 4.3 %collective-permute-start.3 = (f32[32,256]{1,0:T(8,128)S(1)}, f32[32,256]{1,0:T(8,128)S(1)}, u32[]{:S(2)}, u32[]{:S(2)}) collective-permute-start(f32[32,256]{1,0:T(8,128)S(1)} %bitcast.8), channel_id=1, source_target_pairs={{0,16},{16,0},{1,17},{17,1},{2,18},{18,2},{3,19},{19,3},{4,20},{20... | collective-permute-start | bytes 98312 | tf_op jit(solution)/shard_map/ppermute | solution.py:680
  31.7 2.7 %copy-start.2 = (f32[264,512]{1,0:T(8,128)S(1)}, f32[264,512]{1,0:T(8,128)}, u32[]{:S(2)}) copy-start(f32[264,512]{1,0:T(8,128)} %refs_3_.9) | copy-start | bytes 1622020
  31.7 2.7 %copy-start.6 = (f32[512]{0:T(512)S(1)}, f32[512]{0:T(512)}, u32[]{:S(2)}) copy-start(f32[512]{0:T(512)} %param.19) | copy-start | bytes 6148
  31.7 2.8 %copy-start.8 = (f32[16]{0:T(128)S(1)}, f32[16]{0:T(128)}, u32[]{:S(2)}) copy-start(f32[16]{0:T(128)} %param.21) | copy-start | bytes 196
  36.4 1.7 %collective-permute-start.4 = (f32[64,256]{1,0:T(8,128)S(1)}, f32[64,256]{1,0:T(8,128)S(1)}, u32[]{:S(2)}, u32[]{:S(2)}) collective-permute-start(f32[64,256]{1,0:T(8,128)S(1)} %get-tuple-element.57), channel_id=1, source_target_pairs={{0,1},{1,0},{2,3},{3,2},{4,5},{5,4},{6,7},{7,6},{8,9},{9,8},{10,11... | collective-permute-start | bytes 196616 | tf_op jit(solution)/shard_map/ppermute | solution.py:680
  36.5 5.2 %collective-permute-start.10 = (f16[32,256]{1,0:T(8,128)(2,1)S(1)}, f16[32,256]{1,0:T(8,128)(2,1)S(1)}, u32[]{:S(2)}, u32[]{:S(2)}) collective-permute-start(f16[32,256]{1,0:T(8,128)(2,1)S(1)} %multiply_convert_fusion), channel_id=1, source_target_pairs={{0,2},{1,3},{2,0},{3,1},{4,6},{5,7},{6,4},{7,5},{8,10},{9,11},{10,... | collective-permute-start | bytes 49160 | tf_op jit(solution)/shard_map/ppermute | solution.py:680
  38.1 4.3 %collective-permute-start.5 = (f32[64,256]{1,0:T(8,128)S(1)}, f32[64,256]{1,0:T(8,128)S(1)}, u32[]{:S(2)}, u32[]{:S(2)}) collective-permute-start(f32[64,256]{1,0:T(8,128)S(1)} %add.21), channel_id=1, source_target_pairs={{0,16},{16,0},{1,17},{17,1},{2,18},{18,2},{3,19},{19,3},{4,20},{20... | collective-permute-start | bytes 196616 | tf_op jit(solution)/shard_map/ppermute | solution.py:680
  39.4 5.7 %collective-permute-start.6 = (f32[64,256]{1,0:T(8,128)S(1)}, f32[64,256]{1,0:T(8,128)S(1)}, u32[]{:S(2)}, u32[]{:S(2)}) collective-permute-start(f32[64,256]{1,0:T(8,128)S(1)} %add.21), channel_id=1, source_target_pairs={{0,2},{1,3},{2,0},{3,1},{4,6},{5,7},{6,4},{7,5},{8,10},{9,11},{10,... | collective-permute-start | bytes 196616 | tf_op jit(solution)/shard_map/ppermute | solution.py:680
  40.5 5.2 %collective-permute-start.7 = (f32[64,256]{1,0:T(8,128)S(1)}, f32[64,256]{1,0:T(8,128)S(1)}, u32[]{:S(2)}, u32[]{:S(2)}) collective-permute-start(f32[64,256]{1,0:T(8,128)S(1)} %add.21), channel_id=1, source_target_pairs={{0,18},{1,19},{2,16},{3,17},{16,2},{17,3},{18,0},{19,1},{4,22},{5,... | collective-permute-start | bytes 196616 | tf_op jit(solution)/shard_map/ppermute | solution.py:853
  42.5 5.9 %collective-permute-start.11 = (f16[64,256]{1,0:T(8,128)(2,1)S(1)}, f16[64,256]{1,0:T(8,128)(2,1)S(1)}, u32[]{:S(2)}, u32[]{:S(2)}) collective-permute-start(f16[64,256]{1,0:T(8,128)(2,1)S(1)} %pad_maximum_fusion.2), channel_id=1, source_target_pairs={{0,8},{4,12},{8,0},{12,4},{1,9},{5,13},{9,1},{13,5},{2,10},{6,14},... | collective-permute-start | bytes 98312 | tf_op jit(solution)/shard_map/ppermute | solution.py:680
  45.7 5.2 %collective-permute-start.8 = (f32[64,256]{1,0:T(8,128)S(1)}, f32[64,256]{1,0:T(8,128)S(1)}, u32[]{:S(2)}, u32[]{:S(2)}) collective-permute-start(f32[64,256]{1,0:T(8,128)S(1)} %add_add_fusion), channel_id=1, source_target_pairs={{0,8},{4,12},{8,0},{12,4},{1,9},{5,13},{9,1},{13,5},{2,10},{6,14},... | collective-permute-start | bytes 196616 | tf_op jit(solution)/shard_map/ppermute | solution.py:680
  48.4 4.3 %collective-permute-start.12 = (f16[128,256]{1,0:T(8,128)(2,1)S(1)}, f16[128,256]{1,0:T(8,128)(2,1)S(1)}, u32[]{:S(2)}, u32[]{:S(2)}) collective-permute-start(f16[128,256]{1,0:T(8,128)(2,1)S(1)} %pad_maximum_fusion.1), channel_id=1, source_target_pairs={{0,4},{4,0},{8,12},{12,8},{1,5},{5,1},{9,13},{13,9},{2,6},{6,2},{1... | collective-permute-start | bytes 196616 | tf_op jit(solution)/shard_map/ppermute | solution.py:680
  52.7 1.7 %collective-permute-start.13 = (f16[256,256]{1,0:T(8,128)(2,1)S(1)}, f16[256,256]{1,0:T(8,128)(2,1)S(1)}, u32[]{:S(2)}, u32[]{:S(2)}) collective-permute-start(f16[256,256]{1,0:T(8,128)(2,1)S(1)} %pad_maximum_fusion), channel_id=1, source_target_pairs={{0,1},{1,0},{2,3},{3,2},{4,5},{5,4},{6,7},{7,6},{8,9},{9,8},{10,11... | collective-permute-start | bytes 393224 | tf_op jit(solution)/shard_map/ppermute | solution.py:680
  52.8 4.5 %collective-permute-start.9 = (f32[64,256]{1,0:T(8,128)S(1)}, f32[64,256]{1,0:T(8,128)S(1)}, u32[]{:S(2)}, u32[]{:S(2)}) collective-permute-start(f32[64,256]{1,0:T(8,128)S(1)} %add.25), channel_id=1, source_target_pairs={{0,4},{4,0},{8,12},{12,8},{1,5},{5,1},{9,13},{13,9},{2,6},{6,2},{1... | collective-permute-start | bytes 196616 | tf_op jit(solution)/shard_map/ppermute | solution.py:680
  57.3 1.3 %collective-permute-start.14 = (f32[64,256]{1,0:T(8,128)S(1)}, f32[64,256]{1,0:T(8,128)S(1)}, u32[]{:S(2)}, u32[]{:S(2)}) collective-permute-start(f32[64,256]{1,0:T(8,128)S(1)} %add.27.refs_0_), channel_id=1, source_target_pairs={{0,1},{1,0},{2,3},{3,2},{4,5},{5,4},{6,7},{7,6},{8,9},{9,8},{10,11... | collective-permute-start | bytes 196616 | tf_op jit(solution)/shard_map/ppermute | solution.py:680

commit v5 on v4

--- a/solution.py
+++ b/solution.py
@@ -52,11 +52,8 @@
 
 
 def moved(value, matrix):
-    high = value.astype(BF16)
-    rest = (value - high.astype(F32)).astype(BF16)
-    return jnp.dot(high, matrix, preferred_element_type=F32) + jnp.dot(
-        rest, matrix, preferred_element_type=F32
-    )
+    both = jnp.dot(jnp.concatenate(split(value), axis=0), matrix, preferred_element_type=F32)
+    return both[: value.shape[0]] + both[value.shape[0] :]
 
 
 def by_segment(pieces, segment):
@@ -226,15 +223,48 @@
 
 
 def prepare_kernel(
-    members, rows, cols, lat_count, south, north, planes, weight, state, force, ends, hu, hv, hvu, cu, cv, w_planes, depth, w_rows
+    members,
+    rows,
+    cols,
+    lat_count,
+    south,
+    north,
+    planes,
+    weight,
+    ids_col,
+    props,
+    w_in,
+    b_in,
+    w_out,
+    state,
+    force,
+    ends,
+    hu,
+    hv,
+    hvu,
+    cu,
+    cv,
+    cv_up,
+    w_planes,
+    low_in,
+    params,
+    low_own,
+    upper_own,
+    w_sum,
+    out_cat,
+    depth,
+    w_rows,
 ):
+    member_terms(
+        members, ids_col, props, w_in, b_in, w_out, low_in, params, low_own, upper_own, w_sum, out_cat
+    )
     patches = cols // PW
     height = rows + 2 * PAD
     wide = rows + 2 * HALO
     edge_rows = (slice(0, HALO), slice(height - HALO, height))
     homes = (state.at[0], state.at[1], state.at[2], force, depth)
     for i, home in enumerate(homes):
-        home[:, PAD : PAD + rows, :] = planes[i]
+        home[0:PW, PAD : PAD + rows, :] = planes[i]
         if i != 3:
             for p in range(PW):
                 for rs in edge_rows:
@@ -252,13 +282,15 @@
     total = lat_count * rows
     cu[span, :] = jnp.where(inside, 0.25 * (CORI_BASE + CORI_SLOPE * (place + 0.5) / total), 0.0)
     cv[span, :] = jnp.where(inside, 0.25 * (CORI_BASE + CORI_SLOPE * place / total), 0.0)
+    above = (row >= -1) & (row < total - 1)
+    cv_up[span, :] = jnp.where(above, 0.25 * (CORI_BASE + CORI_SLOPE * (place + 1) / total), 0.0)
     for p in range(PW):
         here = depth[p, span, :]
         if p > 0:
             hu[p, span, :] = HALF_DEPTH * (here + depth[p - 1, span, :])
         vertical(depth.at[p], hv.at[p], hvu.at[p], inside, rows)
-    ends[0] = depth[0]
-    ends[1] = depth[PW - 1]
+    ends[0] = depth[0, 0:height]
+    ends[1] = depth[PW - 1, 0:height]
     for h in range(w_rows.shape[0]):
         cs = slice(h * LANES, (h + 1) * LANES)
         w_rows[h] = weight[:, cs].astype(F32)
@@ -308,85 +340,71 @@
                 vel[i - 1, m] = part * GRAVITY
 
 
-def flow_step(src, src_rim, dst, dst_rim, force, force_rim, hus, hvs, hvus, cu, cv, last_mask, rows, patches):
+def flow_step(src, src_rim, dst, dst_rim, force, force_rim, hus, hvs, hvus, cu, cv, cv_up, last_mask, rows, patches):
     strip = PW
-    end = PAD + rows + HALO
-    half = (rows + 2 * HALO) // 2
+    wide = rows + 2 * HALO
+    start = PAD - HALO
     keep = 1.0 - DRAG_RATE
-    for r0 in range(PAD - HALO, end, half):
-        here, up, down = pl.ds(r0, half), pl.ds(r0 + 1, half), pl.ds(r0 - 1, half)
-        last = lane_ids(half) % patches == patches - 1
-
-        def wrap_left(plane, rim):
-            return pltpu.roll(jnp.where(last, rim, plane), 1, 1)
-
-        def wrap_right(plane, rim):
-            return jnp.where(last, pltpu.roll(rim, PW - 1, 1), pltpu.roll(plane, LANES - 1, 1))
-
-        def of(planes, rim, i, p):
-            return rim.at[i] if p == strip else planes.at[i, p]
-
-        def new_level(p, fx, fx_right):
-            n_up = of(src, src_rim, 2, p)[up, :]
-            n = of(src, src_rim, 2, p)[here, :]
-            fy = hvus[p][here, :] * n_up - hvs[p][here, :] * n
-            level = of(src, src_rim, 0, p)[here, :] - ((fx_right - fx) + fy)
-            of(dst, dst_rim, 0, p)[here, :] = level
-            return level, n, n + n_up
-
-        def new_flow(p, e, e_right, em, em_right, n, v, level, level_left):
-            u = (e + e_right) + (em + em_right)
-            push = force_rim[here, :] if p == strip else force[p, here, :]
-            of(dst, dst_rim, 1, p)[here, :] = (
-                keep * e + cu[here, :] * v - (level - level_left) + push
-            )
-            level_down = of(dst, dst_rim, 0, p)[down, :]
-            north = keep * n - cv[here, :] * u - (level - level_down)
-            home = of(dst, dst_rim, 2, p)
-            if r0 + half == end:
-                home[pl.ds(r0, half - HALO), :] = north[: half - HALO]
-                home[pl.ds(end - HALO, HALO), :] = north[half - HALO :] * last_mask
-            else:
-                home[here, :] = north
-
-        e_rim = src_rim[1, here, :]
-        em_rim = src_rim[1, down, :]
-        fx_rim = hus[strip][here, :] * e_rim
-        level_rim, n_rim, vs_rim = new_level(strip, fx_rim, pltpu.roll(fx_rim, LANES - 1, 1))
-        new_flow(
-            strip,
-            e_rim,
-            pltpu.roll(e_rim, LANES - 1, 1),
-            em_rim,
-            pltpu.roll(em_rim, LANES - 1, 1),
-            n_rim,
-            vs_rim + pltpu.roll(vs_rim, 1, 1),
-            level_rim,
-            pltpu.roll(level_rim, 1, 1),
-        )
-        e_end = wrap_right(src[1, 0, here, :], e_rim)
-        em_end = wrap_right(src[1, 0, down, :], em_rim)
-        e_last = src[1, PW - 1, here, :]
-        level_last, n_last, vs_last = new_level(
-            PW - 1, hus[PW - 1][here, :] * e_last, hus[PW + 1][here, :] * e_end
-        )
-        level_left = wrap_left(level_last, level_rim)
-        vs_left = wrap_left(vs_last, vs_rim)
-        e = src[1, 0, here, :]
-        em = src[1, 0, down, :]
-        fx = hus[0][here, :] * e
-        for p in range(PW):
-            if p < PW - 1:
-                e_right = src[1, p + 1, here, :]
-                em_right = src[1, p + 1, down, :]
-                fx_right = hus[p + 1][here, :] * e_right
-                level, n, vs = new_level(p, fx, fx_right)
-            else:
-                e_right, em_right, fx_right = e_end, em_end, None
-                level, n, vs = level_last, n_last, vs_last
-            new_flow(p, e, e_right, em, em_right, n, vs + vs_left, level, level_left)
-            level_left, vs_left, e, em, fx = level, vs, e_right, em_right, fx_right
-            yield
+    here = pl.ds(start, wide)
+    last = lane_ids(wide) % patches == patches - 1
+
+    def wrap_left(plane, rim):
+        return pltpu.roll(jnp.where(last, rim, plane), 1, 1)
+
+    def wrap_right(plane, rim):
+        return jnp.where(last, pltpu.roll(rim, PW - 1, 1), pltpu.roll(plane, LANES - 1, 1))
+
+    def of(planes, rim, i, p):
+        return rim.at[i] if p == strip else planes.at[i, p]
+
+    def new_level(p, fx, fx_right):
+        n = of(src, src_rim, 2, p)[here, :]
+        n_up = pltpu.roll(n, wide - 1, 0)
+        fy = hvus[p][here, :] * n_up - hvs[p][here, :] * n
+        level = of(src, src_rim, 0, p)[here, :] - ((fx_right - fx) + fy)
+        of(dst, dst_rim, 0, p)[here, :] = level
+        return level, n, n + n_up
+
+    def new_flow(p, e, e_right, n, v, level, level_left):
+        u = e + e_right
+        push = force_rim[here, :] if p == strip else force[p, here, :]
+        of(dst, dst_rim, 1, p)[here, :] = keep * e + cu[here, :] * v - (level - level_left) + push
+        below = pltpu.roll(level - cv_up[here, :] * u, 1, 0)
+        north = keep * n - cv[here, :] * u - level + below
+        home = of(dst, dst_rim, 2, p)
+        home[pl.ds(start, wide - HALO), :] = north[: wide - HALO]
+        home[pl.ds(start + wide - HALO, HALO), :] = north[wide - HALO :] * last_mask
+
+    e_rim = src_rim[1, here, :]
+    fx_rim = hus[strip][here, :] * e_rim
+    level_rim, n_rim, vs_rim = new_level(strip, fx_rim, pltpu.roll(fx_rim, LANES - 1, 1))
+    new_flow(
+        strip,
+        e_rim,
+        pltpu.roll(e_rim, LANES - 1, 1),
+        n_rim,
+        vs_rim + pltpu.roll(vs_rim, 1, 1),
+        level_rim,
+        pltpu.roll(level_rim, 1, 1),
+    )
+    e = src[1, 0, here, :]
+    e_end = wrap_right(e, e_rim)
+    level_last, n_last, vs_last = new_level(
+        PW - 1, hus[PW - 1][here, :] * src[1, PW - 1, here, :], hus[PW + 1][here, :] * e_end
+    )
+    level_left = wrap_left(level_last, level_rim)
+    vs_left = wrap_left(vs_last, vs_rim)
+    fx = hus[0][here, :] * e
+    for p in range(PW):
+        if p < PW - 1:
+            e_right = src[1, p + 1, here, :]
+            fx_right = hus[p + 1][here, :] * e_right
+            level, n, vs = new_level(p, fx, fx_right)
+        else:
+            e_right, fx_right = e_end, None
+            level, n, vs = level_last, n_last, vs_last
+        new_flow(p, e, e_right, n, vs + vs_left, level, level_left)
+        level_left, vs_left, e, fx = level, vs, e_right, fx_right
 
 
 def flow_kernel(
@@ -402,6 +420,7 @@
     hvu,
     cu,
     cv,
+    cv_up,
     w_planes,
     side,
     east,
@@ -426,14 +445,9 @@
     height = rows + 2 * PAD
     wide = rows + 2 * HALO
     span = slice(PAD - HALO, PAD + rows + HALO)
-    state_a[...] = state[...]
+    state_a[:, :, span, :] = state[:, :, span, :]
     for rs in (slice(0, HALO), slice(height - HALO, height)):
         depth_rim[rs, :] = jnp.zeros((HALO, LANES), F32)
-        for i in range(3):
-            rim_a[i, rs, :] = jnp.zeros((HALO, LANES), F32)
-            rim_b[i, rs, :] = jnp.zeros((HALO, LANES), F32)
-            for p in range(PW):
-                state_b[i, p, rs, :] = jnp.zeros((HALO, LANES), F32)
     rim_homes = (rim_a.at[0], rim_a.at[1], rim_a.at[2], force_rim, depth_rim)
     for n in range(3):
         rs = slice(n * wide, (n + 1) * wide)
@@ -464,7 +478,7 @@
         step = 2 * turn + sub
         total = None
         for b in range(count):
-            cells = state[0, :, PAD + b * PH : PAD + (b + 1) * PH, :].reshape(PW * PH, LANES)
+            cells = state[0, 0:PW, PAD + b * PH : PAD + (b + 1) * PH, :].reshape(PW * PH, LANES)
             cells_t = cells.T.astype(BF16)
             act = jnp.tanh(jnp.dot(cells_t, w_planes[...], preferred_element_type=F32))
             total = act if total is None else total + act
@@ -474,39 +488,29 @@
                 to = slice(b * patches, (b + 1) * patches)
                 patch_t[m, to, :] = cells_t[rs]
                 slope[m, to, :] = fall[rs]
-            yield
         sums = jnp.sum(total.reshape(members, patches, total.shape[1]), axis=1)
         partial[turn, sub * members : (sub + 1) * members, :] = sums
         for m in range(members):
             gram[step * members + m] = lax.dot_general(
                 patch_t[m], slope[m], (((0,), (0,)), ((), ())), preferred_element_type=F32
             )
-            yield
-
-    def beside(flow, embed):
-        for n, _ in enumerate(flow):
-            if n % 3 == 2:
-                next(embed, None)
-        for _ in embed:
-            pass
 
     def step_of(src, src_rim, dst, dst_rim):
-        return flow_step(
-            src, src_rim, dst, dst_rim, force, force_rim, hus, hvs, hvus, cu, cv, last_mask, rows, patches
+        flow_step(
+            src, src_rim, dst, dst_rim, force, force_rim, hus, hvs, hvus, cu, cv, cv_up, last_mask, rows, patches
         )
 
     def two_steps(turn, carry):
-        beside(
-            step_of(state_a, rim_a, state_b, rim_b),
-            embed_step(state_a, jnp.maximum(turn - 1, 0), 1),
-        )
-        beside(step_of(state_b, rim_b, state_a, rim_a), embed_step(state_b, turn, 0))
+        step_of(state_a, rim_a, state_b, rim_b)
+        embed_step(state_a, jnp.maximum(turn - 1, 0), 1)
+        step_of(state_b, rim_b, state_a, rim_a)
+        embed_step(state_b, turn, 0)
         return carry
 
     lax.fori_loop(0, STEPS // 2, two_steps, 0)
-    final[...] = state_a[...]
-    for _ in embed_step(state_a, STEPS // 2 - 1, 1):
-        pass
+    inner = slice(PAD, PAD + rows)
+    final[:, :, inner, :] = state_a[:, :, inner, :]
+    embed_step(state_a, STEPS // 2 - 1, 1)
 
 
 def split(value):
@@ -522,44 +526,54 @@
     return dot(a[0], b[0], ca, cb) + (dot(a[0], b[1], ca, cb) + dot(a[1], b[0], ca, cb))
 
 
-def member_params(ids_col, props):
+def member_terms(
+    members, ids_col, props, w_in, b_in, w_out, low_in, ends, low_own, upper_own, w_sum, out_cat
+):
     count = props.shape[0]
+    half = props.shape[1] // 2
     hot = jnp.where(ids_col[...] == lax.broadcasted_iota(jnp.int32, (count, count), 1), 1.0, 0.0)
-    return jnp.dot(hot, props[...], precision=PRECISE, preferred_element_type=F32)
+    params = jnp.dot(hot, props[...], precision=PRECISE, preferred_element_type=F32)
+    low = mm(split(params[:, :half]), split(w_in[:half, :])) + b_in[...]
+    ends[...] = params
+    low_in[...] = low
+    samples = low_own.shape[0]
+    slot = lax.broadcasted_iota(jnp.int32, (samples, count), 1)
+    row = lax.broadcasted_iota(jnp.int32, (samples, count), 0)
+    hot = jnp.where(slot == lax.axis_index("grp") * members + row % members, 1.0, 0.0)
+    low_own[...] = jnp.dot(hot, low, precision=PRECISE, preferred_element_type=F32)
+    upper_own[...] = jnp.dot(hot, params[:, half:], precision=PRECISE, preferred_element_type=F32)
+    high, rest = split(w_in[half:, :])
+    w_sum[0] = high
+    w_sum[1] = rest
+    high, rest = split(w_out[...].T)
+    out_cat[...] = jnp.concatenate([high, high, rest], axis=1)
 
 
 def repeated(rows, count):
     return jnp.concatenate([rows] * count, axis=0)
 
 
-def flow_grads(lower_in, upper, summary, w_in, w_out, b_out):
+def flow_grads(lower_in, upper, summary, w_sum, out_cat, b_out):
     half = upper.shape[1]
     width = 2 * half
     sums = split(summary)
-    w_sum = split(w_in[half:, :])
     hidden = jnp.tanh(mm(sums, w_sum) + lower_in)
     hid = split(hidden)
-    out_w = split(w_out[...])
-    both = dot(hid[0], jnp.concatenate(out_w, axis=1))
-    raw = both[:, :width] + both[:, width:] + dot(hid[1], out_w[0]) + b_out[...]
+    both = dot(hid[0], out_cat[:, width:])
+    raw = both[:, :width] + both[:, width:] + dot(hid[1], out_cat[:, :width]) + b_out[...]
     log_scale = jnp.tanh(raw[:, :half])
     grown = upper * jnp.exp(log_scale)
     latent = grown + raw[:, half:]
     d_scale = (latent * grown - 1.0) * (1.0 - log_scale * log_scale)
     d_raw = jnp.concatenate([d_scale, latent], axis=1)
     d_r = split(d_raw)
-    d_hidden = dot(
-        jnp.concatenate([d_r[0], d_r[1], d_r[0]], axis=1),
-        jnp.concatenate([out_w[0], out_w[0], out_w[1]], axis=1),
-        1,
-        1,
-    )
+    d_hidden = dot(jnp.concatenate([d_r[0], d_r[1], d_r[0]], axis=1), out_cat[...], 1, 1)
     d_hidden = d_hidden * (1.0 - hidden * hidden)
-    return sums, hid, d_raw, d_r, d_hidden, w_sum
+    return sums, hid, d_raw, d_r, d_hidden
 
 
 def local_kernel(
-    members, inv_root, mine, theirs, ids, props, w_in, b_in, w_out, b_out, gram, kept, sent, own, total
+    inv_root, mine, theirs, low_in, upper, w_sum, out_cat, b_out, gram, kept, sent, own, total
 ):
     sums = (mine[...] + theirs[...]) * inv_root
     count = sums.shape[0]
@@ -570,17 +584,9 @@
         def _():
             own[...] = sums[part * items : (part + 1) * items, :]
 
-    params = member_params(ids, props)
-    half = params.shape[1] // 2
-    low = split(params[:, :half])
-    low_in = mm(low, split(w_in[:half, :])) + b_in[...]
-    slot = lax.broadcasted_iota(jnp.int32, (count, params.shape[0]), 1)
-    row = lax.broadcasted_iota(jnp.int32, (count, params.shape[0]), 0)
-    hot = jnp.where(slot == lax.axis_index("grp") * members + row % members, 1.0, 0.0)
-    low_in = jnp.dot(hot, low_in, precision=PRECISE, preferred_element_type=F32)
-    upper = jnp.dot(hot, params[:, half:], precision=PRECISE, preferred_element_type=F32)
-    _, _, _, _, d_hidden, w_sum = flow_grads(low_in, upper, sums, w_in, w_out, b_out)
-    d_summary = mm(split(d_hidden), w_sum, 1, 1) * inv_root
+    w_pair = (w_sum[0], w_sum[1])
+    d_hidden = flow_grads(low_in[...], upper[...], sums, w_pair, out_cat, b_out)[-1]
+    d_summary = mm(split(d_hidden), w_pair, 1, 1) * inv_root
     acc = gram[0] * d_summary[0:1, :]
     for i in range(1, count):
         acc = acc + gram[i] * d_summary[i : i + 1, :]
@@ -592,7 +598,7 @@
 
 
 def couple_kernel(
-    members, lat_count, grp_count, order, summary, ids, props, w_in, b_in, w_out, b_out, rows, square, sorted_sums, staged
+    members, lat_count, grp_count, order, summary, low_in, ends, w_sum, out_cat, b_out, rows, square, sorted_sums, staged
 ):
     per = summary.shape[0] // len(order)
     for index, (lat_flip, grp_flip) in enumerate(order):
@@ -600,17 +606,21 @@
         sorted_sums[pl.ds(pl.multiple_of(block * per, per), per), :] = summary[
             index * per : (index + 1) * per, :
         ]
-    params = member_params(ids, props)
+    params = ends[...]
     half = params.shape[1] // 2
-    low_in = mm(split(params[:, :half]), split(w_in[:half, :])) + b_in[...]
     groups = [slice(g * members, (g + 1) * members) for g in range(grp_count)]
     steps = per // members
     spread = lambda value: jnp.concatenate(
         [repeated(value[rs], steps) for rs in groups] * lat_count, axis=0
     )
     lower = spread(params[:, :half])
-    sums, hid, d_raw, d_r, d_hidden, _ = flow_grads(
-        spread(low_in), spread(params[:, half:]), sorted_sums[...], w_in, w_out, b_out
+    sums, hid, d_raw, d_r, d_hidden = flow_grads(
+        spread(low_in[...]),
+        spread(params[:, half:]),
+        sorted_sums[...],
+        (w_sum[0], w_sum[1]),
+        out_cat,
+        b_out,
     )
     low = split(lower)
     context = [jnp.concatenate([sums[n], low[n]], axis=1) for n in range(2)]
@@ -756,7 +766,11 @@
     west = neighbour(rim, "lon", 1)
     east = west if lon_count == 2 else neighbour(rim, "lon", -1)
 
-    plane = (PW, height, LANES)
+    def after(value, *others):
+        return lax.optimization_barrier((value,) + others)[0]
+
+    b_out = couple_out_bias.reshape(1, -1)
+    plane = (PW, height + HALO, LANES)
     prepared = pl.pallas_call(
         lambda *refs: prepare_kernel(members, rows, cols, lat_count, *refs),
         out_shape=(
@@ -768,10 +782,17 @@
             shape(*plane),
             shape(height, LANES),
             shape(height, LANES),
+            shape(height, LANES),
             shape(cells, feats, dtype=BF16),
+            shape(proposals.shape[0], hid),
+            shape(*proposals.shape),
+            shape(samples, hid),
+            shape(samples, width // 2),
+            shape(2, feats, hid, dtype=BF16),
+            shape(hid, 3 * width, dtype=BF16),
         ),
-        in_specs=[vmem()] * 4,
-        out_specs=(vmem(),) * 9,
+        in_specs=[vmem()] * 9,
+        out_specs=(vmem(),) * 16,
         scratch_shapes=[
             pltpu.VMEM(plane, F32),
             pltpu.VMEM((feats // LANES, cells, LANES), F32),
@@ -779,7 +800,18 @@
         compiler_params=params_of(16),
         cost_estimate=pl.CostEstimate(flops=10**9, bytes_accessed=4 * MEBI, transcendentals=0),
         name="prepare",
-    )(south, north, planes, conv_weight)
+    )(
+        south,
+        north,
+        planes,
+        conv_weight,
+        member_ids.reshape(-1, 1),
+        proposals,
+        couple_in,
+        couple_in_bias.reshape(1, -1),
+        couple_out.T,
+    )
+    prepared, (low_in, ends, low_own, upper_own, w_sum, out_cat) = prepared[:10], prepared[10:]
 
     partial, gram, final = pl.pallas_call(
         lambda *refs: flow_kernel(members, rows, cols, lat_count, *refs),
@@ -788,7 +820,7 @@
             shape(samples, cells, feats),
             shape(3, *plane),
         ),
-        in_specs=[vmem()] * 12,
+        in_specs=[vmem()] * 13,
         out_specs=(vmem(),) * 3,
         scratch_shapes=[
             pltpu.VMEM((3, *plane), F32),
@@ -825,22 +857,16 @@
     others, surface_out, velocity_out = lax.optimization_barrier((others, surface_out, velocity_out))
     summaries = (partial + others) * inv_root
 
-    ids_col = member_ids.reshape(-1, 1)
-    b_in = couple_in_bias.reshape(1, -1)
-    b_out = couple_out_bias.reshape(1, -1)
     items = samples // lon_count
     kept, sent, own = pl.pallas_call(
-        lambda *refs: local_kernel(members, inv_root, *refs),
+        lambda *refs: local_kernel(inv_root, *refs),
         out_shape=(shape(cells // 2, feats), shape(cells // 2, feats), shape(items, feats)),
-        in_specs=[vmem()] * 9,
+        in_specs=[vmem()] * 8,
         out_specs=(vmem(),) * 3,
         scratch_shapes=[pltpu.VMEM((cells, feats), F32)],
         compiler_params=params_of(16),
         name="local_loss",
-    )(partial, others, ids_col, proposals, couple_in, b_in, couple_out, b_out, gram)
-
-    def after(value, *others):
-        return lax.optimization_barrier((value,) + others)[0]
+    )(partial, others, low_own, upper_own, w_sum, out_cat, b_out, gram)
 
     def gather(axis, flip):
         both = jnp.concatenate([gathered, swapped(gathered, axis, flip)], axis=0)
@@ -857,7 +883,7 @@
         )
         by_lon = swapped(conv, "lon", 1)
         gathered = after(gathered, by_lon)
-        conv = (conv + by_lon) + (swapped(conv, "grp", 2) + corner)
+        conv = (conv + corner) + (swapped(conv, "grp", 2) + by_lon)
     else:
         conv = conv + swapped(conv, "grp", 2)
         for flip in flips("lon"):
@@ -878,7 +904,7 @@
     couple, square = pl.pallas_call(
         lambda *refs: couple_kernel(members, lat_count, grp_count, order, *refs),
         out_shape=(shape(low_rows, LANES), shape(1, LANES)),
-        in_specs=[vmem()] * 7,
+        in_specs=[vmem()] * 6,
         out_specs=(vmem(), vmem()),
         scratch_shapes=[
             pltpu.VMEM((len(order) * samples, feats), F32),
@@ -887,7 +913,7 @@
         compiler_params=params_of(24),
         cost_estimate=pl.CostEstimate(flops=3 * 10**9, bytes_accessed=3 * MEBI, transcendentals=0),
         name="couple_grads",
-    )(gathered.astype(F32), ids_col, proposals, couple_in, b_in, couple_out, b_out)
+    )(gathered.astype(F32), low_in, ends, w_sum, out_cat, b_out)
 
     conv = conv + after(by_lat, couple, square)
     conv_other = swapped(conv, "grp", 1)

time: 60 us -> 58.3 us (0.972)
  waiting for transfers between devices: 8.29 us -> 10.9 us
  starting transfers between devices: 23.1 us -> 21.2 us
  Pallas kernels: 26.3 us -> 24.8 us
  local copies, waits for them, and re-layouts: 1.01 us -> 0.14 us
    ppermute x11, waiting for transfers between devices: 4.98 us -> 7.01 us  [swapped(): return lax.ppermute(value, axis, [(i, i ^ flip) for i in range(count)])]
    ppermute x11, starting transfers between devices: 14.2 us -> 12.4 us  [swapped(): return lax.ppermute(value, axis, [(i, i ^ flip) for i in range(count)])]
    pallas_call x1, Pallas kernels: 10.1 us -> 8.94 us  [shards(): pl.pallas_call(lambda *refs: flow_kernel(members, rows, cols, lat_count,...]
    ppermute x2, waiting for transfers between devices: 1.12 us -> 2.05 us  [from_lat(): lax.ppermute(value, 'lat', [(i, i + step) for i in range(count) if 0 <= i...]
    unnamed x21 -> x22, local copies, waits for them, and re-layouts: 0.92 us -> 0.05 us
  transfers between devices with their start and end apart: 15 -> 15, of which waited for: 8 -> 9; matrix products, arithmetic and copies ran while one was open for 2% -> 0% of each run, Pallas kernels for 18% -> 18%
where the time goes in v5:
time: 58.3 us; the launch traced here: 58.1 us
  Pallas kernels  24.8 us (43%)
  starting transfers between devices  21.2 us (36%)
  waiting for transfers between devices  10.9 us (19%)
  between operations  0.88 us (2%)
    ppermute x11, starting transfers between devices, swapped(): return lax.ppermute(value, axis, [(i, i ^ flip) for i in range(count)])  12.4 us
    pallas_call x1, Pallas kernels, shards(): pl.pallas_call(lambda *refs: flow_kernel(members, rows, cols, lat_count,...  8.94 us
    ppermute x11, waiting for transfers between devices, swapped(): return lax.ppermute(value, axis, [(i, i ^ flip) for i in range(count)])  7.01 us
    ppermute x2, starting transfers between devices, from_lat(): lax.ppermute(value, 'lat', [(i, i + step) for i in range(count) if 0 <= i...  6.23 us
    pallas_call x1, Pallas kernels, shards(): pl.pallas_call(lambda *refs: planar_kernel(members, *refs), out_shape=(sh...  3.88 us
    pallas_call x1, Pallas kernels, shards(): pl.pallas_call(lambda *refs: back_kernel(members, *refs), out_shape=(shap...  2.61 us
    pallas_call x1, Pallas kernels, shards(): pl.pallas_call(lambda *refs: pack_kernel(members, *refs), out_shape=(shap...  2.47 us
    pallas_call x1, Pallas kernels, shards(): pl.pallas_call(lambda *refs: couple_kernel(members, lat_count, grp_count,...  2.43 us
  transfers between devices with their start and end apart: 15, of which 9 were waited for; matrix products, arithmetic and copies ran while one was open for 0% of the time, Pallas kernels for 18%

profile of v5, /device:TPU:0, one launch (start us, length us, event | category | flops | bytes accessed | tf_op | source)
XLA Modules:
  0.0 58.1 jit_solution(7045017833366004328)
XLA Ops:
  0.7 2.5 %pack_rows.1 = (bf16[144,512]{1,0:T(8,128)(2,1)}, bf16[144,512]{1,0:T(8,128)(2,1)}) custom-call(s32[16]{0:T(128)} %refs_0_.3, f32[4,64,512]{2,1,0:T(8,128)} %refs_1_.3, f32[2,4,64,512]{3,2,1,0:T(8,128)} %refs_2_.3, s32[64,512]{1,0:T(8,128)} %refs_3_.4, bf16[16,64,512]{2,1,0:T(8,128)(2,1)} %refs_4_.3, f32[16,16]{1,0:T(8,128)} %refs_5_.5), custom_call_target="tpu_custom_call" | custom-call | tf_op jit(solution)/shard_map/pack_rows/pallas_call | solution.py:727
  3.2 4.9 %collective-permute-start = (bf16[144,512]{1,0:T(8,128)(2,1)}, bf16[144,512]{1,0:T(8,128)(2,1)S(1)}, u32[]{:S(2)}, u32[]{:S(2)}) collective-permute-start(bf16[144,512]{1,0:T(8,128)(2,1)} %get-tuple-element.41), channel_id=1, source_target_pairs={{0,4},{4,8},{8,12},{1,5},{5,9},{9,13},{2,6},{6,10},{10,14},{3,7},{... | collective-permute-start | bytes 442376 | tf_op jit(solution)/shard_map/ppermute | solution.py:685
  8.1 1.3 %collective-permute-start.1 = (bf16[144,512]{1,0:T(8,128)(2,1)}, bf16[144,512]{1,0:T(8,128)(2,1)S(1)}, u32[]{:S(2)}, u32[]{:S(2)}) collective-permute-start(bf16[144,512]{1,0:T(8,128)(2,1)} %get-tuple-element.42), channel_id=1, source_target_pairs={{4,0},{8,4},{12,8},{5,1},{9,5},{13,9},{6,2},{10,6},{14,10},{7,3},{... | collective-permute-start | bytes 442376 | tf_op jit(solution)/shard_map/ppermute | solution.py:685
  9.4 0.0 copy-done.5
  9.4 0.1 copy.15.refs_4_
  9.5 0.0 copy-done.1
  9.5 0.0 copy-start.7
  9.6 0.0 copy-start.8
  9.6 0.0 copy-start.9
  9.6 0.0 copy-start.10
  9.6 3.9 %to_planes.1 = (f32[5,16,64,128]{3,2,1,0:T(8,128)S(1)}, bf16[320,128]{1,0:T(8,128)(2,1)S(1)}) custom-call(s32[16]{0:T(128)S(1)} %copy-done.5, f32[4,64,512]{2,1,0:T(8,128)S(1)} %copy-done.2, f32[2,4,64,512]{3,2,1,0:T(8,128)S(1)} %copy-done, s32[64,512]{1,0:T(8,128)S(1)} %copy-done.3, bf16[16,64,512]{2,1,0:T(8,128)(2,1)S(1)} %copy-done.1, f32[16,16]{1,0:T(8,128)S(1)} %copy-done.4), custom_call_target="tpu_custom_call" | custom-call | flops 2000000000 | bytes 6291456 | tf_op jit(solution)/shard_map/to_planes/pallas_call | solution.py:747
  13.5 0.0 collective-permute-done.refs_0_
  13.5 2.0 %collective-permute-done.1.refs_1_ = bf16[144,512]{1,0:T(8,128)(2,1)S(1)} collective-permute-done((bf16[144,512]{1,0:T(8,128)(2,1)}, bf16[144,512]{1,0:T(8,128)(2,1)S(1)}, u32[]{:S(2)}, u32[]{:S(2)}) %collective-permute-start.1) | collective-permute-done | bytes 147488 | tf_op jit(solution)/shard_map/ppermute | solution.py:685
  15.5 0.2 rim.1.refs_10_
  15.8 1.5 %collective-permute-start.2 = (bf16[240,128]{1,0:T(8,128)(2,1)S(1)}, bf16[240,128]{1,0:T(8,128)(2,1)S(1)}, u32[]{:S(2)}, u32[]{:S(2)}) collective-permute-start(bf16[240,128]{1,0:T(8,128)(2,1)S(1)} %rim.1.refs_10_), channel_id=1, source_target_pairs={{0,16},{16,0},{1,17},{17,1},{2,18},{18,2},{3,19},{19,3},{4,20},{20... | collective-permute-start | bytes 184328 | tf_op jit(solution)/shard_map/ppermute | solution.py:680
  17.3 0.0 copy-done.8
  17.3 0.0 copy-done.10
  17.3 1.6 %prepare.1 = (f32[3,16,104,128]{3,2,1,0:T(8,128)S(1)}, f32[16,104,128]{2,1,0:T(8,128)S(1)}, f32[2,96,128]{2,1,0:T(8,128)S(1)}, f32[16,104,128]{2,1,0:T(8,128)S(1...) custom-call(bf16[144,512]{1,0:T(8,128)(2,1)S(1)} %collective-permute, ...), custom_call_target="tpu_custom_call" | custom-call | flops 1000000000 | bytes 4194304 | tf_op jit(solution)/shard_map/prepare/pallas_call | solution.py:774
  18.9 1.1 %collective-permute-done.2.refs_11_.refs_12_ = bf16[240,128]{1,0:T(8,128)(2,1)S(1)} collective-permute-done((bf16[240,128]{1,0:T(8,128)(2,1)S(1)}, bf16[240,128]{1,0:T(8,128)(2,1)S(1)}, u32[]{:S(2)}, u32[]{:S(2)}) %collective-permute-start.2) | collective-permute-done | bytes 61472 | tf_op jit(solution)/shard_map/ppermute | solution.py:680
  20.0 8.9 %flow_embed.1 = (f32[4,8,256]{2,1,0:T(8,128)S(1)}, f32[32,128,256]{2,1,0:T(8,128)S(1)}, f32[3,16,104,128]{3,2,1,0:T(8,128)S(1)}) custom-call(f32[3,16,104,128]{3,2,1,0:T(8,128)S(1)} %get-tuple-element.44.refs_0_, f32[16,104,128]{2,1,0:T(8,128)S(1)} %get-tuple-element.45.refs_1_, f32[2,96,128]{2,1,0:T(8,128)S(1)} %get-tuple-element.46.refs_2_, ...), custom_call_target="tpu_custom_call" | custom-call | tf_op jit(solution)/shard_map/flow_embed/pallas_call | solution.py:816
  29.0 1.6 %collective-permute-start.3 = (f32[32,256]{1,0:T(8,128)S(1)}, f32[32,256]{1,0:T(8,128)S(1)}, u32[]{:S(2)}, u32[]{:S(2)}) collective-permute-start(f32[32,256]{1,0:T(8,128)S(1)} %bitcast.9), channel_id=1, source_target_pairs={{0,16},{16,0},{1,17},{17,1},{2,18},{18,2},{3,19},{19,3},{4,20},{20... | collective-permute-start | bytes 98312 | tf_op jit(solution)/shard_map/ppermute | solution.py:690
  30.5 2.6 %from_planes.1 = (f32[4,64,512]{2,1,0:T(8,128)}, f32[2,4,64,512]{3,2,1,0:T(8,128)}) custom-call(f32[3,16,104,128]{3,2,1,0:T(8,128)S(1)} %get-tuple-element.56.refs_0_), custom_call_target="tpu_custom_call" | custom-call | flops 2000000000 | bytes 6291456 | tf_op jit(solution)/shard_map/from_planes/pallas_call | solution.py:847
  33.1 0.0 collective-permute-done.3.refs_1_
  33.1 1.5 %local_loss.1 = (f32[64,256]{1,0:T(8,128)S(1)}, f32[64,256]{1,0:T(8,128)S(1)}, f32[16,256]{1,0:T(8,128)}) custom-call(f32[32,256]{1,0:T(8,128)S(1)} %bitcast.10, f32[32,256]{1,0:T(8,128)S(1)} %collective-permute-done.3.refs_1_, f32[32,512]{1,0:T(8,128)S(1)} %get-tuple-element.62.refs_2_, f32[32,8]{1,0:T(8,128)S(1)} %get-tuple-element.63.refs_3_, ...), custom_call_target="tpu_custom_call" | custom-call | tf_op jit(solution)/shard_map/local_loss/pallas_call | solution.py:861
  34.7 0.1 collective-permute-start.4
  34.8 1.6 %collective-permute-start.10 = (f16[32,256]{1,0:T(8,128)(2,1)S(1)}, f16[32,256]{1,0:T(8,128)(2,1)S(1)}, u32[]{:S(2)}, u32[]{:S(2)}) collective-permute-start(f16[32,256]{1,0:T(8,128)(2,1)S(1)} %multiply_convert_fusion), channel_id=1, source_target_pairs={{0,2},{1,3},{2,0},{3,1},{4,6},{5,7},{6,4},{7,5},{8,10},{9,11},{10,... | collective-permute-start | bytes 49160 | tf_op jit(solution)/shard_map/ppermute | solution.py:690
  36.4 0.0 collective-permute-done.4
  36.4 1.4 %collective-permute-start.7 = (f32[64,256]{1,0:T(8,128)S(1)}, f32[64,256]{1,0:T(8,128)S(1)}, u32[]{:S(2)}, u32[]{:S(2)}) collective-permute-start(f32[64,256]{1,0:T(8,128)S(1)} %add.21), channel_id=1, source_target_pairs={{0,16},{16,0},{1,17},{17,1},{2,18},{18,2},{3,19},{19,3},{4,20},{20... | collective-permute-start | bytes 196616 | tf_op jit(solution)/shard_map/ppermute | solution.py:690
  37.8 1.2 %collective-permute-start.6 = (f32[64,256]{1,0:T(8,128)S(1)}, f32[64,256]{1,0:T(8,128)S(1)}, u32[]{:S(2)}, u32[]{:S(2)}) collective-permute-start(f32[64,256]{1,0:T(8,128)S(1)} %add.21), channel_id=1, source_target_pairs={{0,2},{1,3},{2,0},{3,1},{4,6},{5,7},{6,4},{7,5},{8,10},{9,11},{10,... | collective-permute-start | bytes 196616 | tf_op jit(solution)/shard_map/ppermute | solution.py:690
  38.9 1.0 %collective-permute-start.5 = (f32[64,256]{1,0:T(8,128)S(1)}, f32[64,256]{1,0:T(8,128)S(1)}, u32[]{:S(2)}, u32[]{:S(2)}) collective-permute-start(f32[64,256]{1,0:T(8,128)S(1)} %add.21), channel_id=1, source_target_pairs={{0,18},{1,19},{2,16},{3,17},{16,2},{17,3},{18,0},{19,1},{4,22},{5,... | collective-permute-start | bytes 196616 | tf_op jit(solution)/shard_map/ppermute | solution.py:879
  40.0 0.0 collective-permute-done.10
  40.0 0.8 %collective-permute-done.7 = f32[64,256]{1,0:T(8,128)S(1)} collective-permute-done((f32[64,256]{1,0:T(8,128)S(1)}, f32[64,256]{1,0:T(8,128)S(1)}, u32[]{:S(2)}, u32[]{:S(2)}) %collective-permute-start.7) | collective-permute-done | bytes 65568 | tf_op jit(solution)/shard_map/ppermute | solution.py:690
  40.7 2.6 %collective-permute-start.11 = (f16[64,256]{1,0:T(8,128)(2,1)S(1)}, f16[64,256]{1,0:T(8,128)(2,1)S(1)}, u32[]{:S(2)}, u32[]{:S(2)}) collective-permute-start(f16[64,256]{1,0:T(8,128)(2,1)S(1)} %pad_maximum_fusion.2), channel_id=1, source_target_pairs={{0,8},{4,12},{8,0},{12,4},{1,9},{5,13},{9,1},{13,5},{2,10},{6,14},... | collective-permute-start | bytes 98312 | tf_op jit(solution)/shard_map/ppermute | solution.py:690
  43.3 0.0 collective-permute-done.6
  43.3 0.8 %collective-permute-done.5 = f32[64,256]{1,0:T(8,128)S(1)} collective-permute-done((f32[64,256]{1,0:T(8,128)S(1)}, f32[64,256]{1,0:T(8,128)S(1)}, u32[]{:S(2)}, u32[]{:S(2)}) %collective-permute-start.5) | collective-permute-done | bytes 65568 | tf_op jit(solution)/shard_map/ppermute | solution.py:879
  44.1 2.6 %collective-permute-start.8 = (f32[64,256]{1,0:T(8,128)S(1)}, f32[64,256]{1,0:T(8,128)S(1)}, u32[]{:S(2)}, u32[]{:S(2)}) collective-permute-start(f32[64,256]{1,0:T(8,128)S(1)} %add_add_fusion), channel_id=1, source_target_pairs={{0,8},{4,12},{8,0},{12,4},{1,9},{5,13},{9,1},{13,5},{2,10},{6,14},... | collective-permute-start | bytes 196616 | tf_op jit(solution)/shard_map/ppermute | solution.py:690
  46.7 0.0 collective-permute-done.11
  46.8 0.7 %collective-permute-start.12 = (f16[128,256]{1,0:T(8,128)(2,1)S(1)}, f16[128,256]{1,0:T(8,128)(2,1)S(1)}, u32[]{:S(2)}, u32[]{:S(2)}) collective-permute-start(f16[128,256]{1,0:T(8,128)(2,1)S(1)} %pad_maximum_fusion.1), channel_id=1, source_target_pairs={{0,4},{4,0},{8,12},{12,8},{1,5},{5,1},{9,13},{13,9},{2,6},{6,2},{1... | collective-permute-start | bytes 196616 | tf_op jit(solution)/shard_map/ppermute | solution.py:690
  47.4 1.9 %collective-permute-done.8 = f32[64,256]{1,0:T(8,128)S(1)} collective-permute-done((f32[64,256]{1,0:T(8,128)S(1)}, f32[64,256]{1,0:T(8,128)S(1)}, u32[]{:S(2)}, u32[]{:S(2)}) %collective-permute-start.8) | collective-permute-done | bytes 65568 | tf_op jit(solution)/shard_map/ppermute | solution.py:690
  49.3 1.8 %collective-permute-done.12 = f16[128,256]{1,0:T(8,128)(2,1)S(1)} collective-permute-done((f16[128,256]{1,0:T(8,128)(2,1)S(1)}, f16[128,256]{1,0:T(8,128)(2,1)S(1)}, u32[]{:S(2)}, u32[]{:S(2)}) %collective-permute-start.12) | collective-permute-done | bytes 65568 | tf_op jit(solution)/shard_map/ppermute | solution.py:690
  51.1 0.1 collective-permute-start.13
  51.2 0.7 %collective-permute-start.9 = (f32[64,256]{1,0:T(8,128)S(1)}, f32[64,256]{1,0:T(8,128)S(1)}, u32[]{:S(2)}, u32[]{:S(2)}) collective-permute-start(f32[64,256]{1,0:T(8,128)S(1)} %add.25), channel_id=1, source_target_pairs={{0,4},{4,0},{8,12},{12,8},{1,5},{5,1},{9,13},{13,9},{2,6},{6,2},{1... | collective-permute-start | bytes 196616 | tf_op jit(solution)/shard_map/ppermute | solution.py:690
  51.9 0.7 %collective-permute-done.13 = f16[256,256]{1,0:T(8,128)(2,1)S(1)} collective-permute-done((f16[256,256]{1,0:T(8,128)(2,1)S(1)}, f16[256,256]{1,0:T(8,128)(2,1)S(1)}, u32[]{:S(2)}, u32[]{:S(2)}) %collective-permute-start.13) | collective-permute-done | bytes 131104 | tf_op jit(solution)/shard_map/ppermute | solution.py:690
  52.6 2.4 %couple_grads.1 = (f32[1128,128]{1,0:T(8,128)S(1)}, f32[1,128]{1,0:T(1,128)S(1)}) custom-call(f32[512,256]{1,0:T(8,128)S(1)} %maximum_convert_fusion.refs_0_, f32[16,512]{1,0:T(8,128)S(1)} %get-tuple-element.73.refs_1_, f32[16,16]{1,0:T(8,128)S(1)} %get-tuple-element.74.refs_2_, bf16[2,256,512]{2,1,0:T(8,128)(2,1)S(1)} %get-tuple-element.64.refs_4_.refs_3_, ...), custom_call_target="tpu_custom_call" | custom-call | flops 3000000000 | bytes 3145728 | tf_op jit(solution)/shard_map/couple_grads/pallas_call | solution.py:904
  55.0 0.7 %collective-permute-done.9 = f32[64,256]{1,0:T(8,128)S(1)} collective-permute-done((f32[64,256]{1,0:T(8,128)S(1)}, f32[64,256]{1,0:T(8,128)S(1)}, u32[]{:S(2)}, u32[]{:S(2)}) %collective-permute-start.9) | collective-permute-done | bytes 65568 | tf_op jit(solution)/shard_map/ppermute | solution.py:690
  55.7 0.1 collective-permute-start.14
  55.8 1.2 %collective-permute-done.14.refs_1_ = f32[64,256]{1,0:T(8,128)S(1)} collective-permute-done((f32[64,256]{1,0:T(8,128)S(1)}, f32[64,256]{1,0:T(8,128)S(1)}, u32[]{:S(2)}, u32[]{:S(2)}) %collective-permute-start.14) | collective-permute-done | bytes 65568 | tf_op jit(solution)/shard_map/ppermute | solution.py:690
  57.1 1.1 %finish.1 = f32[1384,128]{1,0:T(8,128)} custom-call(f32[64,256]{1,0:T(8,128)S(1)} %add.27.refs_0_, f32[64,256]{1,0:T(8,128)S(1)} %collective-permute-done.14.refs_1_, f32[1128,128]{1,0:T(8,128)S(1)} %get-tuple-element.75.refs_2_, f32[1,128]{1,0:T(1,128)S(1)} %get-tuple-element.76.refs_3_), custom_call_target="tpu_custom_call" | custom-call | tf_op jit(solution)/shard_map/finish/pallas_call | solution.py:921
  (23 shorter events, 0.2 us)
Async XLA Ops:
  0.6 8.8 %copy-start.5 = (s32[16]{0:T(128)S(1)}, s32[16]{0:T(128)}, u32[]{:S(2)}) copy-start(s32[16]{0:T(128)} %refs_0_.3) | copy-start | bytes 196
  0.6 8.9 %copy-start.4 = (f32[16,16]{1,0:T(8,128)S(1)}, f32[16,16]{1,0:T(8,128)}, u32[]{:S(2)}) copy-start(f32[16,16]{1,0:T(8,128)} %refs_5_.5) | copy-start | bytes 3076
  0.7 8.9 %copy-start.1 = (bf16[16,64,512]{2,1,0:T(8,128)(2,1)S(1)}, bf16[16,64,512]{2,1,0:T(8,128)(2,1)}, u32[]{:S(2)}) copy-start(bf16[16,64,512]{2,1,0:T(8,128)(2,1)} %refs_4_.3) | copy-start | bytes 3145732
  0.7 8.9 %copy-start.3 = (s32[64,512]{1,0:T(8,128)S(1)}, s32[64,512]{1,0:T(8,128)}, u32[]{:S(2)}) copy-start(s32[64,512]{1,0:T(8,128)} %refs_3_.4) | copy-start | bytes 393220
  0.7 8.9 %copy-start = (f32[2,4,64,512]{3,2,1,0:T(8,128)S(1)}, f32[2,4,64,512]{3,2,1,0:T(8,128)}, u32[]{:S(2)}) copy-start(f32[2,4,64,512]{3,2,1,0:T(8,128)} %refs_2_.3) | copy-start | bytes 3145732
  0.7 8.9 %copy-start.2 = (f32[4,64,512]{2,1,0:T(8,128)S(1)}, f32[4,64,512]{2,1,0:T(8,128)}, u32[]{:S(2)}) copy-start(f32[4,64,512]{2,1,0:T(8,128)} %refs_1_.3) | copy-start | bytes 1572868
  3.2 10.3 %collective-permute-start = (bf16[144,512]{1,0:T(8,128)(2,1)}, bf16[144,512]{1,0:T(8,128)(2,1)S(1)}, u32[]{:S(2)}, u32[]{:S(2)}) collective-permute-start(bf16[144,512]{1,0:T(8,128)(2,1)} %get-tuple-element.41), channel_id=1, source_target_pairs={{0,4},{4,8},{8,12},{1,5},{5,9},{9,13},{2,6},{6,10},{10,14},{3,7},{... | collective-permute-start | bytes 442376 | tf_op jit(solution)/shard_map/ppermute | solution.py:685
  8.1 7.4 %collective-permute-start.1 = (bf16[144,512]{1,0:T(8,128)(2,1)}, bf16[144,512]{1,0:T(8,128)(2,1)S(1)}, u32[]{:S(2)}, u32[]{:S(2)}) collective-permute-start(bf16[144,512]{1,0:T(8,128)(2,1)} %get-tuple-element.42), channel_id=1, source_target_pairs={{4,0},{8,4},{12,8},{5,1},{9,5},{13,9},{6,2},{10,6},{14,10},{7,3},{... | collective-permute-start | bytes 442376 | tf_op jit(solution)/shard_map/ppermute | solution.py:685
  9.5 7.7 %copy-start.7 = (f32[264,512]{1,0:T(8,128)S(1)}, f32[264,512]{1,0:T(8,128)}, u32[]{:S(2)}) copy-start(f32[264,512]{1,0:T(8,128)} %refs_6_.1) | copy-start | bytes 1622020
  9.6 7.7 %copy-start.8 = (bf16[128,256]{1,0:T(8,128)(2,1)S(1)}, bf16[128,256]{1,0:T(8,128)(2,1)}, u32[]{:S(2)}) copy-start(bf16[128,256]{1,0:T(8,128)(2,1)} %refs_3_.5) | copy-start | bytes 196612
  9.6 7.7 %copy-start.9 = (f32[512,16]{0,1:T(8,128)S(1)}, f32[512,16]{0,1:T(8,128)}, u32[]{:S(2)}) copy-start(f32[512,16]{0,1:T(8,128)} %param.20) | copy-start | bytes 98308
  9.6 7.7 %copy-start.10 = (f32[512]{0:T(512)S(1)}, f32[512]{0:T(512)}, u32[]{:S(2)}) copy-start(f32[512]{0:T(512)} %param.19) | copy-start | bytes 6148
  15.8 4.3 %collective-permute-start.2 = (bf16[240,128]{1,0:T(8,128)(2,1)S(1)}, bf16[240,128]{1,0:T(8,128)(2,1)S(1)}, u32[]{:S(2)}, u32[]{:S(2)}) collective-permute-start(bf16[240,128]{1,0:T(8,128)(2,1)S(1)} %rim.1.refs_10_), channel_id=1, source_target_pairs={{0,16},{16,0},{1,17},{17,1},{2,18},{18,2},{3,19},{19,3},{4,20},{20... | collective-permute-start | bytes 184328 | tf_op jit(solution)/shard_map/ppermute | solution.py:680
  29.0 4.2 %collective-permute-start.3 = (f32[32,256]{1,0:T(8,128)S(1)}, f32[32,256]{1,0:T(8,128)S(1)}, u32[]{:S(2)}, u32[]{:S(2)}) collective-permute-start(f32[32,256]{1,0:T(8,128)S(1)} %bitcast.9), channel_id=1, source_target_pairs={{0,16},{16,0},{1,17},{17,1},{2,18},{18,2},{3,19},{19,3},{4,20},{20... | collective-permute-start | bytes 98312 | tf_op jit(solution)/shard_map/ppermute | solution.py:690
  30.5 2.6 %copy-start.6 = (f32[16]{0:T(128)S(1)}, f32[16]{0:T(128)}, u32[]{:S(2)}) copy-start(f32[16]{0:T(128)} %param.21) | copy-start | bytes 196
  34.7 1.7 %collective-permute-start.4 = (f32[64,256]{1,0:T(8,128)S(1)}, f32[64,256]{1,0:T(8,128)S(1)}, u32[]{:S(2)}, u32[]{:S(2)}) collective-permute-start(f32[64,256]{1,0:T(8,128)S(1)} %get-tuple-element.69), channel_id=1, source_target_pairs={{0,1},{1,0},{2,3},{3,2},{4,5},{5,4},{6,7},{7,6},{8,9},{9,8},{10,11... | collective-permute-start | bytes 196616 | tf_op jit(solution)/shard_map/ppermute | solution.py:690
  34.8 5.2 %collective-permute-start.10 = (f16[32,256]{1,0:T(8,128)(2,1)S(1)}, f16[32,256]{1,0:T(8,128)(2,1)S(1)}, u32[]{:S(2)}, u32[]{:S(2)}) collective-permute-start(f16[32,256]{1,0:T(8,128)(2,1)S(1)} %multiply_convert_fusion), channel_id=1, source_target_pairs={{0,2},{1,3},{2,0},{3,1},{4,6},{5,7},{6,4},{7,5},{8,10},{9,11},{10,... | collective-permute-start | bytes 49160 | tf_op jit(solution)/shard_map/ppermute | solution.py:690
  36.4 4.3 %collective-permute-start.7 = (f32[64,256]{1,0:T(8,128)S(1)}, f32[64,256]{1,0:T(8,128)S(1)}, u32[]{:S(2)}, u32[]{:S(2)}) collective-permute-start(f32[64,256]{1,0:T(8,128)S(1)} %add.21), channel_id=1, source_target_pairs={{0,16},{16,0},{1,17},{17,1},{2,18},{18,2},{3,19},{19,3},{4,20},{20... | collective-permute-start | bytes 196616 | tf_op jit(solution)/shard_map/ppermute | solution.py:690
  37.8 5.6 %collective-permute-start.6 = (f32[64,256]{1,0:T(8,128)S(1)}, f32[64,256]{1,0:T(8,128)S(1)}, u32[]{:S(2)}, u32[]{:S(2)}) collective-permute-start(f32[64,256]{1,0:T(8,128)S(1)} %add.21), channel_id=1, source_target_pairs={{0,2},{1,3},{2,0},{3,1},{4,6},{5,7},{6,4},{7,5},{8,10},{9,11},{10,... | collective-permute-start | bytes 196616 | tf_op jit(solution)/shard_map/ppermute | solution.py:690
  38.9 5.2 %collective-permute-start.5 = (f32[64,256]{1,0:T(8,128)S(1)}, f32[64,256]{1,0:T(8,128)S(1)}, u32[]{:S(2)}, u32[]{:S(2)}) collective-permute-start(f32[64,256]{1,0:T(8,128)S(1)} %add.21), channel_id=1, source_target_pairs={{0,18},{1,19},{2,16},{3,17},{16,2},{17,3},{18,0},{19,1},{4,22},{5,... | collective-permute-start | bytes 196616 | tf_op jit(solution)/shard_map/ppermute | solution.py:879
  40.7 6.0 %collective-permute-start.11 = (f16[64,256]{1,0:T(8,128)(2,1)S(1)}, f16[64,256]{1,0:T(8,128)(2,1)S(1)}, u32[]{:S(2)}, u32[]{:S(2)}) collective-permute-start(f16[64,256]{1,0:T(8,128)(2,1)S(1)} %pad_maximum_fusion.2), channel_id=1, source_target_pairs={{0,8},{4,12},{8,0},{12,4},{1,9},{5,13},{9,1},{13,5},{2,10},{6,14},... | collective-permute-start | bytes 98312 | tf_op jit(solution)/shard_map/ppermute | solution.py:690
  44.1 5.2 %collective-permute-start.8 = (f32[64,256]{1,0:T(8,128)S(1)}, f32[64,256]{1,0:T(8,128)S(1)}, u32[]{:S(2)}, u32[]{:S(2)}) collective-permute-start(f32[64,256]{1,0:T(8,128)S(1)} %add_add_fusion), channel_id=1, source_target_pairs={{0,8},{4,12},{8,0},{12,4},{1,9},{5,13},{9,1},{13,5},{2,10},{6,14},... | collective-permute-start | bytes 196616 | tf_op jit(solution)/shard_map/ppermute | solution.py:690
  46.8 4.3 %collective-permute-start.12 = (f16[128,256]{1,0:T(8,128)(2,1)S(1)}, f16[128,256]{1,0:T(8,128)(2,1)S(1)}, u32[]{:S(2)}, u32[]{:S(2)}) collective-permute-start(f16[128,256]{1,0:T(8,128)(2,1)S(1)} %pad_maximum_fusion.1), channel_id=1, source_target_pairs={{0,4},{4,0},{8,12},{12,8},{1,5},{5,1},{9,13},{13,9},{2,6},{6,2},{1... | collective-permute-start | bytes 196616 | tf_op jit(solution)/shard_map/ppermute | solution.py:690
  51.1 1.4 %collective-permute-start.13 = (f16[256,256]{1,0:T(8,128)(2,1)S(1)}, f16[256,256]{1,0:T(8,128)(2,1)S(1)}, u32[]{:S(2)}, u32[]{:S(2)}) collective-permute-start(f16[256,256]{1,0:T(8,128)(2,1)S(1)} %pad_maximum_fusion), channel_id=1, source_target_pairs={{0,1},{1,0},{2,3},{3,2},{4,5},{5,4},{6,7},{7,6},{8,9},{9,8},{10,11... | collective-permute-start | bytes 393224 | tf_op jit(solution)/shard_map/ppermute | solution.py:690
  51.2 4.5 %collective-permute-start.9 = (f32[64,256]{1,0:T(8,128)S(1)}, f32[64,256]{1,0:T(8,128)S(1)}, u32[]{:S(2)}, u32[]{:S(2)}) collective-permute-start(f32[64,256]{1,0:T(8,128)S(1)} %add.25), channel_id=1, source_target_pairs={{0,4},{4,0},{8,12},{12,8},{1,5},{5,1},{9,13},{13,9},{2,6},{6,2},{1... | collective-permute-start | bytes 196616 | tf_op jit(solution)/shard_map/ppermute | solution.py:690
  55.7 1.3 %collective-permute-start.14 = (f32[64,256]{1,0:T(8,128)S(1)}, f32[64,256]{1,0:T(8,128)S(1)}, u32[]{:S(2)}, u32[]{:S(2)}) collective-permute-start(f32[64,256]{1,0:T(8,128)S(1)} %add.27.refs_0_), channel_id=1, source_target_pairs={{0,1},{1,0},{2,3},{3,2},{4,5},{5,4},{6,7},{7,6},{8,9},{9,8},{10,11... | collective-permute-start | bytes 196616 | tf_op jit(solution)/shard_map/ppermute | solution.py:690

commit v6 on v5

--- a/solution.py
+++ b/solution.py
@@ -125,7 +125,7 @@
         copies.append((sea.at[:, rs, :], cells.at[side, 0]))
         copies.append((vel.at[0, :, rs, :], cells.at[side, 1]))
         copies.append((vel.at[1, :, rs, :], cells.at[side, 2]))
-        copies.append((levels.at[rs, :], depth.at[side]))
+        copies.append((levels.at[pl.ds(w0, 16), :], depth.at[side]))
         copies.append((wind.at[:, pl.ds(w0, 16), :], basis.at[side]))
     started = [pltpu.make_async_copy(a, b, sems.at[n]) for n, (a, b) in enumerate(copies)]
     for copy in started:
@@ -138,7 +138,8 @@
         force = forcing_rows(coeff, basis.at[side], members, keep)
         blocks = [cells[side, i, m] for i in range(3) for m in range(members)]
         blocks += force
-        blocks += [depth[side].astype(F32), jnp.zeros((HALO, cols), F32)]
+        rest = slice(HALO, 16) if side == 0 else slice(0, 16 - HALO)
+        blocks += [depth[side, part, :].astype(F32) for part in (keep, rest)]
         for g in range(0, len(blocks), 2):
             pair = jnp.concatenate(blocks[g : g + 2], axis=0)
             out[g * HALO : (g + 2) * HALO, :] = pair.astype(BF16)
@@ -157,6 +158,8 @@
     scale = 1.0 / GRAVITY
     full = (members * rows, cols)
     fields = [sea[...].reshape(full), vel[0].reshape(full), vel[1].reshape(full), force, depth]
+    west = [pltpu.roll(depth[:, cols - LANES :], 1, 1)] * members
+    side[5 * rows : 6 * rows, :] = edges_of(west, west, patches).astype(BF16)
     for i, value in enumerate(fields):
         starts = [m * rows if i < 4 else 0 for m in range(members)]
         edge = edges_of(
@@ -177,31 +180,34 @@
 def starts_of(i, members):
     if i < 4:
         return [(i * members + m) * HALO for m in range(members)]
-    return [4 * members * HALO] * members
+    return [(4 * members + i - 4) * HALO] * members
 
 
 def rim_kernel(members, patches, south, north, side, out):
-    rows = side.shape[0] // 5
+    rows = side.shape[0] // 6
     cols = south.shape[1]
     low, high = south[...].astype(F32), north[...].astype(F32)
+
+    def edges(plain, i, turn):
+        starts = starts_of(i, members)
+        lasts = [plain[s : s + HALO, cols - LANES :] for s in starts]
+        return edges_of(
+            [plain[s : s + HALO, :LANES] for s in starts],
+            [turned(last, turn) for last in lasts],
+            patches,
+        )
+
     wholes = []
-    for i in range(5):
-        ends = [
-            edges_of(
-                [plain[s : s + HALO, :LANES] for s in starts_of(i, members)],
-                [plain[s : s + HALO, cols - LANES :] for s in starts_of(i, members)],
-                patches,
-            )
-            for plain in (low, high)
-        ]
+    for i in range(6):
+        ends = [edges(plain, min(i, 4), 1 if i == 5 else 0) for plain in (low, high)]
         own = side[i * rows : (i + 1) * rows, :].astype(F32)
         wholes.append(jnp.concatenate([ends[0], own, ends[1]], axis=0))
     wide = rows + 2 * HALO
-    for n, i in enumerate((0, 2, 4)):
-        pair = wholes[i]
-        if i + 1 < len(wholes):
-            pair = pair + pltpu.roll(wholes[i + 1], 2 * HALO, 1)
+    for n in range(3):
+        pair = wholes[2 * n] + pltpu.roll(wholes[2 * n + 1], 2 * HALO, 1)
         out[n * wide : (n + 1) * wide, :] = pair.astype(BF16)
+    behind = edges(low, 5, 0)
+    out[3 * wide : 3 * wide + 2 * HALO, :] = jnp.concatenate([behind, behind], axis=0).astype(BF16)
 
 
 def rims_of(own, from_east, from_west, patches):
@@ -276,6 +282,10 @@
             parts = [spread[s : s + HALO] for s in starts_of(i, members)]
             for k, plane in enumerate(planes_from(parts, patches)):
                 home[k, r0 : r0 + HALO, :] = plane if i in (0, 4) else plane * (1.0 / GRAVITY)
+        if r0 < PAD:
+            parts = [spread[s : s + HALO] for s in starts_of(5, members)]
+            for k, plane in enumerate(planes_from(parts, patches)):
+                depth[k, 0:HALO, :] = plane
     span = slice(PAD - HALO, PAD + rows + HALO)
     row, inside = row_ids(rows, lat_count)
     place = row.astype(F32)
@@ -433,6 +443,7 @@
     rim_b,
     force_rim,
     depth_rim,
+    west_rim,
     hu_rim,
     hv_rim,
     hvu_rim,
@@ -446,21 +457,23 @@
     wide = rows + 2 * HALO
     span = slice(PAD - HALO, PAD + rows + HALO)
     state_a[:, :, span, :] = state[:, :, span, :]
-    for rs in (slice(0, HALO), slice(height - HALO, height)):
-        depth_rim[rs, :] = jnp.zeros((HALO, LANES), F32)
-    rim_homes = (rim_a.at[0], rim_a.at[1], rim_a.at[2], force_rim, depth_rim)
+    depth_rim[height - HALO : height, :] = jnp.zeros((HALO, LANES), F32)
+    behind = slice(3 * wide, 3 * wide + 2 * HALO)
+    got = [ref[behind, :].astype(F32)[:HALO] for ref in (side, east, west)]
+    depth_rim[0:HALO, :] = rims_of(*got, patches)[0]
+    rim_homes = (rim_a.at[0], rim_a.at[1], rim_a.at[2], force_rim, depth_rim, west_rim)
     for n in range(3):
         rs = slice(n * wide, (n + 1) * wide)
         got = [ref[rs, :].astype(F32) for ref in (side, east, west)]
         for i, rim in zip((2 * n, 2 * n + 1), rims_of(*got, patches)):
-            if i < len(rim_homes):
-                rim_homes[i][span, :] = rim if i in (0, 4) else rim * (1.0 / GRAVITY)
+            rim_homes[i][span, :] = rim * (1.0 / GRAVITY) if i in (1, 2, 3) else rim
     _, inside = row_ids(rows, lat_count)
     last = lane_ids(wide) % patches == patches - 1
     rim = depth_rim[span, :]
     left = pltpu.roll(jnp.where(last, rim, ends[1, span, :]), 1, 1)
     first = HALF_DEPTH * (ends[0, span, :] + left)
-    rim = HALF_DEPTH * (rim + pltpu.roll(rim, 1, 1))
+    outer = lane_ids(wide) % patches >= 3 * HALO
+    rim = HALF_DEPTH * (rim + jnp.where(outer, west_rim[span, :], pltpu.roll(rim, 1, 1)))
     hu_rim[0, span, :] = first
     hu_rim[1, span, :] = rim
     hu_rim[2, span, :] = jnp.where(
@@ -732,7 +745,7 @@
         scratch_shapes=[
             pltpu.SMEM(member_ids.shape, jnp.int32),
             pltpu.VMEM((2, 3, members, HALO, cols), F32),
-            pltpu.VMEM((2, HALO, cols), jnp.int32),
+            pltpu.VMEM((2, 16, cols), jnp.int32),
             pltpu.VMEM((2, wind_basis.shape[0], 16, cols), BF16),
             pltpu.VMEM(proposals.shape, F32),
             pltpu.SemaphoreType.DMA((12,)),
@@ -746,7 +759,7 @@
 
     planes, side = pl.pallas_call(
         lambda *refs: planar_kernel(members, *refs),
-        out_shape=(shape(5, PW, rows, LANES), shape(5 * rows, LANES, dtype=BF16)),
+        out_shape=(shape(5, PW, rows, LANES), shape(6 * rows, LANES, dtype=BF16)),
         in_specs=[smem()] + [vmem()] * 5,
         out_specs=(vmem(), vmem()),
         compiler_params=params_of(32),
@@ -757,7 +770,7 @@
     wide = rows + 2 * HALO
     rim = pl.pallas_call(
         lambda *refs: rim_kernel(members, patches, *refs),
-        out_shape=shape(3 * wide, LANES, dtype=BF16),
+        out_shape=shape(3 * wide + 2 * HALO, LANES, dtype=BF16),
         in_specs=[vmem()] * 3,
         out_specs=vmem(),
         compiler_params=params_of(16),
@@ -828,6 +841,7 @@
             pltpu.VMEM((3, height, LANES), F32),
             pltpu.VMEM((height, LANES), F32),
             pltpu.VMEM((height, LANES), F32),
+            pltpu.VMEM((height, LANES), F32),
             pltpu.VMEM((3, height, LANES), F32),
             pltpu.VMEM((height, LANES), F32),
             pltpu.VMEM((height, LANES), F32),

time: 58.3 us -> 58.5 us (level)
  no operation moved by 1% of the time
where the time goes in v6:
time: 58.5 us; the launch traced here: 58.3 us
  Pallas kernels  24.9 us (43%)
  starting transfers between devices  21.4 us (37%)
  waiting for transfers between devices  10.8 us (18%)
  between operations  0.88 us (2%)
    ppermute x11, starting transfers between devices, swapped(): return lax.ppermute(value, axis, [(i, i ^ flip) for i in range(count)])  12.6 us
    pallas_call x1, Pallas kernels, shards(): pl.pallas_call(lambda *refs: flow_kernel(members, rows, cols, lat_count,...  8.96 us
    ppermute x11, waiting for transfers between devices, swapped(): return lax.ppermute(value, axis, [(i, i ^ flip) for i in range(count)])  6.91 us
    ppermute x2, starting transfers between devices, from_lat(): lax.ppermute(value, 'lat', [(i, i + step) for i in range(count) if 0 <= i...  6.23 us
    pallas_call x1, Pallas kernels, shards(): pl.pallas_call(lambda *refs: planar_kernel(members, *refs), out_shape=(sh...  3.92 us
    pallas_call x1, Pallas kernels, shards(): pl.pallas_call(lambda *refs: back_kernel(members, *refs), out_shape=(shap...  2.61 us
    pallas_call x1, Pallas kernels, shards(): pl.pallas_call(lambda *refs: pack_kernel(members, *refs), out_shape=(shap...  2.49 us
    pallas_call x1, Pallas kernels, shards(): pl.pallas_call(lambda *refs: couple_kernel(members, lat_count, grp_count,...  2.43 us
  transfers between devices with their start and end apart: 15, of which 9 were waited for; matrix products, arithmetic and copies ran while one was open for 0% of the time, Pallas kernels for 18%

profile of v6, /device:TPU:0, one launch (start us, length us, event | category | flops | bytes accessed | tf_op | source)
XLA Modules:
  0.0 58.3 jit_solution(5649602066940327781)
XLA Ops:
  0.6 0.0 copy-start.5
  0.6 0.0 copy-start.4
  0.7 0.0 copy-start.1
  0.7 0.0 copy-start.3
  0.7 2.5 %pack_rows.1 = (bf16[144,512]{1,0:T(8,128)(2,1)}, bf16[144,512]{1,0:T(8,128)(2,1)}) custom-call(s32[16]{0:T(128)} %refs_0_.3, f32[4,64,512]{2,1,0:T(8,128)} %refs_1_.3, f32[2,4,64,512]{3,2,1,0:T(8,128)} %refs_2_.3, s32[64,512]{1,0:T(8,128)} %refs_3_.4, bf16[16,64,512]{2,1,0:T(8,128)(2,1)} %refs_4_.3, f32[16,16]{1,0:T(8,128)} %refs_5_.5), custom_call_target="tpu_custom_call" | custom-call | tf_op jit(solution)/shard_map/pack_rows/pallas_call | solution.py:740
  3.2 4.9 %collective-permute-start = (bf16[144,512]{1,0:T(8,128)(2,1)}, bf16[144,512]{1,0:T(8,128)(2,1)S(1)}, u32[]{:S(2)}, u32[]{:S(2)}) collective-permute-start(bf16[144,512]{1,0:T(8,128)(2,1)} %get-tuple-element.41), channel_id=1, source_target_pairs={{0,4},{4,8},{8,12},{1,5},{5,9},{9,13},{2,6},{6,10},{10,14},{3,7},{... | collective-permute-start | bytes 442376 | tf_op jit(solution)/shard_map/ppermute | solution.py:698
  8.1 1.3 %collective-permute-start.1 = (bf16[144,512]{1,0:T(8,128)(2,1)}, bf16[144,512]{1,0:T(8,128)(2,1)S(1)}, u32[]{:S(2)}, u32[]{:S(2)}) collective-permute-start(bf16[144,512]{1,0:T(8,128)(2,1)} %get-tuple-element.42), channel_id=1, source_target_pairs={{4,0},{8,4},{12,8},{5,1},{9,5},{13,9},{6,2},{10,6},{14,10},{7,3},{... | collective-permute-start | bytes 442376 | tf_op jit(solution)/shard_map/ppermute | solution.py:698
  9.4 0.1 copy.15.refs_4_
  9.6 0.0 copy-start.7
  9.6 0.0 copy-start.8
  9.6 0.0 copy-start.9
  9.6 0.0 copy-start.10
  9.6 3.9 %to_planes.1 = (f32[5,16,64,128]{3,2,1,0:T(8,128)S(1)}, bf16[384,128]{1,0:T(8,128)(2,1)S(1)}) custom-call(s32[16]{0:T(128)S(1)} %copy-done.5, f32[4,64,512]{2,1,0:T(8,128)S(1)} %copy-done.2, f32[2,4,64,512]{3,2,1,0:T(8,128)S(1)} %copy-done, s32[64,512]{1,0:T(8,128)S(1)} %copy-done.3, bf16[16,64,512]{2,1,0:T(8,128)(2,1)S(1)} %copy-done.1, f32[16,16]{1,0:T(8,128)S(1)} %copy-done.4), custom_call_target="tpu_custom_call" | custom-call | flops 2000000000 | bytes 6291456 | tf_op jit(solution)/shard_map/to_planes/pallas_call | solution.py:760
  13.5 0.0 collective-permute-done.refs_0_
  13.5 2.0 %collective-permute-done.1.refs_1_ = bf16[144,512]{1,0:T(8,128)(2,1)S(1)} collective-permute-done((bf16[144,512]{1,0:T(8,128)(2,1)}, bf16[144,512]{1,0:T(8,128)(2,1)S(1)}, u32[]{:S(2)}, u32[]{:S(2)}) %collective-permute-start.1) | collective-permute-done | bytes 147488 | tf_op jit(solution)/shard_map/ppermute | solution.py:698
  15.5 0.3 rim.1.refs_10_
  15.8 1.6 %collective-permute-start.2 = (bf16[256,128]{1,0:T(8,128)(2,1)S(1)}, bf16[256,128]{1,0:T(8,128)(2,1)S(1)}, u32[]{:S(2)}, u32[]{:S(2)}) collective-permute-start(bf16[256,128]{1,0:T(8,128)(2,1)S(1)} %rim.1.refs_10_), channel_id=1, source_target_pairs={{0,16},{16,0},{1,17},{17,1},{2,18},{18,2},{3,19},{19,3},{4,20},{20... | collective-permute-start | bytes 196616 | tf_op jit(solution)/shard_map/ppermute | solution.py:693
  17.4 1.6 %prepare.1 = (f32[3,16,104,128]{3,2,1,0:T(8,128)S(1)}, f32[16,104,128]{2,1,0:T(8,128)S(1)}, f32[2,96,128]{2,1,0:T(8,128)S(1)}, f32[16,104,128]{2,1,0:T(8,128)S(1...) custom-call(bf16[144,512]{1,0:T(8,128)(2,1)S(1)} %collective-permute, ...), custom_call_target="tpu_custom_call" | custom-call | flops 1000000000 | bytes 4194304 | tf_op jit(solution)/shard_map/prepare/pallas_call | solution.py:787
  19.0 1.1 %collective-permute-done.2.refs_11_.refs_12_ = bf16[256,128]{1,0:T(8,128)(2,1)S(1)} collective-permute-done((bf16[256,128]{1,0:T(8,128)(2,1)S(1)}, bf16[256,128]{1,0:T(8,128)(2,1)S(1)}, u32[]{:S(2)}, u32[]{:S(2)}) %collective-permute-start.2) | collective-permute-done | bytes 65568 | tf_op jit(solution)/shard_map/ppermute | solution.py:693
  20.2 9.0 %flow_embed.1 = (f32[4,8,256]{2,1,0:T(8,128)S(1)}, f32[32,128,256]{2,1,0:T(8,128)S(1)}, f32[3,16,104,128]{3,2,1,0:T(8,128)S(1)}) custom-call(f32[3,16,104,128]{3,2,1,0:T(8,128)S(1)} %get-tuple-element.44.refs_0_, f32[16,104,128]{2,1,0:T(8,128)S(1)} %get-tuple-element.45.refs_1_, f32[2,96,128]{2,1,0:T(8,128)S(1)} %get-tuple-element.46.refs_2_, ...), custom_call_target="tpu_custom_call" | custom-call | tf_op jit(solution)/shard_map/flow_embed/pallas_call | solution.py:829
  29.1 1.6 %collective-permute-start.3 = (f32[32,256]{1,0:T(8,128)S(1)}, f32[32,256]{1,0:T(8,128)S(1)}, u32[]{:S(2)}, u32[]{:S(2)}) collective-permute-start(f32[32,256]{1,0:T(8,128)S(1)} %bitcast.9), channel_id=1, source_target_pairs={{0,16},{16,0},{1,17},{17,1},{2,18},{18,2},{3,19},{19,3},{4,20},{20... | collective-permute-start | bytes 98312 | tf_op jit(solution)/shard_map/ppermute | solution.py:703
  30.7 2.6 %from_planes.1 = (f32[4,64,512]{2,1,0:T(8,128)}, f32[2,4,64,512]{3,2,1,0:T(8,128)}) custom-call(f32[3,16,104,128]{3,2,1,0:T(8,128)S(1)} %get-tuple-element.56.refs_0_), custom_call_target="tpu_custom_call" | custom-call | flops 2000000000 | bytes 6291456 | tf_op jit(solution)/shard_map/from_planes/pallas_call | solution.py:861
  33.3 0.0 collective-permute-done.3.refs_1_
  33.3 1.5 %local_loss.1 = (f32[64,256]{1,0:T(8,128)S(1)}, f32[64,256]{1,0:T(8,128)S(1)}, f32[16,256]{1,0:T(8,128)}) custom-call(f32[32,256]{1,0:T(8,128)S(1)} %bitcast.10, f32[32,256]{1,0:T(8,128)S(1)} %collective-permute-done.3.refs_1_, f32[32,512]{1,0:T(8,128)S(1)} %get-tuple-element.62.refs_2_, f32[32,8]{1,0:T(8,128)S(1)} %get-tuple-element.63.refs_3_, ...), custom_call_target="tpu_custom_call" | custom-call | tf_op jit(solution)/shard_map/local_loss/pallas_call | solution.py:875
  34.8 0.1 collective-permute-start.4
  34.9 1.6 %collective-permute-start.10 = (f16[32,256]{1,0:T(8,128)(2,1)S(1)}, f16[32,256]{1,0:T(8,128)(2,1)S(1)}, u32[]{:S(2)}, u32[]{:S(2)}) collective-permute-start(f16[32,256]{1,0:T(8,128)(2,1)S(1)} %multiply_convert_fusion), channel_id=1, source_target_pairs={{0,2},{1,3},{2,0},{3,1},{4,6},{5,7},{6,4},{7,5},{8,10},{9,11},{10,... | collective-permute-start | bytes 49160 | tf_op jit(solution)/shard_map/ppermute | solution.py:703
  36.5 0.0 collective-permute-done.4
  36.6 1.4 %collective-permute-start.7 = (f32[64,256]{1,0:T(8,128)S(1)}, f32[64,256]{1,0:T(8,128)S(1)}, u32[]{:S(2)}, u32[]{:S(2)}) collective-permute-start(f32[64,256]{1,0:T(8,128)S(1)} %add.21), channel_id=1, source_target_pairs={{0,16},{16,0},{1,17},{17,1},{2,18},{18,2},{3,19},{19,3},{4,20},{20... | collective-permute-start | bytes 196616 | tf_op jit(solution)/shard_map/ppermute | solution.py:703
  37.9 1.2 %collective-permute-start.6 = (f32[64,256]{1,0:T(8,128)S(1)}, f32[64,256]{1,0:T(8,128)S(1)}, u32[]{:S(2)}, u32[]{:S(2)}) collective-permute-start(f32[64,256]{1,0:T(8,128)S(1)} %add.21), channel_id=1, source_target_pairs={{0,2},{1,3},{2,0},{3,1},{4,6},{5,7},{6,4},{7,5},{8,10},{9,11},{10,... | collective-permute-start | bytes 196616 | tf_op jit(solution)/shard_map/ppermute | solution.py:703
  39.1 1.0 %collective-permute-start.5 = (f32[64,256]{1,0:T(8,128)S(1)}, f32[64,256]{1,0:T(8,128)S(1)}, u32[]{:S(2)}, u32[]{:S(2)}) collective-permute-start(f32[64,256]{1,0:T(8,128)S(1)} %add.21), channel_id=1, source_target_pairs={{0,18},{1,19},{2,16},{3,17},{16,2},{17,3},{18,0},{19,1},{4,22},{5,... | collective-permute-start | bytes 196616 | tf_op jit(solution)/shard_map/ppermute | solution.py:893
  40.1 0.0 collective-permute-done.10
  40.1 0.8 %collective-permute-done.7 = f32[64,256]{1,0:T(8,128)S(1)} collective-permute-done((f32[64,256]{1,0:T(8,128)S(1)}, f32[64,256]{1,0:T(8,128)S(1)}, u32[]{:S(2)}, u32[]{:S(2)}) %collective-permute-start.7) | collective-permute-done | bytes 65568 | tf_op jit(solution)/shard_map/ppermute | solution.py:703
  40.9 2.6 %collective-permute-start.11 = (f16[64,256]{1,0:T(8,128)(2,1)S(1)}, f16[64,256]{1,0:T(8,128)(2,1)S(1)}, u32[]{:S(2)}, u32[]{:S(2)}) collective-permute-start(f16[64,256]{1,0:T(8,128)(2,1)S(1)} %pad_maximum_fusion.2), channel_id=1, source_target_pairs={{0,8},{4,12},{8,0},{12,4},{1,9},{5,13},{9,1},{13,5},{2,10},{6,14},... | collective-permute-start | bytes 98312 | tf_op jit(solution)/shard_map/ppermute | solution.py:703
  43.5 0.0 collective-permute-done.6
  43.5 0.8 %collective-permute-done.5 = f32[64,256]{1,0:T(8,128)S(1)} collective-permute-done((f32[64,256]{1,0:T(8,128)S(1)}, f32[64,256]{1,0:T(8,128)S(1)}, u32[]{:S(2)}, u32[]{:S(2)}) %collective-permute-start.5) | collective-permute-done | bytes 65568 | tf_op jit(solution)/shard_map/ppermute | solution.py:893
  44.3 2.6 %collective-permute-start.8 = (f32[64,256]{1,0:T(8,128)S(1)}, f32[64,256]{1,0:T(8,128)S(1)}, u32[]{:S(2)}, u32[]{:S(2)}) collective-permute-start(f32[64,256]{1,0:T(8,128)S(1)} %add_add_fusion), channel_id=1, source_target_pairs={{0,8},{4,12},{8,0},{12,4},{1,9},{5,13},{9,1},{13,5},{2,10},{6,14},... | collective-permute-start | bytes 196616 | tf_op jit(solution)/shard_map/ppermute | solution.py:703
  46.9 0.0 collective-permute-done.11
  46.9 0.7 %collective-permute-start.12 = (f16[128,256]{1,0:T(8,128)(2,1)S(1)}, f16[128,256]{1,0:T(8,128)(2,1)S(1)}, u32[]{:S(2)}, u32[]{:S(2)}) collective-permute-start(f16[128,256]{1,0:T(8,128)(2,1)S(1)} %pad_maximum_fusion.1), channel_id=1, source_target_pairs={{0,4},{4,0},{8,12},{12,8},{1,5},{5,1},{9,13},{13,9},{2,6},{6,2},{1... | collective-permute-start | bytes 196616 | tf_op jit(solution)/shard_map/ppermute | solution.py:703
  47.7 1.8 %collective-permute-done.8 = f32[64,256]{1,0:T(8,128)S(1)} collective-permute-done((f32[64,256]{1,0:T(8,128)S(1)}, f32[64,256]{1,0:T(8,128)S(1)}, u32[]{:S(2)}, u32[]{:S(2)}) %collective-permute-start.8) | collective-permute-done | bytes 65568 | tf_op jit(solution)/shard_map/ppermute | solution.py:703
  49.5 1.8 %collective-permute-done.12 = f16[128,256]{1,0:T(8,128)(2,1)S(1)} collective-permute-done((f16[128,256]{1,0:T(8,128)(2,1)S(1)}, f16[128,256]{1,0:T(8,128)(2,1)S(1)}, u32[]{:S(2)}, u32[]{:S(2)}) %collective-permute-start.12) | collective-permute-done | bytes 65568 | tf_op jit(solution)/shard_map/ppermute | solution.py:703
  51.3 0.1 collective-permute-start.13
  51.4 0.7 %collective-permute-start.9 = (f32[64,256]{1,0:T(8,128)S(1)}, f32[64,256]{1,0:T(8,128)S(1)}, u32[]{:S(2)}, u32[]{:S(2)}) collective-permute-start(f32[64,256]{1,0:T(8,128)S(1)} %add.25), channel_id=1, source_target_pairs={{0,4},{4,0},{8,12},{12,8},{1,5},{5,1},{9,13},{13,9},{2,6},{6,2},{1... | collective-permute-start | bytes 196616 | tf_op jit(solution)/shard_map/ppermute | solution.py:703
  52.1 0.6 %collective-permute-done.13 = f16[256,256]{1,0:T(8,128)(2,1)S(1)} collective-permute-done((f16[256,256]{1,0:T(8,128)(2,1)S(1)}, f16[256,256]{1,0:T(8,128)(2,1)S(1)}, u32[]{:S(2)}, u32[]{:S(2)}) %collective-permute-start.13) | collective-permute-done | bytes 131104 | tf_op jit(solution)/shard_map/ppermute | solution.py:703
  52.8 2.4 %couple_grads.1 = (f32[1128,128]{1,0:T(8,128)S(1)}, f32[1,128]{1,0:T(1,128)S(1)}) custom-call(f32[512,256]{1,0:T(8,128)S(1)} %maximum_convert_fusion.refs_0_, f32[16,512]{1,0:T(8,128)S(1)} %get-tuple-element.73.refs_1_, f32[16,16]{1,0:T(8,128)S(1)} %get-tuple-element.74.refs_2_, bf16[2,256,512]{2,1,0:T(8,128)(2,1)S(1)} %get-tuple-element.64.refs_4_.refs_3_, ...), custom_call_target="tpu_custom_call" | custom-call | flops 3000000000 | bytes 3145728 | tf_op jit(solution)/shard_map/couple_grads/pallas_call | solution.py:918
  55.2 0.7 %collective-permute-done.9 = f32[64,256]{1,0:T(8,128)S(1)} collective-permute-done((f32[64,256]{1,0:T(8,128)S(1)}, f32[64,256]{1,0:T(8,128)S(1)}, u32[]{:S(2)}, u32[]{:S(2)}) %collective-permute-start.9) | collective-permute-done | bytes 65568 | tf_op jit(solution)/shard_map/ppermute | solution.py:703
  55.9 0.1 collective-permute-start.14
  56.0 1.2 %collective-permute-done.14.refs_1_ = f32[64,256]{1,0:T(8,128)S(1)} collective-permute-done((f32[64,256]{1,0:T(8,128)S(1)}, f32[64,256]{1,0:T(8,128)S(1)}, u32[]{:S(2)}, u32[]{:S(2)}) %collective-permute-start.14) | collective-permute-done | bytes 65568 | tf_op jit(solution)/shard_map/ppermute | solution.py:703
  57.2 1.1 %finish.1 = f32[1384,128]{1,0:T(8,128)} custom-call(f32[64,256]{1,0:T(8,128)S(1)} %add.27.refs_0_, f32[64,256]{1,0:T(8,128)S(1)} %collective-permute-done.14.refs_1_, f32[1128,128]{1,0:T(8,128)S(1)} %get-tuple-element.75.refs_2_, f32[1,128]{1,0:T(1,128)S(1)} %get-tuple-element.76.refs_3_), custom_call_target="tpu_custom_call" | custom-call | tf_op jit(solution)/shard_map/finish/pallas_call | solution.py:935
  (23 shorter events, 0.2 us)
Async XLA Ops:
  0.6 8.8 %copy-start.5 = (s32[16]{0:T(128)S(1)}, s32[16]{0:T(128)}, u32[]{:S(2)}) copy-start(s32[16]{0:T(128)} %refs_0_.3) | copy-start | bytes 196
  0.6 8.9 %copy-start.4 = (f32[16,16]{1,0:T(8,128)S(1)}, f32[16,16]{1,0:T(8,128)}, u32[]{:S(2)}) copy-start(f32[16,16]{1,0:T(8,128)} %refs_5_.5) | copy-start | bytes 3076
  0.7 8.9 %copy-start.1 = (bf16[16,64,512]{2,1,0:T(8,128)(2,1)S(1)}, bf16[16,64,512]{2,1,0:T(8,128)(2,1)}, u32[]{:S(2)}) copy-start(bf16[16,64,512]{2,1,0:T(8,128)(2,1)} %refs_4_.3) | copy-start | bytes 3145732
  0.7 8.9 %copy-start.3 = (s32[64,512]{1,0:T(8,128)S(1)}, s32[64,512]{1,0:T(8,128)}, u32[]{:S(2)}) copy-start(s32[64,512]{1,0:T(8,128)} %refs_3_.4) | copy-start | bytes 393220
  0.7 8.9 %copy-start = (f32[2,4,64,512]{3,2,1,0:T(8,128)S(1)}, f32[2,4,64,512]{3,2,1,0:T(8,128)}, u32[]{:S(2)}) copy-start(f32[2,4,64,512]{3,2,1,0:T(8,128)} %refs_2_.3) | copy-start | bytes 3145732
  0.7 8.9 %copy-start.2 = (f32[4,64,512]{2,1,0:T(8,128)S(1)}, f32[4,64,512]{2,1,0:T(8,128)}, u32[]{:S(2)}) copy-start(f32[4,64,512]{2,1,0:T(8,128)} %refs_1_.3) | copy-start | bytes 1572868
  3.2 10.4 %collective-permute-start = (bf16[144,512]{1,0:T(8,128)(2,1)}, bf16[144,512]{1,0:T(8,128)(2,1)S(1)}, u32[]{:S(2)}, u32[]{:S(2)}) collective-permute-start(bf16[144,512]{1,0:T(8,128)(2,1)} %get-tuple-element.41), channel_id=1, source_target_pairs={{0,4},{4,8},{8,12},{1,5},{5,9},{9,13},{2,6},{6,10},{10,14},{3,7},{... | collective-permute-start | bytes 442376 | tf_op jit(solution)/shard_map/ppermute | solution.py:698
  8.1 7.4 %collective-permute-start.1 = (bf16[144,512]{1,0:T(8,128)(2,1)}, bf16[144,512]{1,0:T(8,128)(2,1)S(1)}, u32[]{:S(2)}, u32[]{:S(2)}) collective-permute-start(bf16[144,512]{1,0:T(8,128)(2,1)} %get-tuple-element.42), channel_id=1, source_target_pairs={{4,0},{8,4},{12,8},{5,1},{9,5},{13,9},{6,2},{10,6},{14,10},{7,3},{... | collective-permute-start | bytes 442376 | tf_op jit(solution)/shard_map/ppermute | solution.py:698
  9.6 7.8 %copy-start.7 = (f32[264,512]{1,0:T(8,128)S(1)}, f32[264,512]{1,0:T(8,128)}, u32[]{:S(2)}) copy-start(f32[264,512]{1,0:T(8,128)} %refs_6_.1) | copy-start | bytes 1622020
  9.6 7.8 %copy-start.8 = (bf16[128,256]{1,0:T(8,128)(2,1)S(1)}, bf16[128,256]{1,0:T(8,128)(2,1)}, u32[]{:S(2)}) copy-start(bf16[128,256]{1,0:T(8,128)(2,1)} %refs_3_.5) | copy-start | bytes 196612
  9.6 7.8 %copy-start.9 = (f32[512,16]{0,1:T(8,128)S(1)}, f32[512,16]{0,1:T(8,128)}, u32[]{:S(2)}) copy-start(f32[512,16]{0,1:T(8,128)} %param.20) | copy-start | bytes 98308
  9.6 7.8 %copy-start.10 = (f32[512]{0:T(512)S(1)}, f32[512]{0:T(512)}, u32[]{:S(2)}) copy-start(f32[512]{0:T(512)} %param.19) | copy-start | bytes 6148
  15.8 4.3 %collective-permute-start.2 = (bf16[256,128]{1,0:T(8,128)(2,1)S(1)}, bf16[256,128]{1,0:T(8,128)(2,1)S(1)}, u32[]{:S(2)}, u32[]{:S(2)}) collective-permute-start(bf16[256,128]{1,0:T(8,128)(2,1)S(1)} %rim.1.refs_10_), channel_id=1, source_target_pairs={{0,16},{16,0},{1,17},{17,1},{2,18},{18,2},{3,19},{19,3},{4,20},{20... | collective-permute-start | bytes 196616 | tf_op jit(solution)/shard_map/ppermute | solution.py:693
  29.1 4.2 %collective-permute-start.3 = (f32[32,256]{1,0:T(8,128)S(1)}, f32[32,256]{1,0:T(8,128)S(1)}, u32[]{:S(2)}, u32[]{:S(2)}) collective-permute-start(f32[32,256]{1,0:T(8,128)S(1)} %bitcast.9), channel_id=1, source_target_pairs={{0,16},{16,0},{1,17},{17,1},{2,18},{18,2},{3,19},{19,3},{4,20},{20... | collective-permute-start | bytes 98312 | tf_op jit(solution)/shard_map/ppermute | solution.py:703
  30.7 2.6 %copy-start.6 = (f32[16]{0:T(128)S(1)}, f32[16]{0:T(128)}, u32[]{:S(2)}) copy-start(f32[16]{0:T(128)} %param.21) | copy-start | bytes 196
  34.8 1.7 %collective-permute-start.4 = (f32[64,256]{1,0:T(8,128)S(1)}, f32[64,256]{1,0:T(8,128)S(1)}, u32[]{:S(2)}, u32[]{:S(2)}) collective-permute-start(f32[64,256]{1,0:T(8,128)S(1)} %get-tuple-element.69), channel_id=1, source_target_pairs={{0,1},{1,0},{2,3},{3,2},{4,5},{5,4},{6,7},{7,6},{8,9},{9,8},{10,11... | collective-permute-start | bytes 196616 | tf_op jit(solution)/shard_map/ppermute | solution.py:703
  34.9 5.2 %collective-permute-start.10 = (f16[32,256]{1,0:T(8,128)(2,1)S(1)}, f16[32,256]{1,0:T(8,128)(2,1)S(1)}, u32[]{:S(2)}, u32[]{:S(2)}) collective-permute-start(f16[32,256]{1,0:T(8,128)(2,1)S(1)} %multiply_convert_fusion), channel_id=1, source_target_pairs={{0,2},{1,3},{2,0},{3,1},{4,6},{5,7},{6,4},{7,5},{8,10},{9,11},{10,... | collective-permute-start | bytes 49160 | tf_op jit(solution)/shard_map/ppermute | solution.py:703
  36.6 4.3 %collective-permute-start.7 = (f32[64,256]{1,0:T(8,128)S(1)}, f32[64,256]{1,0:T(8,128)S(1)}, u32[]{:S(2)}, u32[]{:S(2)}) collective-permute-start(f32[64,256]{1,0:T(8,128)S(1)} %add.21), channel_id=1, source_target_pairs={{0,16},{16,0},{1,17},{17,1},{2,18},{18,2},{3,19},{19,3},{4,20},{20... | collective-permute-start | bytes 196616 | tf_op jit(solution)/shard_map/ppermute | solution.py:703
  37.9 5.6 %collective-permute-start.6 = (f32[64,256]{1,0:T(8,128)S(1)}, f32[64,256]{1,0:T(8,128)S(1)}, u32[]{:S(2)}, u32[]{:S(2)}) collective-permute-start(f32[64,256]{1,0:T(8,128)S(1)} %add.21), channel_id=1, source_target_pairs={{0,2},{1,3},{2,0},{3,1},{4,6},{5,7},{6,4},{7,5},{8,10},{9,11},{10,... | collective-permute-start | bytes 196616 | tf_op jit(solution)/shard_map/ppermute | solution.py:703
  39.1 5.2 %collective-permute-start.5 = (f32[64,256]{1,0:T(8,128)S(1)}, f32[64,256]{1,0:T(8,128)S(1)}, u32[]{:S(2)}, u32[]{:S(2)}) collective-permute-start(f32[64,256]{1,0:T(8,128)S(1)} %add.21), channel_id=1, source_target_pairs={{0,18},{1,19},{2,16},{3,17},{16,2},{17,3},{18,0},{19,1},{4,22},{5,... | collective-permute-start | bytes 196616 | tf_op jit(solution)/shard_map/ppermute | solution.py:893
  40.9 6.0 %collective-permute-start.11 = (f16[64,256]{1,0:T(8,128)(2,1)S(1)}, f16[64,256]{1,0:T(8,128)(2,1)S(1)}, u32[]{:S(2)}, u32[]{:S(2)}) collective-permute-start(f16[64,256]{1,0:T(8,128)(2,1)S(1)} %pad_maximum_fusion.2), channel_id=1, source_target_pairs={{0,8},{4,12},{8,0},{12,4},{1,9},{5,13},{9,1},{13,5},{2,10},{6,14},... | collective-permute-start | bytes 98312 | tf_op jit(solution)/shard_map/ppermute | solution.py:703
  44.3 5.2 %collective-permute-start.8 = (f32[64,256]{1,0:T(8,128)S(1)}, f32[64,256]{1,0:T(8,128)S(1)}, u32[]{:S(2)}, u32[]{:S(2)}) collective-permute-start(f32[64,256]{1,0:T(8,128)S(1)} %add_add_fusion), channel_id=1, source_target_pairs={{0,8},{4,12},{8,0},{12,4},{1,9},{5,13},{9,1},{13,5},{2,10},{6,14},... | collective-permute-start | bytes 196616 | tf_op jit(solution)/shard_map/ppermute | solution.py:703
  46.9 4.3 %collective-permute-start.12 = (f16[128,256]{1,0:T(8,128)(2,1)S(1)}, f16[128,256]{1,0:T(8,128)(2,1)S(1)}, u32[]{:S(2)}, u32[]{:S(2)}) collective-permute-start(f16[128,256]{1,0:T(8,128)(2,1)S(1)} %pad_maximum_fusion.1), channel_id=1, source_target_pairs={{0,4},{4,0},{8,12},{12,8},{1,5},{5,1},{9,13},{13,9},{2,6},{6,2},{1... | collective-permute-start | bytes 196616 | tf_op jit(solution)/shard_map/ppermute | solution.py:703
  51.3 1.4 %collective-permute-start.13 = (f16[256,256]{1,0:T(8,128)(2,1)S(1)}, f16[256,256]{1,0:T(8,128)(2,1)S(1)}, u32[]{:S(2)}, u32[]{:S(2)}) collective-permute-start(f16[256,256]{1,0:T(8,128)(2,1)S(1)} %pad_maximum_fusion), channel_id=1, source_target_pairs={{0,1},{1,0},{2,3},{3,2},{4,5},{5,4},{6,7},{7,6},{8,9},{9,8},{10,11... | collective-permute-start | bytes 393224 | tf_op jit(solution)/shard_map/ppermute | solution.py:703
  51.4 4.5 %collective-permute-start.9 = (f32[64,256]{1,0:T(8,128)S(1)}, f32[64,256]{1,0:T(8,128)S(1)}, u32[]{:S(2)}, u32[]{:S(2)}) collective-permute-start(f32[64,256]{1,0:T(8,128)S(1)} %add.25), channel_id=1, source_target_pairs={{0,4},{4,0},{8,12},{12,8},{1,5},{5,1},{9,13},{13,9},{2,6},{6,2},{1... | collective-permute-start | bytes 196616 | tf_op jit(solution)/shard_map/ppermute | solution.py:703
  55.9 1.3 %collective-permute-start.14 = (f32[64,256]{1,0:T(8,128)S(1)}, f32[64,256]{1,0:T(8,128)S(1)}, u32[]{:S(2)}, u32[]{:S(2)}) collective-permute-start(f32[64,256]{1,0:T(8,128)S(1)} %add.27.refs_0_), channel_id=1, source_target_pairs={{0,1},{1,0},{2,3},{3,2},{4,5},{5,4},{6,7},{7,6},{8,9},{9,8},{10,11... | collective-permute-start | bytes 196616 | tf_op jit(solution)/shard_map/ppermute | solution.py:703

commit v7 on v6

--- a/solution.py
+++ b/solution.py
@@ -350,7 +350,7 @@
                 vel[i - 1, m] = part * GRAVITY
 
 
-def flow_step(src, src_rim, dst, dst_rim, force, force_rim, hus, hvs, hvus, cu, cv, cv_up, last_mask, rows, patches):
+def flow_step(src, src_rim, dst, dst_rim, force, force_rim, hus, hvs, hvus, cu, cv, cv_up, last_mask, rows, patches, ending):
     strip = PW
     wide = rows + 2 * HALO
     start = PAD - HALO
@@ -388,15 +388,16 @@
     e_rim = src_rim[1, here, :]
     fx_rim = hus[strip][here, :] * e_rim
     level_rim, n_rim, vs_rim = new_level(strip, fx_rim, pltpu.roll(fx_rim, LANES - 1, 1))
-    new_flow(
-        strip,
-        e_rim,
-        pltpu.roll(e_rim, LANES - 1, 1),
-        n_rim,
-        vs_rim + pltpu.roll(vs_rim, 1, 1),
-        level_rim,
-        pltpu.roll(level_rim, 1, 1),
-    )
+    if not ending:
+        new_flow(
+            strip,
+            e_rim,
+            pltpu.roll(e_rim, LANES - 1, 1),
+            n_rim,
+            vs_rim + pltpu.roll(vs_rim, 1, 1),
+            level_rim,
+            pltpu.roll(level_rim, 1, 1),
+        )
     e = src[1, 0, here, :]
     e_end = wrap_right(e, e_rim)
     level_last, n_last, vs_last = new_level(
@@ -508,19 +509,17 @@
                 patch_t[m], slope[m], (((0,), (0,)), ((), ())), preferred_element_type=F32
             )
 
-    def step_of(src, src_rim, dst, dst_rim):
+    def step_of(src, src_rim, dst, dst_rim, ending=False):
         flow_step(
-            src, src_rim, dst, dst_rim, force, force_rim, hus, hvs, hvus, cu, cv, cv_up, last_mask, rows, patches
+            src, src_rim, dst, dst_rim, force, force_rim, hus, hvs, hvus, cu, cv, cv_up, last_mask, rows, patches, ending
         )
 
-    def two_steps(turn, carry):
-        step_of(state_a, rim_a, state_b, rim_b)
-        embed_step(state_a, jnp.maximum(turn - 1, 0), 1)
-        step_of(state_b, rim_b, state_a, rim_a)
-        embed_step(state_b, turn, 0)
-        return carry
-
-    lax.fori_loop(0, STEPS // 2, two_steps, 0)
+    one, two = (state_a, rim_a), (state_b, rim_b)
+    step_of(*one, *two)
+    for step in range(1, STEPS):
+        src, dst = (two, one) if step % 2 else (one, two)
+        step_of(*src, *dst, step == STEPS - 1)
+        embed_step(src[0], (step - 1) // 2, (step - 1) % 2)
     inner = slice(PAD, PAD + rows)
     final[:, :, inner, :] = state_a[:, :, inner, :]
     embed_step(state_a, STEPS // 2 - 1, 1)

time: 58.5 us -> 57.4 us (0.981)
  Pallas kernels: 24.9 us -> 23.8 us
    pallas_call x1, Pallas kernels: 8.96 us -> 8.03 us  [shards(): pl.pallas_call(lambda *refs: flow_kernel(members, rows, cols, lat_count,...]
  transfers between devices with their start and end apart: 15 -> 15, of which waited for: 9 -> 9; matrix products, arithmetic and copies ran while one was open for 0% -> 0% of each run, Pallas kernels for 18% -> 19%
where the time goes in v7:
time: 57.4 us; the launch traced here: 57.2 us
  Pallas kernels  23.8 us (41%)
  starting transfers between devices  21.4 us (37%)
  waiting for transfers between devices  10.8 us (19%)
  between operations  0.88 us (2%)
    ppermute x11, starting transfers between devices, swapped(): return lax.ppermute(value, axis, [(i, i ^ flip) for i in range(count)])  12.5 us
    pallas_call x1, Pallas kernels, shards(): pl.pallas_call(lambda *refs: flow_kernel(members, rows, cols, lat_count,...  8.03 us
    ppermute x11, waiting for transfers between devices, swapped(): return lax.ppermute(value, axis, [(i, i ^ flip) for i in range(count)])  6.91 us
    ppermute x2, starting transfers between devices, from_lat(): lax.ppermute(value, 'lat', [(i, i + step) for i in range(count) if 0 <= i...  6.23 us
    pallas_call x1, Pallas kernels, shards(): pl.pallas_call(lambda *refs: planar_kernel(members, *refs), out_shape=(sh...  3.92 us
    pallas_call x1, Pallas kernels, shards(): pl.pallas_call(lambda *refs: back_kernel(members, *refs), out_shape=(shap...  2.62 us
    pallas_call x1, Pallas kernels, shards(): pl.pallas_call(lambda *refs: pack_kernel(members, *refs), out_shape=(shap...  2.49 us
    pallas_call x1, Pallas kernels, shards(): pl.pallas_call(lambda *refs: couple_kernel(members, lat_count, grp_count,...  2.43 us
  transfers between devices with their start and end apart: 15, of which 9 were waited for; matrix products, arithmetic and copies ran while one was open for 0% of the time, Pallas kernels for 19%

profile of v7, /device:TPU:0, one launch (start us, length us, event | category | flops | bytes accessed | tf_op | source)
XLA Modules:
  0.0 57.2 jit_solution(8767997124917678139)
XLA Ops:
  0.6 0.0 copy-start.5
  0.6 0.0 copy-start.4
  0.7 0.0 copy-start.1
  0.7 0.0 copy-start.3
  0.7 2.5 %pack_rows.1 = (bf16[144,512]{1,0:T(8,128)(2,1)}, bf16[144,512]{1,0:T(8,128)(2,1)}) custom-call(s32[16]{0:T(128)} %refs_0_.3, f32[4,64,512]{2,1,0:T(8,128)} %refs_1_.3, f32[2,4,64,512]{3,2,1,0:T(8,128)} %refs_2_.3, s32[64,512]{1,0:T(8,128)} %refs_3_.4, bf16[16,64,512]{2,1,0:T(8,128)(2,1)} %refs_4_.3, f32[16,16]{1,0:T(8,128)} %refs_5_.5), custom_call_target="tpu_custom_call" | custom-call | tf_op jit(solution)/shard_map/pack_rows/pallas_call | solution.py:739
  3.2 4.9 %collective-permute-start = (bf16[144,512]{1,0:T(8,128)(2,1)}, bf16[144,512]{1,0:T(8,128)(2,1)S(1)}, u32[]{:S(2)}, u32[]{:S(2)}) collective-permute-start(bf16[144,512]{1,0:T(8,128)(2,1)} %get-tuple-element.41), channel_id=1, source_target_pairs={{0,4},{4,8},{8,12},{1,5},{5,9},{9,13},{2,6},{6,10},{10,14},{3,7},{... | collective-permute-start | bytes 442376 | tf_op jit(solution)/shard_map/ppermute | solution.py:697
  8.1 1.3 %collective-permute-start.1 = (bf16[144,512]{1,0:T(8,128)(2,1)}, bf16[144,512]{1,0:T(8,128)(2,1)S(1)}, u32[]{:S(2)}, u32[]{:S(2)}) collective-permute-start(bf16[144,512]{1,0:T(8,128)(2,1)} %get-tuple-element.42), channel_id=1, source_target_pairs={{4,0},{8,4},{12,8},{5,1},{9,5},{13,9},{6,2},{10,6},{14,10},{7,3},{... | collective-permute-start | bytes 442376 | tf_op jit(solution)/shard_map/ppermute | solution.py:697
  9.4 0.1 copy.15.refs_4_
  9.6 0.0 copy-start.7
  9.6 0.0 copy-start.8
  9.6 0.0 copy-start.9
  9.6 0.0 copy-start.10
  9.6 3.9 %to_planes.1 = (f32[5,16,64,128]{3,2,1,0:T(8,128)S(1)}, bf16[384,128]{1,0:T(8,128)(2,1)S(1)}) custom-call(s32[16]{0:T(128)S(1)} %copy-done.5, f32[4,64,512]{2,1,0:T(8,128)S(1)} %copy-done.2, f32[2,4,64,512]{3,2,1,0:T(8,128)S(1)} %copy-done, s32[64,512]{1,0:T(8,128)S(1)} %copy-done.3, bf16[16,64,512]{2,1,0:T(8,128)(2,1)S(1)} %copy-done.1, f32[16,16]{1,0:T(8,128)S(1)} %copy-done.4), custom_call_target="tpu_custom_call" | custom-call | flops 2000000000 | bytes 6291456 | tf_op jit(solution)/shard_map/to_planes/pallas_call | solution.py:759
  13.5 0.0 collective-permute-done.refs_0_
  13.5 2.0 %collective-permute-done.1.refs_1_ = bf16[144,512]{1,0:T(8,128)(2,1)S(1)} collective-permute-done((bf16[144,512]{1,0:T(8,128)(2,1)}, bf16[144,512]{1,0:T(8,128)(2,1)S(1)}, u32[]{:S(2)}, u32[]{:S(2)}) %collective-permute-start.1) | collective-permute-done | bytes 147488 | tf_op jit(solution)/shard_map/ppermute | solution.py:697
  15.5 0.3 rim.1.refs_10_
  15.8 1.6 %collective-permute-start.2 = (bf16[256,128]{1,0:T(8,128)(2,1)S(1)}, bf16[256,128]{1,0:T(8,128)(2,1)S(1)}, u32[]{:S(2)}, u32[]{:S(2)}) collective-permute-start(bf16[256,128]{1,0:T(8,128)(2,1)S(1)} %rim.1.refs_10_), channel_id=1, source_target_pairs={{0,16},{16,0},{1,17},{17,1},{2,18},{18,2},{3,19},{19,3},{4,20},{20... | collective-permute-start | bytes 196616 | tf_op jit(solution)/shard_map/ppermute | solution.py:692
  17.4 1.6 %prepare.1 = (f32[3,16,104,128]{3,2,1,0:T(8,128)S(1)}, f32[16,104,128]{2,1,0:T(8,128)S(1)}, f32[2,96,128]{2,1,0:T(8,128)S(1)}, f32[16,104,128]{2,1,0:T(8,128)S(1...) custom-call(bf16[144,512]{1,0:T(8,128)(2,1)S(1)} %collective-permute, ...), custom_call_target="tpu_custom_call" | custom-call | flops 1000000000 | bytes 4194304 | tf_op jit(solution)/shard_map/prepare/pallas_call | solution.py:786
  19.0 1.1 %collective-permute-done.2.refs_11_.refs_12_ = bf16[256,128]{1,0:T(8,128)(2,1)S(1)} collective-permute-done((bf16[256,128]{1,0:T(8,128)(2,1)S(1)}, bf16[256,128]{1,0:T(8,128)(2,1)S(1)}, u32[]{:S(2)}, u32[]{:S(2)}) %collective-permute-start.2) | collective-permute-done | bytes 65568 | tf_op jit(solution)/shard_map/ppermute | solution.py:692
  20.2 8.0 %flow_embed.1 = (f32[4,8,256]{2,1,0:T(8,128)S(1)}, f32[32,128,256]{2,1,0:T(8,128)S(1)}, f32[3,16,104,128]{3,2,1,0:T(8,128)S(1)}) custom-call(f32[3,16,104,128]{3,2,1,0:T(8,128)S(1)} %get-tuple-element.44.refs_0_, f32[16,104,128]{2,1,0:T(8,128)S(1)} %get-tuple-element.45.refs_1_, f32[2,96,128]{2,1,0:T(8,128)S(1)} %get-tuple-element.46.refs_2_, ...), custom_call_target="tpu_custom_call" | custom-call | tf_op jit(solution)/shard_map/flow_embed/pallas_call | solution.py:828
  28.2 1.6 %collective-permute-start.3 = (f32[32,256]{1,0:T(8,128)S(1)}, f32[32,256]{1,0:T(8,128)S(1)}, u32[]{:S(2)}, u32[]{:S(2)}) collective-permute-start(f32[32,256]{1,0:T(8,128)S(1)} %bitcast.9), channel_id=1, source_target_pairs={{0,16},{16,0},{1,17},{17,1},{2,18},{18,2},{3,19},{19,3},{4,20},{20... | collective-permute-start | bytes 98312 | tf_op jit(solution)/shard_map/ppermute | solution.py:702
  29.8 2.6 %from_planes.1 = (f32[4,64,512]{2,1,0:T(8,128)}, f32[2,4,64,512]{3,2,1,0:T(8,128)}) custom-call(f32[3,16,104,128]{3,2,1,0:T(8,128)S(1)} %get-tuple-element.56.refs_0_), custom_call_target="tpu_custom_call" | custom-call | flops 2000000000 | bytes 6291456 | tf_op jit(solution)/shard_map/from_planes/pallas_call | solution.py:860
  32.4 0.0 collective-permute-done.3.refs_1_
  32.4 1.4 %local_loss.1 = (f32[64,256]{1,0:T(8,128)S(1)}, f32[64,256]{1,0:T(8,128)S(1)}, f32[16,256]{1,0:T(8,128)}) custom-call(f32[32,256]{1,0:T(8,128)S(1)} %bitcast.10, f32[32,256]{1,0:T(8,128)S(1)} %collective-permute-done.3.refs_1_, f32[32,512]{1,0:T(8,128)S(1)} %get-tuple-element.62.refs_2_, f32[32,8]{1,0:T(8,128)S(1)} %get-tuple-element.63.refs_3_, ...), custom_call_target="tpu_custom_call" | custom-call | tf_op jit(solution)/shard_map/local_loss/pallas_call | solution.py:874
  33.8 0.1 collective-permute-start.4
  33.8 1.6 %collective-permute-start.10 = (f16[32,256]{1,0:T(8,128)(2,1)S(1)}, f16[32,256]{1,0:T(8,128)(2,1)S(1)}, u32[]{:S(2)}, u32[]{:S(2)}) collective-permute-start(f16[32,256]{1,0:T(8,128)(2,1)S(1)} %multiply_convert_fusion), channel_id=1, source_target_pairs={{0,2},{1,3},{2,0},{3,1},{4,6},{5,7},{6,4},{7,5},{8,10},{9,11},{10,... | collective-permute-start | bytes 49160 | tf_op jit(solution)/shard_map/ppermute | solution.py:702
  35.4 0.0 collective-permute-done.4
  35.4 1.4 %collective-permute-start.7 = (f32[64,256]{1,0:T(8,128)S(1)}, f32[64,256]{1,0:T(8,128)S(1)}, u32[]{:S(2)}, u32[]{:S(2)}) collective-permute-start(f32[64,256]{1,0:T(8,128)S(1)} %add.21), channel_id=1, source_target_pairs={{0,16},{16,0},{1,17},{17,1},{2,18},{18,2},{3,19},{19,3},{4,20},{20... | collective-permute-start | bytes 196616 | tf_op jit(solution)/shard_map/ppermute | solution.py:702
  36.8 1.2 %collective-permute-start.6 = (f32[64,256]{1,0:T(8,128)S(1)}, f32[64,256]{1,0:T(8,128)S(1)}, u32[]{:S(2)}, u32[]{:S(2)}) collective-permute-start(f32[64,256]{1,0:T(8,128)S(1)} %add.21), channel_id=1, source_target_pairs={{0,2},{1,3},{2,0},{3,1},{4,6},{5,7},{6,4},{7,5},{8,10},{9,11},{10,... | collective-permute-start | bytes 196616 | tf_op jit(solution)/shard_map/ppermute | solution.py:702
  38.0 1.0 %collective-permute-start.5 = (f32[64,256]{1,0:T(8,128)S(1)}, f32[64,256]{1,0:T(8,128)S(1)}, u32[]{:S(2)}, u32[]{:S(2)}) collective-permute-start(f32[64,256]{1,0:T(8,128)S(1)} %add.21), channel_id=1, source_target_pairs={{0,18},{1,19},{2,16},{3,17},{16,2},{17,3},{18,0},{19,1},{4,22},{5,... | collective-permute-start | bytes 196616 | tf_op jit(solution)/shard_map/ppermute | solution.py:892
  39.0 0.0 collective-permute-done.10
  39.0 0.8 %collective-permute-done.7 = f32[64,256]{1,0:T(8,128)S(1)} collective-permute-done((f32[64,256]{1,0:T(8,128)S(1)}, f32[64,256]{1,0:T(8,128)S(1)}, u32[]{:S(2)}, u32[]{:S(2)}) %collective-permute-start.7) | collective-permute-done | bytes 65568 | tf_op jit(solution)/shard_map/ppermute | solution.py:702
  39.8 2.6 %collective-permute-start.11 = (f16[64,256]{1,0:T(8,128)(2,1)S(1)}, f16[64,256]{1,0:T(8,128)(2,1)S(1)}, u32[]{:S(2)}, u32[]{:S(2)}) collective-permute-start(f16[64,256]{1,0:T(8,128)(2,1)S(1)} %pad_maximum_fusion.2), channel_id=1, source_target_pairs={{0,8},{4,12},{8,0},{12,4},{1,9},{5,13},{9,1},{13,5},{2,10},{6,14},... | collective-permute-start | bytes 98312 | tf_op jit(solution)/shard_map/ppermute | solution.py:702
  42.4 0.0 collective-permute-done.6
  42.4 0.8 %collective-permute-done.5 = f32[64,256]{1,0:T(8,128)S(1)} collective-permute-done((f32[64,256]{1,0:T(8,128)S(1)}, f32[64,256]{1,0:T(8,128)S(1)}, u32[]{:S(2)}, u32[]{:S(2)}) %collective-permute-start.5) | collective-permute-done | bytes 65568 | tf_op jit(solution)/shard_map/ppermute | solution.py:892
  43.1 2.6 %collective-permute-start.8 = (f32[64,256]{1,0:T(8,128)S(1)}, f32[64,256]{1,0:T(8,128)S(1)}, u32[]{:S(2)}, u32[]{:S(2)}) collective-permute-start(f32[64,256]{1,0:T(8,128)S(1)} %add_add_fusion), channel_id=1, source_target_pairs={{0,8},{4,12},{8,0},{12,4},{1,9},{5,13},{9,1},{13,5},{2,10},{6,14},... | collective-permute-start | bytes 196616 | tf_op jit(solution)/shard_map/ppermute | solution.py:702
  45.8 0.0 collective-permute-done.11
  45.8 0.7 %collective-permute-start.12 = (f16[128,256]{1,0:T(8,128)(2,1)S(1)}, f16[128,256]{1,0:T(8,128)(2,1)S(1)}, u32[]{:S(2)}, u32[]{:S(2)}) collective-permute-start(f16[128,256]{1,0:T(8,128)(2,1)S(1)} %pad_maximum_fusion.1), channel_id=1, source_target_pairs={{0,4},{4,0},{8,12},{12,8},{1,5},{5,1},{9,13},{13,9},{2,6},{6,2},{1... | collective-permute-start | bytes 196616 | tf_op jit(solution)/shard_map/ppermute | solution.py:702
  46.5 1.8 %collective-permute-done.8 = f32[64,256]{1,0:T(8,128)S(1)} collective-permute-done((f32[64,256]{1,0:T(8,128)S(1)}, f32[64,256]{1,0:T(8,128)S(1)}, u32[]{:S(2)}, u32[]{:S(2)}) %collective-permute-start.8) | collective-permute-done | bytes 65568 | tf_op jit(solution)/shard_map/ppermute | solution.py:702
  48.4 1.8 %collective-permute-done.12 = f16[128,256]{1,0:T(8,128)(2,1)S(1)} collective-permute-done((f16[128,256]{1,0:T(8,128)(2,1)S(1)}, f16[128,256]{1,0:T(8,128)(2,1)S(1)}, u32[]{:S(2)}, u32[]{:S(2)}) %collective-permute-start.12) | collective-permute-done | bytes 65568 | tf_op jit(solution)/shard_map/ppermute | solution.py:702
  50.2 0.1 collective-permute-start.13
  50.3 0.7 %collective-permute-start.9 = (f32[64,256]{1,0:T(8,128)S(1)}, f32[64,256]{1,0:T(8,128)S(1)}, u32[]{:S(2)}, u32[]{:S(2)}) collective-permute-start(f32[64,256]{1,0:T(8,128)S(1)} %add.25), channel_id=1, source_target_pairs={{0,4},{4,0},{8,12},{12,8},{1,5},{5,1},{9,13},{13,9},{2,6},{6,2},{1... | collective-permute-start | bytes 196616 | tf_op jit(solution)/shard_map/ppermute | solution.py:702
  51.0 0.6 %collective-permute-done.13 = f16[256,256]{1,0:T(8,128)(2,1)S(1)} collective-permute-done((f16[256,256]{1,0:T(8,128)(2,1)S(1)}, f16[256,256]{1,0:T(8,128)(2,1)S(1)}, u32[]{:S(2)}, u32[]{:S(2)}) %collective-permute-start.13) | collective-permute-done | bytes 131104 | tf_op jit(solution)/shard_map/ppermute | solution.py:702
  51.6 2.4 %couple_grads.1 = (f32[1128,128]{1,0:T(8,128)S(1)}, f32[1,128]{1,0:T(1,128)S(1)}) custom-call(f32[512,256]{1,0:T(8,128)S(1)} %maximum_convert_fusion.refs_0_, f32[16,512]{1,0:T(8,128)S(1)} %get-tuple-element.73.refs_1_, f32[16,16]{1,0:T(8,128)S(1)} %get-tuple-element.74.refs_2_, bf16[2,256,512]{2,1,0:T(8,128)(2,1)S(1)} %get-tuple-element.64.refs_4_.refs_3_, ...), custom_call_target="tpu_custom_call" | custom-call | flops 3000000000 | bytes 3145728 | tf_op jit(solution)/shard_map/couple_grads/pallas_call | solution.py:917
  54.1 0.7 %collective-permute-done.9 = f32[64,256]{1,0:T(8,128)S(1)} collective-permute-done((f32[64,256]{1,0:T(8,128)S(1)}, f32[64,256]{1,0:T(8,128)S(1)}, u32[]{:S(2)}, u32[]{:S(2)}) %collective-permute-start.9) | collective-permute-done | bytes 65568 | tf_op jit(solution)/shard_map/ppermute | solution.py:702
  54.8 0.1 collective-permute-start.14
  54.9 1.2 %collective-permute-done.14.refs_1_ = f32[64,256]{1,0:T(8,128)S(1)} collective-permute-done((f32[64,256]{1,0:T(8,128)S(1)}, f32[64,256]{1,0:T(8,128)S(1)}, u32[]{:S(2)}, u32[]{:S(2)}) %collective-permute-start.14) | collective-permute-done | bytes 65568 | tf_op jit(solution)/shard_map/ppermute | solution.py:702
  56.1 1.1 %finish.1 = f32[1384,128]{1,0:T(8,128)} custom-call(f32[64,256]{1,0:T(8,128)S(1)} %add.27.refs_0_, f32[64,256]{1,0:T(8,128)S(1)} %collective-permute-done.14.refs_1_, f32[1128,128]{1,0:T(8,128)S(1)} %get-tuple-element.75.refs_2_, f32[1,128]{1,0:T(1,128)S(1)} %get-tuple-element.76.refs_3_), custom_call_target="tpu_custom_call" | custom-call | tf_op jit(solution)/shard_map/finish/pallas_call | solution.py:934
  (23 shorter events, 0.2 us)
Async XLA Ops:
  0.6 8.8 %copy-start.5 = (s32[16]{0:T(128)S(1)}, s32[16]{0:T(128)}, u32[]{:S(2)}) copy-start(s32[16]{0:T(128)} %refs_0_.3) | copy-start | bytes 196
  0.6 8.9 %copy-start.4 = (f32[16,16]{1,0:T(8,128)S(1)}, f32[16,16]{1,0:T(8,128)}, u32[]{:S(2)}) copy-start(f32[16,16]{1,0:T(8,128)} %refs_5_.5) | copy-start | bytes 3076
  0.7 8.9 %copy-start.1 = (bf16[16,64,512]{2,1,0:T(8,128)(2,1)S(1)}, bf16[16,64,512]{2,1,0:T(8,128)(2,1)}, u32[]{:S(2)}) copy-start(bf16[16,64,512]{2,1,0:T(8,128)(2,1)} %refs_4_.3) | copy-start | bytes 3145732
  0.7 8.9 %copy-start.3 = (s32[64,512]{1,0:T(8,128)S(1)}, s32[64,512]{1,0:T(8,128)}, u32[]{:S(2)}) copy-start(s32[64,512]{1,0:T(8,128)} %refs_3_.4) | copy-start | bytes 393220
  0.7 8.9 %copy-start = (f32[2,4,64,512]{3,2,1,0:T(8,128)S(1)}, f32[2,4,64,512]{3,2,1,0:T(8,128)}, u32[]{:S(2)}) copy-start(f32[2,4,64,512]{3,2,1,0:T(8,128)} %refs_2_.3) | copy-start | bytes 3145732
  0.7 8.9 %copy-start.2 = (f32[4,64,512]{2,1,0:T(8,128)S(1)}, f32[4,64,512]{2,1,0:T(8,128)}, u32[]{:S(2)}) copy-start(f32[4,64,512]{2,1,0:T(8,128)} %refs_1_.3) | copy-start | bytes 1572868
  3.2 10.4 %collective-permute-start = (bf16[144,512]{1,0:T(8,128)(2,1)}, bf16[144,512]{1,0:T(8,128)(2,1)S(1)}, u32[]{:S(2)}, u32[]{:S(2)}) collective-permute-start(bf16[144,512]{1,0:T(8,128)(2,1)} %get-tuple-element.41), channel_id=1, source_target_pairs={{0,4},{4,8},{8,12},{1,5},{5,9},{9,13},{2,6},{6,10},{10,14},{3,7},{... | collective-permute-start | bytes 442376 | tf_op jit(solution)/shard_map/ppermute | solution.py:697
  8.1 7.4 %collective-permute-start.1 = (bf16[144,512]{1,0:T(8,128)(2,1)}, bf16[144,512]{1,0:T(8,128)(2,1)S(1)}, u32[]{:S(2)}, u32[]{:S(2)}) collective-permute-start(bf16[144,512]{1,0:T(8,128)(2,1)} %get-tuple-element.42), channel_id=1, source_target_pairs={{4,0},{8,4},{12,8},{5,1},{9,5},{13,9},{6,2},{10,6},{14,10},{7,3},{... | collective-permute-start | bytes 442376 | tf_op jit(solution)/shard_map/ppermute | solution.py:697
  9.6 7.8 %copy-start.7 = (f32[264,512]{1,0:T(8,128)S(1)}, f32[264,512]{1,0:T(8,128)}, u32[]{:S(2)}) copy-start(f32[264,512]{1,0:T(8,128)} %refs_6_.1) | copy-start | bytes 1622020
  9.6 7.8 %copy-start.8 = (bf16[128,256]{1,0:T(8,128)(2,1)S(1)}, bf16[128,256]{1,0:T(8,128)(2,1)}, u32[]{:S(2)}) copy-start(bf16[128,256]{1,0:T(8,128)(2,1)} %refs_3_.5) | copy-start | bytes 196612
  9.6 7.8 %copy-start.9 = (f32[512,16]{0,1:T(8,128)S(1)}, f32[512,16]{0,1:T(8,128)}, u32[]{:S(2)}) copy-start(f32[512,16]{0,1:T(8,128)} %param.20) | copy-start | bytes 98308
  9.6 7.8 %copy-start.10 = (f32[512]{0:T(512)S(1)}, f32[512]{0:T(512)}, u32[]{:S(2)}) copy-start(f32[512]{0:T(512)} %param.19) | copy-start | bytes 6148
  15.8 4.3 %collective-permute-start.2 = (bf16[256,128]{1,0:T(8,128)(2,1)S(1)}, bf16[256,128]{1,0:T(8,128)(2,1)S(1)}, u32[]{:S(2)}, u32[]{:S(2)}) collective-permute-start(bf16[256,128]{1,0:T(8,128)(2,1)S(1)} %rim.1.refs_10_), channel_id=1, source_target_pairs={{0,16},{16,0},{1,17},{17,1},{2,18},{18,2},{3,19},{19,3},{4,20},{20... | collective-permute-start | bytes 196616 | tf_op jit(solution)/shard_map/ppermute | solution.py:692
  28.2 4.2 %collective-permute-start.3 = (f32[32,256]{1,0:T(8,128)S(1)}, f32[32,256]{1,0:T(8,128)S(1)}, u32[]{:S(2)}, u32[]{:S(2)}) collective-permute-start(f32[32,256]{1,0:T(8,128)S(1)} %bitcast.9), channel_id=1, source_target_pairs={{0,16},{16,0},{1,17},{17,1},{2,18},{18,2},{3,19},{19,3},{4,20},{20... | collective-permute-start | bytes 98312 | tf_op jit(solution)/shard_map/ppermute | solution.py:702
  29.8 2.6 %copy-start.6 = (f32[16]{0:T(128)S(1)}, f32[16]{0:T(128)}, u32[]{:S(2)}) copy-start(f32[16]{0:T(128)} %param.21) | copy-start | bytes 196
  33.8 1.7 %collective-permute-start.4 = (f32[64,256]{1,0:T(8,128)S(1)}, f32[64,256]{1,0:T(8,128)S(1)}, u32[]{:S(2)}, u32[]{:S(2)}) collective-permute-start(f32[64,256]{1,0:T(8,128)S(1)} %get-tuple-element.69), channel_id=1, source_target_pairs={{0,1},{1,0},{2,3},{3,2},{4,5},{5,4},{6,7},{7,6},{8,9},{9,8},{10,11... | collective-permute-start | bytes 196616 | tf_op jit(solution)/shard_map/ppermute | solution.py:702
  33.8 5.2 %collective-permute-start.10 = (f16[32,256]{1,0:T(8,128)(2,1)S(1)}, f16[32,256]{1,0:T(8,128)(2,1)S(1)}, u32[]{:S(2)}, u32[]{:S(2)}) collective-permute-start(f16[32,256]{1,0:T(8,128)(2,1)S(1)} %multiply_convert_fusion), channel_id=1, source_target_pairs={{0,2},{1,3},{2,0},{3,1},{4,6},{5,7},{6,4},{7,5},{8,10},{9,11},{10,... | collective-permute-start | bytes 49160 | tf_op jit(solution)/shard_map/ppermute | solution.py:702
  35.4 4.3 %collective-permute-start.7 = (f32[64,256]{1,0:T(8,128)S(1)}, f32[64,256]{1,0:T(8,128)S(1)}, u32[]{:S(2)}, u32[]{:S(2)}) collective-permute-start(f32[64,256]{1,0:T(8,128)S(1)} %add.21), channel_id=1, source_target_pairs={{0,16},{16,0},{1,17},{17,1},{2,18},{18,2},{3,19},{19,3},{4,20},{20... | collective-permute-start | bytes 196616 | tf_op jit(solution)/shard_map/ppermute | solution.py:702
  36.8 5.6 %collective-permute-start.6 = (f32[64,256]{1,0:T(8,128)S(1)}, f32[64,256]{1,0:T(8,128)S(1)}, u32[]{:S(2)}, u32[]{:S(2)}) collective-permute-start(f32[64,256]{1,0:T(8,128)S(1)} %add.21), channel_id=1, source_target_pairs={{0,2},{1,3},{2,0},{3,1},{4,6},{5,7},{6,4},{7,5},{8,10},{9,11},{10,... | collective-permute-start | bytes 196616 | tf_op jit(solution)/shard_map/ppermute | solution.py:702
  38.0 5.2 %collective-permute-start.5 = (f32[64,256]{1,0:T(8,128)S(1)}, f32[64,256]{1,0:T(8,128)S(1)}, u32[]{:S(2)}, u32[]{:S(2)}) collective-permute-start(f32[64,256]{1,0:T(8,128)S(1)} %add.21), channel_id=1, source_target_pairs={{0,18},{1,19},{2,16},{3,17},{16,2},{17,3},{18,0},{19,1},{4,22},{5,... | collective-permute-start | bytes 196616 | tf_op jit(solution)/shard_map/ppermute | solution.py:892
  39.8 6.0 %collective-permute-start.11 = (f16[64,256]{1,0:T(8,128)(2,1)S(1)}, f16[64,256]{1,0:T(8,128)(2,1)S(1)}, u32[]{:S(2)}, u32[]{:S(2)}) collective-permute-start(f16[64,256]{1,0:T(8,128)(2,1)S(1)} %pad_maximum_fusion.2), channel_id=1, source_target_pairs={{0,8},{4,12},{8,0},{12,4},{1,9},{5,13},{9,1},{13,5},{2,10},{6,14},... | collective-permute-start | bytes 98312 | tf_op jit(solution)/shard_map/ppermute | solution.py:702
  43.1 5.2 %collective-permute-start.8 = (f32[64,256]{1,0:T(8,128)S(1)}, f32[64,256]{1,0:T(8,128)S(1)}, u32[]{:S(2)}, u32[]{:S(2)}) collective-permute-start(f32[64,256]{1,0:T(8,128)S(1)} %add_add_fusion), channel_id=1, source_target_pairs={{0,8},{4,12},{8,0},{12,4},{1,9},{5,13},{9,1},{13,5},{2,10},{6,14},... | collective-permute-start | bytes 196616 | tf_op jit(solution)/shard_map/ppermute | solution.py:702
  45.8 4.3 %collective-permute-start.12 = (f16[128,256]{1,0:T(8,128)(2,1)S(1)}, f16[128,256]{1,0:T(8,128)(2,1)S(1)}, u32[]{:S(2)}, u32[]{:S(2)}) collective-permute-start(f16[128,256]{1,0:T(8,128)(2,1)S(1)} %pad_maximum_fusion.1), channel_id=1, source_target_pairs={{0,4},{4,0},{8,12},{12,8},{1,5},{5,1},{9,13},{13,9},{2,6},{6,2},{1... | collective-permute-start | bytes 196616 | tf_op jit(solution)/shard_map/ppermute | solution.py:702
  50.2 1.4 %collective-permute-start.13 = (f16[256,256]{1,0:T(8,128)(2,1)S(1)}, f16[256,256]{1,0:T(8,128)(2,1)S(1)}, u32[]{:S(2)}, u32[]{:S(2)}) collective-permute-start(f16[256,256]{1,0:T(8,128)(2,1)S(1)} %pad_maximum_fusion), channel_id=1, source_target_pairs={{0,1},{1,0},{2,3},{3,2},{4,5},{5,4},{6,7},{7,6},{8,9},{9,8},{10,11... | collective-permute-start | bytes 393224 | tf_op jit(solution)/shard_map/ppermute | solution.py:702
  50.3 4.5 %collective-permute-start.9 = (f32[64,256]{1,0:T(8,128)S(1)}, f32[64,256]{1,0:T(8,128)S(1)}, u32[]{:S(2)}, u32[]{:S(2)}) collective-permute-start(f32[64,256]{1,0:T(8,128)S(1)} %add.25), channel_id=1, source_target_pairs={{0,4},{4,0},{8,12},{12,8},{1,5},{5,1},{9,13},{13,9},{2,6},{6,2},{1... | collective-permute-start | bytes 196616 | tf_op jit(solution)/shard_map/ppermute | solution.py:702
  54.8 1.3 %collective-permute-start.14 = (f32[64,256]{1,0:T(8,128)S(1)}, f32[64,256]{1,0:T(8,128)S(1)}, u32[]{:S(2)}, u32[]{:S(2)}) collective-permute-start(f32[64,256]{1,0:T(8,128)S(1)} %add.27.refs_0_), channel_id=1, source_target_pairs={{0,1},{1,0},{2,3},{3,2},{4,5},{5,4},{6,7},{7,6},{8,9},{9,8},{10,11... | collective-permute-start | bytes 196616 | tf_op jit(solution)/shard_map/ppermute | solution.py:702

commit v8 on v7

--- a/solution.py
+++ b/solution.py
@@ -130,10 +130,13 @@
     started = [pltpu.make_async_copy(a, b, sems.at[n]) for n, (a, b) in enumerate(copies)]
     for copy in started:
         copy.start()
-    for copy in started:
+    for copy in started[:2]:
         copy.wait()
     coeff = coefficients(members, ids, props)
+    each = (len(copies) - 2) // 2
     for side, out in ((0, low), (1, high)):
+        for copy in started[2 + side * each : 2 + (side + 1) * each]:
+            copy.wait()
         keep = slice(0, HALO) if side == 0 else slice(16 - HALO, 16)
         force = forcing_rows(coeff, basis.at[side], members, keep)
         blocks = [cells[side, i, m] for i in range(3) for m in range(members)]

time: 57.4 us -> 57.2 us (level)
  no operation moved by 1% of the time
where the time goes in v8:
time: 57.2 us; the launch traced here: 57 us
  Pallas kernels  23.6 us (41%)
  starting transfers between devices  21.4 us (37%)
  waiting for transfers between devices  10.8 us (19%)
  between operations  0.88 us (2%)
    ppermute x11, starting transfers between devices, swapped(): return lax.ppermute(value, axis, [(i, i ^ flip) for i in range(count)])  12.5 us
    pallas_call x1, Pallas kernels, shards(): pl.pallas_call(lambda *refs: flow_kernel(members, rows, cols, lat_count,...  8.03 us
    ppermute x11, waiting for transfers between devices, swapped(): return lax.ppermute(value, axis, [(i, i ^ flip) for i in range(count)])  6.91 us
    ppermute x2, starting transfers between devices, from_lat(): lax.ppermute(value, 'lat', [(i, i + step) for i in range(count) if 0 <= i...  6.23 us
    pallas_call x1, Pallas kernels, shards(): pl.pallas_call(lambda *refs: planar_kernel(members, *refs), out_shape=(sh...  3.92 us
    pallas_call x1, Pallas kernels, shards(): pl.pallas_call(lambda *refs: back_kernel(members, *refs), out_shape=(shap...  2.62 us
    pallas_call x1, Pallas kernels, shards(): pl.pallas_call(lambda *refs: couple_kernel(members, lat_count, grp_count,...  2.43 us
    pallas_call x1, Pallas kernels, shards(): pl.pallas_call(lambda *refs: pack_kernel(members, *refs), out_shape=(shap...  2.29 us
  transfers between devices with their start and end apart: 15, of which 9 were waited for; matrix products, arithmetic and copies ran while one was open for 0% of the time, Pallas kernels for 19%

profile of v8, /device:TPU:0, one launch (start us, length us, event | category | flops | bytes accessed | tf_op | source)
XLA Modules:
  0.0 57.0 jit_solution(11695604167342348823)
XLA Ops:
  0.6 0.0 copy-start.5
  0.6 0.0 copy-start.4
  0.7 0.0 copy-start.1
  0.7 0.0 copy-start.3
  0.7 2.3 %pack_rows.1 = (bf16[144,512]{1,0:T(8,128)(2,1)}, bf16[144,512]{1,0:T(8,128)(2,1)}) custom-call(s32[16]{0:T(128)} %refs_0_.3, f32[4,64,512]{2,1,0:T(8,128)} %refs_1_.3, f32[2,4,64,512]{3,2,1,0:T(8,128)} %refs_2_.3, s32[64,512]{1,0:T(8,128)} %refs_3_.4, bf16[16,64,512]{2,1,0:T(8,128)(2,1)} %refs_4_.3, f32[16,16]{1,0:T(8,128)} %refs_5_.5), custom_call_target="tpu_custom_call" | custom-call | tf_op jit(solution)/shard_map/pack_rows/pallas_call | solution.py:742
  3.0 4.9 %collective-permute-start = (bf16[144,512]{1,0:T(8,128)(2,1)}, bf16[144,512]{1,0:T(8,128)(2,1)S(1)}, u32[]{:S(2)}, u32[]{:S(2)}) collective-permute-start(bf16[144,512]{1,0:T(8,128)(2,1)} %get-tuple-element.41), channel_id=1, source_target_pairs={{0,4},{4,8},{8,12},{1,5},{5,9},{9,13},{2,6},{6,10},{10,14},{3,7},{... | collective-permute-start | bytes 442376 | tf_op jit(solution)/shard_map/ppermute | solution.py:700
  7.9 1.3 %collective-permute-start.1 = (bf16[144,512]{1,0:T(8,128)(2,1)}, bf16[144,512]{1,0:T(8,128)(2,1)S(1)}, u32[]{:S(2)}, u32[]{:S(2)}) collective-permute-start(bf16[144,512]{1,0:T(8,128)(2,1)} %get-tuple-element.42), channel_id=1, source_target_pairs={{4,0},{8,4},{12,8},{5,1},{9,5},{13,9},{6,2},{10,6},{14,10},{7,3},{... | collective-permute-start | bytes 442376 | tf_op jit(solution)/shard_map/ppermute | solution.py:700
  9.2 0.1 copy.15.refs_4_
  9.4 0.0 copy-start.7
  9.4 0.0 copy-start.8
  9.4 0.0 copy-start.9
  9.4 0.0 copy-start.10
  9.4 3.9 %to_planes.1 = (f32[5,16,64,128]{3,2,1,0:T(8,128)S(1)}, bf16[384,128]{1,0:T(8,128)(2,1)S(1)}) custom-call(s32[16]{0:T(128)S(1)} %copy-done.5, f32[4,64,512]{2,1,0:T(8,128)S(1)} %copy-done.2, f32[2,4,64,512]{3,2,1,0:T(8,128)S(1)} %copy-done, s32[64,512]{1,0:T(8,128)S(1)} %copy-done.3, bf16[16,64,512]{2,1,0:T(8,128)(2,1)S(1)} %copy-done.1, f32[16,16]{1,0:T(8,128)S(1)} %copy-done.4), custom_call_target="tpu_custom_call" | custom-call | flops 2000000000 | bytes 6291456 | tf_op jit(solution)/shard_map/to_planes/pallas_call | solution.py:762
  13.3 0.0 collective-permute-done.refs_0_
  13.3 2.0 %collective-permute-done.1.refs_1_ = bf16[144,512]{1,0:T(8,128)(2,1)S(1)} collective-permute-done((bf16[144,512]{1,0:T(8,128)(2,1)}, bf16[144,512]{1,0:T(8,128)(2,1)S(1)}, u32[]{:S(2)}, u32[]{:S(2)}) %collective-permute-start.1) | collective-permute-done | bytes 147488 | tf_op jit(solution)/shard_map/ppermute | solution.py:700
  15.3 0.3 rim.1.refs_10_
  15.6 1.6 %collective-permute-start.2 = (bf16[256,128]{1,0:T(8,128)(2,1)S(1)}, bf16[256,128]{1,0:T(8,128)(2,1)S(1)}, u32[]{:S(2)}, u32[]{:S(2)}) collective-permute-start(bf16[256,128]{1,0:T(8,128)(2,1)S(1)} %rim.1.refs_10_), channel_id=1, source_target_pairs={{0,16},{16,0},{1,17},{17,1},{2,18},{18,2},{3,19},{19,3},{4,20},{20... | collective-permute-start | bytes 196616 | tf_op jit(solution)/shard_map/ppermute | solution.py:695
  17.2 1.6 %prepare.1 = (f32[3,16,104,128]{3,2,1,0:T(8,128)S(1)}, f32[16,104,128]{2,1,0:T(8,128)S(1)}, f32[2,96,128]{2,1,0:T(8,128)S(1)}, f32[16,104,128]{2,1,0:T(8,128)S(1...) custom-call(bf16[144,512]{1,0:T(8,128)(2,1)S(1)} %collective-permute, ...), custom_call_target="tpu_custom_call" | custom-call | flops 1000000000 | bytes 4194304 | tf_op jit(solution)/shard_map/prepare/pallas_call | solution.py:789
  18.8 1.1 %collective-permute-done.2.refs_11_.refs_12_ = bf16[256,128]{1,0:T(8,128)(2,1)S(1)} collective-permute-done((bf16[256,128]{1,0:T(8,128)(2,1)S(1)}, bf16[256,128]{1,0:T(8,128)(2,1)S(1)}, u32[]{:S(2)}, u32[]{:S(2)}) %collective-permute-start.2) | collective-permute-done | bytes 65568 | tf_op jit(solution)/shard_map/ppermute | solution.py:695
  20.0 8.0 %flow_embed.1 = (f32[4,8,256]{2,1,0:T(8,128)S(1)}, f32[32,128,256]{2,1,0:T(8,128)S(1)}, f32[3,16,104,128]{3,2,1,0:T(8,128)S(1)}) custom-call(f32[3,16,104,128]{3,2,1,0:T(8,128)S(1)} %get-tuple-element.44.refs_0_, f32[16,104,128]{2,1,0:T(8,128)S(1)} %get-tuple-element.45.refs_1_, f32[2,96,128]{2,1,0:T(8,128)S(1)} %get-tuple-element.46.refs_2_, ...), custom_call_target="tpu_custom_call" | custom-call | tf_op jit(solution)/shard_map/flow_embed/pallas_call | solution.py:831
  28.0 1.6 %collective-permute-start.3 = (f32[32,256]{1,0:T(8,128)S(1)}, f32[32,256]{1,0:T(8,128)S(1)}, u32[]{:S(2)}, u32[]{:S(2)}) collective-permute-start(f32[32,256]{1,0:T(8,128)S(1)} %bitcast.9), channel_id=1, source_target_pairs={{0,16},{16,0},{1,17},{17,1},{2,18},{18,2},{3,19},{19,3},{4,20},{20... | collective-permute-start | bytes 98312 | tf_op jit(solution)/shard_map/ppermute | solution.py:705
  29.6 2.6 %from_planes.1 = (f32[4,64,512]{2,1,0:T(8,128)}, f32[2,4,64,512]{3,2,1,0:T(8,128)}) custom-call(f32[3,16,104,128]{3,2,1,0:T(8,128)S(1)} %get-tuple-element.56.refs_0_), custom_call_target="tpu_custom_call" | custom-call | flops 2000000000 | bytes 6291456 | tf_op jit(solution)/shard_map/from_planes/pallas_call | solution.py:863
  32.2 0.0 collective-permute-done.3.refs_1_
  32.2 1.4 %local_loss.1 = (f32[64,256]{1,0:T(8,128)S(1)}, f32[64,256]{1,0:T(8,128)S(1)}, f32[16,256]{1,0:T(8,128)}) custom-call(f32[32,256]{1,0:T(8,128)S(1)} %bitcast.10, f32[32,256]{1,0:T(8,128)S(1)} %collective-permute-done.3.refs_1_, f32[32,512]{1,0:T(8,128)S(1)} %get-tuple-element.62.refs_2_, f32[32,8]{1,0:T(8,128)S(1)} %get-tuple-element.63.refs_3_, ...), custom_call_target="tpu_custom_call" | custom-call | tf_op jit(solution)/shard_map/local_loss/pallas_call | solution.py:877
  33.5 0.1 collective-permute-start.4
  33.6 1.6 %collective-permute-start.10 = (f16[32,256]{1,0:T(8,128)(2,1)S(1)}, f16[32,256]{1,0:T(8,128)(2,1)S(1)}, u32[]{:S(2)}, u32[]{:S(2)}) collective-permute-start(f16[32,256]{1,0:T(8,128)(2,1)S(1)} %multiply_convert_fusion), channel_id=1, source_target_pairs={{0,2},{1,3},{2,0},{3,1},{4,6},{5,7},{6,4},{7,5},{8,10},{9,11},{10,... | collective-permute-start | bytes 49160 | tf_op jit(solution)/shard_map/ppermute | solution.py:705
  35.2 0.0 collective-permute-done.4
  35.2 1.4 %collective-permute-start.7 = (f32[64,256]{1,0:T(8,128)S(1)}, f32[64,256]{1,0:T(8,128)S(1)}, u32[]{:S(2)}, u32[]{:S(2)}) collective-permute-start(f32[64,256]{1,0:T(8,128)S(1)} %add.21), channel_id=1, source_target_pairs={{0,16},{16,0},{1,17},{17,1},{2,18},{18,2},{3,19},{19,3},{4,20},{20... | collective-permute-start | bytes 196616 | tf_op jit(solution)/shard_map/ppermute | solution.py:705
  36.6 1.2 %collective-permute-start.6 = (f32[64,256]{1,0:T(8,128)S(1)}, f32[64,256]{1,0:T(8,128)S(1)}, u32[]{:S(2)}, u32[]{:S(2)}) collective-permute-start(f32[64,256]{1,0:T(8,128)S(1)} %add.21), channel_id=1, source_target_pairs={{0,2},{1,3},{2,0},{3,1},{4,6},{5,7},{6,4},{7,5},{8,10},{9,11},{10,... | collective-permute-start | bytes 196616 | tf_op jit(solution)/shard_map/ppermute | solution.py:705
  37.8 1.0 %collective-permute-start.5 = (f32[64,256]{1,0:T(8,128)S(1)}, f32[64,256]{1,0:T(8,128)S(1)}, u32[]{:S(2)}, u32[]{:S(2)}) collective-permute-start(f32[64,256]{1,0:T(8,128)S(1)} %add.21), channel_id=1, source_target_pairs={{0,18},{1,19},{2,16},{3,17},{16,2},{17,3},{18,0},{19,1},{4,22},{5,... | collective-permute-start | bytes 196616 | tf_op jit(solution)/shard_map/ppermute | solution.py:895
  38.8 0.0 collective-permute-done.10
  38.8 0.8 %collective-permute-done.7 = f32[64,256]{1,0:T(8,128)S(1)} collective-permute-done((f32[64,256]{1,0:T(8,128)S(1)}, f32[64,256]{1,0:T(8,128)S(1)}, u32[]{:S(2)}, u32[]{:S(2)}) %collective-permute-start.7) | collective-permute-done | bytes 65568 | tf_op jit(solution)/shard_map/ppermute | solution.py:705
  39.6 2.6 %collective-permute-start.11 = (f16[64,256]{1,0:T(8,128)(2,1)S(1)}, f16[64,256]{1,0:T(8,128)(2,1)S(1)}, u32[]{:S(2)}, u32[]{:S(2)}) collective-permute-start(f16[64,256]{1,0:T(8,128)(2,1)S(1)} %pad_maximum_fusion.2), channel_id=1, source_target_pairs={{0,8},{4,12},{8,0},{12,4},{1,9},{5,13},{9,1},{13,5},{2,10},{6,14},... | collective-permute-start | bytes 98312 | tf_op jit(solution)/shard_map/ppermute | solution.py:705
  42.2 0.0 collective-permute-done.6
  42.2 0.8 %collective-permute-done.5 = f32[64,256]{1,0:T(8,128)S(1)} collective-permute-done((f32[64,256]{1,0:T(8,128)S(1)}, f32[64,256]{1,0:T(8,128)S(1)}, u32[]{:S(2)}, u32[]{:S(2)}) %collective-permute-start.5) | collective-permute-done | bytes 65568 | tf_op jit(solution)/shard_map/ppermute | solution.py:895
  42.9 2.6 %collective-permute-start.8 = (f32[64,256]{1,0:T(8,128)S(1)}, f32[64,256]{1,0:T(8,128)S(1)}, u32[]{:S(2)}, u32[]{:S(2)}) collective-permute-start(f32[64,256]{1,0:T(8,128)S(1)} %add_add_fusion), channel_id=1, source_target_pairs={{0,8},{4,12},{8,0},{12,4},{1,9},{5,13},{9,1},{13,5},{2,10},{6,14},... | collective-permute-start | bytes 196616 | tf_op jit(solution)/shard_map/ppermute | solution.py:705
  45.6 0.0 collective-permute-done.11
  45.6 0.7 %collective-permute-start.12 = (f16[128,256]{1,0:T(8,128)(2,1)S(1)}, f16[128,256]{1,0:T(8,128)(2,1)S(1)}, u32[]{:S(2)}, u32[]{:S(2)}) collective-permute-start(f16[128,256]{1,0:T(8,128)(2,1)S(1)} %pad_maximum_fusion.1), channel_id=1, source_target_pairs={{0,4},{4,0},{8,12},{12,8},{1,5},{5,1},{9,13},{13,9},{2,6},{6,2},{1... | collective-permute-start | bytes 196616 | tf_op jit(solution)/shard_map/ppermute | solution.py:705
  46.3 1.8 %collective-permute-done.8 = f32[64,256]{1,0:T(8,128)S(1)} collective-permute-done((f32[64,256]{1,0:T(8,128)S(1)}, f32[64,256]{1,0:T(8,128)S(1)}, u32[]{:S(2)}, u32[]{:S(2)}) %collective-permute-start.8) | collective-permute-done | bytes 65568 | tf_op jit(solution)/shard_map/ppermute | solution.py:705
  48.2 1.8 %collective-permute-done.12 = f16[128,256]{1,0:T(8,128)(2,1)S(1)} collective-permute-done((f16[128,256]{1,0:T(8,128)(2,1)S(1)}, f16[128,256]{1,0:T(8,128)(2,1)S(1)}, u32[]{:S(2)}, u32[]{:S(2)}) %collective-permute-start.12) | collective-permute-done | bytes 65568 | tf_op jit(solution)/shard_map/ppermute | solution.py:705
  50.0 0.1 collective-permute-start.13
  50.1 0.7 %collective-permute-start.9 = (f32[64,256]{1,0:T(8,128)S(1)}, f32[64,256]{1,0:T(8,128)S(1)}, u32[]{:S(2)}, u32[]{:S(2)}) collective-permute-start(f32[64,256]{1,0:T(8,128)S(1)} %add.25), channel_id=1, source_target_pairs={{0,4},{4,0},{8,12},{12,8},{1,5},{5,1},{9,13},{13,9},{2,6},{6,2},{1... | collective-permute-start | bytes 196616 | tf_op jit(solution)/shard_map/ppermute | solution.py:705
  50.8 0.6 %collective-permute-done.13 = f16[256,256]{1,0:T(8,128)(2,1)S(1)} collective-permute-done((f16[256,256]{1,0:T(8,128)(2,1)S(1)}, f16[256,256]{1,0:T(8,128)(2,1)S(1)}, u32[]{:S(2)}, u32[]{:S(2)}) %collective-permute-start.13) | collective-permute-done | bytes 131104 | tf_op jit(solution)/shard_map/ppermute | solution.py:705
  51.4 2.4 %couple_grads.1 = (f32[1128,128]{1,0:T(8,128)S(1)}, f32[1,128]{1,0:T(1,128)S(1)}) custom-call(f32[512,256]{1,0:T(8,128)S(1)} %maximum_convert_fusion.refs_0_, f32[16,512]{1,0:T(8,128)S(1)} %get-tuple-element.73.refs_1_, f32[16,16]{1,0:T(8,128)S(1)} %get-tuple-element.74.refs_2_, bf16[2,256,512]{2,1,0:T(8,128)(2,1)S(1)} %get-tuple-element.64.refs_4_.refs_3_, ...), custom_call_target="tpu_custom_call" | custom-call | flops 3000000000 | bytes 3145728 | tf_op jit(solution)/shard_map/couple_grads/pallas_call | solution.py:920
  53.9 0.7 %collective-permute-done.9 = f32[64,256]{1,0:T(8,128)S(1)} collective-permute-done((f32[64,256]{1,0:T(8,128)S(1)}, f32[64,256]{1,0:T(8,128)S(1)}, u32[]{:S(2)}, u32[]{:S(2)}) %collective-permute-start.9) | collective-permute-done | bytes 65568 | tf_op jit(solution)/shard_map/ppermute | solution.py:705
  54.6 0.1 collective-permute-start.14
  54.7 1.2 %collective-permute-done.14.refs_1_ = f32[64,256]{1,0:T(8,128)S(1)} collective-permute-done((f32[64,256]{1,0:T(8,128)S(1)}, f32[64,256]{1,0:T(8,128)S(1)}, u32[]{:S(2)}, u32[]{:S(2)}) %collective-permute-start.14) | collective-permute-done | bytes 65568 | tf_op jit(solution)/shard_map/ppermute | solution.py:705
  55.9 1.1 %finish.1 = f32[1384,128]{1,0:T(8,128)} custom-call(f32[64,256]{1,0:T(8,128)S(1)} %add.27.refs_0_, f32[64,256]{1,0:T(8,128)S(1)} %collective-permute-done.14.refs_1_, f32[1128,128]{1,0:T(8,128)S(1)} %get-tuple-element.75.refs_2_, f32[1,128]{1,0:T(1,128)S(1)} %get-tuple-element.76.refs_3_), custom_call_target="tpu_custom_call" | custom-call | tf_op jit(solution)/shard_map/finish/pallas_call | solution.py:937
  (23 shorter events, 0.2 us)
Async XLA Ops:
  0.6 8.6 %copy-start.5 = (s32[16]{0:T(128)S(1)}, s32[16]{0:T(128)}, u32[]{:S(2)}) copy-start(s32[16]{0:T(128)} %refs_0_.3) | copy-start | bytes 196
  0.6 8.7 %copy-start.4 = (f32[16,16]{1,0:T(8,128)S(1)}, f32[16,16]{1,0:T(8,128)}, u32[]{:S(2)}) copy-start(f32[16,16]{1,0:T(8,128)} %refs_5_.5) | copy-start | bytes 3076
  0.7 8.7 %copy-start.1 = (bf16[16,64,512]{2,1,0:T(8,128)(2,1)S(1)}, bf16[16,64,512]{2,1,0:T(8,128)(2,1)}, u32[]{:S(2)}) copy-start(bf16[16,64,512]{2,1,0:T(8,128)(2,1)} %refs_4_.3) | copy-start | bytes 3145732
  0.7 8.7 %copy-start.3 = (s32[64,512]{1,0:T(8,128)S(1)}, s32[64,512]{1,0:T(8,128)}, u32[]{:S(2)}) copy-start(s32[64,512]{1,0:T(8,128)} %refs_3_.4) | copy-start | bytes 393220
  0.7 8.7 %copy-start = (f32[2,4,64,512]{3,2,1,0:T(8,128)S(1)}, f32[2,4,64,512]{3,2,1,0:T(8,128)}, u32[]{:S(2)}) copy-start(f32[2,4,64,512]{3,2,1,0:T(8,128)} %refs_2_.3) | copy-start | bytes 3145732
  0.7 8.7 %copy-start.2 = (f32[4,64,512]{2,1,0:T(8,128)S(1)}, f32[4,64,512]{2,1,0:T(8,128)}, u32[]{:S(2)}) copy-start(f32[4,64,512]{2,1,0:T(8,128)} %refs_1_.3) | copy-start | bytes 1572868
  3.0 10.3 %collective-permute-start = (bf16[144,512]{1,0:T(8,128)(2,1)}, bf16[144,512]{1,0:T(8,128)(2,1)S(1)}, u32[]{:S(2)}, u32[]{:S(2)}) collective-permute-start(bf16[144,512]{1,0:T(8,128)(2,1)} %get-tuple-element.41), channel_id=1, source_target_pairs={{0,4},{4,8},{8,12},{1,5},{5,9},{9,13},{2,6},{6,10},{10,14},{3,7},{... | collective-permute-start | bytes 442376 | tf_op jit(solution)/shard_map/ppermute | solution.py:700
  7.9 7.4 %collective-permute-start.1 = (bf16[144,512]{1,0:T(8,128)(2,1)}, bf16[144,512]{1,0:T(8,128)(2,1)S(1)}, u32[]{:S(2)}, u32[]{:S(2)}) collective-permute-start(bf16[144,512]{1,0:T(8,128)(2,1)} %get-tuple-element.42), channel_id=1, source_target_pairs={{4,0},{8,4},{12,8},{5,1},{9,5},{13,9},{6,2},{10,6},{14,10},{7,3},{... | collective-permute-start | bytes 442376 | tf_op jit(solution)/shard_map/ppermute | solution.py:700
  9.4 7.8 %copy-start.7 = (f32[264,512]{1,0:T(8,128)S(1)}, f32[264,512]{1,0:T(8,128)}, u32[]{:S(2)}) copy-start(f32[264,512]{1,0:T(8,128)} %refs_6_.1) | copy-start | bytes 1622020
  9.4 7.8 %copy-start.8 = (bf16[128,256]{1,0:T(8,128)(2,1)S(1)}, bf16[128,256]{1,0:T(8,128)(2,1)}, u32[]{:S(2)}) copy-start(bf16[128,256]{1,0:T(8,128)(2,1)} %refs_3_.5) | copy-start | bytes 196612
  9.4 7.8 %copy-start.9 = (f32[512,16]{0,1:T(8,128)S(1)}, f32[512,16]{0,1:T(8,128)}, u32[]{:S(2)}) copy-start(f32[512,16]{0,1:T(8,128)} %param.20) | copy-start | bytes 98308
  9.4 7.8 %copy-start.10 = (f32[512]{0:T(512)S(1)}, f32[512]{0:T(512)}, u32[]{:S(2)}) copy-start(f32[512]{0:T(512)} %param.19) | copy-start | bytes 6148
  15.6 4.3 %collective-permute-start.2 = (bf16[256,128]{1,0:T(8,128)(2,1)S(1)}, bf16[256,128]{1,0:T(8,128)(2,1)S(1)}, u32[]{:S(2)}, u32[]{:S(2)}) collective-permute-start(bf16[256,128]{1,0:T(8,128)(2,1)S(1)} %rim.1.refs_10_), channel_id=1, source_target_pairs={{0,16},{16,0},{1,17},{17,1},{2,18},{18,2},{3,19},{19,3},{4,20},{20... | collective-permute-start | bytes 196616 | tf_op jit(solution)/shard_map/ppermute | solution.py:695
  28.0 4.2 %collective-permute-start.3 = (f32[32,256]{1,0:T(8,128)S(1)}, f32[32,256]{1,0:T(8,128)S(1)}, u32[]{:S(2)}, u32[]{:S(2)}) collective-permute-start(f32[32,256]{1,0:T(8,128)S(1)} %bitcast.9), channel_id=1, source_target_pairs={{0,16},{16,0},{1,17},{17,1},{2,18},{18,2},{3,19},{19,3},{4,20},{20... | collective-permute-start | bytes 98312 | tf_op jit(solution)/shard_map/ppermute | solution.py:705
  29.6 2.6 %copy-start.6 = (f32[16]{0:T(128)S(1)}, f32[16]{0:T(128)}, u32[]{:S(2)}) copy-start(f32[16]{0:T(128)} %param.21) | copy-start | bytes 196
  33.5 1.7 %collective-permute-start.4 = (f32[64,256]{1,0:T(8,128)S(1)}, f32[64,256]{1,0:T(8,128)S(1)}, u32[]{:S(2)}, u32[]{:S(2)}) collective-permute-start(f32[64,256]{1,0:T(8,128)S(1)} %get-tuple-element.69), channel_id=1, source_target_pairs={{0,1},{1,0},{2,3},{3,2},{4,5},{5,4},{6,7},{7,6},{8,9},{9,8},{10,11... | collective-permute-start | bytes 196616 | tf_op jit(solution)/shard_map/ppermute | solution.py:705
  33.6 5.2 %collective-permute-start.10 = (f16[32,256]{1,0:T(8,128)(2,1)S(1)}, f16[32,256]{1,0:T(8,128)(2,1)S(1)}, u32[]{:S(2)}, u32[]{:S(2)}) collective-permute-start(f16[32,256]{1,0:T(8,128)(2,1)S(1)} %multiply_convert_fusion), channel_id=1, source_target_pairs={{0,2},{1,3},{2,0},{3,1},{4,6},{5,7},{6,4},{7,5},{8,10},{9,11},{10,... | collective-permute-start | bytes 49160 | tf_op jit(solution)/shard_map/ppermute | solution.py:705
  35.2 4.3 %collective-permute-start.7 = (f32[64,256]{1,0:T(8,128)S(1)}, f32[64,256]{1,0:T(8,128)S(1)}, u32[]{:S(2)}, u32[]{:S(2)}) collective-permute-start(f32[64,256]{1,0:T(8,128)S(1)} %add.21), channel_id=1, source_target_pairs={{0,16},{16,0},{1,17},{17,1},{2,18},{18,2},{3,19},{19,3},{4,20},{20... | collective-permute-start | bytes 196616 | tf_op jit(solution)/shard_map/ppermute | solution.py:705
  36.6 5.6 %collective-permute-start.6 = (f32[64,256]{1,0:T(8,128)S(1)}, f32[64,256]{1,0:T(8,128)S(1)}, u32[]{:S(2)}, u32[]{:S(2)}) collective-permute-start(f32[64,256]{1,0:T(8,128)S(1)} %add.21), channel_id=1, source_target_pairs={{0,2},{1,3},{2,0},{3,1},{4,6},{5,7},{6,4},{7,5},{8,10},{9,11},{10,... | collective-permute-start | bytes 196616 | tf_op jit(solution)/shard_map/ppermute | solution.py:705
  37.8 5.2 %collective-permute-start.5 = (f32[64,256]{1,0:T(8,128)S(1)}, f32[64,256]{1,0:T(8,128)S(1)}, u32[]{:S(2)}, u32[]{:S(2)}) collective-permute-start(f32[64,256]{1,0:T(8,128)S(1)} %add.21), channel_id=1, source_target_pairs={{0,18},{1,19},{2,16},{3,17},{16,2},{17,3},{18,0},{19,1},{4,22},{5,... | collective-permute-start | bytes 196616 | tf_op jit(solution)/shard_map/ppermute | solution.py:895
  39.6 6.0 %collective-permute-start.11 = (f16[64,256]{1,0:T(8,128)(2,1)S(1)}, f16[64,256]{1,0:T(8,128)(2,1)S(1)}, u32[]{:S(2)}, u32[]{:S(2)}) collective-permute-start(f16[64,256]{1,0:T(8,128)(2,1)S(1)} %pad_maximum_fusion.2), channel_id=1, source_target_pairs={{0,8},{4,12},{8,0},{12,4},{1,9},{5,13},{9,1},{13,5},{2,10},{6,14},... | collective-permute-start | bytes 98312 | tf_op jit(solution)/shard_map/ppermute | solution.py:705
  42.9 5.2 %collective-permute-start.8 = (f32[64,256]{1,0:T(8,128)S(1)}, f32[64,256]{1,0:T(8,128)S(1)}, u32[]{:S(2)}, u32[]{:S(2)}) collective-permute-start(f32[64,256]{1,0:T(8,128)S(1)} %add_add_fusion), channel_id=1, source_target_pairs={{0,8},{4,12},{8,0},{12,4},{1,9},{5,13},{9,1},{13,5},{2,10},{6,14},... | collective-permute-start | bytes 196616 | tf_op jit(solution)/shard_map/ppermute | solution.py:705
  45.6 4.3 %collective-permute-start.12 = (f16[128,256]{1,0:T(8,128)(2,1)S(1)}, f16[128,256]{1,0:T(8,128)(2,1)S(1)}, u32[]{:S(2)}, u32[]{:S(2)}) collective-permute-start(f16[128,256]{1,0:T(8,128)(2,1)S(1)} %pad_maximum_fusion.1), channel_id=1, source_target_pairs={{0,4},{4,0},{8,12},{12,8},{1,5},{5,1},{9,13},{13,9},{2,6},{6,2},{1... | collective-permute-start | bytes 196616 | tf_op jit(solution)/shard_map/ppermute | solution.py:705
  50.0 1.4 %collective-permute-start.13 = (f16[256,256]{1,0:T(8,128)(2,1)S(1)}, f16[256,256]{1,0:T(8,128)(2,1)S(1)}, u32[]{:S(2)}, u32[]{:S(2)}) collective-permute-start(f16[256,256]{1,0:T(8,128)(2,1)S(1)} %pad_maximum_fusion), channel_id=1, source_target_pairs={{0,1},{1,0},{2,3},{3,2},{4,5},{5,4},{6,7},{7,6},{8,9},{9,8},{10,11... | collective-permute-start | bytes 393224 | tf_op jit(solution)/shard_map/ppermute | solution.py:705
  50.1 4.5 %collective-permute-start.9 = (f32[64,256]{1,0:T(8,128)S(1)}, f32[64,256]{1,0:T(8,128)S(1)}, u32[]{:S(2)}, u32[]{:S(2)}) collective-permute-start(f32[64,256]{1,0:T(8,128)S(1)} %add.25), channel_id=1, source_target_pairs={{0,4},{4,0},{8,12},{12,8},{1,5},{5,1},{9,13},{13,9},{2,6},{6,2},{1... | collective-permute-start | bytes 196616 | tf_op jit(solution)/shard_map/ppermute | solution.py:705
  54.6 1.3 %collective-permute-start.14 = (f32[64,256]{1,0:T(8,128)S(1)}, f32[64,256]{1,0:T(8,128)S(1)}, u32[]{:S(2)}, u32[]{:S(2)}) collective-permute-start(f32[64,256]{1,0:T(8,128)S(1)} %add.27.refs_0_), channel_id=1, source_target_pairs={{0,1},{1,0},{2,3},{3,2},{4,5},{5,4},{6,7},{7,6},{8,9},{9,8},{10,11... | collective-permute-start | bytes 196616 | tf_op jit(solution)/shard_map/ppermute | solution.py:705
